TPU v7x, 32 devices: a whole 2x2x4 slice. The times are simulated.
32 devices in a mesh: groups: 2 (over y), facex: 4 (over z), facey: 2 (over x), lev: 2 (over core).
Axes of the slice: x: 2, y: 2, z: 4, core: 2. Of those that a mesh axis runs over, the one named last changes fastest.
Arguments:
- tracer: float32 [8, 48, 64, 256], P('lev', 'groups', 'facex', 'facey'), parts along dimension 1, may hold values from -6 to 6
- west_courant: float32 [48, 64, 256], P('groups', 'facex', 'facey'), parts along dimension 0, may hold values from -0.24 to 0.24
- south_courant: float32 [48, 64, 256], P('groups', 'facex', 'facey'), parts along dimension 0, may hold values from -0.24 to 0.24
- mixing: float32 [46, 64, 256], P('groups', 'facex', 'facey'), parts along dimension 0, may hold values from 0.05 to 5
- adjoint_later: float32 [8, 48, 64, 256], P('lev', 'groups', 'facex', 'facey'), parts along dimension 1, may hold values from -6 to 6
- emission_scale: float32 [64, 256], P('facex', 'facey'), may hold values from 0.3 to 3
- send_cells: int32 [4, 2, 16, 32], P('facex', 'facey', 'groups'), parts along dimension 2, may hold values from 0 to 2047
- send_counts: int32 [4, 2, 16], P('facex', 'facey', 'groups'), parts along dimension 2, may hold values from 0 to 32, as said below
- kernels: float32 [4, 2, 16, 24, 32], P('facex', 'facey', 'groups'), parts along dimension 2, may hold values from 0.02 to 0.2
- observed: float32 [4, 2, 16, 32], P('facex', 'facey', 'groups'), parts along dimension 2, may hold values from -8 to 8
- error_weight: float32 [4, 2, 16, 32], P('facex', 'facey', 'groups'), parts along dimension 2, may hold values from 1 to 4
- regrid_index: int32 [4, 2, 16, 128], P('facex', 'facey'), may hold values from 0 to 2047, as said below
- regrid_weight: float32 [4, 2, 16, 128], P('facex', 'facey'), may hold values from 0.02 to 0.12
Outputs:
- advanced: float32 [8, 48, 64, 256], P('lev', 'groups', 'facex', 'facey'), parts along dimension 1
- gradient_latlon: float32 [8, 4, 2, 256], P('lev', 'facex', 'facey', 'groups'), parts along dimension 3
There are 2 independent parts, one for each index of `groups`. A program takes and returns all parts, laid end to end along the dimension named above; an argument that names none is the same for every part. Nothing has to cross between parts.
Inputs may be any that keep to these rules, and one draw needn't show every extreme that they name: `send_counts`: slots at and beyond the count are unused. In every draw one owner holds 32 soundings from every tile. `regrid_index`: x * 32 + r of a cell in the band of the lat-lon tile.
All inputs are finite; a program needn't handle non-finite values.
Results may differ from a plain program's by a relative error of at most 0.0003.
Values sent between devices are 32-bit elements; how exact they have to be, the bound alone decides.
No kernel may reach another device: no remote copies, remote signals or barrier semaphores. Data moves between devices by JAX's collectives and lax.ppermute only.
A program may use at most 128 MiB of HBM per device.

v0:
```python
import jax
import jax.numpy as jnp
from jax import lax
from jax.sharding import PartitionSpec as P


def with_halo(cells, sides, width):
    for axis, dim in sides:
        count = lax.axis_size(axis)
        head = lax.slice_in_dim(cells, 0, width, axis=dim)
        tail = lax.slice_in_dim(cells, cells.shape[dim] - width, cells.shape[dim], axis=dim)
        cells = jnp.concatenate(
            [
                lax.ppermute(tail, axis, [(i, (i + 1) % count) for i in range(count)]),
                cells,
                lax.ppermute(head, axis, [((i + 1) % count, i) for i in range(count)]),
            ],
            axis=dim,
        )
    return cells


def factor(mixing):
    levels = mixing.shape[0] + 1
    inverse = []
    upper_ratio = []
    for level_index in range(levels):
        diagonal = 1.0 + jnp.zeros_like(mixing[0])
        if level_index > 0:
            diagonal = diagonal + mixing[level_index - 1]
        if level_index < levels - 1:
            diagonal = diagonal + mixing[level_index]
        if level_index > 0:
            diagonal = (
                diagonal
                - mixing[level_index - 1] * mixing[level_index - 1] * inverse[level_index - 1]
            )
        inverse.append(1.0 / diagonal)
        if level_index < levels - 1:
            upper_ratio.append(-mixing[level_index] * inverse[level_index])
    return (inverse, upper_ratio)


def solve_column(source, mixing, inverse, upper_ratio):
    levels = len(inverse)
    forward = []
    for level_index in range(levels):
        running = source[:, level_index]
        if level_index > 0:
            running = running + mixing[level_index - 1] * forward[level_index - 1]
        forward.append(running * inverse[level_index])
    result = list(forward)
    for level_index in range(levels - 2, -1, -1):
        result[level_index] = (
            forward[level_index] - upper_ratio[level_index] * result[level_index + 1]
        )
    return jnp.stack(result, axis=1)


def advance(
    middle,
    west_side,
    east_side,
    south_side,
    north_side,
    west_courant,
    courant_east,
    south_courant,
    courant_north,
):
    flux_west = jnp.maximum(west_courant, 0.0) * west_side + jnp.minimum(west_courant, 0.0) * middle
    flux_east = jnp.maximum(courant_east, 0.0) * middle + jnp.minimum(courant_east, 0.0) * east_side
    flux_south = (
        jnp.maximum(south_courant, 0.0) * south_side + jnp.minimum(south_courant, 0.0) * middle
    )
    flux_north = (
        jnp.maximum(courant_north, 0.0) * middle + jnp.minimum(courant_north, 0.0) * north_side
    )
    return middle + flux_west - flux_east + flux_south - flux_north


def retreat(
    middle,
    west_side,
    east_side,
    south_side,
    north_side,
    west_courant,
    courant_east,
    south_courant,
    courant_north,
):
    along_x = (
        (jnp.minimum(west_courant, 0.0) - jnp.maximum(courant_east, 0.0)) * middle
        + jnp.maximum(courant_east, 0.0) * east_side
        - jnp.minimum(west_courant, 0.0) * west_side
    )
    along_y = (
        (jnp.minimum(south_courant, 0.0) - jnp.maximum(courant_north, 0.0)) * middle
        + jnp.maximum(courant_north, 0.0) * north_side
        - jnp.minimum(south_courant, 0.0) * south_side
    )
    return middle + along_x + along_y


def rimmed(values):
    padded = with_halo(values, (("facex", 2), ("facey", 3)), 1)
    position = lax.axis_index("facey")
    last_index = lax.axis_size("facey") - 1
    lower_rim = jnp.where(position == 0, 0.0, padded[..., :1])
    upper_rim = jnp.where(position == last_index, 0.0, padded[..., -1:])
    return jnp.concatenate([lower_rim, padded[..., 1:-1], upper_rim], axis=-1)


def pieces(padded):
    return (
        padded[..., 1:-1, 1:-1],
        padded[..., :-2, 1:-1],
        padded[..., 2:, 1:-1],
        padded[..., 1:-1, :-2],
        padded[..., 1:-1, 2:],
    )


def to_owners(values):
    return (
        lax.all_to_all(values[0], ("facex", "facey"), split_axis=0, concat_axis=0, tiled=True),
        lax.all_to_all(values[1], ("facex", "facey"), split_axis=0, concat_axis=0, tiled=True),
    )


def to_sources(values):
    return lax.all_to_all(values, ("facex", "facey"), split_axis=0, concat_axis=0, tiled=True)


def tracer_total(values):
    return lax.psum(values, "lev")


def weigh_residual(modeled, counts, observed, weights, slot_count):
    live = jnp.arange(slot_count)[None, :] < counts[:, None]
    return jnp.where(live, weights * (modeled - observed), 0.0)


def local(
    tracer,
    west_courant,
    south_courant,
    mixing,
    adjoint_later,
    emission_scale,
    send_cells,
    send_counts,
    kernels,
    observed,
    error_weight,
    regrid_index,
    regrid_weight,
):
    carried = tracer.shape[0]
    levels = tracer.shape[1]
    rows_here = tracer.shape[2]
    cols_here = tracer.shape[3]
    tiles_count = kernels.shape[2]
    slot_count = kernels.shape[4]
    inverse, upper_ratio = factor(mixing)
    stacked = jnp.concatenate([tracer, west_courant[None], south_courant[None]], axis=0)
    padded = rimmed(stacked)
    courant_east = padded[carried, :, 2:, 1:-1]
    courant_north = padded[carried + 1, :, 1:-1, 2:]
    middle, west_side, east_side, south_side, north_side = pieces(padded[:carried])
    upwinded = advance(
        middle,
        west_side,
        east_side,
        south_side,
        north_side,
        west_courant,
        courant_east,
        south_courant,
        courant_north,
    )
    advanced = solve_column(upwinded, mixing, inverse, upper_ratio)
    cell_ids = send_cells.reshape(-1)
    flat_field = advanced.reshape(carried, levels, rows_here * cols_here)
    picked = jnp.take(flat_field, cell_ids, axis=2).reshape(
        carried, levels, tiles_count, slot_count
    )
    column_total = jnp.sum(picked, axis=0).transpose(1, 0, 2)
    counts_here = send_counts.reshape(tiles_count)
    kernel_own = kernels.reshape(tiles_count, levels, slot_count)
    observed_own = observed.reshape(tiles_count, slot_count)
    weight_own = error_weight.reshape(tiles_count, slot_count)
    got_columns, got_counts = to_owners((column_total, counts_here))
    modeled = tracer_total(jnp.sum(kernel_own * got_columns, axis=1))
    weighted = weigh_residual(modeled, got_counts, observed_own, weight_own, slot_count)
    returned = to_sources(kernel_own * weighted[:, None, :])
    forcing = (
        jnp.zeros((levels, rows_here * cols_here), jnp.float32)
        .at[:, cell_ids]
        .add(returned.transpose(1, 0, 2).reshape(levels, -1))
    )
    forced = adjoint_later + forcing.reshape(levels, rows_here, cols_here)[None]
    smoothed = solve_column(forced, mixing, inverse, upper_ratio)
    middle, west_side, east_side, south_side, north_side = pieces(rimmed(smoothed))
    swept_back = retreat(
        middle,
        west_side,
        east_side,
        south_side,
        north_side,
        west_courant,
        courant_east,
        south_courant,
        courant_north,
    )
    surface = swept_back[:, 0] * emission_scale
    band_rows = lax.all_to_all(surface, "facex", split_axis=2, concat_axis=1, tiled=True)
    band_flat = band_rows.reshape(carried, -1)
    tap_count = regrid_index.shape[2]
    cell_count = regrid_index.shape[3]
    tap_ids = regrid_index.reshape(tap_count * cell_count)
    gathered = jnp.take(band_flat, tap_ids, axis=1).reshape(carried, tap_count, cell_count)
    latlon = jnp.sum(gathered * regrid_weight.reshape(1, tap_count, cell_count), axis=1)
    return (advanced, latlon[:, None, None, :])


def solution(mesh):
    in_specs = (
        P("lev", "groups", "facex", "facey"),
        P("groups", "facex", "facey"),
        P("groups", "facex", "facey"),
        P("groups", "facex", "facey"),
        P("lev", "groups", "facex", "facey"),
        P("facex", "facey"),
        P("facex", "facey", "groups", None),
        P("facex", "facey", "groups"),
        P("facex", "facey", "groups", None, None),
        P("facex", "facey", "groups", None),
        P("facex", "facey", "groups", None),
        P("facex", "facey", None, None),
        P("facex", "facey", None, None),
    )
    out_specs = (P("lev", "groups", "facex", "facey"), P("lev", "facex", "facey", "groups"))
    return jax.shard_map(local, mesh=mesh, in_specs=in_specs, out_specs=out_specs, check_vma=False)
```

profile of v0, /device:TPU:0, one launch (start us, length us, event | category | flops | bytes accessed | tf_op | source)
XLA Modules:
  0.0 141.1 jit_solution(11133697826532840864)
XLA Ops:
  0.7 1.4 %copy.121 = s32[8,1,1]{2,1,0:T(1,128)} copy(s32[8,1,1]{0,2,1:T(1,128)} %bitcast.306) | data formatting | bytes 64 | tf_op jit(solution)/shard_map/all_to_all | solution.py:128
  2.1 7.3 %all-to-all-start = ((s32[8,1,1]{2,1,0:T(1,128)}), s32[8,1,1]{2,1,0:T(1,128)S(1)}, u32[]{:S(2)}, u32[]{:S(2)}) async-start(s32[8,1,1]{2,1,0:T(1,128)} %copy.121), calls=%async_computation | async-start | bytes 8192 | tf_op jit(solution)/shard_map/all_to_all | solution.py:128
  9.4 1.4 %pad_maximum_fusion.22 = (f32[6,24,1,128]{3,2,1,0:T(1,128)S(1)}, f32[6,24,1,128]{3,2,1,0:T(1,128)S(1)}) fusion(f32[1,24,16,128]{3,2,1,0:T(8,128)} %bitcast.205, f32[1,24,16,128]{3,2,1,0:T(8,128)} %bitcast.209, f32[4,24,16,128]{3,2,1,0:T(8,128)} %param.13), kind=kLoop, calls=%fused_computation.107 | loop fusion | flops 73728 | bytes 1327104 | tf_op jit(solution)/shard_map/slice | solution.py:11
  10.8 2.1 %collective-permute-start = (f32[6,24,1,128]{3,2,1,0:T(1,128)S(1)}, f32[6,24,1,128]{3,2,1,0:T(1,128)S(1)}, u32[]{:S(2)}, u32[]{:S(2)}) collective-permute-start(f32[6,24,1,128]{3,2,1,0:T(1,128)S(1)} %get-tuple-element.121), channel_id=1, source_target_pairs={{0,4},{4,8},{8,12},{12,0},{1,5},{5,9},{9,13},{13,1},{2,6},{6,10},{... | collective-permute-start | bytes 221192 | tf_op jit(solution)/shard_map/ppermute | solution.py:14
  12.8 1.9 %collective-permute-start.1 = (f32[6,24,1,128]{3,2,1,0:T(1,128)S(1)}, f32[6,24,1,128]{3,2,1,0:T(1,128)S(1)}, u32[]{:S(2)}, u32[]{:S(2)}) collective-permute-start(f32[6,24,1,128]{3,2,1,0:T(1,128)S(1)} %get-tuple-element.122), channel_id=1, source_target_pairs={{4,0},{8,4},{12,8},{0,12},{5,1},{9,5},{13,9},{1,13},{6,2},{10,6},{... | collective-permute-start | bytes 221192 | tf_op jit(solution)/shard_map/ppermute | solution.py:16
  15.5 0.8 reshape.158
  16.3 1.3 compare_and_fusion
  18.8 1.3 multiply_bitcast_fusion.21
  20.2 1.3 multiply_bitcast_fusion.20
  21.5 1.3 multiply_bitcast_fusion.19
  22.8 1.3 multiply_bitcast_fusion.18
  24.1 1.3 multiply_bitcast_fusion.17
  25.5 1.3 multiply_bitcast_fusion.16
  26.8 1.3 multiply_bitcast_fusion.15
  28.1 1.3 multiply_bitcast_fusion.14
  29.4 1.3 multiply_bitcast_fusion.13
  40.4 1.8 %fusion.102 = (f32[6,24,18,1]{3,2,1,0:T(8,128)}, f32[6,24,18,1]{3,2,1,0:T(8,128)S(1)}) fusion(f32[6,24,18,128]{3,2,1,0:T(8,128)S(1)} %pad_maximum_fusion), kind=kLoop, calls=%fused_computation.352 | loop fusion | bytes 41472 | tf_op jit(solution)/shard_map/slice | solution.py:11
  42.2 2.2 %copy.117 = f32[6,24,18,1]{1,3,2,0:T(1,128)S(1)} copy(f32[6,24,18,1]{3,2,1,0:T(8,128)} %get-tuple-element.115) | data formatting | bytes 20736 | tf_op jit(solution)/shard_map/slice | solution.py:11
  44.4 2.0 %collective-permute-start.2 = (f32[6,24,18,1]{1,3,2,0:T(1,128)S(1)}, f32[6,24,18,1]{1,3,2,0:T(1,128)S(1)}, u32[]{:S(2)}, u32[]{:S(2)}) collective-permute-start(f32[6,24,18,1]{1,3,2,0:T(1,128)S(1)} %copy.117), channel_id=1, source_target_pairs={{0,2},{2,0},{1,3},{3,1},{4,6},{6,4},{5,7},{7,5},{8,10},{10,8},{9,1... | collective-permute-start | bytes 31112 | tf_op jit(solution)/shard_map/ppermute | solution.py:14
  48.5 1.9 %copy.118 = f32[6,24,18,1]{3,2,1,0:T(8,128)} copy(f32[6,24,18,1]{1,3,2,0:T(1,128)S(1)} %collective-permute-done.2) | data formatting | bytes 20736 | tf_op jit(solution)/shard_map/ppermute | solution.py:14
  50.6 2.0 %collective-permute-done.3 = f32[6,24,18,1]{1,3,2,0:T(1,128)S(1)} collective-permute-done((f32[6,24,18,1]{1,3,2,0:T(1,128)S(1)}, f32[6,24,18,1]{1,3,2,0:T(1,128)S(1)}, u32[]{:S(2)}, u32[]{:S(2)}) %collective-permute-start.3) | collective-permute-done | bytes 10400 | tf_op jit(solution)/shard_map/ppermute | solution.py:16
  52.6 1.9 %copy.120 = f32[6,24,18,1]{3,2,1,0:T(8,128)} copy(f32[6,24,18,1]{1,3,2,0:T(1,128)S(1)} %collective-permute-done.3) | data formatting | bytes 20736 | tf_op jit(solution)/shard_map/ppermute | solution.py:16
  54.5 1.6 %broadcast_select_fusion = f32[6,24,18,1]{3,2,1,0:T(8,128)S(1)} fusion(f32[6,24,18,1]{3,2,1,0:T(8,128)} %copy.120, pred[]{:T(512)S(6)} %eq.9), kind=kLoop, calls=%fused_computation.6 | loop fusion | flops 2592 | bytes 20737 | tf_op jit(solution)/shard_map/jit(_where)/select_n | solution.py:111
  56.1 1.0 fusion.15
  57.6 2.6 %fusion.2 = f32[4,24,16,128]{3,2,1,0:T(8,128)S(1)} fusion(f32[6,24,18,1]{3,2,1,0:T(8,128)S(1)} %broadcast_select_fusion, f32[6,24,1,128]{3,2,1,0:T(1,128)} %copy-done.8, f32[6,24,1,128]{3,2,1,0:T(1,128)} %copy-done.7, f32[1,24,16,128]{3,2,1,0:T(8,128)S(1)} %bitcast.208, f32[1,24,16,128]{3,2,1,0:T(8,128)S(1)} %bitcast.212, f32[4,24,16,128]{3,2,1,0:T(8,128)S(1)} %copy-done, ...), kind=kLoop, calls=%fused_computation.11 | loop fusion | flops 6291456 | bytes 3707136 | tf_op jit(solution)/shard_map/sub | solution.py:79
  60.6 1.1 fusion.56
  61.7 1.2 constant_dynamic-update-slice_fusion.23
  63.5 1.1 stack.129
  64.7 3.1 %copy.122 = f32[4,24,2048]{1,0,2:T(4,128)} copy(f32[4,24,2048]{2,1,0:T(8,128)S(1)} %stack.129) | data formatting | bytes 1572864 | tf_op jit(solution)/shard_map/stack | solution.py:57
  67.8 3.3 %gather_fusion = f32[256,4,24]{2,1,0:T(4,128)S(1)} fusion(f32[4,24,2048]{1,0,2:T(4,128)} %copy.122, s32[1024]{0:T(1024)} %pad_clamp_fusion), kind=kCustom, calls=%fused_computation | custom fusion | bytes 197632 | tf_op jit(solution)/shard_map/jit(_take)/gather | solution.py:186
  72.4 3.3 %all-to-all-start.1 = ((f32[8,1,768]{2,1,0:T(1,128)}), f32[8,1,768]{2,1,0:T(1,128)S(1)}, u32[]{:S(2)}, u32[]{:S(2)}) async-start(f32[8,1,768]{2,1,0:T(1,128)} %reshape.193), calls=%async_computation.1 | async-start | bytes 49152 | tf_op jit(solution)/shard_map/all_to_all | solution.py:127
  75.8 6.6 %all-to-all-done.1 = f32[8,1,768]{2,1,0:T(1,128)S(1)} async-done(((f32[8,1,768]{2,1,0:T(1,128)}), f32[8,1,768]{2,1,0:T(1,128)S(1)}, u32[]{:S(2)}, u32[]{:S(2)}) %all-to-all-start.1) | async-done | bytes 24608 | tf_op jit(solution)/shard_map/all_to_all | solution.py:127
  83.6 2.6 %psum.7 = f32[8,32]{1,0:T(8,128)S(1)} all-reduce(f32[8,32]{1,0:T(8,128)S(1)} %fusion.16), channel_id=1, replica_groups=mesh['groups'=2,'facex'=4,'facey'=2,'lev'=2] {'lev'}, use_global_device_ids=true, to_apply=%region_2.3 | all-reduce | flops 256 | bytes 2048 | tf_op jit(solution)/shard_map/psum | solution.py:137
  87.0 3.3 %all-to-all-start.2 = ((f32[8,1,768]{2,1,0:T(1,128)}), f32[8,1,768]{2,1,0:T(1,128)S(1)}, u32[]{:S(2)}, u32[]{:S(2)}) async-start(f32[8,1,768]{2,1,0:T(1,128)} %reshape.195), calls=%async_computation.2 | async-start | bytes 49152 | tf_op jit(solution)/shard_map/all_to_all | solution.py:133
  90.4 6.5 %all-to-all-done.2 = f32[8,1,768]{2,1,0:T(1,128)S(1)} async-done(((f32[8,1,768]{2,1,0:T(1,128)}), f32[8,1,768]{2,1,0:T(1,128)S(1)}, u32[]{:S(2)}, u32[]{:S(2)}) %all-to-all-start.2) | async-done | bytes 24608 | tf_op jit(solution)/shard_map/all_to_all | solution.py:133
  97.8 2.0 %scatter_custom_fusion = f32[24,2048]{0,1:T(8,128)S(1)} fusion(s32[256]{0:T(256)} %bitcast.305, f32[256,24]{1,0:T(8,128)S(1)} %copy.126, f32[]{:T(128)} %constant.14.clone.1), kind=kCustom, calls=%fused_computation.39 | custom fusion | flops 6144 | bytes 197120 | tf_op jit(solution)/shard_map/scatter-add | solution.py:201
  100.4 1.4 %constant_dynamic-update-slice_fusion.47 = (f32[4,24,16,128]{3,2,1,0:T(8,128)S(1)}, f32[4,1,16,128]{3,2,1,0:T(8,128)S(1)}, f32[4,1,16,128]{3,2,1,0:T(8,128)S(1)}...) fusion(f32[4,24,16,128]{3,2,1,0:T(8,128)S(1)} %broadcast_add_fu, ...), kind=kLoop, calls=%fused_computation.97 | loop fusion | flops 950271 | bytes 2113536
  102.9 3.4 %collective-permute-start.4 = (f32[4,24,1,128]{3,2,1,0:T(1,128)S(1)}, f32[4,24,1,128]{3,2,1,0:T(1,128)S(1)}, u32[]{:S(2)}, u32[]{:S(2)}) collective-permute-start(f32[4,24,1,128]{3,2,1,0:T(1,128)S(1)} %get-tuple-element.124), channel_id=1, source_target_pairs={{4,0},{8,4},{12,8},{0,12},{5,1},{9,5},{13,9},{1,13},{6,2},{10,6},{... | collective-permute-start | bytes 147464 | tf_op jit(solution)/shard_map/ppermute | solution.py:16
  106.9 1.4 %collective-permute-done.5 = f32[4,24,1,128]{3,2,1,0:T(1,128)S(1)} collective-permute-done((f32[4,24,1,128]{3,2,1,0:T(1,128)S(1)}, f32[4,24,1,128]{3,2,1,0:T(1,128)S(1)}, u32[]{:S(2)}, u32[]{:S(2)}) %collective-permute-start.5) | collective-permute-done | bytes 49184 | tf_op jit(solution)/shard_map/ppermute | solution.py:14
  110.2 1.1 copy.128
  111.8 1.4 constant_dynamic-update-slice_fusion.1
  116.5 1.6 %collective-permute-start.7 = (f32[4,24,18,1]{1,0,3,2:T(4,128)S(1)}, f32[4,24,18,1]{1,0,3,2:T(4,128)S(1)}, u32[]{:S(2)}, u32[]{:S(2)}) collective-permute-start(f32[4,24,18,1]{1,0,3,2:T(4,128)S(1)} %copy.130), channel_id=1, source_target_pairs={{0,2},{2,0},{1,3},{3,1},{4,6},{6,4},{5,7},{7,5},{8,10},{10,8},{9,1... | collective-permute-start | bytes 20744 | tf_op jit(solution)/shard_map/ppermute | solution.py:14
  118.6 1.9 %collective-permute-done.7 = f32[4,24,18,1]{1,0,3,2:T(4,128)S(1)} collective-permute-done((f32[4,24,18,1]{1,0,3,2:T(4,128)S(1)}, f32[4,24,18,1]{1,0,3,2:T(4,128)S(1)}, u32[]{:S(2)}, u32[]{:S(2)}) %collective-permute-start.7) | collective-permute-done | bytes 6944 | tf_op jit(solution)/shard_map/ppermute | solution.py:14
  121.4 0.8 reshape.197
  122.2 4.5 %all-to-all-start.3 = ((f32[4,1,2048]{2,1,0:T(1,128)}), f32[4,1,2048]{2,1,0:T(1,128)S(1)}, u32[]{:S(2)}, u32[]{:S(2)}) async-start(f32[4,1,2048]{2,1,0:T(1,128)} %reshape.197), calls=%async_computation.3 | async-start | bytes 65536 | tf_op jit(solution)/shard_map/all_to_all | solution.py:218
  127.3 5.0 %all-to-all-done.3 = f32[4,1,2048]{2,1,0:T(1,128)S(1)} async-done(((f32[4,1,2048]{2,1,0:T(1,128)}), f32[4,1,2048]{2,1,0:T(1,128)S(1)}, u32[]{:S(2)}, u32[]{:S(2)}) %all-to-all-start.3) | async-done | bytes 32800 | tf_op jit(solution)/shard_map/all_to_all | solution.py:218
  133.2 1.1 copy.133
  134.3 5.5 %gather_fusion.1 = f32[2048,4]{1,0:T(8,128)S(1)} fusion(f32[4,2048]{0,1:T(8,128)S(1)} %bitcast.214, s32[2048]{0:T(1024)S(1)} %copy-done.92), kind=kCustom, calls=%fused_computation.1 | custom fusion | bytes 73728 | tf_op jit(solution)/shard_map/jit(_take)/gather | solution.py:223
  (320 shorter events, 30.4 us)
Async XLA Ops:
  0.6 39.3 %copy-start = (f32[4,24,16,128]{3,2,1,0:T(8,128)S(1)}, f32[4,24,16,128]{3,2,1,0:T(8,128)}, u32[]{:S(2)}) copy-start(f32[4,24,16,128]{3,2,1,0:T(8,128)} %param.13) | copy-start | bytes 2359300
  0.6 39.3 %copy-start.1 = (f32[24,16,128]{2,1,0:T(8,128)S(1)}, f32[24,16,128]{2,1,0:T(8,128)}, u32[]{:S(2)}) copy-start(f32[24,16,128]{2,1,0:T(8,128)} %param.15) | copy-start | bytes 589828
  0.7 39.3 %copy-start.2 = (f32[24,16,128]{2,1,0:T(8,128)S(1)}, f32[24,16,128]{2,1,0:T(8,128)}, u32[]{:S(2)}) copy-start(f32[24,16,128]{2,1,0:T(8,128)} %param.14) | copy-start | bytes 589828
  0.7 30.1 %copy-start.3 = (f32[23,16,128]{2,1,0:T(8,128)S(1)}, f32[23,16,128]{2,1,0:T(8,128)}, u32[]{:S(2)}) copy-start(f32[23,16,128]{2,1,0:T(8,128)} %param.16) | copy-start | bytes 565252
  2.1 44.8 %all-to-all-start = ((s32[8,1,1]{2,1,0:T(1,128)}), s32[8,1,1]{2,1,0:T(1,128)S(1)}, u32[]{:S(2)}, u32[]{:S(2)}) async-start(s32[8,1,1]{2,1,0:T(1,128)} %copy.121), calls=%async_computation | async-start | bytes 8192 | tf_op jit(solution)/shard_map/all_to_all | solution.py:128
  10.8 29.2 %collective-permute-start = (f32[6,24,1,128]{3,2,1,0:T(1,128)S(1)}, f32[6,24,1,128]{3,2,1,0:T(1,128)S(1)}, u32[]{:S(2)}, u32[]{:S(2)}) collective-permute-start(f32[6,24,1,128]{3,2,1,0:T(1,128)S(1)} %get-tuple-element.121), channel_id=1, source_target_pairs={{0,4},{4,8},{8,12},{12,0},{1,5},{5,9},{9,13},{13,1},{2,6},{6,10},{... | collective-permute-start | bytes 221192 | tf_op jit(solution)/shard_map/ppermute | solution.py:14
  12.8 27.1 %collective-permute-start.1 = (f32[6,24,1,128]{3,2,1,0:T(1,128)S(1)}, f32[6,24,1,128]{3,2,1,0:T(1,128)S(1)}, u32[]{:S(2)}, u32[]{:S(2)}) collective-permute-start(f32[6,24,1,128]{3,2,1,0:T(1,128)S(1)} %get-tuple-element.122), channel_id=1, source_target_pairs={{4,0},{8,4},{12,8},{0,12},{5,1},{9,5},{13,9},{1,13},{6,2},{10,6},{... | collective-permute-start | bytes 221192 | tf_op jit(solution)/shard_map/ppermute | solution.py:16
  16.3 30.1 %copy-start.96 = (s32[256,1]{0,1:T(1,128)}, s32[256,1]{0,1:T(1,128)S(1)}, u32[]{:S(2)}) copy-start(s32[256,1]{0,1:T(1,128)S(1)} %compare_select_fusion.2) | copy-start | bytes 3076
  26.8 13.5 %copy-start.13 = (f32[1,16,128]{2,1,0:T(8,128)}, f32[1,16,128]{2,1,0:T(8,128)S(1)}, u32[]{:S(2)}) copy-start(f32[1,16,128]{2,1,0:T(8,128)S(1)} %get-tuple-element.71) | copy-start | bytes 24580
  29.4 10.9 %copy-start.15 = (f32[1,16,128]{2,1,0:T(8,128)}, f32[1,16,128]{2,1,0:T(8,128)S(1)}, u32[]{:S(2)}) copy-start(f32[1,16,128]{2,1,0:T(8,128)S(1)} %get-tuple-element.75) | copy-start | bytes 24580
  31.4 8.9 %copy-start.17 = (f32[1,16,128]{2,1,0:T(8,128)}, f32[1,16,128]{2,1,0:T(8,128)S(1)}, u32[]{:S(2)}) copy-start(f32[1,16,128]{2,1,0:T(8,128)S(1)} %get-tuple-element.79) | copy-start | bytes 24580
  32.6 7.7 %copy-start.19 = (f32[1,16,128]{2,1,0:T(8,128)}, f32[1,16,128]{2,1,0:T(8,128)S(1)}, u32[]{:S(2)}) copy-start(f32[1,16,128]{2,1,0:T(8,128)S(1)} %get-tuple-element.83) | copy-start | bytes 24580
  33.8 6.5 %copy-start.21 = (f32[1,16,128]{2,1,0:T(8,128)}, f32[1,16,128]{2,1,0:T(8,128)S(1)}, u32[]{:S(2)}) copy-start(f32[1,16,128]{2,1,0:T(8,128)S(1)} %get-tuple-element.87) | copy-start | bytes 24580
  35.0 5.3 %copy-start.23 = (f32[1,16,128]{2,1,0:T(8,128)}, f32[1,16,128]{2,1,0:T(8,128)S(1)}, u32[]{:S(2)}) copy-start(f32[1,16,128]{2,1,0:T(8,128)S(1)} %get-tuple-element.91) | copy-start | bytes 24580
  40.0 16.2 %copy-start.7 = (f32[6,24,1,128]{3,2,1,0:T(1,128)}, f32[6,24,1,128]{3,2,1,0:T(1,128)S(1)}, u32[]{:S(2)}) copy-start(f32[6,24,1,128]{3,2,1,0:T(1,128)S(1)} %collective-permute-done) | copy-start | bytes 221188
  40.0 16.1 %copy-start.8 = (f32[6,24,1,128]{3,2,1,0:T(1,128)}, f32[6,24,1,128]{3,2,1,0:T(1,128)S(1)}, u32[]{:S(2)}) copy-start(f32[6,24,1,128]{3,2,1,0:T(1,128)S(1)} %collective-permute-done.1) | copy-start | bytes 221188
  44.4 4.2 %collective-permute-start.2 = (f32[6,24,18,1]{1,3,2,0:T(1,128)S(1)}, f32[6,24,18,1]{1,3,2,0:T(1,128)S(1)}, u32[]{:S(2)}, u32[]{:S(2)}) collective-permute-start(f32[6,24,18,1]{1,3,2,0:T(1,128)S(1)} %copy.117), channel_id=1, source_target_pairs={{0,2},{2,0},{1,3},{3,1},{4,6},{6,4},{5,7},{7,5},{8,10},{10,8},{9,1... | collective-permute-start | bytes 31112 | tf_op jit(solution)/shard_map/ppermute | solution.py:14
  48.4 4.2 %collective-permute-start.3 = (f32[6,24,18,1]{1,3,2,0:T(1,128)S(1)}, f32[6,24,18,1]{1,3,2,0:T(1,128)S(1)}, u32[]{:S(2)}, u32[]{:S(2)}) collective-permute-start(f32[6,24,18,1]{1,3,2,0:T(1,128)S(1)} %copy.119), channel_id=1, source_target_pairs={{2,0},{0,2},{3,1},{1,3},{6,4},{4,6},{7,5},{5,7},{10,8},{8,10},{11,... | collective-permute-start | bytes 31112 | tf_op jit(solution)/shard_map/ppermute | solution.py:16
  57.5 4.1 %copy-start.30 = (f32[1,16,128]{2,1,0:T(8,128)S(1)}, f32[1,16,128]{2,1,0:T(8,128)}, u32[]{:S(2)}) copy-start(f32[1,16,128]{2,1,0:T(8,128)} %copy-done.29) | copy-start | bytes 24580
  57.5 4.1 %copy-start.47 = (f32[16,128]{1,0:T(8,128)S(1)}, f32[16,128]{1,0:T(8,128)}, u32[]{:S(2)}) copy-start(f32[16,128]{1,0:T(8,128)} %get-tuple-element.133) | copy-start | bytes 24580
  57.5 4.1 %copy-start.49 = (f32[16,128]{1,0:T(8,128)S(1)}, f32[16,128]{1,0:T(8,128)}, u32[]{:S(2)}) copy-start(f32[16,128]{1,0:T(8,128)} %get-tuple-element.134) | copy-start | bytes 24580
  57.5 4.1 %copy-start.51 = (f32[16,128]{1,0:T(8,128)S(1)}, f32[16,128]{1,0:T(8,128)}, u32[]{:S(2)}) copy-start(f32[16,128]{1,0:T(8,128)} %get-tuple-element.145) | copy-start | bytes 24580
  57.5 4.1 %copy-start.75 = (f32[16,128]{1,0:T(8,128)S(1)}, f32[16,128]{1,0:T(8,128)}, u32[]{:S(2)}) copy-start(f32[16,128]{1,0:T(8,128)} %get-tuple-element.100) | copy-start | bytes 24580
  57.6 4.1 %copy-start.77 = (f32[16,128]{1,0:T(8,128)S(1)}, f32[16,128]{1,0:T(8,128)}, u32[]{:S(2)}) copy-start(f32[16,128]{1,0:T(8,128)} %get-tuple-element.96) | copy-start | bytes 24580
  57.6 4.1 %copy-start.79 = (f32[16,128]{1,0:T(8,128)S(1)}, f32[16,128]{1,0:T(8,128)}, u32[]{:S(2)}) copy-start(f32[16,128]{1,0:T(8,128)} %get-tuple-element.92) | copy-start | bytes 24580
  57.6 4.1 %copy-start.81 = (f32[16,128]{1,0:T(8,128)S(1)}, f32[16,128]{1,0:T(8,128)}, u32[]{:S(2)}) copy-start(f32[16,128]{1,0:T(8,128)} %get-tuple-element.88) | copy-start | bytes 24580
  57.6 4.1 %copy-start.83 = (f32[16,128]{1,0:T(8,128)S(1)}, f32[16,128]{1,0:T(8,128)}, u32[]{:S(2)}) copy-start(f32[16,128]{1,0:T(8,128)} %get-tuple-element.80) | copy-start | bytes 24580
  64.7 6.5 %copy-start.101 = (pred[256]{0:T(512)(128)(4,1)S(1)}, pred[256]{0:T(512)(128)(4,1)}, u32[]{:S(2)}) copy-start(pred[256]{0:T(512)(128)(4,1)} %compare_and_fusion.1) | copy-start | bytes 772
  64.7 18.9 %copy-start.9 = (f32[1,1,8,24,32]{4,3,2,1,0:T(8,128)S(1)}, f32[1,1,8,24,32]{4,3,2,1,0:T(8,128)}, u32[]{:S(2)}) copy-start(f32[1,1,8,24,32]{4,3,2,1,0:T(8,128)} %param.21) | copy-start | bytes 73732
  64.7 21.5 %copy-start.97 = (f32[1,1,8,32]{3,2,1,0:T(8,128)S(1)}, f32[1,1,8,32]{3,2,1,0:T(8,128)}, u32[]{:S(2)}) copy-start(f32[1,1,8,32]{3,2,1,0:T(8,128)} %param.22) | copy-start | bytes 3076
  64.7 21.5 %copy-start.98 = (f32[1,1,8,32]{3,2,1,0:T(8,128)S(1)}, f32[1,1,8,32]{3,2,1,0:T(8,128)}, u32[]{:S(2)}) copy-start(f32[1,1,8,32]{3,2,1,0:T(8,128)} %param.23) | copy-start | bytes 3076
  64.7 21.5 %copy-start.99 = (s32[8]{0:T(128)S(1)}, s32[8]{0:T(128)}, u32[]{:S(2)}) copy-start(s32[8]{0:T(128)} %reduce.2) | copy-start | bytes 100
  72.4 9.9 %all-to-all-start.1 = ((f32[8,1,768]{2,1,0:T(1,128)}), f32[8,1,768]{2,1,0:T(1,128)S(1)}, u32[]{:S(2)}, u32[]{:S(2)}) async-start(f32[8,1,768]{2,1,0:T(1,128)} %reshape.193), calls=%async_computation.1 | async-start | bytes 49152 | tf_op jit(solution)/shard_map/all_to_all | solution.py:127
  83.5 16.6 %copy-start.6 = (f32[4,24,16,128]{3,2,1,0:T(8,128)S(1)}, f32[4,24,16,128]{3,2,1,0:T(8,128)}, u32[]{:S(2)}) copy-start(f32[4,24,16,128]{3,2,1,0:T(8,128)} %param.17) | copy-start | bytes 2359300
  87.0 9.9 %all-to-all-start.2 = ((f32[8,1,768]{2,1,0:T(1,128)}), f32[8,1,768]{2,1,0:T(1,128)S(1)}, u32[]{:S(2)}, u32[]{:S(2)}) async-start(f32[8,1,768]{2,1,0:T(1,128)} %reshape.195), calls=%async_computation.2 | async-start | bytes 49152 | tf_op jit(solution)/shard_map/all_to_all | solution.py:133
  90.3 9.8 %copy-start.100 = (f32[4,24,16,128]{3,2,1,0:T(8,128)}, f32[4,24,16,128]{3,2,1,0:T(8,128)S(1)}, u32[]{:S(2)}) copy-start(f32[4,24,16,128]{3,2,1,0:T(8,128)S(1)} %constant_dynamic-update-slice_fusion.3) | copy-start | bytes 2359300
  102.4 5.9 %collective-permute-start.5 = (f32[4,24,1,128]{3,2,1,0:T(1,128)S(1)}, f32[4,24,1,128]{3,2,1,0:T(1,128)S(1)}, u32[]{:S(2)}, u32[]{:S(2)}) collective-permute-start(f32[4,24,1,128]{3,2,1,0:T(1,128)S(1)} %get-tuple-element.123), channel_id=1, source_target_pairs={{0,4},{4,8},{8,12},{12,0},{1,5},{5,9},{9,13},{13,1},{2,6},{6,10},{... | collective-permute-start | bytes 147464 | tf_op jit(solution)/shard_map/ppermute | solution.py:14
  102.9 5.5 %collective-permute-start.4 = (f32[4,24,1,128]{3,2,1,0:T(1,128)S(1)}, f32[4,24,1,128]{3,2,1,0:T(1,128)S(1)}, u32[]{:S(2)}, u32[]{:S(2)}) collective-permute-start(f32[4,24,1,128]{3,2,1,0:T(1,128)S(1)} %get-tuple-element.124), channel_id=1, source_target_pairs={{4,0},{8,4},{12,8},{0,12},{5,1},{9,5},{13,9},{1,13},{6,2},{10,6},{... | collective-permute-start | bytes 147464 | tf_op jit(solution)/shard_map/ppermute | solution.py:16
  111.3 6.8 %collective-permute-start.6 = (f32[4,24,18,1]{1,0,3,2:T(4,128)}, f32[4,24,18,1]{1,0,3,2:T(4,128)S(1)}, u32[]{:S(2)}, u32[]{:S(2)}) collective-permute-start(f32[4,24,18,1]{1,0,3,2:T(4,128)} %copy.128), channel_id=1, source_target_pairs={{2,0},{0,2},{3,1},{1,3},{6,4},{4,6},{7,5},{5,7},{10,8},{8,10},{11,... | collective-permute-start | bytes 20744 | tf_op jit(solution)/shard_map/ppermute | solution.py:16
  116.0 5.1 %copy-start.33 = (f32[4,24,1,128]{3,2,1,0:T(1,128)S(1)}, f32[4,24,1,128]{3,2,1,0:T(1,128)}, u32[]{:S(2)}) copy-start(f32[4,24,1,128]{3,2,1,0:T(1,128)} %copy-done.32) | copy-start | bytes 147460
  116.0 5.1 %copy-start.35 = (f32[4,24,1,128]{3,2,1,0:T(1,128)S(1)}, f32[4,24,1,128]{3,2,1,0:T(1,128)}, u32[]{:S(2)}) copy-start(f32[4,24,1,128]{3,2,1,0:T(1,128)} %copy-done.34) | copy-start | bytes 147460
  116.0 5.1 %copy-start.93 = (f32[16,128]{1,0:T(8,128)S(1)}, f32[16,128]{1,0:T(8,128)}, u32[]{:S(2)}) copy-start(f32[16,128]{1,0:T(8,128)} %param.18) | copy-start | bytes 24580
  116.5 4.0 %collective-permute-start.7 = (f32[4,24,18,1]{1,0,3,2:T(4,128)S(1)}, f32[4,24,18,1]{1,0,3,2:T(4,128)S(1)}, u32[]{:S(2)}, u32[]{:S(2)}) collective-permute-start(f32[4,24,18,1]{1,0,3,2:T(4,128)S(1)} %copy.130), channel_id=1, source_target_pairs={{0,2},{2,0},{1,3},{3,1},{4,6},{6,4},{5,7},{7,5},{8,10},{10,8},{9,1... | collective-permute-start | bytes 20744 | tf_op jit(solution)/shard_map/ppermute | solution.py:14
  121.1 5.6 %copy-start.11 = (f32[4,1,16,128]{3,2,1,0:T(8,128)S(1)}, f32[4,1,16,128]{3,2,1,0:T(8,128)}, u32[]{:S(2)}) copy-start(f32[4,1,16,128]{3,2,1,0:T(8,128)} %copy-done.10) | copy-start | bytes 98308
  121.2 13.1 %copy-start.92 = (s32[2048]{0:T(1024)S(1)}, s32[2048]{0:T(1024)}, u32[]{:S(2)}) copy-start(s32[2048]{0:T(1024)} %broadcast_clamp_fusion) | copy-start | bytes 24580
  121.2 18.5 %copy-start.94 = (f32[1,1,16,128]{3,2,1,0:T(8,128)S(1)}, f32[1,1,16,128]{3,2,1,0:T(8,128)}, u32[]{:S(2)}) copy-start(f32[1,1,16,128]{3,2,1,0:T(8,128)} %param.25) | copy-start | bytes 24580
  121.2 18.5 %copy-start.95 = (pred[16,128]{1,0:T(8,128)(4,1)S(1)}, pred[16,128]{1,0:T(8,128)(4,1)}, u32[]{:S(2)}) copy-start(pred[16,128]{1,0:T(8,128)(4,1)} %compare_and_fusion) | copy-start | bytes 6148
  122.2 10.1 %all-to-all-start.3 = ((f32[4,1,2048]{2,1,0:T(1,128)}), f32[4,1,2048]{2,1,0:T(1,128)S(1)}, u32[]{:S(2)}, u32[]{:S(2)}) async-start(f32[4,1,2048]{2,1,0:T(1,128)} %reshape.197), calls=%async_computation.3 | async-start | bytes 65536 | tf_op jit(solution)/shard_map/all_to_all | solution.py:218
  (66 other events, 161.7 us)
where the time goes:
time: 143 us; the launch traced here: 141 us
  other arithmetic  41.3 us (29%)
  local copies, waits for them, and re-layouts  40.9 us (29%)
  starting transfers between devices  30.4 us (21%)
  waiting for transfers between devices  23.5 us (16%)
  blocking collectives  2.61 us (2%)
  between operations  2.51 us (2%)
    mul x22, other arithmetic, solve_column(): upper_ratio[level_index] * result[level_index + 1]  19.8 us
    unnamed x244, local copies, waits for them, and re-layouts  7.45 us
    all_to_all x1, starting transfers between devices, to_owners(): lax.all_to_all(values[1], ('facex', 'facey'), split_axis=0, concat_axis=0...  7.25 us
    all_to_all x1, waiting for transfers between devices, to_owners(): lax.all_to_all(values[0], ('facex', 'facey'), split_axis=0, concat_axis=0...  6.55 us
    all_to_all x1, waiting for transfers between devices, to_sources(): lax.all_to_all(values, ('facex', 'facey'), split_axis=0, concat_axis=0, t...  6.54 us
    ppermute x4, starting transfers between devices, with_halo(): lax.ppermute(tail, axis, [(i, (i + 1) % count) for i in range(count)])  6.11 us
    ppermute x4, starting transfers between devices, with_halo(): lax.ppermute(head, axis, [((i + 1) % count, i) for i in range(count)])  5.86 us
    gather x1, local copies, waits for them, and re-layouts, local(): jnp.take(band_flat, tap_ids, axis=1).reshape(carried, tap_count, cell_count)  5.47 us
  transfers between devices with their start and end apart: 12, of which 6 were waited for; matrix products, arithmetic and copies ran while one was open for 29% of the time, Pallas kernels for 0%

commit v1 on v0

v1 whole, which is shorter than its diff:
```python
import functools

import jax
import jax.numpy as jnp
from jax import lax
from jax.experimental import pallas as pl
from jax.experimental.pallas import tpu as pltpu
from jax.sharding import PartitionSpec as P

F32 = jnp.float32
BF16 = jnp.bfloat16
LANES = 128


def call(body, outs, ins, name, flops, smem=()):
    moved = sum(4 * a.size for a in ins) + sum(4 * o.size for o in outs)
    return pl.pallas_call(
        body,
        out_shape=outs,
        in_specs=[
            pl.BlockSpec(memory_space=pltpu.SMEM if i in smem else pltpu.VMEM)
            for i in range(len(ins))
        ],
        out_specs=[pl.BlockSpec(memory_space=pltpu.VMEM)] * len(outs),
        compiler_params=pltpu.CompilerParams(vmem_limit_bytes=40 << 20),
        cost_estimate=pl.CostEstimate(flops=flops, bytes_accessed=moved, transcendentals=0),
        name=name,
    )(*ins)


def shape(*dims, dtype=F32):
    return jax.ShapeDtypeStruct(dims, dtype)


def iota(dims, axis):
    return lax.broadcasted_iota(jnp.int32, dims, axis)


def halves(values):
    high = values.astype(BF16)
    return high, (values - high.astype(F32)).astype(BF16)


def tile_of(sizes):
    return lax.axis_index("facex") * sizes[1] + lax.axis_index("facey")


def is_even(axis):
    return lax.rem(lax.axis_index(axis), 2) == 0


def down(values):
    rolled = pltpu.roll(values, 1, 0)
    return jnp.where(iota(values.shape, 0) == 0, 0.0, rolled)


def up(values):
    rows = values.shape[0]
    rolled = pltpu.roll(values, rows - 1, 0)
    return jnp.where(iota(values.shape, 0) == rows - 1, 0.0, rolled)


def right(values):
    rolled = pltpu.roll(values, 1, 1)
    return jnp.where(iota(values.shape, 1) == 0, 0.0, rolled)


def left(values):
    lanes = values.shape[1]
    rolled = pltpu.roll(values, lanes - 1, 1)
    return jnp.where(iota(values.shape, 1) == lanes - 1, 0.0, rolled)


def inner_step(cells, west, south):
    flux_x = jnp.maximum(west, 0.0) * down(cells) + jnp.minimum(west, 0.0) * cells
    flux_y = jnp.maximum(south, 0.0) * right(cells) + jnp.minimum(south, 0.0) * cells
    return cells + flux_x - up(flux_x) + flux_y - left(flux_y)


def pack_kernel(sizes, plan, *refs):
    tracer, west, south, scale, kernels, observed, weights = refs[:7]
    rows_out = refs[7:9]
    lanes_out = refs[9 : 9 + plan["y_ops"]]
    own_out = refs[9 + plan["y_ops"]]
    block_outs = refs[10 + plan["y_ops"] :]
    carried, levels, cx, cy = tracer.shape
    me = tile_of(sizes)

    def block(offset):
        where_to = jnp.bitwise_xor(me, offset)
        mine = kernels[where_to]
        last = jnp.concatenate(
            [
                observed[pl.ds(where_to, 1), :],
                weights[pl.ds(where_to, 1), :],
                jnp.zeros((6, mine.shape[1]), F32),
            ],
            axis=0,
        )
        return jnp.concatenate([mine[8 * g : 8 * g + 8] for g in range(levels // 8)] + [last], axis=1)

    even_x = is_even("facex")
    head = (carried + 1) * levels
    for number, out in enumerate(rows_out):
        sends_last = even_x if number == 0 else jnp.logical_not(even_x)
        row = jnp.where(sends_last, cx - 1, 0)
        for level in range(levels):
            for t in range(carried):
                out[t * levels + level : t * levels + level + 1, :] = tracer[
                    t, level, pl.ds(row, 1), :
                ]
            out[carried * levels + level : carried * levels + level + 1, :] = west[
                level, pl.ds(row, 1), :
            ]
        out[head : head + 8, :] = jnp.broadcast_to(scale[pl.ds(row, 1), :], (8, cy))
        if plan["x_blocks"][number]:
            out[head + 8 : head + 16, :] = block(plan["x_blocks"][number])
    even_y = is_even("facey")
    lane = iota((cx, cy), 1)
    for number, out in enumerate(lanes_out):
        sends_last = even_y if number == 0 else jnp.logical_not(even_y)
        edge = jnp.where(sends_last, cy - 1, 0)
        packed = jnp.zeros((cx, cy), F32)
        for f in range(carried + 1):
            for level in range(levels):
                values = tracer[f, level] if f < carried else south[level]
                spot = f * levels + level
                moved = pltpu.roll(values, lax.rem(spot + cy - edge, cy), 1)
                packed = jnp.where(lane == spot, moved, packed)
        out[0:cx, :] = packed
        if number == 0:
            out[cx : cx + 8, :] = block(plan["y_block"])
    own_out[...] = block(0)
    first_core = lax.axis_index("lev") == 0
    for out, (for_first, for_second) in zip(block_outs, plan["pairs"]):
        out[...] = block(jnp.where(first_core, for_first, for_second))


def factor_kernel(sizes, *refs):
    (tracer, west, south, mixing, adjoint, cells, counts) = refs[:7]
    inverse_out, ratio_out, base_out, inner_out, columns_out, rows_out, picks_out, live_out = refs[7:]
    carried, levels, cx, cy = tracer.shape
    owners, cap = cells.shape
    slots = owners * cap
    me = tile_of(sizes)
    first = []
    before = None
    for level in range(levels):
        diagonal = jnp.ones((cx, cy), F32)
        if level > 0:
            diagonal = diagonal + mixing[level - 1]
        if level < levels - 1:
            diagonal = diagonal + mixing[level]
        if level > 0:
            diagonal = diagonal - mixing[level - 1] * mixing[level - 1] * before
        inverse = 1.0 / diagonal
        inverse_out[level] = inverse
        if level < levels - 1:
            ratio_out[level] = mixing[level] * inverse
        first.append(inverse if level == 0 else mixing[level - 1] * first[-1] * inverse)
        before = inverse
    weight = first
    for level in range(levels - 2, -1, -1):
        weight[level] = first[level] + ratio_out[level] * weight[level + 1]
    for t in range(carried):
        total = weight[0] * adjoint[t, 0]
        for level in range(1, levels):
            total = total + weight[level] * adjoint[t, level]
        base_out[t] = total
    for level in range(levels):
        total = tracer[0, level]
        for t in range(1, carried):
            total = total + tracer[t, level]
        inner_out[level] = inner_step(total, west[level], south[level])
    cell_parts = []
    live_parts = []
    slot = iota((1, cap), 1)
    for offset in range(owners):
        owner = jnp.bitwise_xor(me, offset)
        cell_parts.append(cells[pl.ds(owner, 1), :])
        live_parts.append(jnp.where(slot < counts[owner], 1.0, 0.0))
    cell = jnp.concatenate(cell_parts, axis=1)
    live_out[...] = jnp.concatenate(live_parts, axis=1)
    x_of = lax.div(cell, cy)
    y_of = lax.rem(cell, cy)
    in_row = jnp.where(iota((cx, slots), 0) == x_of, 1.0, 0.0)
    in_lane = jnp.where(iota((cy, slots), 0) == y_of, 1.0, 0.0).astype(BF16)
    rows_out[...] = in_row
    picks_out[...] = in_lane
    high, low = halves(jnp.concatenate(weight, axis=0))
    picked = jnp.dot(high, in_lane, preferred_element_type=F32)
    picked = picked + jnp.dot(low, in_lane, preferred_element_type=F32)
    for level in range(levels):
        part = picked[level * cx : (level + 1) * cx] * in_row
        columns_out[level : level + 1, :] = jnp.sum(part, axis=0, keepdims=True)


def sides(first, second):
    even_x = is_even("facex")
    return jnp.where(even_x, second, first), jnp.where(even_x, first, second)


def seam_lanes(number, sent, got, carried, levels):
    cy = sent.shape[1]
    spot = carried * levels
    lane = iota(sent.shape, 1)

    def spread(values):
        result = jnp.zeros_like(values)
        for t in range(carried):
            moved = pltpu.roll(values, (t * levels - spot) % cy, 1)
            inside = jnp.logical_and(lane >= t * levels, lane < (t + 1) * levels)
            result = jnp.where(inside, moved, result)
        return result

    even_y = is_even("facey")
    north = even_y if number == 0 else jnp.logical_not(even_y)
    beyond = spread(got)
    inside = spread(sent)
    to_north = -(jnp.maximum(beyond, 0.0) * sent + jnp.minimum(beyond, 0.0) * got)
    to_south = jnp.maximum(inside, 0.0) * got
    return jnp.where(north, to_north, to_south), jnp.where(north, cy - 1, 0)


def observe_kernel(sizes, plan, carried, *refs):
    refs = list(refs)
    inner, mixing, inverse, ratio, columns, in_row, in_lane, live = refs[:8]
    sent = refs[8:10]
    got = refs[10:12]
    refs = refs[12:]
    y_sent = refs[: plan["y_ops"]]
    y_got = refs[plan["y_ops"] : 2 * plan["y_ops"]]
    refs = refs[2 * plan["y_ops"] :]
    own = refs[0]
    n_pairs = len(plan["pairs"])
    pair_got = refs[1 : 1 + n_pairs]
    swapped = refs[1 + n_pairs] if n_pairs else None
    modeled_out, state_out = refs[-2:]
    levels, cx, cy = inner.shape
    slots = in_row.shape[1]
    head = (carried + 1) * levels

    def summed(rows):
        total = rows[0:levels]
        for t in range(1, carried):
            total = total + rows[t * levels : (t + 1) * levels]
        return total

    beyond_west, beyond_east = sides(got[0][0:head], got[1][0:head])
    at_west, at_east = sides(sent[0][0:head], sent[1][0:head])
    spot = carried * levels
    face_west = at_west[spot:head]
    face_east = beyond_east[spot:head]
    from_west = jnp.maximum(face_west, 0.0) * summed(beyond_west)
    from_east = -(
        jnp.maximum(face_east, 0.0) * summed(at_east) + jnp.minimum(face_east, 0.0) * summed(beyond_east)
    )
    lane_parts = []
    for number in range(plan["y_ops"]):
        part, spot_y = seam_lanes(number, y_sent[number][0:cx, :], y_got[number][0:cx, :], carried, levels)
        total = part
        for t in range(1, carried):
            total = total + pltpu.roll(part, (-t * levels) % cy, 1)
        lane_parts.append((total, spot_y))
    lane = iota((cx, cy), 1)
    row = iota((cx, cy), 0)
    forward = []
    for level in range(levels):
        value = inner[level]
        value = value + jnp.where(row == 0, from_west[level : level + 1], 0.0)
        value = value + jnp.where(row == cx - 1, from_east[level : level + 1], 0.0)
        for total, spot_y in lane_parts:
            moved = pltpu.roll(total, lax.rem(spot_y - level + cy, cy), 1)
            value = value + jnp.where(lane == spot_y, moved, 0.0)
        if level > 0:
            value = value + mixing[level - 1] * forward[-1]
        forward.append(value * inverse[level])
    result = forward
    for level in range(levels - 2, -1, -1):
        result[level] = forward[level] + ratio[level] * result[level + 1]
    high, low = halves(jnp.concatenate(result, axis=0))
    picks = in_lane[...]
    picked = jnp.dot(high, picks, preferred_element_type=F32)
    picked = picked + jnp.dot(low, picks, preferred_element_type=F32)

    blocks = {0: own[...], plan["y_block"]: y_got[0][cx : cx + 8, :]}
    for number in range(2):
        if plan["x_blocks"][number]:
            blocks[plan["x_blocks"][number]] = got[number][head + 8 : head + 16, :]
    first_core = lax.axis_index("lev") == 0
    for number, (for_first, for_second) in enumerate(plan["pairs"]):
        mine = pair_got[number][...]
        other = swapped[8 * number : 8 * number + 8, :]
        if for_first == for_second:
            blocks[for_first] = mine
        else:
            blocks[for_first] = jnp.where(first_core, mine, other)
            blocks[for_second] = jnp.where(first_core, other, mine)
    cap = slots // len(blocks)
    per_tile = LANES // cap
    group_of_lane = lax.div(iota((8, LANES), 1), cap)

    def gathered(group):
        tiles = []
        for start in range(0, len(blocks), per_tile):
            tile = jnp.zeros((8, LANES), F32)
            for a in range(per_tile):
                moved = pltpu.roll(blocks[start + a], (cap * (a - group)) % LANES, 1)
                tile = jnp.where(group_of_lane == a, moved, tile)
            tiles.append(tile)
        return jnp.concatenate(tiles, axis=1)

    groups = [gathered(g) for g in range(levels // 8)]
    last = gathered(levels // 8)
    total = jnp.zeros((cx, slots), F32)
    sensitivity = jnp.zeros((8, slots), F32)
    for g, kernel in enumerate(groups):
        sensitivity = sensitivity + kernel * columns[8 * g : 8 * g + 8, :]
        for l in range(8):
            level = 8 * g + l
            total = total + kernel[l : l + 1] * picked[level * cx : (level + 1) * cx]
    modeled_out[...] = jnp.sum(total * in_row[...], axis=0, keepdims=True)
    gain = jnp.sum(sensitivity, axis=0, keepdims=True) * last[1:2] * live[...]
    state_out[...] = jnp.concatenate([gain, last[0:1]], axis=0)


def force_kernel(plan, *refs):
    modeled, modeled_other, state, in_row, in_lane, base, base_other = refs[:7]
    near_out = refs[7]
    rim_outs = refs[8:]
    carried, cx, cy = base.shape
    misfit = modeled[...] + modeled_other[...] - state[1:2, :]
    force = state[0:1, :] * misfit
    high, low = halves(in_row[...] * force)
    picks = in_lane[...]
    dims = (((1,), (1,)), ((), ()))
    scattered = lax.dot_general(high, picks, dims, preferred_element_type=F32)
    scattered = scattered + lax.dot_general(low, picks, dims, preferred_element_type=F32)
    lane = iota((cx, cy), 1)
    even_y = is_even("facey")
    edges = []
    for number in range(len(rim_outs)):
        sends_last = even_y if number == 0 else jnp.logical_not(even_y)
        edges.append(jnp.where(sends_last, cy - 1, 0))
    rims = [jnp.zeros((cx, cy), F32) for _ in rim_outs]
    for t in range(2 * carried):
        values = scattered + (base[t] if t < carried else base_other[t - carried])
        near_out[t] = values
        for number, edge in enumerate(edges):
            moved = pltpu.roll(values, lax.rem(t + cy - edge, cy), 1)
            rims[number] = jnp.where(lane == t, moved, rims[number])
    for rim, out in zip(rims, rim_outs):
        out[...] = rim


def surface_kernel(sizes, plan, carried, levels, *refs):
    near, west, south, scale = refs[:4]
    got = refs[4:6]
    y_got = refs[6 : 6 + plan["y_ops"]]
    rims = refs[6 + plan["y_ops"] : 6 + 2 * plan["y_ops"]]
    outs = refs[6 + 2 * plan["y_ops"] :]
    tracers, cx, cy = near.shape
    band = cy // sizes[0]
    per_tile = min(tracers, LANES // band)
    spot = carried * levels
    head = (carried + 1) * levels
    lane = iota((cx, cy), 1)
    row = iota((cx, cy), 0)
    even_y = is_even("facey")
    face_west = west[...]
    face_south = south[...]
    scales = scale[...]
    beyond_west, beyond_east = sides(got[0][head : head + 1], got[1][head : head + 1])
    _, east_wind = sides(got[0][spot : spot + 1], got[1][spot : spot + 1])
    face_east = jnp.where(row == cx - 1, east_wind, pltpu.roll(face_west, cx - 1, 0))
    face_north = left(face_south)
    norths = []
    for number in range(plan["y_ops"]):
        norths.append(even_y if number == 0 else jnp.logical_not(even_y))
        moved = pltpu.roll(y_got[number][0:cx, :], cy - 1 - spot, 1)
        keep = jnp.logical_and(lane == cy - 1, norths[number])
        face_north = jnp.where(keep, moved, face_north)
    to_middle = 1.0 + jnp.minimum(face_west, 0.0) - jnp.maximum(face_east, 0.0)
    to_middle = scales * (to_middle + jnp.minimum(face_south, 0.0) - jnp.maximum(face_north, 0.0))
    to_east = jnp.where(row == cx - 1, 0.0, scales * jnp.maximum(face_east, 0.0))
    to_west = jnp.where(row == 0, 0.0, scales * jnp.minimum(face_west, 0.0))
    to_north = scales * jnp.maximum(face_north, 0.0)
    to_south = scales * jnp.minimum(face_south, 0.0)
    west_gain = beyond_west * jnp.maximum(face_west[0:1], 0.0)
    east_gain = -beyond_east * jnp.minimum(face_east[cx - 1 : cx], 0.0)
    filler = jnp.zeros((6, cy), F32)
    grown = []
    for t in range(tracers):
        values = near[t]
        north_side = left(values)
        south_side = right(values)
        for number in range(plan["y_ops"]):
            rim = rims[number][...]
            at_north = jnp.logical_and(lane == cy - 1, norths[number])
            at_south = jnp.logical_and(lane == 0, jnp.logical_not(norths[number]))
            north_side = jnp.where(at_north, pltpu.roll(rim, (cy - 1 - t) % cy, 1), north_side)
            south_side = jnp.where(at_south, pltpu.roll(rim, (-t) % cy, 1), south_side)
        swept = to_middle * values + to_east * pltpu.roll(values, cx - 1, 0) - to_west * pltpu.roll(values, 1, 0)
        swept = swept + to_north * north_side - to_south * south_side
        grown.append(
            jnp.concatenate(
                [swept, west_gain * values[0:1], east_gain * values[cx - 1 : cx], filler], axis=0
            )
        )
    rows = cx + 8
    group_of_lane = lax.div(iota((rows, cy), 1), band)
    first_core = lax.axis_index("lev") == 0
    place = lax.axis_index("facex")
    for out, (for_first, for_second) in zip(outs, plan["bands"]):
        offset = for_first if for_first == for_second else jnp.where(first_core, for_first, for_second)
        target = jnp.bitwise_xor(place, offset)
        count = carried if for_first == for_second else tracers
        for start in range(0, count, per_tile):
            tile = jnp.zeros((rows, cy), F32)
            for a in range(min(per_tile, count - start)):
                moved = pltpu.roll(grown[start + a], lax.rem(band * a + cy - band * target, cy), 1)
                tile = jnp.where(group_of_lane == a, moved, tile)
            out[start // per_tile * rows : (start // per_tile + 1) * rows, :] = tile


def regrid_kernel(sizes, plan, carried, cx, band, *refs):
    index, weight = refs[:2]
    blocks = refs[2:-1]
    out = refs[-1]
    taps, cells = index.shape
    tracers = 2 * carried
    rows = cx + 8
    per_tile = min(tracers, LANES // band)
    lane = iota((rows, LANES), 1)
    row = iota((rows, cells), 0)
    first_core = lax.axis_index("lev") == 0
    place = lax.axis_index("facex")
    around = sizes[0] * cx
    parts = []
    row_places = []
    for block, (for_first, for_second) in zip(blocks, plan["bands"]):
        offset = for_first if for_first == for_second else jnp.where(first_core, for_first, for_second)
        start = jnp.bitwise_xor(place, offset) * cx
        places = start + row
        places = jnp.where(row == cx, lax.rem(start + around - 1, around), places)
        places = jnp.where(row == cx + 1, lax.rem(start + cx, around), places)
        row_places.append(places)
        count = carried if for_first == for_second else tracers
        mine = []
        for t in range(count):
            tile = block[t // per_tile * rows : (t // per_tile + 1) * rows, :]
            a = t % per_tile
            values = tile if a == 0 else pltpu.roll(tile, (-band * a) % LANES, 1)
            high = values.astype(BF16).astype(F32)
            low = pltpu.roll(values - high, band, 1)
            both = jnp.where(lane < band, high, jnp.where(lane < 2 * band, low, 0.0))
            mine.append(both.astype(BF16))
        parts.append(mine)
    left_side = jnp.concatenate([jnp.concatenate(mine, axis=0) for mine in parts], axis=0)
    spread = iota((LANES, cells), 0)
    in_band = lax.rem(spread, band)
    used = spread < 2 * band
    totals = [[jnp.zeros((rows, cells), F32) for _ in mine] for mine in parts]
    for tap in range(taps):
        place_of = index[tap : tap + 1, :]
        column = lax.div(place_of, band)
        in_lane = lax.rem(place_of, band)
        picks = jnp.where(jnp.logical_and(in_band == in_lane, used), 1.0, 0.0).astype(BF16)
        picked = jnp.dot(left_side, picks, preferred_element_type=F32)
        at = 0
        for number, mine in enumerate(parts):
            chosen = jnp.where(row_places[number] == column, weight[tap : tap + 1, :], 0.0)
            for t in range(len(mine)):
                totals[number][t] = totals[number][t] + chosen * picked[at : at + rows]
                at += rows
    sums = [jnp.zeros((1, cells), F32) for _ in range(tracers)]
    for mine in totals:
        for t, total in enumerate(mine):
            sums[t] = sums[t] + jnp.sum(total, axis=0, keepdims=True)
    out[...] = jnp.concatenate(sums, axis=0)


def advance_kernel(plan, *refs):
    tracer, west, south, mixing, inverse, ratio = refs[:6]
    sent = refs[6:8]
    got = refs[8:10]
    y_sent = refs[10 : 10 + plan["y_ops"]]
    y_got = refs[10 + plan["y_ops"] : 10 + 2 * plan["y_ops"]]
    out = refs[-1]
    carried, levels, cx, cy = tracer.shape
    head = (carried + 1) * levels
    spot = carried * levels
    beyond_west, beyond_east = sides(got[0][0:head], got[1][0:head])
    at_west, at_east = sides(sent[0][0:head], sent[1][0:head])
    face_west = at_west[spot:head]
    face_east = beyond_east[spot:head]
    lane = iota((cx, cy), 1)
    row = iota((cx, cy), 0)
    seams = [
        seam_lanes(n, y_sent[n][0:cx, :], y_got[n][0:cx, :], carried, levels) for n in range(plan["y_ops"])
    ]
    for t in range(carried):
        part = slice(t * levels, (t + 1) * levels)
        from_west = jnp.maximum(face_west, 0.0) * beyond_west[part]
        from_east = -(
            jnp.maximum(face_east, 0.0) * at_east[part] + jnp.minimum(face_east, 0.0) * beyond_east[part]
        )
        result = []
        for level in range(levels):
            value = inner_step(tracer[t, level], west[level], south[level])
            value = value + jnp.where(row == 0, from_west[level : level + 1], 0.0)
            value = value + jnp.where(row == cx - 1, from_east[level : level + 1], 0.0)
            for packed, spot_y in seams:
                moved = pltpu.roll(packed, lax.rem(spot_y - (t * levels + level) + 2 * cy, cy), 1)
                value = value + jnp.where(lane == spot_y, moved, 0.0)
            if level > 0:
                value = value + mixing[level - 1] * result[-1]
            result.append(value * inverse[level])
        out[t, levels - 1] = result[-1]
        for level in range(levels - 2, -1, -1):
            result[level] = result[level] + ratio[level] * result[level + 1]
            out[t, level] = result[level]


GROUP = ("facex", "facey", "lev")


def exchange(values, sizes, rule):
    many_x, many_y, cores = sizes
    pairs = []
    for x in range(many_x):
        for y in range(many_y):
            for c in range(cores):
                to = rule(x, y, c)
                if to is not None:
                    pairs.append(((x * many_y + y) * cores + c, (to[0] * many_y + to[1]) * cores + to[2]))
    return lax.ppermute(values, GROUP, pairs)


def make_plan(sizes):
    many_x, many_y, _ = sizes
    tiles = many_x * many_y
    x_blocks = [many_y, (many_x - 1) * many_y if many_x == 4 else 0]
    taken = {0, 1, *x_blocks}
    rest = [d for d in range(tiles) if d not in taken]
    rest.sort(key=lambda d: (d // many_y != many_x // 2, d))
    pairs = [(rest[n], rest[min(n + 1, len(rest) - 1)]) for n in range(0, len(rest), 2)]
    others = list(range(many_x - 1, 1, -1))
    bands = [(0, 0), (1, 1)] + [(others[n], others[n + 1]) for n in range(0, len(others), 2)]
    return {
        "x_blocks": x_blocks,
        "y_block": 1,
        "y_ops": 1 if many_y == 2 else 2,
        "pairs": pairs,
        "bands": bands,
    }


def local(
    sizes,
    tracer,
    west_courant,
    south_courant,
    mixing,
    adjoint_later,
    emission_scale,
    send_cells,
    send_counts,
    kernels,
    observed,
    error_weight,
    regrid_index,
    regrid_weight,
):
    plan = make_plan(sizes)
    many_x, many_y, _ = sizes
    carried, levels, cx, cy = tracer.shape
    owners, cap = send_cells.shape[2:]
    slots = owners * cap
    taps, ll = regrid_index.shape[2:]
    head = (carried + 1) * levels
    y_ops = plan["y_ops"]
    band = cy // many_x

    def next_x(number):
        def rule(x, y, c):
            step = 1 if (x % 2 == 0) == (number == 0) else -1
            return ((x + step) % many_x, y, c)

        return rule

    def next_y(number):
        def rule(x, y, c):
            to = y + (1 if (y % 2 == 0) == (number == 0) else -1)
            return (x, to, c) if 0 <= to < many_y else None

        return rule

    def jump(for_first, for_second):
        def rule(x, y, c):
            d = for_first if c == 0 else for_second
            return (x ^ (d // many_y), y ^ (d % many_y), c)

        return rule

    def other_core(values):
        return exchange(values, sizes, lambda x, y, c: (x, y, 1 - c))

    row_shapes = [shape(head + (16 if plan["x_blocks"][n] else 8), cy) for n in range(2)]
    lane_shapes = [shape(cx + (8 if n == 0 else 0), cy) for n in range(y_ops)]
    packed = call(
        functools.partial(pack_kernel, sizes, plan),
        row_shapes + lane_shapes + [shape(8, LANES)] * (1 + len(plan["pairs"])),
        [
            tracer,
            west_courant,
            south_courant,
            emission_scale,
            kernels.reshape(owners, levels, cap),
            observed.reshape(owners, cap),
            error_weight.reshape(owners, cap),
        ],
        "pack",
        100000,
    )
    rows_sent = packed[:2]
    lanes_sent = packed[2 : 2 + y_ops]
    own_block = packed[2 + y_ops]
    pair_sent = packed[3 + y_ops :]
    rows_got = [exchange(rows_sent[n], sizes, next_x(n)) for n in range(2)]
    lanes_got = [exchange(lanes_sent[n], sizes, next_y(n)) for n in range(y_ops)]
    pair_got = [exchange(s, sizes, jump(*p)) for s, p in zip(pair_sent, plan["pairs"])]
    inverse, ratio, base, inner, columns, in_row, in_lane, live = call(
        functools.partial(factor_kernel, sizes),
        [
            shape(levels, cx, cy),
            shape(levels - 1, cx, cy),
            shape(carried, cx, cy),
            shape(levels, cx, cy),
            shape(levels, slots),
            shape(cx, slots),
            shape(cy, slots, dtype=BF16),
            shape(1, slots),
        ],
        [
            tracer,
            west_courant,
            south_courant,
            mixing,
            adjoint_later,
            send_cells.reshape(owners, cap),
            send_counts.reshape(owners),
        ],
        "factor",
        3000000,
        smem=(6,),
    )
    base_other = other_core(base)
    swapped = [other_core(jnp.concatenate(pair_got, axis=0))] if pair_got else []
    modeled, state = call(
        functools.partial(observe_kernel, sizes, plan, carried),
        [shape(1, slots), shape(2, slots)],
        [inner, mixing, inverse, ratio, columns, in_row, in_lane, live]
        + list(rows_sent)
        + rows_got
        + list(lanes_sent)
        + lanes_got
        + [own_block]
        + pair_got
        + swapped,
        "observe",
        2000000,
    )
    modeled_other = other_core(modeled)
    (advanced,) = call(
        functools.partial(advance_kernel, plan),
        [shape(*tracer.shape)],
        [tracer, west_courant, south_courant, mixing, inverse, ratio]
        + list(rows_sent)
        + rows_got
        + list(lanes_sent)
        + lanes_got,
        "advance",
        6000000,
    )
    near, *rims_sent = call(
        functools.partial(force_kernel, plan),
        [shape(2 * carried, cx, cy)] + [shape(cx, cy)] * y_ops,
        [modeled, modeled_other, state, in_row, in_lane, base, base_other],
        "force",
        200000,
    )
    rims_got = [exchange(rims_sent[n], sizes, next_y(n)) for n in range(y_ops)]
    per_tile = min(2 * carried, LANES // band)

    def band_shape(first, second):
        count = carried if first == second else 2 * carried
        return shape(-(-count // per_tile) * (cx + 8), cy)

    band_sent = call(
        functools.partial(surface_kernel, sizes, plan, carried, levels),
        [band_shape(*b) for b in plan["bands"]],
        [near, west_courant[0], south_courant[0], emission_scale] + rows_got + lanes_got + rims_got,
        "surface",
        400000,
    )
    band_got = [
        s if first == second == 0 else exchange(s, sizes, jump(first * many_y, second * many_y))
        for s, (first, second) in zip(band_sent, plan["bands"])
    ]
    (sums,) = call(
        functools.partial(regrid_kernel, sizes, plan, carried, cx, band),
        [shape(2 * carried, ll)],
        [regrid_index.reshape(taps, ll), regrid_weight.reshape(taps, ll)] + band_got,
        "regrid",
        1000000,
    )
    sums_other = other_core(sums[carried:])
    latlon = sums[:carried] + sums_other
    return (advanced, latlon[:, None, None, :])


def solution(mesh):
    in_specs = (
        P("lev", "groups", "facex", "facey"),
        P("groups", "facex", "facey"),
        P("groups", "facex", "facey"),
        P("groups", "facex", "facey"),
        P("lev", "groups", "facex", "facey"),
        P("facex", "facey"),
        P("facex", "facey", "groups", None),
        P("facex", "facey", "groups"),
        P("facex", "facey", "groups", None, None),
        P("facex", "facey", "groups", None),
        P("facex", "facey", "groups", None),
        P("facex", "facey", None, None),
        P("facex", "facey", None, None),
    )
    out_specs = (P("lev", "groups", "facex", "facey"), P("lev", "facex", "facey", "groups"))
    sizes = tuple(mesh.shape[axis] for axis in GROUP)
    return jax.shard_map(
        functools.partial(local, sizes), mesh=mesh, in_specs=in_specs, out_specs=out_specs, check_vma=False
    )
```

time: 143 us -> 40 us (0.28); the launches traced: 141 us -> 39.6 us
  other arithmetic: 41.3 us -> 0.58 us
  local copies, waits for them, and re-layouts: 40.9 us -> 6.62 us
  starting transfers between devices: 30.4 us -> 13.2 us
  waiting for transfers between devices: 23.5 us -> 9.51 us
  Pallas kernels: 0 us -> 8.9 us
  blocking collectives: 2.61 us -> 0 us
  between operations: 2.51 us -> 0.76 us
    mul x27 -> x0, other arithmetic: 21.8 us -> none  [the longest x22 19.8 us: solve_column(): upper_ratio[level_index] * result[level_index + 1]]
    all_to_all x4 -> x0, starting transfers between devices: 18.4 us -> none  [the longest x1 7.25 us: to_owners(): lax.all_to_all(values[1], ('facex', 'facey'), split_axis=0, concat_axis=0...]
    all_to_all x4 -> x0, waiting for transfers between devices: 18.1 us -> none  [the longest x1 6.55 us: to_owners(): lax.all_to_all(values[0], ('facex', 'facey'), split_axis=0, concat_axis=0...]
    slice x13 -> x1, local copies, waits for them, and re-layouts: 9.57 us -> 0.01 us  [local(): sums_other = other_core(sums[carried:])]
    pallas_call x0 -> x7, Pallas kernels: none -> 8.9 us  [call(): pl.pallas_call(body, out_shape=outs, in_specs=[pl.BlockSpec(memory_space=...]
    gather x2 -> x0, local copies, waits for them, and re-layouts: 8.8 us -> none  [the longest x1 5.47 us: local(): jnp.take(band_flat, tap_ids, axis=1).reshape(carried, tap_count, cell_count)]
    another operation x3 -> x0, local copies, waits for them, and re-layouts: 4.84 us -> none  [solve_column(): return jnp.stack(result, axis=1)]
    ppermute x8 -> x12, waiting for transfers between devices: 5.34 us -> 9.51 us  [exchange(): return lax.ppermute(values, GROUP, pairs)]
  transfers between devices with their start and end apart: 12 -> 12, of which waited for: 6 -> 5; matrix products, arithmetic and copies ran while one was open for 29% -> 0% of each run, Pallas kernels for 0% -> 18%
where the time goes in v1:
time: 40 us; the launch traced here: 39.6 us
  starting transfers between devices  13.2 us (33%)
  waiting for transfers between devices  9.51 us (24%)
  Pallas kernels  8.9 us (22%)
  local copies, waits for them, and re-layouts  6.62 us (17%)
  between operations  0.76 us (2%)
  other arithmetic  0.58 us (1%)
    ppermute x12, starting transfers between devices, exchange(): return lax.ppermute(values, GROUP, pairs)  13.2 us
    ppermute x12, waiting for transfers between devices, exchange(): return lax.ppermute(values, GROUP, pairs)  9.51 us
    pallas_call x7, Pallas kernels, call(): pl.pallas_call(body, out_shape=outs, in_specs=[pl.BlockSpec(memory_space=...  8.9 us
    unnamed x32, local copies, waits for them, and re-layouts  6.62 us
  transfers between devices with their start and end apart: 12, of which 5 were waited for; matrix products, arithmetic and copies ran while one was open for 0% of the time, Pallas kernels for 18%

profile of v1, /device:TPU:0, one launch (start us, length us, event | category | flops | bytes accessed | tf_op | source)
XLA Modules:
  0.0 39.6 jit_solution(5455470805108374743)
XLA Ops:
  0.6 0.0 copy-start.12
  0.6 0.7 %copy-done.12 = f32[1,1,8,32]{3,2,1,0:T(8,128)S(1)} copy-done((f32[1,1,8,32]{3,2,1,0:T(8,128)S(1)}, f32[1,1,8,32]{3,2,1,0:T(8,128)}, u32[]{:S(2)}) %copy-start.12) | copy-done | bytes 1048
  1.3 1.1 %copy-done = f32[4,24,16,128]{3,2,1,0:T(8,128)S(1)} copy-done((f32[4,24,16,128]{3,2,1,0:T(8,128)S(1)}, f32[4,24,16,128]{3,2,1,0:T(8,128)}, u32[]{:S(2)}) %copy-start) | copy-done | bytes 786456
  2.5 0.9 %copy-done.2 = f32[24,16,128]{2,1,0:T(8,128)S(1)} copy-done((f32[24,16,128]{2,1,0:T(8,128)S(1)}, f32[24,16,128]{2,1,0:T(8,128)}, u32[]{:S(2)}) %copy-start.2) | copy-done | bytes 196632
  3.4 0.9 %copy-done.4 = f32[24,16,128]{2,1,0:T(8,128)S(1)} copy-done((f32[24,16,128]{2,1,0:T(8,128)S(1)}, f32[24,16,128]{2,1,0:T(8,128)}, u32[]{:S(2)}) %copy-start.4) | copy-done | bytes 196632
  4.3 0.9 %copy-done.8 = f32[1,1,8,24,32]{4,3,2,1,0:T(8,128)S(1)} copy-done((f32[1,1,8,24,32]{4,3,2,1,0:T(8,128)S(1)}, f32[1,1,8,24,32]{4,3,2,1,0:T(8,128)}, u32[]{:S(2)}) %copy-start.8) | copy-done | bytes 24600
  5.2 0.7 %copy-done.9 = f32[16,128]{1,0:T(8,128)S(1)} copy-done((f32[16,128]{1,0:T(8,128)S(1)}, f32[16,128]{1,0:T(8,128)}, u32[]{:S(2)}) %copy-start.9) | copy-done | bytes 8216
  5.9 0.7 %copy-done.13 = f32[1,1,8,32]{3,2,1,0:T(8,128)S(1)} copy-done((f32[1,1,8,32]{3,2,1,0:T(8,128)S(1)}, f32[1,1,8,32]{3,2,1,0:T(8,128)}, u32[]{:S(2)}) %copy-start.13) | copy-done | bytes 1048
  6.6 0.4 %pack.1 = (f32[136,128]{1,0:T(8,128)S(1)}, f32[136,128]{1,0:T(8,128)S(1)}, f32[24,128]{1,0:T(8,128)S(1)}, f32[8,128]{1,0:T(8,128)S(1)}, f32[8,128]{1,0:T(8,128)S(1)}, /*index=5*/f32[8,128]{1,0:T(8,128)S(1)}) custom-call(f32[4,24,16,128]{3,2,1,0:T(8,128)S(1)} %copy-done, f32[24,16,128]{2,1,0:T(8,128)S(1)} %copy-done.2, f32[24,16,128]{2,1,0:T(8,128)S(1)} %copy-done.4, ...), custom_call_target="tpu_custom_call" | custom-call | flops 100000 | bytes 1378304 | tf_op jit(solution)/shard_map/pack/pallas_call | solution.py:17
  7.0 4.1 %collective-permute-start.3 = (f32[8,128]{1,0:T(8,128)S(1)}, f32[8,128]{1,0:T(8,128)S(1)}, u32[]{:S(2)}, u32[]{:S(2)}) collective-permute-start(f32[8,128]{1,0:T(8,128)S(1)} %get-tuple-element.34), channel_id=1, source_target_pairs={{0,8},{1,11},{2,10},{3,9},{4,12},{5,15},{6,14},{7,13},{8,0},{9,3},... | collective-permute-start | bytes 12296 | tf_op jit(solution)/shard_map/ppermute | solution.py:537
  11.1 2.5 %collective-permute-start.4 = (f32[8,128]{1,0:T(8,128)S(1)}, f32[8,128]{1,0:T(8,128)S(1)}, u32[]{:S(2)}, u32[]{:S(2)}) collective-permute-start(f32[8,128]{1,0:T(8,128)S(1)} %get-tuple-element.35), channel_id=1, source_target_pairs={{0,6},{1,15},{2,4},{3,13},{4,2},{5,11},{6,0},{7,9},{8,14},{9,7},{1... | collective-permute-start | bytes 12296 | tf_op jit(solution)/shard_map/ppermute | solution.py:537
  13.6 0.5 %collective-permute-start.2 = (f32[24,128]{1,0:T(8,128)S(1)}, f32[24,128]{1,0:T(8,128)S(1)}, u32[]{:S(2)}, u32[]{:S(2)}) collective-permute-start(f32[24,128]{1,0:T(8,128)S(1)} %get-tuple-element.27.refs_10_.refs_12_), channel_id=1, source_target_pairs={{0,2},{1,3},{2,0},{3,1},{4,6},{5,7},{6,4},{7,5},{8,10},{9,11},{10,... | collective-permute-start | bytes 36872 | tf_op jit(solution)/shard_map/ppermute | solution.py:537
  14.2 0.5 %collective-permute-start = (f32[136,128]{1,0:T(8,128)S(1)}, f32[136,128]{1,0:T(8,128)S(1)}, u32[]{:S(2)}, u32[]{:S(2)}) collective-permute-start(f32[136,128]{1,0:T(8,128)S(1)} %get-tuple-element.25.refs_6_.refs_8_), channel_id=1, source_target_pairs={{0,4},{1,5},{2,6},{3,7},{4,0},{5,1},{6,2},{7,3},{8,12},{9,13},{10,... | collective-permute-start | bytes 208904 | tf_op jit(solution)/shard_map/ppermute | solution.py:537
  14.6 1.3 %collective-permute-start.1 = (f32[136,128]{1,0:T(8,128)S(1)}, f32[136,128]{1,0:T(8,128)S(1)}, u32[]{:S(2)}, u32[]{:S(2)}) collective-permute-start(f32[136,128]{1,0:T(8,128)S(1)} %get-tuple-element.26.refs_7_.refs_9_), channel_id=1, source_target_pairs={{0,12},{1,13},{2,14},{3,15},{4,8},{5,9},{6,10},{7,11},{8,4},{9,5},... | collective-permute-start | bytes 208904 | tf_op jit(solution)/shard_map/ppermute | solution.py:537
  16.0 0.0 copy-done.6
  16.0 0.0 copy-done.7
  16.0 0.0 copy-done.14
  16.0 0.6 %copy-done.15 = s32[1,1,8]{2,1,0:T(1,128)S(1)} copy-done((s32[1,1,8]{2,1,0:T(1,128)S(1)}, s32[1,1,8]{2,1,0:T(1,128)}, u32[]{:S(2)}) %copy-start.15) | copy-done | bytes 56
  16.6 1.1 %factor.1 = (f32[24,16,128]{2,1,0:T(8,128)S(1)}, f32[23,16,128]{2,1,0:T(8,128)S(1)}, f32[4,16,128]{2,1,0:T(8,128)S(1)}, f32[24,16,128]{2,1,0:T(8,128)S(1)}, f32[...) custom-call(f32[4,24,16,128]{3,2,1,0:T(8,128)S(1)} %copy-done, ...), custom_call_target="tpu_custom_call" | custom-call | flops 3000000 | bytes 2943008 | tf_op jit(solution)/shard_map/factor/pallas_call | solution.py:17
  17.7 0.0 collective-permute-done.3.refs_15_
  17.8 0.6 %collective-permute-start.7 = (f32[4,16,128]{2,1,0:T(8,128)S(1)}, f32[4,16,128]{2,1,0:T(8,128)S(1)}, u32[]{:S(2)}, u32[]{:S(2)}) collective-permute-start(f32[4,16,128]{2,1,0:T(8,128)S(1)} %get-tuple-element.38.refs_5_), channel_id=1, source_target_pairs={{0,1},{1,0},{2,3},{3,2},{4,5},{5,4},{6,7},{7,6},{8,9},{9,8},{10,11... | collective-permute-start | bytes 98312 | tf_op jit(solution)/shard_map/ppermute | solution.py:537
  18.3 0.0 collective-permute-done.4.refs_16_
  18.3 0.1 collective-permute-start.5
  18.4 1.1 %collective-permute-done.5.refs_17_ = f32[16,128]{1,0:T(8,128)S(1)} collective-permute-done((f32[16,128]{1,0:T(8,128)S(1)}, f32[16,128]{1,0:T(8,128)S(1)}, u32[]{:S(2)}, u32[]{:S(2)}) %collective-permute-start.5) | collective-permute-done | bytes 8224 | tf_op jit(solution)/shard_map/ppermute | solution.py:537
  19.5 0.0 collective-permute-done.2.refs_11_.refs_13_.refs_6_
  19.5 0.0 collective-permute-done.refs_8_.refs_10_.refs_4_
  19.5 1.3 %collective-permute-done.1.refs_9_.refs_11_.refs_5_ = f32[136,128]{1,0:T(8,128)S(1)} collective-permute-done((f32[136,128]{1,0:T(8,128)S(1)}, f32[136,128]{1,0:T(8,128)S(1)}, u32[]{:S(2)}, u32[]{:S(2)}) %collective-permute-start.1) | collective-permute-done | bytes 69664 | tf_op jit(solution)/shard_map/ppermute | solution.py:537
  20.8 0.6 %observe.1 = (f32[1,256]{1,0:T(1,128)S(1)}, f32[2,256]{1,0:T(2,128)S(1)}) custom-call(f32[24,16,128]{2,1,0:T(8,128)S(1)} %get-tuple-element.28.refs_0_, f32[23,16,128]{2,1,0:T(8,128)S(1)} %copy-done.6, f32[24,16,128]{2,1,0:T(8,128)S(1)} %get-tuple-element.23.refs_4_.refs_2_, f32[23,16,128]{2,1,0:T(8,128)S(1)} %get-tuple-element.24.refs_5_.refs_3_, ...), custom_call_target="tpu_custom_call" | custom-call | flops 2000000 | bytes 1269760 | tf_op jit(solution)/shard_map/observe/pallas_call | solution.py:17
  21.4 0.1 collective-permute-start.6
  21.5 0.0 collective-permute-done.7.refs_6_
  21.5 1.1 %collective-permute-done.6.refs_1_ = f32[1,256]{1,0:T(1,128)S(1)} collective-permute-done((f32[1,256]{1,0:T(1,128)S(1)}, f32[1,256]{1,0:T(1,128)S(1)}, u32[]{:S(2)}, u32[]{:S(2)}) %collective-permute-start.6) | collective-permute-done | bytes 1056 | tf_op jit(solution)/shard_map/ppermute | solution.py:537
  22.6 0.2 force.1
  22.8 1.5 %collective-permute-start.8 = (f32[16,128]{1,0:T(8,128)S(1)}, f32[16,128]{1,0:T(8,128)S(1)}, u32[]{:S(2)}, u32[]{:S(2)}) collective-permute-start(f32[16,128]{1,0:T(8,128)S(1)} %get-tuple-element.40), channel_id=1, source_target_pairs={{0,2},{1,3},{2,0},{3,1},{4,6},{5,7},{6,4},{7,5},{8,10},{9,11},{10,... | collective-permute-start | bytes 24584 | tf_op jit(solution)/shard_map/ppermute | solution.py:537
  24.3 0.0 copy-done.3
  24.3 0.0 copy-done.5
  24.3 2.2 %collective-permute-done.8.refs_7_ = f32[16,128]{1,0:T(8,128)S(1)} collective-permute-done((f32[16,128]{1,0:T(8,128)S(1)}, f32[16,128]{1,0:T(8,128)S(1)}, u32[]{:S(2)}, u32[]{:S(2)}) %collective-permute-start.8) | collective-permute-done | bytes 8224 | tf_op jit(solution)/shard_map/ppermute | solution.py:537
  26.6 0.2 surface.1
  26.8 0.0 copy-start.10
  26.8 2.0 %collective-permute-start.10 = (f32[48,128]{1,0:T(8,128)S(1)}, f32[48,128]{1,0:T(8,128)S(1)}, u32[]{:S(2)}, u32[]{:S(2)}) collective-permute-start(f32[48,128]{1,0:T(8,128)S(1)} %get-tuple-element.43), channel_id=1, source_target_pairs={{0,12},{1,9},{2,14},{3,11},{4,8},{5,13},{6,10},{7,15},{8,4},{9,1},... | collective-permute-start | bytes 73736 | tf_op jit(solution)/shard_map/ppermute | solution.py:537
  28.8 0.0 collective-permute-start.9
  28.8 3.8 %collective-permute-done.9.refs_3_ = f32[24,128]{1,0:T(8,128)S(1)} collective-permute-done((f32[24,128]{1,0:T(8,128)S(1)}, f32[24,128]{1,0:T(8,128)S(1)}, u32[]{:S(2)}, u32[]{:S(2)}) %collective-permute-start.9) | collective-permute-done | bytes 12320 | tf_op jit(solution)/shard_map/ppermute | solution.py:537
  32.6 0.0 collective-permute-done.10.refs_4_
  32.6 0.0 copy-done.11
  32.6 0.7 %regrid.1 = f32[8,128]{1,0:T(8,128)S(1)} custom-call(s32[16,128]{1,0:T(8,128)S(1)} %bitcast.15, f32[16,128]{1,0:T(8,128)S(1)} %bitcast.16, f32[24,128]{1,0:T(8,128)S(1)} %get-tuple-element.41.refs_2_, f32[24,128]{1,0:T(8,128)S(1)} %collective-permute-done.9.refs_3_, f32[48,128]{1,0:T(8,128)S(1)} %collective-permute-done.10.refs_4_), custom_call_target="tpu_custom_call" | custom-call | flops 1000000 | bytes 69632 | tf_op jit(solution)/shard_map/regrid/pallas_call | solution.py:17
  33.4 0.1 collective-permute-start.11
  33.4 5.6 %advance.1 = f32[4,24,16,128]{3,2,1,0:T(8,128)} custom-call(f32[4,24,16,128]{3,2,1,0:T(8,128)S(1)} %copy-done.1, f32[24,16,128]{2,1,0:T(8,128)S(1)} %copy-done.3, f32[24,16,128]{2,1,0:T(8,128)S(1)} %copy-done.5, f32[23,16,128]{2,1,0:T(8,128)S(1)} %copy-done.6, f32[24,16,128]{2,1,0:T(8,128)S(1)} %get-tuple-element.23.refs_4_.refs_2_, ...), custom_call_target="tpu_custom_call" | custom-call | flops 6000000 | bytes 2842624 | tf_op jit(solution)/shard_map/advance/pallas_call | solution.py:17
  39.0 0.0 collective-permute-done.11
  39.0 0.6 %slice_add_fusion = f32[4,128]{1,0:T(4,128)} fusion(f32[4,128]{1,0:T(4,128)S(1)} %collective-permute-done.11, f32[8,128]{1,0:T(8,128)S(1)} %regrid.1), kind=kLoop, calls=%fused_computation.3 | loop fusion | flops 512 | bytes 6144 | tf_op jit(solution)/shard_map/add | solution.py:719
  (19 shorter events, 0.0 us)
Async XLA Ops:
  0.6 0.7 %copy-start.12 = (f32[1,1,8,32]{3,2,1,0:T(8,128)S(1)}, f32[1,1,8,32]{3,2,1,0:T(8,128)}, u32[]{:S(2)}) copy-start(f32[1,1,8,32]{3,2,1,0:T(8,128)} %param.22) | copy-start | bytes 3076
  1.3 1.1 %copy-start = (f32[4,24,16,128]{3,2,1,0:T(8,128)S(1)}, f32[4,24,16,128]{3,2,1,0:T(8,128)}, u32[]{:S(2)}) copy-start(f32[4,24,16,128]{3,2,1,0:T(8,128)} %refs_0_.5) | copy-start | bytes 2359300
  2.5 0.9 %copy-start.2 = (f32[24,16,128]{2,1,0:T(8,128)S(1)}, f32[24,16,128]{2,1,0:T(8,128)}, u32[]{:S(2)}) copy-start(f32[24,16,128]{2,1,0:T(8,128)} %refs_1_.6) | copy-start | bytes 589828
  3.4 0.9 %copy-start.4 = (f32[24,16,128]{2,1,0:T(8,128)S(1)}, f32[24,16,128]{2,1,0:T(8,128)}, u32[]{:S(2)}) copy-start(f32[24,16,128]{2,1,0:T(8,128)} %refs_2_.5) | copy-start | bytes 589828
  4.3 0.9 %copy-start.8 = (f32[1,1,8,24,32]{4,3,2,1,0:T(8,128)S(1)}, f32[1,1,8,24,32]{4,3,2,1,0:T(8,128)}, u32[]{:S(2)}) copy-start(f32[1,1,8,24,32]{4,3,2,1,0:T(8,128)} %param.21) | copy-start | bytes 73732
  5.2 0.7 %copy-start.9 = (f32[16,128]{1,0:T(8,128)S(1)}, f32[16,128]{1,0:T(8,128)}, u32[]{:S(2)}) copy-start(f32[16,128]{1,0:T(8,128)} %refs_3_.7) | copy-start | bytes 24580
  5.9 0.7 %copy-start.13 = (f32[1,1,8,32]{3,2,1,0:T(8,128)S(1)}, f32[1,1,8,32]{3,2,1,0:T(8,128)}, u32[]{:S(2)}) copy-start(f32[1,1,8,32]{3,2,1,0:T(8,128)} %param.23) | copy-start | bytes 3076
  6.6 9.4 %copy-start.6 = (f32[23,16,128]{2,1,0:T(8,128)S(1)}, f32[23,16,128]{2,1,0:T(8,128)}, u32[]{:S(2)}) copy-start(f32[23,16,128]{2,1,0:T(8,128)} %refs_1_.7) | copy-start | bytes 565252
  6.6 9.4 %copy-start.7 = (f32[4,24,16,128]{3,2,1,0:T(8,128)S(1)}, f32[4,24,16,128]{3,2,1,0:T(8,128)}, u32[]{:S(2)}) copy-start(f32[4,24,16,128]{3,2,1,0:T(8,128)} %refs_4_.1) | copy-start | bytes 2359300
  7.0 10.7 %collective-permute-start.3 = (f32[8,128]{1,0:T(8,128)S(1)}, f32[8,128]{1,0:T(8,128)S(1)}, u32[]{:S(2)}, u32[]{:S(2)}) collective-permute-start(f32[8,128]{1,0:T(8,128)S(1)} %get-tuple-element.34), channel_id=1, source_target_pairs={{0,8},{1,11},{2,10},{3,9},{4,12},{5,15},{6,14},{7,13},{8,0},{9,3},... | collective-permute-start | bytes 12296 | tf_op jit(solution)/shard_map/ppermute | solution.py:537
  11.1 7.2 %collective-permute-start.4 = (f32[8,128]{1,0:T(8,128)S(1)}, f32[8,128]{1,0:T(8,128)S(1)}, u32[]{:S(2)}, u32[]{:S(2)}) collective-permute-start(f32[8,128]{1,0:T(8,128)S(1)} %get-tuple-element.35), channel_id=1, source_target_pairs={{0,6},{1,15},{2,4},{3,13},{4,2},{5,11},{6,0},{7,9},{8,14},{9,7},{1... | collective-permute-start | bytes 12296 | tf_op jit(solution)/shard_map/ppermute | solution.py:537
  13.6 2.3 %copy-start.14 = (s32[1,1,8,32]{3,2,1,0:T(8,128)S(1)}, s32[1,1,8,32]{3,2,1,0:T(8,128)}, u32[]{:S(2)}) copy-start(s32[1,1,8,32]{3,2,1,0:T(8,128)} %param.19) | copy-start | bytes 3076
  13.6 5.9 %collective-permute-start.2 = (f32[24,128]{1,0:T(8,128)S(1)}, f32[24,128]{1,0:T(8,128)S(1)}, u32[]{:S(2)}, u32[]{:S(2)}) collective-permute-start(f32[24,128]{1,0:T(8,128)S(1)} %get-tuple-element.27.refs_10_.refs_12_), channel_id=1, source_target_pairs={{0,2},{1,3},{2,0},{3,1},{4,6},{5,7},{6,4},{7,5},{8,10},{9,11},{10,... | collective-permute-start | bytes 36872 | tf_op jit(solution)/shard_map/ppermute | solution.py:537
  14.2 5.3 %collective-permute-start = (f32[136,128]{1,0:T(8,128)S(1)}, f32[136,128]{1,0:T(8,128)S(1)}, u32[]{:S(2)}, u32[]{:S(2)}) collective-permute-start(f32[136,128]{1,0:T(8,128)S(1)} %get-tuple-element.25.refs_6_.refs_8_), channel_id=1, source_target_pairs={{0,4},{1,5},{2,6},{3,7},{4,0},{5,1},{6,2},{7,3},{8,12},{9,13},{10,... | collective-permute-start | bytes 208904 | tf_op jit(solution)/shard_map/ppermute | solution.py:537
  14.6 6.2 %collective-permute-start.1 = (f32[136,128]{1,0:T(8,128)S(1)}, f32[136,128]{1,0:T(8,128)S(1)}, u32[]{:S(2)}, u32[]{:S(2)}) collective-permute-start(f32[136,128]{1,0:T(8,128)S(1)} %get-tuple-element.26.refs_7_.refs_9_), channel_id=1, source_target_pairs={{0,12},{1,13},{2,14},{3,15},{4,8},{5,9},{6,10},{7,11},{8,4},{9,5},... | collective-permute-start | bytes 208904 | tf_op jit(solution)/shard_map/ppermute | solution.py:537
  16.0 0.7 %copy-start.15 = (s32[1,1,8]{2,1,0:T(1,128)S(1)}, s32[1,1,8]{2,1,0:T(1,128)}, u32[]{:S(2)}) copy-start(s32[1,1,8]{2,1,0:T(1,128)} %param.20) | copy-start | bytes 100
  17.8 3.7 %collective-permute-start.7 = (f32[4,16,128]{2,1,0:T(8,128)S(1)}, f32[4,16,128]{2,1,0:T(8,128)S(1)}, u32[]{:S(2)}, u32[]{:S(2)}) collective-permute-start(f32[4,16,128]{2,1,0:T(8,128)S(1)} %get-tuple-element.38.refs_5_), channel_id=1, source_target_pairs={{0,1},{1,0},{2,3},{3,2},{4,5},{5,4},{6,7},{7,6},{8,9},{9,8},{10,11... | collective-permute-start | bytes 98312 | tf_op jit(solution)/shard_map/ppermute | solution.py:537
  18.3 1.2 %collective-permute-start.5 = (f32[16,128]{1,0:T(8,128)S(1)}, f32[16,128]{1,0:T(8,128)S(1)}, u32[]{:S(2)}, u32[]{:S(2)}) collective-permute-start(f32[16,128]{1,0:T(8,128)S(1)} %pad_maximum_fusion), channel_id=1, source_target_pairs={{0,1},{1,0},{2,3},{3,2},{4,5},{5,4},{6,7},{7,6},{8,9},{9,8},{10,11... | collective-permute-start | bytes 24584 | tf_op jit(solution)/shard_map/ppermute | solution.py:537
  20.8 3.6 %copy-start.3 = (f32[24,16,128]{2,1,0:T(8,128)S(1)}, f32[24,16,128]{2,1,0:T(8,128)}, u32[]{:S(2)}) copy-start(f32[24,16,128]{2,1,0:T(8,128)} %refs_1_.6) | copy-start | bytes 589828
  20.8 3.6 %copy-start.5 = (f32[24,16,128]{2,1,0:T(8,128)S(1)}, f32[24,16,128]{2,1,0:T(8,128)}, u32[]{:S(2)}) copy-start(f32[24,16,128]{2,1,0:T(8,128)} %refs_2_.5) | copy-start | bytes 589828
  20.8 12.7 %copy-start.1 = (f32[4,24,16,128]{3,2,1,0:T(8,128)S(1)}, f32[4,24,16,128]{3,2,1,0:T(8,128)}, u32[]{:S(2)}) copy-start(f32[4,24,16,128]{3,2,1,0:T(8,128)} %refs_0_.5) | copy-start | bytes 2359300
  21.4 1.2 %collective-permute-start.6 = (f32[1,256]{1,0:T(1,128)S(1)}, f32[1,256]{1,0:T(1,128)S(1)}, u32[]{:S(2)}, u32[]{:S(2)}) collective-permute-start(f32[1,256]{1,0:T(1,128)S(1)} %get-tuple-element.36.refs_0_), channel_id=1, source_target_pairs={{0,1},{1,0},{2,3},{3,2},{4,5},{5,4},{6,7},{7,6},{8,9},{9,8},{10,11... | collective-permute-start | bytes 3080 | tf_op jit(solution)/shard_map/ppermute | solution.py:537
  22.8 3.7 %collective-permute-start.8 = (f32[16,128]{1,0:T(8,128)S(1)}, f32[16,128]{1,0:T(8,128)S(1)}, u32[]{:S(2)}, u32[]{:S(2)}) collective-permute-start(f32[16,128]{1,0:T(8,128)S(1)} %get-tuple-element.40), channel_id=1, source_target_pairs={{0,2},{1,3},{2,0},{3,1},{4,6},{5,7},{6,4},{7,5},{8,10},{9,11},{10,... | collective-permute-start | bytes 24584 | tf_op jit(solution)/shard_map/ppermute | solution.py:537
  26.6 6.0 %copy-start.11 = (f32[1,1,16,128]{3,2,1,0:T(8,128)S(1)}, f32[1,1,16,128]{3,2,1,0:T(8,128)}, u32[]{:S(2)}) copy-start(f32[1,1,16,128]{3,2,1,0:T(8,128)} %param.25) | copy-start | bytes 24580
  26.8 5.8 %copy-start.10 = (s32[1,1,16,128]{3,2,1,0:T(8,128)S(1)}, s32[1,1,16,128]{3,2,1,0:T(8,128)}, u32[]{:S(2)}) copy-start(s32[1,1,16,128]{3,2,1,0:T(8,128)} %param.24) | copy-start | bytes 24580
  26.8 5.8 %collective-permute-start.10 = (f32[48,128]{1,0:T(8,128)S(1)}, f32[48,128]{1,0:T(8,128)S(1)}, u32[]{:S(2)}, u32[]{:S(2)}) collective-permute-start(f32[48,128]{1,0:T(8,128)S(1)} %get-tuple-element.43), channel_id=1, source_target_pairs={{0,12},{1,9},{2,14},{3,11},{4,8},{5,13},{6,10},{7,15},{8,4},{9,1},... | collective-permute-start | bytes 73736 | tf_op jit(solution)/shard_map/ppermute | solution.py:537
  28.8 3.8 %collective-permute-start.9 = (f32[24,128]{1,0:T(8,128)S(1)}, f32[24,128]{1,0:T(8,128)S(1)}, u32[]{:S(2)}, u32[]{:S(2)}) collective-permute-start(f32[24,128]{1,0:T(8,128)S(1)} %get-tuple-element.42), channel_id=1, source_target_pairs={{0,4},{1,5},{2,6},{3,7},{4,0},{5,1},{6,2},{7,3},{8,12},{9,13},{10,... | collective-permute-start | bytes 36872 | tf_op jit(solution)/shard_map/ppermute | solution.py:537
  33.4 5.7 %collective-permute-start.11 = (f32[4,128]{1,0:T(4,128)S(1)}, f32[4,128]{1,0:T(4,128)S(1)}, u32[]{:S(2)}, u32[]{:S(2)}) collective-permute-start(f32[4,128]{1,0:T(4,128)S(1)} %slice.15), channel_id=1, source_target_pairs={{0,1},{1,0},{2,3},{3,2},{4,5},{5,4},{6,7},{7,6},{8,9},{9,8},{10,11... | collective-permute-start | bytes 6152 | tf_op jit(solution)/shard_map/ppermute | solution.py:537

commit v2 on v1

--- a/solution.py
+++ b/solution.py
@@ -12,16 +12,21 @@
 LANES = 128
 
 
-def call(body, outs, ins, name, flops, smem=()):
+def call(body, outs, ins, name, flops, smem=(), hbm=(), scratch=(), out_hbm=()):
     moved = sum(4 * a.size for a in ins) + sum(4 * o.size for o in outs)
+    ins = [pltpu.with_memory_space_constraint(a, pltpu.HBM) if i in hbm else a for i, a in enumerate(ins)]
+
+    def space(number):
+        return pltpu.SMEM if number in smem else pltpu.HBM if number in hbm else pltpu.VMEM
+
     return pl.pallas_call(
         body,
         out_shape=outs,
-        in_specs=[
-            pl.BlockSpec(memory_space=pltpu.SMEM if i in smem else pltpu.VMEM)
-            for i in range(len(ins))
+        in_specs=[pl.BlockSpec(memory_space=space(i)) for i in range(len(ins))],
+        out_specs=[
+            pl.BlockSpec(memory_space=pltpu.HBM if i in out_hbm else pltpu.VMEM) for i in range(len(outs))
         ],
-        out_specs=[pl.BlockSpec(memory_space=pltpu.VMEM)] * len(outs),
+        scratch_shapes=scratch,
         compiler_params=pltpu.CompilerParams(vmem_limit_bytes=40 << 20),
         cost_estimate=pl.CostEstimate(flops=flops, bytes_accessed=moved, transcendentals=0),
         name=name,
@@ -49,11 +54,6 @@
     return lax.rem(lax.axis_index(axis), 2) == 0
 
 
-def down(values):
-    rolled = pltpu.roll(values, 1, 0)
-    return jnp.where(iota(values.shape, 0) == 0, 0.0, rolled)
-
-
 def up(values):
     rows = values.shape[0]
     rolled = pltpu.roll(values, rows - 1, 0)
@@ -71,20 +71,47 @@
     return jnp.where(iota(values.shape, 1) == lanes - 1, 0.0, rolled)
 
 
-def inner_step(cells, west, south):
-    flux_x = jnp.maximum(west, 0.0) * down(cells) + jnp.minimum(west, 0.0) * cells
-    flux_y = jnp.maximum(south, 0.0) * right(cells) + jnp.minimum(south, 0.0) * cells
-    return cells + flux_x - up(flux_x) + flux_y - left(flux_y)
+def shares(west, south):
+    east, north = up(west), left(south)
+    middle = 1.0 + jnp.minimum(west, 0.0) - jnp.maximum(east, 0.0)
+    middle = middle + jnp.minimum(south, 0.0) - jnp.maximum(north, 0.0)
+    row, lane = iota(west.shape, 0), iota(west.shape, 1)
+    return (
+        middle,
+        jnp.where(row == 0, 0.0, jnp.maximum(west, 0.0)),
+        -jnp.minimum(east, 0.0),
+        jnp.where(lane == 0, 0.0, jnp.maximum(south, 0.0)),
+        -jnp.minimum(north, 0.0),
+    )
+
+
+def mix(parts, cells):
+    rows, lanes = cells.shape
+    middle, west, east, south, north = parts
+    total = middle * cells + west * pltpu.roll(cells, 1, 0) + east * pltpu.roll(cells, rows - 1, 0)
+    return total + south * pltpu.roll(cells, 1, 1) + north * pltpu.roll(cells, lanes - 1, 1)
 
 
 def pack_kernel(sizes, plan, *refs):
-    tracer, west, south, scale, kernels, observed, weights = refs[:7]
-    rows_out = refs[7:9]
-    lanes_out = refs[9 : 9 + plan["y_ops"]]
-    own_out = refs[9 + plan["y_ops"]]
-    block_outs = refs[10 + plan["y_ops"] :]
+    sources, refs = refs[:9], refs[9:]
+    rows_out, refs = refs[:2], refs[2:]
+    lanes_out, refs = refs[: plan["y_ops"]], refs[plan["y_ops"] :]
+    own_out, refs = refs[0], refs[1:]
+    block_outs, refs = refs[: len(plan["pairs"])], refs[len(plan["pairs"]) :]
+    cell_out, live_out, tracer, west, south, scale, kernels, observed, weights, cells, counts, done = refs
     carried, levels, cx, cy = tracer.shape
     me = tile_of(sizes)
+    copies = [
+        pltpu.make_async_copy(source, target, done.at[number])
+        for number, (source, target) in enumerate(
+            zip(sources[1:], (west, south, scale, kernels, observed, weights, cells, counts))
+        )
+    ]
+    copies += [
+        pltpu.make_async_copy(sources[0].at[t], tracer.at[t], done.at[8 + t]) for t in range(carried)
+    ]
+    for number in (3, 4, 5, 6, 7, 0, 2, *range(8, 8 + carried), 1):
+        copies[number].start()
 
     def block(offset):
         where_to = jnp.bitwise_xor(me, offset)
@@ -99,50 +126,70 @@
         )
         return jnp.concatenate([mine[8 * g : 8 * g + 8] for g in range(levels // 8)] + [last], axis=1)
 
-    even_x = is_even("facex")
+    for number in (3, 4, 5):
+        copies[number].wait()
     head = (carried + 1) * levels
     for number, out in enumerate(rows_out):
-        sends_last = even_x if number == 0 else jnp.logical_not(even_x)
-        row = jnp.where(sends_last, cx - 1, 0)
-        for level in range(levels):
-            for t in range(carried):
-                out[t * levels + level : t * levels + level + 1, :] = tracer[
-                    t, level, pl.ds(row, 1), :
-                ]
-            out[carried * levels + level : carried * levels + level + 1, :] = west[
-                level, pl.ds(row, 1), :
-            ]
-        out[head : head + 8, :] = jnp.broadcast_to(scale[pl.ds(row, 1), :], (8, cy))
         if plan["x_blocks"][number]:
             out[head + 8 : head + 16, :] = block(plan["x_blocks"][number])
-    even_y = is_even("facey")
-    lane = iota((cx, cy), 1)
-    for number, out in enumerate(lanes_out):
-        sends_last = even_y if number == 0 else jnp.logical_not(even_y)
-        edge = jnp.where(sends_last, cy - 1, 0)
-        packed = jnp.zeros((cx, cy), F32)
-        for f in range(carried + 1):
-            for level in range(levels):
-                values = tracer[f, level] if f < carried else south[level]
-                spot = f * levels + level
-                moved = pltpu.roll(values, lax.rem(spot + cy - edge, cy), 1)
-                packed = jnp.where(lane == spot, moved, packed)
-        out[0:cx, :] = packed
-        if number == 0:
-            out[cx : cx + 8, :] = block(plan["y_block"])
+    lanes_out[0][cx : cx + 8, :] = block(plan["y_block"])
     own_out[...] = block(0)
     first_core = lax.axis_index("lev") == 0
     for out, (for_first, for_second) in zip(block_outs, plan["pairs"]):
         out[...] = block(jnp.where(first_core, for_first, for_second))
 
+    owners, cap = cells.shape
+    slot = iota((1, cap), 1)
+    copies[6].wait()
+    copies[7].wait()
+    cell_parts = []
+    live_parts = []
+    for offset in range(owners):
+        owner = jnp.bitwise_xor(me, offset)
+        cell_parts.append(cells[pl.ds(owner, 1), :])
+        live_parts.append(jnp.where(slot < counts[owner], 1.0, 0.0))
+    cell_out[...] = jnp.concatenate(cell_parts, axis=1)
+    live_out[...] = jnp.concatenate(live_parts, axis=1)
+
+    even_x = is_even("facex")
+    even_y = is_even("facey")
+    last_row = [
+        jnp.where(even_x if number == 0 else jnp.logical_not(even_x), cx - 1, 0)
+        for number in range(len(rows_out))
+    ]
+    edge = [
+        jnp.where(even_y if number == 0 else jnp.logical_not(even_y), cy - 1, 0)
+        for number in range(len(lanes_out))
+    ]
+    lane = iota((cx, cy), 1)
+    copies[0].wait()
+    copies[2].wait()
+    for row, out in zip(last_row, rows_out):
+        for level in range(levels):
+            spot = carried * levels + level
+            out[spot : spot + 1, :] = west[level, pl.ds(row, 1), :]
+        out[head : head + 8, :] = jnp.broadcast_to(scale[pl.ds(row, 1), :], (8, cy))
+    packed = [jnp.zeros((cx, cy), F32) for _ in lanes_out]
+    for f in range(carried + 1):
+        copies[8 + f if f < carried else 1].wait()
+        for level in range(levels):
+            spot = f * levels + level
+            values = tracer[f, level] if f < carried else south[level]
+            for number, at in enumerate(edge):
+                moved = pltpu.roll(values, lax.rem(spot + cy - at, cy), 1)
+                packed[number] = jnp.where(lane == spot, moved, packed[number])
+            if f < carried:
+                for row, out in zip(last_row, rows_out):
+                    out[spot : spot + 1, :] = tracer[f, level, pl.ds(row, 1), :]
+    for values, out in zip(packed, lanes_out):
+        out[0:cx, :] = values
+
 
 def factor_kernel(sizes, *refs):
-    (tracer, west, south, mixing, adjoint, cells, counts) = refs[:7]
-    inverse_out, ratio_out, base_out, inner_out, columns_out, rows_out, picks_out, live_out = refs[7:]
+    (tracer, west, south, mixing, adjoint, cells) = refs[:6]
+    inverse_out, ratio_out, base_out, inner_out, shares_out, columns_out, rows_out, picks_out = refs[6:]
     carried, levels, cx, cy = tracer.shape
-    owners, cap = cells.shape
-    slots = owners * cap
-    me = tile_of(sizes)
+    slots = cells.shape[1]
     first = []
     before = None
     for level in range(levels):
@@ -159,6 +206,7 @@
             ratio_out[level] = mixing[level] * inverse
         first.append(inverse if level == 0 else mixing[level - 1] * first[-1] * inverse)
         before = inverse
+    ratio_out[levels - 1] = jnp.zeros((cx, cy), F32)
     weight = first
     for level in range(levels - 2, -1, -1):
         weight[level] = first[level] + ratio_out[level] * weight[level + 1]
@@ -171,16 +219,11 @@
         total = tracer[0, level]
         for t in range(1, carried):
             total = total + tracer[t, level]
-        inner_out[level] = inner_step(total, west[level], south[level])
-    cell_parts = []
-    live_parts = []
-    slot = iota((1, cap), 1)
-    for offset in range(owners):
-        owner = jnp.bitwise_xor(me, offset)
-        cell_parts.append(cells[pl.ds(owner, 1), :])
-        live_parts.append(jnp.where(slot < counts[owner], 1.0, 0.0))
-    cell = jnp.concatenate(cell_parts, axis=1)
-    live_out[...] = jnp.concatenate(live_parts, axis=1)
+        parts = shares(west[level], south[level])
+        for number, part in enumerate(parts):
+            shares_out[number, level] = part
+        inner_out[level] = mix(parts, total)
+    cell = cells[...]
     x_of = lax.div(cell, cy)
     y_of = lax.rem(cell, cy)
     in_row = jnp.where(iota((cx, slots), 0) == x_of, 1.0, 0.0)
@@ -481,12 +524,12 @@
 
 
 def advance_kernel(plan, *refs):
-    tracer, west, south, mixing, inverse, ratio = refs[:6]
-    sent = refs[6:8]
-    got = refs[8:10]
-    y_sent = refs[10 : 10 + plan["y_ops"]]
-    y_got = refs[10 + plan["y_ops"] : 10 + 2 * plan["y_ops"]]
-    out = refs[-1]
+    tracer, parts, mixing, inverse, ratio = refs[:5]
+    sent = refs[5:7]
+    got = refs[7:9]
+    y_sent = refs[9 : 9 + plan["y_ops"]]
+    y_got = refs[9 + plan["y_ops"] : 9 + 2 * plan["y_ops"]]
+    target, out, west_rows, east_rows, done = refs[-5:]
     carried, levels, cx, cy = tracer.shape
     head = (carried + 1) * levels
     spot = carried * levels
@@ -494,32 +537,62 @@
     at_west, at_east = sides(sent[0][0:head], sent[1][0:head])
     face_west = at_west[spot:head]
     face_east = beyond_east[spot:head]
+    for t in range(carried):
+        part = slice(t * levels, (t + 1) * levels)
+        west_rows[part, :] = jnp.maximum(face_west, 0.0) * beyond_west[part]
+        east_rows[part, :] = -(
+            jnp.maximum(face_east, 0.0) * at_east[part] + jnp.minimum(face_east, 0.0) * beyond_east[part]
+        )
     lane = iota((cx, cy), 1)
     row = iota((cx, cy), 0)
     seams = [
         seam_lanes(n, y_sent[n][0:cx, :], y_got[n][0:cx, :], carried, levels) for n in range(plan["y_ops"])
     ]
-    for t in range(carried):
-        part = slice(t * levels, (t + 1) * levels)
-        from_west = jnp.maximum(face_west, 0.0) * beyond_west[part]
-        from_east = -(
-            jnp.maximum(face_east, 0.0) * at_east[part] + jnp.minimum(face_east, 0.0) * beyond_east[part]
-        )
-        result = []
-        for level in range(levels):
-            value = inner_step(tracer[t, level], west[level], south[level])
-            value = value + jnp.where(row == 0, from_west[level : level + 1], 0.0)
-            value = value + jnp.where(row == cx - 1, from_east[level : level + 1], 0.0)
-            for packed, spot_y in seams:
-                moved = pltpu.roll(packed, lax.rem(spot_y - (t * levels + level) + 2 * cy, cy), 1)
-                value = value + jnp.where(lane == spot_y, moved, 0.0)
-            if level > 0:
-                value = value + mixing[level - 1] * result[-1]
-            result.append(value * inverse[level])
-        out[t, levels - 1] = result[-1]
-        for level in range(levels - 2, -1, -1):
-            result[level] = result[level] + ratio[level] * result[level + 1]
-            out[t, level] = result[level]
+    stride = 4
+
+    def forward(step, before):
+        mixed = []
+        for k in range(stride):
+            level = step * stride + k
+            weights = [parts[n, level] for n in range(5)]
+            mixed.append([])
+            for t in range(carried):
+                value = mix(weights, tracer[t, level])
+                value = value + jnp.where(row == 0, west_rows[pl.ds(t * levels + level, 1), :], 0.0)
+                value = value + jnp.where(row == cx - 1, east_rows[pl.ds(t * levels + level, 1), :], 0.0)
+                for packed, spot_y in seams:
+                    moved = pltpu.roll(packed, lax.rem(spot_y - (t * levels + level) + 2 * cy, cy), 1)
+                    value = value + jnp.where(lane == spot_y, moved, 0.0)
+                mixed[k].append(value)
+        for k in range(stride):
+            level = step * stride + k
+            from_below = mixing[jnp.maximum(level - 1, 0)]
+            scaled = inverse[level]
+            after = []
+            for t in range(carried):
+                value = (mixed[k][t] + from_below * before[t]) * scaled
+                out[t, level] = value
+                after.append(value)
+            before = after
+        return tuple(before)
+
+    def copy(step):
+        part = pl.ds(levels - (step + 1) * stride, stride)
+        return pltpu.make_async_copy(out.at[:, part], target.at[:, part], done.at[step])
+
+    start = tuple(jnp.zeros((cx, cy), F32) for _ in range(carried))
+    lax.fori_loop(0, levels // stride, forward, start)
+    above = list(start)
+    for step in range(levels // stride):
+        for k in range(stride):
+            level = levels - 1 - step * stride - k
+            factor = ratio[level]
+            for t in range(carried):
+                above[t] = out[t, level] + factor * above[t]
+                out[t, level] = above[t]
+        copy(step).start()
+    for step in range(levels // stride):
+        copy(step).wait()
 
 
 GROUP = ("facex", "facey", "lev")
@@ -610,7 +683,11 @@
     lane_shapes = [shape(cx + (8 if n == 0 else 0), cy) for n in range(y_ops)]
     packed = call(
         functools.partial(pack_kernel, sizes, plan),
-        row_shapes + lane_shapes + [shape(8, LANES)] * (1 + len(plan["pairs"])),
+        row_shapes
+        + lane_shapes
+        + [shape(8, LANES)] * (1 + len(plan["pairs"]))
+        + [shape(1, slots, dtype=jnp.int32), shape(1, slots)]
+        + [shape(*tracer.shape), shape(*west_courant.shape), shape(*south_courant.shape)],
         [
             tracer,
             west_courant,
@@ -619,28 +696,41 @@
             kernels.reshape(owners, levels, cap),
             observed.reshape(owners, cap),
             error_weight.reshape(owners, cap),
+            send_cells.reshape(owners, cap),
+            send_counts.reshape(owners),
         ],
         "pack",
         100000,
+        hbm=range(9),
+        scratch=[
+            pltpu.VMEM((cx, cy), F32),
+            pltpu.VMEM((owners, levels, cap), F32),
+            pltpu.VMEM((owners, cap), F32),
+            pltpu.VMEM((owners, cap), F32),
+            pltpu.VMEM((owners, cap), jnp.int32),
+            pltpu.SMEM((owners,), jnp.int32),
+            pltpu.SemaphoreType.DMA((8 + carried,)),
+        ],
     )
     rows_sent = packed[:2]
     lanes_sent = packed[2 : 2 + y_ops]
     own_block = packed[2 + y_ops]
-    pair_sent = packed[3 + y_ops :]
+    pair_sent = packed[3 + y_ops : -5]
+    cell, live, tracer, west_courant, south_courant = packed[-5:]
     rows_got = [exchange(rows_sent[n], sizes, next_x(n)) for n in range(2)]
     lanes_got = [exchange(lanes_sent[n], sizes, next_y(n)) for n in range(y_ops)]
     pair_got = [exchange(s, sizes, jump(*p)) for s, p in zip(pair_sent, plan["pairs"])]
-    inverse, ratio, base, inner, columns, in_row, in_lane, live = call(
+    inverse, ratio, base, inner, parts, columns, in_row, in_lane = call(
         functools.partial(factor_kernel, sizes),
         [
             shape(levels, cx, cy),
-            shape(levels - 1, cx, cy),
+            shape(levels, cx, cy),
             shape(carried, cx, cy),
             shape(levels, cx, cy),
+            shape(5, levels, cx, cy),
             shape(levels, slots),
             shape(cx, slots),
             shape(cy, slots, dtype=BF16),
-            shape(1, slots),
         ],
         [
             tracer,
@@ -648,12 +738,10 @@
             south_courant,
             mixing,
             adjoint_later,
-            send_cells.reshape(owners, cap),
-            send_counts.reshape(owners),
+            cell,
         ],
         "factor",
         3000000,
-        smem=(6,),
     )
     base_other = other_core(base)
     swapped = [other_core(jnp.concatenate(pair_got, axis=0))] if pair_got else []
@@ -672,25 +760,31 @@
         2000000,
     )
     modeled_other = other_core(modeled)
+    near, *rims_sent = call(
+        functools.partial(force_kernel, plan),
+        [shape(2 * carried, cx, cy)] + [shape(cx, cy)] * y_ops,
+        [modeled, modeled_other, state, in_row, in_lane, base, base_other],
+        "force",
+        200000,
+    )
+    rims_got = [exchange(rims_sent[n], sizes, next_y(n)) for n in range(y_ops)]
+    held, *_ = lax.optimization_barrier((tracer, *rims_sent))
     (advanced,) = call(
         functools.partial(advance_kernel, plan),
         [shape(*tracer.shape)],
-        [tracer, west_courant, south_courant, mixing, inverse, ratio]
+        [held, parts, mixing, inverse, ratio]
         + list(rows_sent)
         + rows_got
         + list(lanes_sent)
         + lanes_got,
         "advance",
         6000000,
-    )
-    near, *rims_sent = call(
-        functools.partial(force_kernel, plan),
-        [shape(2 * carried, cx, cy)] + [shape(cx, cy)] * y_ops,
-        [modeled, modeled_other, state, in_row, in_lane, base, base_other],
-        "force",
-        200000,
-    )
-    rims_got = [exchange(rims_sent[n], sizes, next_y(n)) for n in range(y_ops)]
+        scratch=[pltpu.VMEM(tracer.shape, F32)]
+        + [pltpu.VMEM((carried * levels, cy), F32)] * 2
+        + [pltpu.SemaphoreType.DMA((levels // 4,))],
+        out_hbm=(0,),
+    )
+    advanced, *rims_got = lax.optimization_barrier((advanced, *rims_got))
     per_tile = min(2 * carried, LANES // band)
 
     def band_shape(first, second):

time: 40 us -> 30.9 us (0.77)
  local copies, waits for them, and re-layouts: 6.62 us -> 0.03 us
  Pallas kernels: 8.9 us -> 6.52 us
    unnamed x32 -> x10, local copies, waits for them, and re-layouts: 6.62 us -> 0.02 us
    pallas_call x7, Pallas kernels: 8.9 us -> 6.52 us  [call(): pl.pallas_call(body, out_shape=outs, in_specs=[pl.BlockSpec(memory_space=...]
  transfers between devices with their start and end apart: 12 -> 12, of which waited for: 5 -> 7; matrix products, arithmetic and copies ran while one was open for 0% -> 0% of each run, Pallas kernels for 18% -> 11%
where the time goes in v2:
time: 30.9 us; the launch traced here: 30.8 us
  starting transfers between devices  13.2 us (43%)
  waiting for transfers between devices  9.65 us (31%)
  Pallas kernels  6.52 us (21%)
  between operations  0.76 us (2%)
  other arithmetic  0.58 us (2%)
    ppermute x12, starting transfers between devices, exchange(): return lax.ppermute(values, GROUP, pairs)  13.2 us
    ppermute x12, waiting for transfers between devices, exchange(): return lax.ppermute(values, GROUP, pairs)  9.65 us
    pallas_call x7, Pallas kernels, call(): pl.pallas_call(body, out_shape=outs, in_specs=[pl.BlockSpec(memory_space=...  6.52 us
  transfers between devices with their start and end apart: 12, of which 7 were waited for; matrix products, arithmetic and copies ran while one was open for 0% of the time, Pallas kernels for 11%

profile of v2, /device:TPU:0, one launch (start us, length us, event | category | flops | bytes accessed | tf_op | source)
XLA Modules:
  0.0 30.8 jit_solution(6080974820403844711)
XLA Ops:
  0.6 0.0 copy-start.1
  0.6 0.0 copy-start
  0.7 2.0 %pack.1 = (f32[136,128]{1,0:T(8,128)S(1)}, f32[136,128]{1,0:T(8,128)S(1)}, f32[24,128]{1,0:T(8,128)S(1)}, f32[8,128]{1,0:T(8,128)S(1)}, f32[8,128]{1,0:T(8,128)S...) custom-call(f32[4,24,16,128]{3,2,1,0:T(8,128)} %refs_0_.1, ...), custom_call_target="tpu_custom_call" | custom-call | flops 100000 | bytes 2561056 | tf_op jit(solution)/shard_map/pack/pallas_call | solution.py:22
  2.6 4.1 %collective-permute-start.3 = (f32[8,128]{1,0:T(8,128)S(1)}, f32[8,128]{1,0:T(8,128)S(1)}, u32[]{:S(2)}, u32[]{:S(2)}) collective-permute-start(f32[8,128]{1,0:T(8,128)S(1)} %get-tuple-element.46), channel_id=1, source_target_pairs={{0,8},{1,11},{2,10},{3,9},{4,12},{5,15},{6,14},{7,13},{8,0},{9,3},... | collective-permute-start | bytes 12296 | tf_op jit(solution)/shard_map/ppermute | solution.py:610
  6.7 2.5 %collective-permute-start.4 = (f32[8,128]{1,0:T(8,128)S(1)}, f32[8,128]{1,0:T(8,128)S(1)}, u32[]{:S(2)}, u32[]{:S(2)}) collective-permute-start(f32[8,128]{1,0:T(8,128)S(1)} %get-tuple-element.47), channel_id=1, source_target_pairs={{0,6},{1,15},{2,4},{3,13},{4,2},{5,11},{6,0},{7,9},{8,14},{9,7},{1... | collective-permute-start | bytes 12296 | tf_op jit(solution)/shard_map/ppermute | solution.py:610
  9.2 0.5 %collective-permute-start.2 = (f32[24,128]{1,0:T(8,128)S(1)}, f32[24,128]{1,0:T(8,128)S(1)}, u32[]{:S(2)}, u32[]{:S(2)}) collective-permute-start(f32[24,128]{1,0:T(8,128)S(1)} %get-tuple-element.44.refs_12_.refs_9_), channel_id=1, source_target_pairs={{0,2},{1,3},{2,0},{3,1},{4,6},{5,7},{6,4},{7,5},{8,10},{9,11},{10,... | collective-permute-start | bytes 36872 | tf_op jit(solution)/shard_map/ppermute | solution.py:610
  9.8 0.4 %collective-permute-start = (f32[136,128]{1,0:T(8,128)S(1)}, f32[136,128]{1,0:T(8,128)S(1)}, u32[]{:S(2)}, u32[]{:S(2)}) collective-permute-start(f32[136,128]{1,0:T(8,128)S(1)} %get-tuple-element.42.refs_8_.refs_5_), channel_id=1, source_target_pairs={{0,4},{1,5},{2,6},{3,7},{4,0},{5,1},{6,2},{7,3},{8,12},{9,13},{10,... | collective-permute-start | bytes 208904 | tf_op jit(solution)/shard_map/ppermute | solution.py:610
  10.2 1.3 %collective-permute-start.1 = (f32[136,128]{1,0:T(8,128)S(1)}, f32[136,128]{1,0:T(8,128)S(1)}, u32[]{:S(2)}, u32[]{:S(2)}) collective-permute-start(f32[136,128]{1,0:T(8,128)S(1)} %get-tuple-element.43.refs_9_.refs_6_), channel_id=1, source_target_pairs={{0,12},{1,13},{2,14},{3,15},{4,8},{5,9},{6,10},{7,11},{8,4},{9,5},... | collective-permute-start | bytes 208904 | tf_op jit(solution)/shard_map/ppermute | solution.py:610
  11.6 0.0 copy-done.1
  11.6 0.0 copy-done
  11.6 0.7 %factor.1 = (f32[24,16,128]{2,1,0:T(8,128)S(1)}, f32[24,16,128]{2,1,0:T(8,128)S(1)}, f32[4,16,128]{2,1,0:T(8,128)S(1)}, f32[24,16,128]{2,1,0:T(8,128)S(1)}, f32[...) custom-call(f32[4,24,16,128]{3,2,1,0:T(8,128)S(1)} %get-tuple-element., ...), custom_call_target="tpu_custom_call" | custom-call | flops 3000000 | bytes 3933184 | tf_op jit(solution)/shard_map/factor/pallas_call | solution.py:22
  12.3 0.0 collective-permute-done.3.refs_15_
  12.3 0.6 %collective-permute-start.7 = (f32[4,16,128]{2,1,0:T(8,128)S(1)}, f32[4,16,128]{2,1,0:T(8,128)S(1)}, u32[]{:S(2)}, u32[]{:S(2)}) collective-permute-start(f32[4,16,128]{2,1,0:T(8,128)S(1)} %get-tuple-element.50.refs_5_), channel_id=1, source_target_pairs={{0,1},{1,0},{2,3},{3,2},{4,5},{5,4},{6,7},{7,6},{8,9},{9,8},{10,11... | collective-permute-start | bytes 98312 | tf_op jit(solution)/shard_map/ppermute | solution.py:610
  12.8 0.0 collective-permute-done.4.refs_16_
  12.9 0.1 collective-permute-start.5
  12.9 1.1 %collective-permute-done.5.refs_17_ = f32[16,128]{1,0:T(8,128)S(1)} collective-permute-done((f32[16,128]{1,0:T(8,128)S(1)}, f32[16,128]{1,0:T(8,128)S(1)}, u32[]{:S(2)}, u32[]{:S(2)}) %collective-permute-start.5) | collective-permute-done | bytes 8224 | tf_op jit(solution)/shard_map/ppermute | solution.py:610
  14.0 0.0 collective-permute-done.2.refs_13_.refs_10_.refs_6_
  14.0 0.1 collective-permute-done.refs_10_.refs_7_.refs_4_
  14.1 2.3 %collective-permute-done.1.refs_11_.refs_8_.refs_5_ = f32[136,128]{1,0:T(8,128)S(1)} collective-permute-done((f32[136,128]{1,0:T(8,128)S(1)}, f32[136,128]{1,0:T(8,128)S(1)}, u32[]{:S(2)}, u32[]{:S(2)}) %collective-permute-start.1) | collective-permute-done | bytes 69664 | tf_op jit(solution)/shard_map/ppermute | solution.py:610
  16.4 0.6 %observe.1 = (f32[1,256]{1,0:T(1,128)S(1)}, f32[2,256]{1,0:T(2,128)S(1)}) custom-call(f32[24,16,128]{2,1,0:T(8,128)S(1)} %get-tuple-element.35.refs_0_, f32[23,16,128]{2,1,0:T(8,128)S(1)} %copy-done, f32[24,16,128]{2,1,0:T(8,128)S(1)} %get-tuple-element.36.refs_2_.refs_3_, f32[24,16,128]{2,1,0:T(8,128)S(1)} %get-tuple-element.37.refs_3_.refs_4_, ...), custom_call_target="tpu_custom_call" | custom-call | flops 2000000 | bytes 1277952 | tf_op jit(solution)/shard_map/observe/pallas_call | solution.py:22
  17.0 0.1 collective-permute-start.6
  17.1 0.0 collective-permute-done.7.refs_6_
  17.1 1.1 %collective-permute-done.6.refs_1_ = f32[1,256]{1,0:T(1,128)S(1)} collective-permute-done((f32[1,256]{1,0:T(1,128)S(1)}, f32[1,256]{1,0:T(1,128)S(1)}, u32[]{:S(2)}, u32[]{:S(2)}) %collective-permute-start.6) | collective-permute-done | bytes 1056 | tf_op jit(solution)/shard_map/ppermute | solution.py:610
  18.2 0.2 force.1
  18.5 1.5 %collective-permute-start.8 = (f32[16,128]{1,0:T(8,128)S(1)}, f32[16,128]{1,0:T(8,128)S(1)}, u32[]{:S(2)}, u32[]{:S(2)}) collective-permute-start(f32[16,128]{1,0:T(8,128)S(1)} %get-tuple-element.51), channel_id=1, source_target_pairs={{0,2},{1,3},{2,0},{3,1},{4,6},{5,7},{6,4},{7,5},{8,10},{9,11},{10,... | collective-permute-start | bytes 24584 | tf_op jit(solution)/shard_map/ppermute | solution.py:610
  20.0 0.0 copy-start.2
  20.0 2.1 %advance.1 = f32[4,24,16,128]{3,2,1,0:T(8,128)} custom-call(f32[4,24,16,128]{3,2,1,0:T(8,128)S(1)} %get-tuple-element.52.refs_0_, f32[5,24,16,128]{3,2,1,0:T(8,128)S(1)} %get-tuple-element.53.refs_1_, f32[23,16,128]{2,1,0:T(8,128)S(1)} %copy-done, f32[24,16,128]{2,1,0:T(8,128)S(1)} %get-tuple-element.36.refs_2_.refs_3_, ...), custom_call_target="tpu_custom_call" | custom-call | flops 6000000 | bytes 3440640 | tf_op jit(solution)/shard_map/advance/pallas_call | solution.py:22
  22.1 0.1 collective-permute-done.8.refs_7_
  22.2 0.0 copy-done.2
  22.2 0.0 copy-start.4
  22.2 0.2 surface.1
  22.4 0.0 copy-start.3
  22.4 2.0 %collective-permute-start.10 = (f32[48,128]{1,0:T(8,128)S(1)}, f32[48,128]{1,0:T(8,128)S(1)}, u32[]{:S(2)}, u32[]{:S(2)}) collective-permute-start(f32[48,128]{1,0:T(8,128)S(1)} %get-tuple-element.59), channel_id=1, source_target_pairs={{0,12},{1,9},{2,14},{3,11},{4,8},{5,13},{6,10},{7,15},{8,4},{9,1},... | collective-permute-start | bytes 73736 | tf_op jit(solution)/shard_map/ppermute | solution.py:610
  24.4 0.0 collective-permute-start.9
  24.4 3.8 %collective-permute-done.9.refs_3_ = f32[24,128]{1,0:T(8,128)S(1)} collective-permute-done((f32[24,128]{1,0:T(8,128)S(1)}, f32[24,128]{1,0:T(8,128)S(1)}, u32[]{:S(2)}, u32[]{:S(2)}) %collective-permute-start.9) | collective-permute-done | bytes 12320 | tf_op jit(solution)/shard_map/ppermute | solution.py:610
  28.2 0.0 collective-permute-done.10.refs_4_
  28.2 0.0 copy-done.4
  28.2 0.0 copy-done.3
  28.2 0.7 %regrid.1 = f32[8,128]{1,0:T(8,128)S(1)} custom-call(s32[16,128]{1,0:T(8,128)S(1)} %bitcast.14, f32[16,128]{1,0:T(8,128)S(1)} %bitcast.15, f32[24,128]{1,0:T(8,128)S(1)} %get-tuple-element.57.refs_2_, f32[24,128]{1,0:T(8,128)S(1)} %collective-permute-done.9.refs_3_, f32[48,128]{1,0:T(8,128)S(1)} %collective-permute-done.10.refs_4_), custom_call_target="tpu_custom_call" | custom-call | flops 1000000 | bytes 69632 | tf_op jit(solution)/shard_map/regrid/pallas_call | solution.py:22
  29.0 0.1 collective-permute-start.11
  29.1 1.1 %collective-permute-done.11 = f32[4,128]{1,0:T(4,128)S(1)} collective-permute-done((f32[4,128]{1,0:T(4,128)S(1)}, f32[4,128]{1,0:T(4,128)S(1)}, u32[]{:S(2)}, u32[]{:S(2)}) %collective-permute-start.11) | collective-permute-done | bytes 2080 | tf_op jit(solution)/shard_map/ppermute | solution.py:610
  30.2 0.6 %slice_add_fusion = f32[4,128]{1,0:T(4,128)} fusion(f32[4,128]{1,0:T(4,128)S(1)} %collective-permute-done.11, f32[8,128]{1,0:T(8,128)S(1)} %regrid.1), kind=kLoop, calls=%fused_computation.3 | loop fusion | flops 512 | bytes 6144 | tf_op jit(solution)/shard_map/add | solution.py:813
  (3 shorter events, 0.0 us)
Async XLA Ops:
  0.6 11.0 %copy-start.1 = (f32[4,24,16,128]{3,2,1,0:T(8,128)S(1)}, f32[4,24,16,128]{3,2,1,0:T(8,128)}, u32[]{:S(2)}) copy-start(f32[4,24,16,128]{3,2,1,0:T(8,128)} %refs_4_.1) | copy-start | bytes 2359300
  0.6 10.9 %copy-start = (f32[23,16,128]{2,1,0:T(8,128)S(1)}, f32[23,16,128]{2,1,0:T(8,128)}, u32[]{:S(2)}) copy-start(f32[23,16,128]{2,1,0:T(8,128)} %refs_2_.3) | copy-start | bytes 565252
  2.6 9.6 %collective-permute-start.3 = (f32[8,128]{1,0:T(8,128)S(1)}, f32[8,128]{1,0:T(8,128)S(1)}, u32[]{:S(2)}, u32[]{:S(2)}) collective-permute-start(f32[8,128]{1,0:T(8,128)S(1)} %get-tuple-element.46), channel_id=1, source_target_pairs={{0,8},{1,11},{2,10},{3,9},{4,12},{5,15},{6,14},{7,13},{8,0},{9,3},... | collective-permute-start | bytes 12296 | tf_op jit(solution)/shard_map/ppermute | solution.py:610
  6.7 6.1 %collective-permute-start.4 = (f32[8,128]{1,0:T(8,128)S(1)}, f32[8,128]{1,0:T(8,128)S(1)}, u32[]{:S(2)}, u32[]{:S(2)}) collective-permute-start(f32[8,128]{1,0:T(8,128)S(1)} %get-tuple-element.47), channel_id=1, source_target_pairs={{0,6},{1,15},{2,4},{3,13},{4,2},{5,11},{6,0},{7,9},{8,14},{9,7},{1... | collective-permute-start | bytes 12296 | tf_op jit(solution)/shard_map/ppermute | solution.py:610
  9.2 4.8 %collective-permute-start.2 = (f32[24,128]{1,0:T(8,128)S(1)}, f32[24,128]{1,0:T(8,128)S(1)}, u32[]{:S(2)}, u32[]{:S(2)}) collective-permute-start(f32[24,128]{1,0:T(8,128)S(1)} %get-tuple-element.44.refs_12_.refs_9_), channel_id=1, source_target_pairs={{0,2},{1,3},{2,0},{3,1},{4,6},{5,7},{6,4},{7,5},{8,10},{9,11},{10,... | collective-permute-start | bytes 36872 | tf_op jit(solution)/shard_map/ppermute | solution.py:610
  9.8 4.3 %collective-permute-start = (f32[136,128]{1,0:T(8,128)S(1)}, f32[136,128]{1,0:T(8,128)S(1)}, u32[]{:S(2)}, u32[]{:S(2)}) collective-permute-start(f32[136,128]{1,0:T(8,128)S(1)} %get-tuple-element.42.refs_8_.refs_5_), channel_id=1, source_target_pairs={{0,4},{1,5},{2,6},{3,7},{4,0},{5,1},{6,2},{7,3},{8,12},{9,13},{10,... | collective-permute-start | bytes 208904 | tf_op jit(solution)/shard_map/ppermute | solution.py:610
  10.2 6.2 %collective-permute-start.1 = (f32[136,128]{1,0:T(8,128)S(1)}, f32[136,128]{1,0:T(8,128)S(1)}, u32[]{:S(2)}, u32[]{:S(2)}) collective-permute-start(f32[136,128]{1,0:T(8,128)S(1)} %get-tuple-element.43.refs_9_.refs_6_), channel_id=1, source_target_pairs={{0,12},{1,13},{2,14},{3,15},{4,8},{5,9},{6,10},{7,11},{8,4},{9,5},... | collective-permute-start | bytes 208904 | tf_op jit(solution)/shard_map/ppermute | solution.py:610
  12.3 4.8 %collective-permute-start.7 = (f32[4,16,128]{2,1,0:T(8,128)S(1)}, f32[4,16,128]{2,1,0:T(8,128)S(1)}, u32[]{:S(2)}, u32[]{:S(2)}) collective-permute-start(f32[4,16,128]{2,1,0:T(8,128)S(1)} %get-tuple-element.50.refs_5_), channel_id=1, source_target_pairs={{0,1},{1,0},{2,3},{3,2},{4,5},{5,4},{6,7},{7,6},{8,9},{9,8},{10,11... | collective-permute-start | bytes 98312 | tf_op jit(solution)/shard_map/ppermute | solution.py:610
  12.9 1.2 %collective-permute-start.5 = (f32[16,128]{1,0:T(8,128)S(1)}, f32[16,128]{1,0:T(8,128)S(1)}, u32[]{:S(2)}, u32[]{:S(2)}) collective-permute-start(f32[16,128]{1,0:T(8,128)S(1)} %pad_maximum_fusion), channel_id=1, source_target_pairs={{0,1},{1,0},{2,3},{3,2},{4,5},{5,4},{6,7},{7,6},{8,9},{9,8},{10,11... | collective-permute-start | bytes 24584 | tf_op jit(solution)/shard_map/ppermute | solution.py:610
  17.0 1.2 %collective-permute-start.6 = (f32[1,256]{1,0:T(1,128)S(1)}, f32[1,256]{1,0:T(1,128)S(1)}, u32[]{:S(2)}, u32[]{:S(2)}) collective-permute-start(f32[1,256]{1,0:T(1,128)S(1)} %get-tuple-element.48.refs_0_), channel_id=1, source_target_pairs={{0,1},{1,0},{2,3},{3,2},{4,5},{5,4},{6,7},{7,6},{8,9},{9,8},{10,11... | collective-permute-start | bytes 3080 | tf_op jit(solution)/shard_map/ppermute | solution.py:610
  18.5 3.7 %collective-permute-start.8 = (f32[16,128]{1,0:T(8,128)S(1)}, f32[16,128]{1,0:T(8,128)S(1)}, u32[]{:S(2)}, u32[]{:S(2)}) collective-permute-start(f32[16,128]{1,0:T(8,128)S(1)} %get-tuple-element.51), channel_id=1, source_target_pairs={{0,2},{1,3},{2,0},{3,1},{4,6},{5,7},{6,4},{7,5},{8,10},{9,11},{10,... | collective-permute-start | bytes 24584 | tf_op jit(solution)/shard_map/ppermute | solution.py:610
  20.0 2.2 %copy-start.2 = (f32[16,128]{1,0:T(8,128)S(1)}, f32[16,128]{1,0:T(8,128)}, u32[]{:S(2)}) copy-start(f32[16,128]{1,0:T(8,128)} %refs_3_.5) | copy-start | bytes 24580
  22.2 6.0 %copy-start.4 = (f32[1,1,16,128]{3,2,1,0:T(8,128)S(1)}, f32[1,1,16,128]{3,2,1,0:T(8,128)}, u32[]{:S(2)}) copy-start(f32[1,1,16,128]{3,2,1,0:T(8,128)} %param.25) | copy-start | bytes 24580
  22.4 5.8 %copy-start.3 = (s32[1,1,16,128]{3,2,1,0:T(8,128)S(1)}, s32[1,1,16,128]{3,2,1,0:T(8,128)}, u32[]{:S(2)}) copy-start(s32[1,1,16,128]{3,2,1,0:T(8,128)} %param.24) | copy-start | bytes 24580
  22.4 5.8 %collective-permute-start.10 = (f32[48,128]{1,0:T(8,128)S(1)}, f32[48,128]{1,0:T(8,128)S(1)}, u32[]{:S(2)}, u32[]{:S(2)}) collective-permute-start(f32[48,128]{1,0:T(8,128)S(1)} %get-tuple-element.59), channel_id=1, source_target_pairs={{0,12},{1,9},{2,14},{3,11},{4,8},{5,13},{6,10},{7,15},{8,4},{9,1},... | collective-permute-start | bytes 73736 | tf_op jit(solution)/shard_map/ppermute | solution.py:610
  24.4 3.8 %collective-permute-start.9 = (f32[24,128]{1,0:T(8,128)S(1)}, f32[24,128]{1,0:T(8,128)S(1)}, u32[]{:S(2)}, u32[]{:S(2)}) collective-permute-start(f32[24,128]{1,0:T(8,128)S(1)} %get-tuple-element.58), channel_id=1, source_target_pairs={{0,4},{1,5},{2,6},{3,7},{4,0},{5,1},{6,2},{7,3},{8,12},{9,13},{10,... | collective-permute-start | bytes 36872 | tf_op jit(solution)/shard_map/ppermute | solution.py:610
  29.0 1.2 %collective-permute-start.11 = (f32[4,128]{1,0:T(4,128)S(1)}, f32[4,128]{1,0:T(4,128)S(1)}, u32[]{:S(2)}, u32[]{:S(2)}) collective-permute-start(f32[4,128]{1,0:T(4,128)S(1)} %slice.15), channel_id=1, source_target_pairs={{0,1},{1,0},{2,3},{3,2},{4,5},{5,4},{6,7},{7,6},{8,9},{9,8},{10,11... | collective-permute-start | bytes 6152 | tf_op jit(solution)/shard_map/ppermute | solution.py:610

commit v3 on v2

--- a/solution.py
+++ b/solution.py
@@ -93,24 +93,24 @@
 
 
 def pack_kernel(sizes, plan, *refs):
-    sources, refs = refs[:9], refs[9:]
-    rows_out, refs = refs[:2], refs[2:]
+    sources, refs = refs[:10], refs[10:]
     lanes_out, refs = refs[: plan["y_ops"]], refs[plan["y_ops"] :]
     own_out, refs = refs[0], refs[1:]
     block_outs, refs = refs[: len(plan["pairs"])], refs[len(plan["pairs"]) :]
-    cell_out, live_out, tracer, west, south, scale, kernels, observed, weights, cells, counts, done = refs
+    cell_out, live_out, tracer, west, south, scale, mixing, *refs = refs
+    kernels, observed, weights, cells, counts, done = refs
     carried, levels, cx, cy = tracer.shape
     me = tile_of(sizes)
     copies = [
         pltpu.make_async_copy(source, target, done.at[number])
         for number, (source, target) in enumerate(
-            zip(sources[1:], (west, south, scale, kernels, observed, weights, cells, counts))
+            zip(sources[1:], (west, south, scale, kernels, observed, weights, cells, counts, mixing))
         )
     ]
     copies += [
-        pltpu.make_async_copy(sources[0].at[t], tracer.at[t], done.at[8 + t]) for t in range(carried)
+        pltpu.make_async_copy(sources[0].at[t], tracer.at[t], done.at[9 + t]) for t in range(carried)
     ]
-    for number in (3, 4, 5, 6, 7, 0, 2, *range(8, 8 + carried), 1):
+    for number in (3, 4, 5, 6, 7, 1, 0, 8, *range(9, 9 + carried), 2):
         copies[number].start()
 
     def block(offset):
@@ -128,12 +128,11 @@
 
     for number in (3, 4, 5):
         copies[number].wait()
-    head = (carried + 1) * levels
-    for number, out in enumerate(rows_out):
-        if plan["x_blocks"][number]:
-            out[head + 8 : head + 16, :] = block(plan["x_blocks"][number])
-    lanes_out[0][cx : cx + 8, :] = block(plan["y_block"])
-    own_out[...] = block(0)
+    for number, offset in enumerate(plan["y_blocks"]):
+        at = plan["y_tiles"] * cx + 8 * number
+        lanes_out[0][at : at + 8, :] = block(offset)
+    for number, offset in enumerate(plan["own_blocks"]):
+        own_out[8 * number : 8 * number + 8, :] = block(offset)
     first_core = lax.axis_index("lev") == 0
     for out, (for_first, for_second) in zip(block_outs, plan["pairs"]):
         out[...] = block(jnp.where(first_core, for_first, for_second))
@@ -148,46 +147,181 @@
         owner = jnp.bitwise_xor(me, offset)
         cell_parts.append(cells[pl.ds(owner, 1), :])
         live_parts.append(jnp.where(slot < counts[owner], 1.0, 0.0))
-    cell_out[...] = jnp.concatenate(cell_parts, axis=1)
-    live_out[...] = jnp.concatenate(live_parts, axis=1)
-
-    even_x = is_even("facex")
+    cell = jnp.concatenate(cell_parts, axis=1)
+    live = jnp.concatenate(live_parts, axis=1)
+    cell_out[...] = cell
+    live_out[...] = live
+    if plan["relay"]:
+        at = plan["y_tiles"] * cx + 8 * len(plan["y_blocks"])
+        strips = owners * cap // LANES
+        for number in range(strips):
+            part = slice(number * LANES, (number + 1) * LANES)
+            lanes_out[0][at + number : at + number + 1, :] = cell[:, part].astype(F32)
+            lanes_out[0][at + strips + number : at + strips + number + 1, :] = live[:, part]
+
     even_y = is_even("facey")
-    last_row = [
-        jnp.where(even_x if number == 0 else jnp.logical_not(even_x), cx - 1, 0)
-        for number in range(len(rows_out))
-    ]
     edge = [
         jnp.where(even_y if number == 0 else jnp.logical_not(even_y), cy - 1, 0)
         for number in range(len(lanes_out))
     ]
     lane = iota((cx, cy), 1)
-    copies[0].wait()
+    packed = [jnp.zeros((cx, cy), F32) for _ in lanes_out]
+    behind = jnp.zeros((cx, cy), F32)
+    inner_edge = jnp.where(edge[0] == 0, 1, cy - 2)
+    for number in (1, 0, 8):
+        copies[number].wait()
+    for level in range(levels):
+        spot = carried * levels + level
+        for number, at in enumerate(edge):
+            moved = pltpu.roll(south[level], lax.rem(spot + cy - at, cy), 1)
+            packed[number] = jnp.where(lane == spot, moved, packed[number])
+        if plan["relay"]:
+            for number, (values, at) in enumerate(
+                ((west[level], edge[0]), (south[level], inner_edge), (mixing[min(level, levels - 2)], edge[0]))
+            ):
+                spot = (number + 1) * levels + level
+                if number < 2 or level < levels - 1:
+                    moved = pltpu.roll(values, lax.rem(spot + cy - at, cy), 1)
+                    behind = jnp.where(lane == spot, moved, behind)
+    for t in range(carried):
+        copies[9 + t].wait()
+        for level in range(levels):
+            spot = t * levels + level
+            values = tracer[t, level]
+            for number, at in enumerate(edge):
+                moved = pltpu.roll(values, lax.rem(spot + cy - at, cy), 1)
+                packed[number] = jnp.where(lane == spot, moved, packed[number])
+    for values, out in zip(packed, lanes_out):
+        out[0:cx, :] = values
+    if plan["relay"]:
+        for level in range(levels):
+            total = tracer[0, level]
+            for t in range(1, carried):
+                total = total + tracer[t, level]
+            moved = pltpu.roll(total, lax.rem(level + cy - inner_edge, cy), 1)
+            behind = jnp.where(lane == level, moved, behind)
+        lanes_out[0][cx : 2 * cx, :] = behind
     copies[2].wait()
-    for row, out in zip(last_row, rows_out):
+
+
+def rows_kernel(plan, tracer, west, scale, blocks, *outs):
+    carried, levels, cx, cy = tracer.shape
+    head = (carried + 1) * levels
+    even_x = is_even("facex")
+    for number, out in enumerate(outs):
+        row = jnp.where(even_x if number == 0 else jnp.logical_not(even_x), cx - 1, 0)
         for level in range(levels):
+            for t in range(carried):
+                spot = t * levels + level
+                out[spot : spot + 1, :] = tracer[t, level, pl.ds(row, 1), :]
             spot = carried * levels + level
             out[spot : spot + 1, :] = west[level, pl.ds(row, 1), :]
         out[head : head + 8, :] = jnp.broadcast_to(scale[pl.ds(row, 1), :], (8, cy))
-    packed = [jnp.zeros((cx, cy), F32) for _ in lanes_out]
-    for f in range(carried + 1):
-        copies[8 + f if f < carried else 1].wait()
-        for level in range(levels):
-            spot = f * levels + level
-            values = tracer[f, level] if f < carried else south[level]
-            for number, at in enumerate(edge):
-                moved = pltpu.roll(values, lax.rem(spot + cy - at, cy), 1)
-                packed[number] = jnp.where(lane == spot, moved, packed[number])
-            if f < carried:
-                for row, out in zip(last_row, rows_out):
-                    out[spot : spot + 1, :] = tracer[f, level, pl.ds(row, 1), :]
-    for values, out in zip(packed, lanes_out):
-        out[0:cx, :] = values
+        if plan["x_blocks"][number] and not plan["relay"]:
+            at = 8 * plan["own_blocks"].index(plan["x_blocks"][number])
+            out[head + 8 : head + 16, :] = blocks[at : at + 8, :]
+
+
+def relay_kernel(plan, head, cx, *refs):
+    rows, blocks, y_got = refs[:2], refs[2], refs[3]
+    outs = refs[4:6]
+    x_outs = refs[6:]
+    base = plan["y_tiles"] * cx
+
+    def fill(out, start, offset):
+        out[start : start + 16, :] = blocks[8 * offset : 8 * offset + 16, :]
+        out[start + 16 : start + 32, :] = y_got[base + 8 * offset : base + 8 * offset + 16, :]
+
+    even_x = is_even("facex")
+    for number, out in enumerate(outs):
+        out[0 : head + 8, :] = rows[number][0 : head + 8, :]
+        row = jnp.where(even_x if number == 0 else jnp.logical_not(even_x), cx - 1, 0)
+        for tile in range(2):
+            out[head + 8 + tile : head + 9 + tile, :] = y_got[pl.ds(tile * cx + row, 1), :]
+        out[head + 10 : head + 16, :] = jnp.zeros((6, out.shape[1]), F32)
+        if plan["x_blocks"][number]:
+            fill(out, head + 16, plan["x_blocks"][number])
+    for out, offset in zip(x_outs, plan["x_ops"]):
+        fill(out, 0, offset)
+
+
+def rim_kernel(plan, carried, levels, cx, y_sent, y_got, *refs):
+    inverse_out, ratio_out, mixing_out, pieces_out, columns_out, rows_out, picks_out, live_out, square = refs
+    cy = y_got.shape[1]
+    slots = live_out.shape[1]
+
+    def turned(values):
+        square[...] = jnp.zeros((LANES, LANES), F32)
+        square[0:cx, :] = values
+        return jnp.transpose(square[...])
+
+    def summed(values):
+        total = values[0:levels]
+        for t in range(1, carried):
+            total = total + values[t * levels : (t + 1) * levels]
+        return total
+
+    spot = carried * levels
+    beyond = turned(y_got[0:cx, :])
+    behind = turned(y_got[cx : 2 * cx, :])
+    mine = turned(y_sent[0:cx, :])
+    north = is_even("facey")
+    second, inner_face = behind[0:levels], behind[2 * levels : 3 * levels]
+    edge_face, own_face = beyond[spot : spot + levels], mine[spot : spot + levels]
+    own_edge = summed(mine)
+    pieces_out[0] = summed(beyond)
+    pieces_out[1] = behind[levels : 2 * levels]
+    pieces_out[2] = edge_face
+    pieces_out[3] = jnp.where(north, inner_face, own_face)
+    pieces_out[4] = jnp.where(north, own_edge, second)
+    pieces_out[5] = jnp.where(north, second, own_edge)
+    mixing_out[...] = behind[3 * levels : 4 * levels]
+
+    def level_of(ref, level):
+        return jnp.broadcast_to(ref[level : level + 1, :], (8, LANES))
+
+    first = []
+    ratios = []
+    before = None
+    for level in range(levels):
+        diagonal = jnp.ones((8, LANES), F32)
+        if level > 0:
+            below = level_of(mixing_out, level - 1)
+            diagonal = diagonal + below
+        if level < levels - 1:
+            diagonal = diagonal + level_of(mixing_out, level)
+        if level > 0:
+            diagonal = diagonal - below * below * before
+        inverse = 1.0 / diagonal
+        ratios.append(level_of(mixing_out, level) * inverse if level < levels - 1 else jnp.zeros((8, LANES), F32))
+        inverse_out[level : level + 1, :] = inverse[0:1]
+        ratio_out[level : level + 1, :] = ratios[-1][0:1]
+        first.append(inverse if level == 0 else below * first[-1] * inverse)
+        before = inverse
+    weight = first
+    for level in range(levels - 2, -1, -1):
+        weight[level] = first[level] + ratios[level] * weight[level + 1]
+    for level in range(levels):
+        square[level : level + 1, :] = weight[level][0:1]
+    at = plan["y_tiles"] * cx + 8 * len(plan["y_blocks"])
+    strips = slots // LANES
+    cell = jnp.concatenate([y_got[at + n : at + n + 1, :] for n in range(strips)], axis=1).astype(jnp.int32)
+    live_out[...] = jnp.concatenate([y_got[at + strips + n : at + strips + n + 1, :] for n in range(strips)], axis=1)
+    on_edge = lax.rem(cell, cy) == jnp.where(north, 0, cy - 1)
+    x_of = jnp.where(on_edge, lax.div(cell, cy), LANES)
+    picks = jnp.where(iota((LANES, slots), 0) == x_of, 1.0, 0.0)
+    rows_out[...] = picks[0:cx]
+    picks = picks.astype(BF16)
+    picks_out[...] = picks
+    high, low = halves(square[0:levels, :])
+    columns_out[...] = jnp.dot(high, picks, preferred_element_type=F32) + jnp.dot(
+        low, picks, preferred_element_type=F32
+    )
 
 
 def factor_kernel(sizes, *refs):
     (tracer, west, south, mixing, adjoint, cells) = refs[:6]
-    inverse_out, ratio_out, base_out, inner_out, shares_out, columns_out, rows_out, picks_out = refs[6:]
+    inverse_out, ratio_out, base_out, inner_out, shares_out, columns_out, rows_out, picks_out, rim_out = refs[6:]
     carried, levels, cx, cy = tracer.shape
     slots = cells.shape[1]
     first = []
@@ -215,6 +349,10 @@
         for level in range(1, levels):
             total = total + weight[level] * adjoint[t, level]
         base_out[t] = total
+        edge = jnp.where(is_even("facey"), cy - 1, 0)
+        moved = pltpu.roll(total, lax.rem(t + cy - edge, cy), 1)
+        rim = jnp.where(iota((cx, cy), 1) == t, moved, jnp.zeros((cx, cy), F32) if t == 0 else rim)
+    rim_out[...] = rim
     for level in range(levels):
         total = tracer[0, level]
         for t in range(1, carried):
@@ -278,7 +416,13 @@
     n_pairs = len(plan["pairs"])
     pair_got = refs[1 : 1 + n_pairs]
     swapped = refs[1 + n_pairs] if n_pairs else None
-    modeled_out, state_out = refs[-2:]
+    if plan["relay"]:
+        x_got = refs[1 : 1 + len(plan["x_ops"])]
+        refs = refs[1 + len(plan["x_ops"]) :]
+        base, rim_base, *rim = refs[:10]
+        parcel, state_out, turn, rise = refs[10:]
+    else:
+        modeled_out, state_out = refs[-2:]
     levels, cx, cy = inner.shape
     slots = in_row.shape[1]
     head = (carried + 1) * levels
@@ -326,10 +470,25 @@
     picked = jnp.dot(high, picks, preferred_element_type=F32)
     picked = picked + jnp.dot(low, picks, preferred_element_type=F32)
 
-    blocks = {0: own[...], plan["y_block"]: y_got[0][cx : cx + 8, :]}
-    for number in range(2):
-        if plan["x_blocks"][number]:
-            blocks[plan["x_blocks"][number]] = got[number][head + 8 : head + 16, :]
+    start = plan["y_tiles"] * cx
+    if plan["relay"]:
+
+        def block_at(ref, row):
+            return ref[row : row + 8, :]
+
+        blocks = {0: block_at(own, 0), 1: block_at(y_got[0], start + 8)}
+        rim_blocks = {0: block_at(y_got[0], start), 1: block_at(own, 8)}
+        carriers = [(offset, got[n], head + 16) for n, offset in enumerate(plan["x_blocks"]) if offset]
+        carriers += [(offset, ref, 0) for offset, ref in zip(plan["x_ops"], x_got)]
+        for offset, ref, row in carriers:
+            blocks[offset], rim_blocks[offset + 1] = block_at(ref, row), block_at(ref, row + 8)
+            rim_blocks[offset], blocks[offset + 1] = block_at(ref, row + 16), block_at(ref, row + 24)
+    else:
+        blocks = {0: own[0:8, :], plan["y_blocks"][0]: y_got[0][start : start + 8, :]}
+        for number in range(2):
+            offset = plan["x_blocks"][number]
+            if offset:
+                blocks[offset] = got[number][head + 8 : head + 16, :]
     first_core = lax.axis_index("lev") == 0
     for number, (for_first, for_second) in enumerate(plan["pairs"]):
         mine = pair_got[number][...]
@@ -343,7 +502,7 @@
     per_tile = LANES // cap
     group_of_lane = lax.div(iota((8, LANES), 1), cap)
 
-    def gathered(group):
+    def gathered(group, blocks):
         tiles = []
         for start in range(0, len(blocks), per_tile):
             tile = jnp.zeros((8, LANES), F32)
@@ -353,8 +512,8 @@
             tiles.append(tile)
         return jnp.concatenate(tiles, axis=1)
 
-    groups = [gathered(g) for g in range(levels // 8)]
-    last = gathered(levels // 8)
+    groups = [gathered(g, blocks) for g in range(levels // 8)]
+    last = gathered(levels // 8, blocks)
     total = jnp.zeros((cx, slots), F32)
     sensitivity = jnp.zeros((8, slots), F32)
     for g, kernel in enumerate(groups):
@@ -362,9 +521,86 @@
         for l in range(8):
             level = 8 * g + l
             total = total + kernel[l : l + 1] * picked[level * cx : (level + 1) * cx]
-    modeled_out[...] = jnp.sum(total * in_row[...], axis=0, keepdims=True)
+    modeled = jnp.sum(total * in_row[...], axis=0, keepdims=True)
     gain = jnp.sum(sensitivity, axis=0, keepdims=True) * last[1:2] * live[...]
-    state_out[...] = jnp.concatenate([gain, last[0:1]], axis=0)
+    if not plan["relay"]:
+        modeled_out[...] = modeled
+        state_out[...] = jnp.concatenate([gain, last[0:1]], axis=0)
+        return
+
+    rim_inverse, rim_ratio, rim_mixing, pieces, rim_columns, rim_rows, rim_picks, rim_live = rim
+    corners_west, corners_east = sides(got[0][head + 8 : head + 16, :], got[1][head + 8 : head + 16, :])
+    turn[...] = jnp.zeros((LANES, LANES), F32)
+    turn[0:1, :] = corners_west[0:1]
+    turn[cx - 1 : cx, :] = corners_east[0:1]
+    turn[2 * cx - 1 : 2 * cx, :] = corners_east[1:2]
+    turned = jnp.transpose(turn[...])
+    ends = turned[0:levels]
+    for t in range(1, carried):
+        ends = ends + turned[t * levels : (t + 1) * levels]
+    end_face = pltpu.roll(turned[levels : 2 * levels], LANES - cx, 1)
+    place = iota((levels, LANES), 1)
+    cells, face_w, face_s, face_n, south_cells, north_cells = (pieces[n] for n in range(6))
+    west_cells = jnp.where(place == 0, ends, pltpu.roll(cells, 1, 1))
+    east_cells = jnp.where(place == cx - 1, ends, pltpu.roll(cells, LANES - 1, 1))
+    face_e = jnp.where(place == cx - 1, end_face, pltpu.roll(face_w, LANES - 1, 1))
+    rise[0:levels, :] = advance_cells(
+        cells, west_cells, east_cells, south_cells, north_cells, face_w, face_e, face_s, face_n
+    )
+
+    def level_of(ref, level):
+        return jnp.broadcast_to(ref[level : level + 1, :], (8, LANES))
+
+    climbed = []
+    for level in range(levels):
+        value = level_of(rise, level)
+        if level > 0:
+            value = value + level_of(rim_mixing, level - 1) * climbed[-1]
+        climbed.append(value * level_of(rim_inverse, level))
+    for level in range(levels - 2, -1, -1):
+        climbed[level] = climbed[level] + level_of(rim_ratio, level) * climbed[level + 1]
+    for level in range(levels):
+        rise[level : level + 1, :] = climbed[level][0:1]
+    high, low = halves(rise[0:levels, :])
+    picks = rim_picks[...]
+    picked = jnp.dot(high, picks, preferred_element_type=F32)
+    picked = picked + jnp.dot(low, picks, preferred_element_type=F32)
+    rim_total = jnp.zeros((8, slots), F32)
+    sensitivity = jnp.zeros((8, slots), F32)
+    for g in range(levels // 8):
+        kernel = gathered(g, rim_blocks)
+        rim_total = rim_total + kernel * picked[8 * g : 8 * g + 8]
+        sensitivity = sensitivity + kernel * rim_columns[8 * g : 8 * g + 8, :]
+    rim_modeled = jnp.sum(rim_total, axis=0, keepdims=True)
+    rim_last = gathered(levels // 8, rim_blocks)
+    rim_gain = jnp.sum(sensitivity, axis=0, keepdims=True) * rim_last[1:2] * rim_live[...]
+    state_out[...] = jnp.concatenate([gain, last[0:1], rim_gain, rim_last[0:1]], axis=0)
+    strips = slots // LANES
+    for number in range(strips):
+        part = slice(number * LANES, (number + 1) * LANES)
+        parcel[number : number + 1, :] = modeled[:, part]
+        parcel[strips + number : strips + number + 1, :] = rim_modeled[:, part]
+    at = plan["parcel"]
+    for t in range(carried):
+        parcel[at + t * cx : at + (t + 1) * cx, :] = base[t]
+    at = at + carried * cx
+    parcel[at : at + cx, :] = rim_base[...]
+    parcel[at + cx : at + 2 * cx, :] = y_got[0][0:cx, :]
+
+
+def advance_cells(cells, west, east, south, north, face_w, face_e, face_s, face_n):
+    flux_w = jnp.maximum(face_w, 0.0) * west + jnp.minimum(face_w, 0.0) * cells
+    flux_e = jnp.maximum(face_e, 0.0) * cells + jnp.minimum(face_e, 0.0) * east
+    flux_s = jnp.maximum(face_s, 0.0) * south + jnp.minimum(face_s, 0.0) * cells
+    flux_n = jnp.maximum(face_n, 0.0) * cells + jnp.minimum(face_n, 0.0) * north
+    return cells + flux_w - flux_e + flux_s - flux_n
+
+
+def scatter(force, in_row, in_lane):
+    high, low = halves(in_row * force)
+    dims = (((1,), (1,)), ((), ()))
+    scattered = lax.dot_general(high, in_lane, dims, preferred_element_type=F32)
+    return scattered + lax.dot_general(low, in_lane, dims, preferred_element_type=F32)
 
 
 def force_kernel(plan, *refs):
@@ -374,11 +610,7 @@
     carried, cx, cy = base.shape
     misfit = modeled[...] + modeled_other[...] - state[1:2, :]
     force = state[0:1, :] * misfit
-    high, low = halves(in_row[...] * force)
-    picks = in_lane[...]
-    dims = (((1,), (1,)), ((), ()))
-    scattered = lax.dot_general(high, picks, dims, preferred_element_type=F32)
-    scattered = scattered + lax.dot_general(low, picks, dims, preferred_element_type=F32)
+    scattered = scatter(force, in_row[...], in_lane[...])
     lane = iota((cx, cy), 1)
     even_y = is_even("facey")
     edges = []
@@ -397,12 +629,41 @@
 
 
 def surface_kernel(sizes, plan, carried, levels, *refs):
-    near, west, south, scale = refs[:4]
-    got = refs[4:6]
-    y_got = refs[6 : 6 + plan["y_ops"]]
-    rims = refs[6 + plan["y_ops"] : 6 + 2 * plan["y_ops"]]
-    outs = refs[6 + 2 * plan["y_ops"] :]
-    tracers, cx, cy = near.shape
+    y_ops = plan["y_ops"]
+    near = refs[0]
+    rims = refs[6 + y_ops : 6 + 2 * y_ops]
+    rim_values = [[rim[...] for rim in rims] for _ in range(near.shape[0])]
+    values = [near[t] for t in range(near.shape[0])]
+    spread_surface(
+        sizes, plan, carried, levels, values, rim_values, refs[1:4], refs[4:6], refs[6 : 6 + y_ops], refs[6 + 2 * y_ops :]
+    )
+
+
+def weigh_kernel(sizes, plan, carried, levels, *refs):
+    parcel, other, state, in_row, in_lane, base, rim_rows, rim_base = refs[:8]
+    cx, cy = base.shape[1:]
+    strips = state.shape[1] // LANES
+
+    def misfit(kind):
+        both = parcel[kind * strips : (kind + 1) * strips, :] + other[kind * strips : (kind + 1) * strips, :]
+        flat = jnp.concatenate([both[n : n + 1] for n in range(strips)], axis=1)
+        return state[2 * kind : 2 * kind + 1, :] * (flat - state[2 * kind + 1 : 2 * kind + 2, :])
+
+    scattered = scatter(misfit(0), in_row[...], in_lane[...])
+    on_rim = jnp.sum(rim_rows[...] * misfit(1), axis=1, keepdims=True)
+    at = plan["parcel"]
+    near = [scattered + base[t] for t in range(carried)]
+    near += [scattered + other[at + t * cx : at + (t + 1) * cx, :] for t in range(carried)]
+    at = at + carried * cx
+    mine, others = other[at : at + cx, :] + on_rim, rim_base[...] + on_rim
+    rims = [[mine if t < carried else others] for t in range(2 * carried)]
+    spread_surface(sizes, plan, carried, levels, near, rims, refs[8:11], refs[11:13], refs[13:14], refs[14:])
+
+
+def spread_surface(sizes, plan, carried, levels, near, rim_values, fields, got, y_got, outs):
+    west, south, scale = fields
+    tracers = len(near)
+    cx, cy = near[0].shape
     band = cy // sizes[0]
     per_tile = min(tracers, LANES // band)
     spot = carried * levels
@@ -438,11 +699,12 @@
         north_side = left(values)
         south_side = right(values)
         for number in range(plan["y_ops"]):
-            rim = rims[number][...]
+            rim = rim_values[t][number]
+            spot_t = t % carried if plan["relay"] else t
             at_north = jnp.logical_and(lane == cy - 1, norths[number])
             at_south = jnp.logical_and(lane == 0, jnp.logical_not(norths[number]))
-            north_side = jnp.where(at_north, pltpu.roll(rim, (cy - 1 - t) % cy, 1), north_side)
-            south_side = jnp.where(at_south, pltpu.roll(rim, (-t) % cy, 1), south_side)
+            north_side = jnp.where(at_north, pltpu.roll(rim, (cy - 1 - spot_t) % cy, 1), north_side)
+            south_side = jnp.where(at_south, pltpu.roll(rim, (-spot_t) % cy, 1), south_side)
         swept = to_middle * values + to_east * pltpu.roll(values, cx - 1, 0) - to_west * pltpu.roll(values, 1, 0)
         swept = swept + to_north * north_side - to_south * south_side
         grown.append(
@@ -458,10 +720,11 @@
         offset = for_first if for_first == for_second else jnp.where(first_core, for_first, for_second)
         target = jnp.bitwise_xor(place, offset)
         count = carried if for_first == for_second else tracers
+        skip = carried if for_first == for_second != 0 and plan["cross"] else 0
         for start in range(0, count, per_tile):
             tile = jnp.zeros((rows, cy), F32)
             for a in range(min(per_tile, count - start)):
-                moved = pltpu.roll(grown[start + a], lax.rem(band * a + cy - band * target, cy), 1)
+                moved = pltpu.roll(grown[skip + start + a], lax.rem(band * a + cy - band * target, cy), 1)
                 tile = jnp.where(group_of_lane == a, moved, tile)
             out[start // per_tile * rows : (start // per_tile + 1) * rows, :] = tile
 
@@ -482,7 +745,8 @@
     parts = []
     row_places = []
     for block, (for_first, for_second) in zip(blocks, plan["bands"]):
-        offset = for_first if for_first == for_second else jnp.where(first_core, for_first, for_second)
+        from_first, from_second = (for_second, for_first) if plan["cross"] else (for_first, for_second)
+        offset = for_first if for_first == for_second else jnp.where(first_core, from_first, from_second)
         start = jnp.bitwise_xor(place, offset) * cx
         places = start + row
         places = jnp.where(row == cx, lax.rem(start + around - 1, around), places)
@@ -518,8 +782,10 @@
                 at += rows
     sums = [jnp.zeros((1, cells), F32) for _ in range(tracers)]
     for mine in totals:
+        skip = carried if len(mine) == tracers and plan["cross"] else 0
         for t, total in enumerate(mine):
-            sums[t] = sums[t] + jnp.sum(total, axis=0, keepdims=True)
+            to = (t + skip) % tracers
+            sums[to] = sums[to] + jnp.sum(total, axis=0, keepdims=True)
     out[...] = jnp.concatenate(sums, axis=0)
 
 
@@ -614,16 +880,30 @@
     many_x, many_y, _ = sizes
     tiles = many_x * many_y
     x_blocks = [many_y, (many_x - 1) * many_y if many_x == 4 else 0]
-    taken = {0, 1, *x_blocks}
-    rest = [d for d in range(tiles) if d not in taken]
-    rest.sort(key=lambda d: (d // many_y != many_x // 2, d))
-    pairs = [(rest[n], rest[min(n + 1, len(rest) - 1)]) for n in range(0, len(rest), 2)]
+    relay = many_y == 2
+    if relay:
+        own_blocks = list(range(tiles))
+        y_blocks = own_blocks
+        x_ops = [offset for offset in own_blocks[2::2] if offset not in x_blocks]
+        pairs = []
+    else:
+        own_blocks = [0] + [offset for offset in x_blocks if offset]
+        y_blocks = [1]
+        x_ops = []
+        rest = [d for d in range(tiles) if d not in {1, *own_blocks}]
+        rest.sort(key=lambda d: (d // many_y != many_x // 2, d))
+        pairs = [(rest[n], rest[min(n + 1, len(rest) - 1)]) for n in range(0, len(rest), 2)]
     others = list(range(many_x - 1, 1, -1))
     bands = [(0, 0), (1, 1)] + [(others[n], others[n + 1]) for n in range(0, len(others), 2)]
     return {
+        "relay": relay,
+        "cross": 1 if relay else 0,
         "x_blocks": x_blocks,
-        "y_block": 1,
+        "x_ops": x_ops,
+        "own_blocks": own_blocks,
+        "y_blocks": y_blocks,
         "y_ops": 1 if many_y == 2 else 2,
+        "y_tiles": 2 if relay else 1,
         "pairs": pairs,
         "bands": bands,
     }
@@ -665,29 +945,33 @@
     def next_y(number):
         def rule(x, y, c):
             to = y + (1 if (y % 2 == 0) == (number == 0) else -1)
-            return (x, to, c) if 0 <= to < many_y else None
+            return (x, to, c ^ plan["cross"]) if 0 <= to < many_y else None
 
         return rule
 
-    def jump(for_first, for_second):
+    def jump(for_first, for_second, cross=0):
         def rule(x, y, c):
             d = for_first if c == 0 else for_second
-            return (x ^ (d // many_y), y ^ (d % many_y), c)
+            return (x ^ (d // many_y), y ^ (d % many_y), c ^ cross)
 
         return rule
 
     def other_core(values):
         return exchange(values, sizes, lambda x, y, c: (x, y, 1 - c))
 
-    row_shapes = [shape(head + (16 if plan["x_blocks"][n] else 8), cy) for n in range(2)]
-    lane_shapes = [shape(cx + (8 if n == 0 else 0), cy) for n in range(y_ops)]
+    strips = slots // LANES
+    plan["parcel"] = -(-2 * strips // 8) * 8
+    extra = 48 if plan["relay"] else 16
+    row_shapes = [shape(head + extra, cy)] * 2
+    y_rows = plan["y_tiles"] * cx + 8 * len(plan["y_blocks"]) + (plan["parcel"] if plan["relay"] else 0)
+    lane_shapes = [shape(y_rows if n == 0 else cx, cy) for n in range(y_ops)]
     packed = call(
         functools.partial(pack_kernel, sizes, plan),
-        row_shapes
-        + lane_shapes
-        + [shape(8, LANES)] * (1 + len(plan["pairs"]))
+        lane_shapes
+        + [shape(8 * len(plan["own_blocks"]), LANES)]
+        + [shape(8, LANES)] * len(plan["pairs"])
         + [shape(1, slots, dtype=jnp.int32), shape(1, slots)]
-        + [shape(*tracer.shape), shape(*west_courant.shape), shape(*south_courant.shape)],
+        + [shape(*a.shape) for a in (tracer, west_courant, south_courant, emission_scale, mixing)],
         [
             tracer,
             west_courant,
@@ -698,29 +982,27 @@
             error_weight.reshape(owners, cap),
             send_cells.reshape(owners, cap),
             send_counts.reshape(owners),
+            mixing,
         ],
         "pack",
         100000,
-        hbm=range(9),
+        hbm=range(10),
         scratch=[
-            pltpu.VMEM((cx, cy), F32),
             pltpu.VMEM((owners, levels, cap), F32),
             pltpu.VMEM((owners, cap), F32),
             pltpu.VMEM((owners, cap), F32),
             pltpu.VMEM((owners, cap), jnp.int32),
             pltpu.SMEM((owners,), jnp.int32),
-            pltpu.SemaphoreType.DMA((8 + carried,)),
+            pltpu.SemaphoreType.DMA((9 + carried,)),
         ],
     )
-    rows_sent = packed[:2]
-    lanes_sent = packed[2 : 2 + y_ops]
-    own_block = packed[2 + y_ops]
-    pair_sent = packed[3 + y_ops : -5]
-    cell, live, tracer, west_courant, south_courant = packed[-5:]
-    rows_got = [exchange(rows_sent[n], sizes, next_x(n)) for n in range(2)]
+    lanes_sent = packed[:y_ops]
+    own_blocks = packed[y_ops]
+    pair_sent = packed[1 + y_ops : -7]
+    cell, live, tracer, west_courant, south_courant, emission_scale, mixing = packed[-7:]
     lanes_got = [exchange(lanes_sent[n], sizes, next_y(n)) for n in range(y_ops)]
-    pair_got = [exchange(s, sizes, jump(*p)) for s, p in zip(pair_sent, plan["pairs"])]
-    inverse, ratio, base, inner, parts, columns, in_row, in_lane = call(
+    held, *_ = lax.optimization_barrier((tracer, *lanes_sent))
+    inverse, ratio, base, inner, parts, columns, in_row, in_lane, base_rim = call(
         functools.partial(factor_kernel, sizes),
         [
             shape(levels, cx, cy),
@@ -731,44 +1013,107 @@
             shape(levels, slots),
             shape(cx, slots),
             shape(cy, slots, dtype=BF16),
+            shape(cx, cy),
         ],
-        [
-            tracer,
-            west_courant,
-            south_courant,
-            mixing,
-            adjoint_later,
-            cell,
-        ],
+        [held, west_courant, south_courant, mixing, adjoint_later, cell],
         "factor",
         3000000,
     )
-    base_other = other_core(base)
-    swapped = [other_core(jnp.concatenate(pair_got, axis=0))] if pair_got else []
-    modeled, state = call(
-        functools.partial(observe_kernel, sizes, plan, carried),
-        [shape(1, slots), shape(2, slots)],
-        [inner, mixing, inverse, ratio, columns, in_row, in_lane, live]
-        + list(rows_sent)
-        + rows_got
-        + list(lanes_sent)
-        + lanes_got
-        + [own_block]
-        + pair_got
-        + swapped,
-        "observe",
-        2000000,
-    )
-    modeled_other = other_core(modeled)
-    near, *rims_sent = call(
-        functools.partial(force_kernel, plan),
-        [shape(2 * carried, cx, cy)] + [shape(cx, cy)] * y_ops,
-        [modeled, modeled_other, state, in_row, in_lane, base, base_other],
-        "force",
-        200000,
-    )
-    rims_got = [exchange(rims_sent[n], sizes, next_y(n)) for n in range(y_ops)]
-    held, *_ = lax.optimization_barrier((tracer, *rims_sent))
+    rows_sent = call(
+        functools.partial(rows_kernel, plan),
+        row_shapes,
+        [tracer, west_courant, emission_scale, own_blocks],
+        "rows",
+        100000,
+    )
+    per_tile = min(2 * carried, LANES // band)
+
+    def band_shape(first, second):
+        count = carried if first == second else 2 * carried
+        return shape(-(-count // per_tile) * (cx + 8), cy)
+
+    band_shapes = [band_shape(*b) for b in plan["bands"]]
+    fields = [west_courant[0], south_courant[0], emission_scale]
+    observe = functools.partial(
+        call, functools.partial(observe_kernel, sizes, plan, carried), name="observe", flops=2000000
+    )
+    if plan["relay"]:
+        base, *lanes_got = lax.optimization_barrier((base, *lanes_got))
+        relayed = call(
+            functools.partial(relay_kernel, plan, head, cx),
+            row_shapes + [shape(32, LANES)] * len(plan["x_ops"]),
+            [*rows_sent, own_blocks, lanes_got[0]],
+            "relay",
+            10000,
+        )
+        rows_sent, x_sent = relayed[:2], relayed[2:]
+        second_got = exchange(rows_sent[1], sizes, next_x(1))
+        x_got = [exchange(s, sizes, jump(d, d, 1)) for s, d in zip(x_sent, plan["x_ops"])]
+        rows_got = [exchange(rows_sent[0], sizes, next_x(0)), second_got]
+        held_y, *_ = lax.optimization_barrier((lanes_got[0], *rows_sent, *x_sent))
+        rim = call(
+            functools.partial(rim_kernel, plan, carried, levels, cx),
+            [
+                shape(levels, LANES),
+                shape(levels, LANES),
+                shape(levels, LANES),
+                shape(6, levels, LANES),
+                shape(levels, slots),
+                shape(cx, slots),
+                shape(LANES, slots, dtype=BF16),
+                shape(1, slots),
+            ],
+            [lanes_sent[0], held_y],
+            "rim",
+            400000,
+            scratch=[pltpu.VMEM((LANES, LANES), F32)],
+        )
+        base_rim, _ = lax.optimization_barrier((base_rim, rim[0]))
+        rim_base = exchange(base_rim, sizes, next_y(0))
+        parcel_rows = plan["parcel"] + (carried + 2) * cx
+        parcel, state = observe(
+            [shape(parcel_rows, cy), shape(4, slots)],
+            [inner, mixing, inverse, ratio, columns, in_row, in_lane, live, *rows_sent, *rows_got]
+            + [*lanes_sent, *lanes_got, own_blocks, *x_got, base, rim_base, *rim],
+            scratch=[pltpu.VMEM((LANES, LANES), F32), pltpu.VMEM((levels, LANES), F32)],
+        )
+        parcel_other = other_core(parcel)
+        band_sent = call(
+            functools.partial(weigh_kernel, sizes, plan, carried, levels),
+            band_shapes,
+            [parcel, parcel_other, state, in_row, in_lane, base, rim[5], rim_base, *fields, *rows_got, *lanes_got],
+            "weigh",
+            500000,
+        )
+        lanes_own = [parcel_other[parcel_rows - cx :]]
+        held, *_ = lax.optimization_barrier((tracer, *band_sent))
+    else:
+        rows_got = [exchange(rows_sent[n], sizes, next_x(n)) for n in range(2)]
+        pair_got = [exchange(s, sizes, jump(*p)) for s, p in zip(pair_sent, plan["pairs"])]
+        base_other = other_core(base)
+        modeled, state = observe(
+            [shape(1, slots), shape(2, slots)],
+            [inner, mixing, inverse, ratio, columns, in_row, in_lane, live, *rows_sent, *rows_got]
+            + [*lanes_sent, *lanes_got, own_blocks, *pair_got]
+            + [other_core(jnp.concatenate(pair_got, axis=0))],
+        )
+        near, *rims_sent = call(
+            functools.partial(force_kernel, plan),
+            [shape(2 * carried, cx, cy)] + [shape(cx, cy)] * y_ops,
+            [modeled, other_core(modeled), state, in_row, in_lane, base, base_other],
+            "force",
+            200000,
+        )
+        rims_got = [exchange(rims_sent[n], sizes, next_y(n)) for n in range(y_ops)]
+        band_sent = call(
+            functools.partial(surface_kernel, sizes, plan, carried, levels),
+            band_shapes,
+            [near, *fields, *rows_got, *lanes_got, *rims_got],
+            "surface",
+            400000,
+        )
+        lanes_own = lanes_got
+        held = tracer
     (advanced,) = call(
         functools.partial(advance_kernel, plan),
         [shape(*tracer.shape)],
@@ -776,7 +1121,7 @@
         + list(rows_sent)
         + rows_got
         + list(lanes_sent)
-        + lanes_got,
+        + lanes_own,
         "advance",
         6000000,
         scratch=[pltpu.VMEM(tracer.shape, F32)]
@@ -784,24 +1129,13 @@
         + [pltpu.SemaphoreType.DMA((levels // 4,))],
         out_hbm=(0,),
     )
-    advanced, *rims_got = lax.optimization_barrier((advanced, *rims_got))
-    per_tile = min(2 * carried, LANES // band)
-
-    def band_shape(first, second):
-        count = carried if first == second else 2 * carried
-        return shape(-(-count // per_tile) * (cx + 8), cy)
-
-    band_sent = call(
-        functools.partial(surface_kernel, sizes, plan, carried, levels),
-        [band_shape(*b) for b in plan["bands"]],
-        [near, west_courant[0], south_courant[0], emission_scale] + rows_got + lanes_got + rims_got,
-        "surface",
-        400000,
-    )
     band_got = [
-        s if first == second == 0 else exchange(s, sizes, jump(first * many_y, second * many_y))
+        s
+        if first == second == 0
+        else exchange(s, sizes, jump(first * many_y, second * many_y, plan["cross"]))
         for s, (first, second) in zip(band_sent, plan["bands"])
     ]
+    advanced, *band_got = lax.optimization_barrier((advanced, *band_got))
     (sums,) = call(
         functools.partial(regrid_kernel, sizes, plan, carried, cx, band),
         [shape(2 * carried, ll)],

time: 30.9 us -> 28 us (0.906)
  waiting for transfers between devices: 9.65 us -> 7.79 us
  starting transfers between devices: 13.2 us -> 11.6 us
  Pallas kernels: 6.52 us -> 7.19 us
    ppermute x12 -> x9, waiting for transfers between devices: 9.65 us -> 7.79 us  [exchange(): return lax.ppermute(values, GROUP, pairs)]
    ppermute x12 -> x9, starting transfers between devices: 13.2 us -> 11.6 us  [exchange(): return lax.ppermute(values, GROUP, pairs)]
    pallas_call x7 -> x9, Pallas kernels: 6.52 us -> 7.19 us  [call(): pl.pallas_call(body, out_shape=outs, in_specs=[pl.BlockSpec(memory_space=...]
  transfers between devices with their start and end apart: 12 -> 9, of which waited for: 7 -> 6; matrix products, arithmetic and copies ran while one was open for 0% -> 0% of each run, Pallas kernels for 11% -> 12%
where the time goes in v3:
time: 28 us; the launch traced here: 27.9 us
  starting transfers between devices  11.6 us (41%)
  waiting for transfers between devices  7.79 us (28%)
  Pallas kernels  7.19 us (26%)
  between operations  0.72 us (3%)
  other arithmetic  0.58 us (2%)
    ppermute x9, starting transfers between devices, exchange(): return lax.ppermute(values, GROUP, pairs)  11.6 us
    ppermute x9, waiting for transfers between devices, exchange(): return lax.ppermute(values, GROUP, pairs)  7.79 us
    pallas_call x9, Pallas kernels, call(): pl.pallas_call(body, out_shape=outs, in_specs=[pl.BlockSpec(memory_space=...  7.19 us
    add x1, other arithmetic, local(): latlon = sums[:carried] + sums_other  0.58 us
  transfers between devices with their start and end apart: 9, of which 6 were waited for; matrix products, arithmetic and copies ran while one was open for 0% of the time, Pallas kernels for 12%

profile of v3, /device:TPU:0, one launch (start us, length us, event | category | flops | bytes accessed | tf_op | source)
XLA Modules:
  0.0 27.9 jit_solution(6597525018456243620)
XLA Ops:
  0.6 2.1 %pack.1 = (f32[104,128]{1,0:T(8,128)S(1)}, f32[64,128]{1,0:T(8,128)S(1)}, s32[1,256]{1,0:T(1,128)S(1)}, f32[1,256]{1,0:T(1,128)S(1)}, f32[4,24,16,128]{3,2,1,0:T...) custom-call(f32[4,24,16,128]{3,2,1,0:T(8,128)} %refs_0_.1, ...), custom_call_target="tpu_custom_call" | custom-call | flops 100000 | bytes 2868256 | tf_op jit(solution)/shard_map/pack/pallas_call | solution.py:22
  2.8 0.0 copy-start
  2.8 2.4 %collective-permute-start = (f32[104,128]{1,0:T(8,128)S(1)}, f32[104,128]{1,0:T(8,128)S(1)}, u32[]{:S(2)}, u32[]{:S(2)}) collective-permute-start(f32[104,128]{1,0:T(8,128)S(1)} %get-tuple-element.49.y_sent.refs_12_.refs_9_), channel_id=1, source_target_pairs={{0,3},{1,2},{2,1},{3,0},{4,7},{5,6},{6,5},{7,4},{8,11},{9,10},{10,... | collective-permute-start | bytes 159752 | tf_op jit(solution)/shard_map/ppermute | solution.py:876
  5.2 0.1 rows.1
  5.3 0.0 copy-done
  5.3 0.7 %factor.1 = (f32[24,16,128]{2,1,0:T(8,128)S(1)}, f32[24,16,128]{2,1,0:T(8,128)S(1)}, f32[4,16,128]{2,1,0:T(8,128)S(1)}, f32[24,16,128]{2,1,0:T(8,128)S(1)}, f32[...) custom-call(f32[4,24,16,128]{3,2,1,0:T(8,128)S(1)} %get-tuple-elemen, ...), custom_call_target="tpu_custom_call" | custom-call | flops 3000000 | bytes 3941376 | tf_op jit(solution)/shard_map/factor/pallas_call | solution.py:22
  6.0 1.5 %collective-permute-done.refs_3_.y_got.refs_13_ = f32[104,128]{1,0:T(8,128)S(1)} collective-permute-done((f32[104,128]{1,0:T(8,128)S(1)}, f32[104,128]{1,0:T(8,128)S(1)}, u32[]{:S(2)}, u32[]{:S(2)}) %collective-permute-start) | collective-permute-done | bytes 53280 | tf_op jit(solution)/shard_map/ppermute | solution.py:876
  7.5 2.6 %collective-permute-start.1 = (f32[168,128]{1,0:T(8,128)S(1)}, f32[168,128]{1,0:T(8,128)S(1)}, u32[]{:S(2)}, u32[]{:S(2)}) collective-permute-start(f32[168,128]{1,0:T(8,128)S(1)} %get-tuple-element.68.refs_8_.refs_5_), channel_id=1, source_target_pairs={{0,4},{1,5},{2,6},{3,7},{4,0},{5,1},{6,2},{7,3},{8,12},{9,13},{10,... | collective-permute-start | bytes 258056 | tf_op jit(solution)/shard_map/ppermute | solution.py:876
  10.0 2.5 %collective-permute-start.2 = (f32[168,128]{1,0:T(8,128)S(1)}, f32[168,128]{1,0:T(8,128)S(1)}, u32[]{:S(2)}, u32[]{:S(2)}) collective-permute-start(f32[168,128]{1,0:T(8,128)S(1)} %get-tuple-element.69.refs_9_.refs_6_), channel_id=1, source_target_pairs={{0,12},{1,13},{2,14},{3,15},{4,8},{5,9},{6,10},{7,11},{8,4},{9,5},... | collective-permute-start | bytes 258056 | tf_op jit(solution)/shard_map/ppermute | solution.py:876
  12.5 0.0 collective-permute-start.3
  12.5 0.4 %rim.1 = (f32[24,128]{1,0:T(8,128)S(1)}, f32[24,128]{1,0:T(8,128)S(1)}, f32[24,128]{1,0:T(8,128)S(1)}, f32[6,24,128]{2,1,0:T(8,128)S(1)}, f32[24,256]{1,0:T(8,12...) custom-call(f32[104,128]{1,0:T(8,128)S(1)} %get-tuple-element.49.y_sent.refs_12_.refs_9_, ...), custom_call_target="tpu_custom_call" | custom-call | flops 400000 | bytes 390144 | tf_op jit(solution)/shard_map/rim/pallas_call | solution.py:22
  13.0 1.4 %collective-permute-start.4 = (f32[16,128]{1,0:T(8,128)S(1)}, f32[16,128]{1,0:T(8,128)S(1)}, u32[]{:S(2)}, u32[]{:S(2)}) collective-permute-start(f32[16,128]{1,0:T(8,128)S(1)} %get-tuple-element.75), channel_id=1, source_target_pairs={{0,3},{1,2},{2,1},{3,0},{4,7},{5,6},{6,5},{7,4},{8,11},{9,10},{10,... | collective-permute-start | bytes 24584 | tf_op jit(solution)/shard_map/ppermute | solution.py:876
  14.4 1.7 %collective-permute-done.4.refs_17_.refs_7_ = f32[16,128]{1,0:T(8,128)S(1)} collective-permute-done((f32[16,128]{1,0:T(8,128)S(1)}, f32[16,128]{1,0:T(8,128)S(1)}, u32[]{:S(2)}, u32[]{:S(2)}) %collective-permute-start.4) | collective-permute-done | bytes 8224 | tf_op jit(solution)/shard_map/ppermute | solution.py:876
  16.1 1.6 %collective-permute-done.3.refs_15_ = f32[32,128]{1,0:T(8,128)S(1)} collective-permute-done((f32[32,128]{1,0:T(8,128)S(1)}, f32[32,128]{1,0:T(8,128)S(1)}, u32[]{:S(2)}, u32[]{:S(2)}) %collective-permute-start.3) | collective-permute-done | bytes 16416 | tf_op jit(solution)/shard_map/ppermute | solution.py:876
  17.7 0.0 collective-permute-done.1.refs_10_.refs_11_.refs_7_
  17.7 0.0 collective-permute-done.2.refs_11_.refs_12_.refs_8_
  17.7 0.7 %observe.1 = (f32[104,128]{1,0:T(8,128)S(1)}, f32[4,256]{1,0:T(4,128)S(1)}) custom-call(f32[24,16,128]{2,1,0:T(8,128)S(1)} %get-tuple-element.55.refs_0_, f32[23,16,128]{2,1,0:T(8,128)S(1)} %get-tuple-element.53.refs_3_.refs_1_.refs_2_, f32[24,16,128]{2,1,0:T(8,128)S(1)} %get-tuple-element.56.refs_2_.refs_3_, ...), custom_call_target="tpu_custom_call" | custom-call | flops 2000000 | bytes 1832960 | tf_op jit(solution)/shard_map/observe/pallas_call | solution.py:22
  18.4 0.1 collective-permute-start.5
  18.6 1.2 %collective-permute-done.5.refs_1_ = f32[104,128]{1,0:T(8,128)S(1)} collective-permute-done((f32[104,128]{1,0:T(8,128)S(1)}, f32[104,128]{1,0:T(8,128)S(1)}, u32[]{:S(2)}, u32[]{:S(2)}) %collective-permute-start.5) | collective-permute-done | bytes 53280 | tf_op jit(solution)/shard_map/ppermute | solution.py:876
  19.7 0.3 %weigh.1 = (f32[24,128]{1,0:T(8,128)S(1)}, f32[24,128]{1,0:T(8,128)S(1)}, f32[48,128]{1,0:T(8,128)S(1)}) custom-call(f32[104,128]{1,0:T(8,128)S(1)} %get-tuple-element.83.refs_0_, f32[104,128]{1,0:T(8,128)S(1)} %collective-permute-done.5.refs_1_, f32[4,256]{1,0:T(4,128)S(1)} %get-tuple-element.84.refs_2_, f32[16,256]{1,0:T(8,128)S(1)} %get-tuple-element.59.refs_5_.refs_3_, ...), custom_call_target="tpu_custom_call" | custom-call | flops 500000 | bytes 614400 | tf_op jit(solution)/shard_map/weigh/pallas_call | solution.py:22
  20.1 2.1 %collective-permute-start.7 = (f32[48,128]{1,0:T(8,128)S(1)}, f32[48,128]{1,0:T(8,128)S(1)}, u32[]{:S(2)}, u32[]{:S(2)}) collective-permute-start(f32[48,128]{1,0:T(8,128)S(1)} %get-tuple-element.87), channel_id=1, source_target_pairs={{0,13},{1,8},{2,15},{3,10},{4,9},{5,12},{6,11},{7,14},{8,5},{9,0},... | collective-permute-start | bytes 73736 | tf_op jit(solution)/shard_map/ppermute | solution.py:876
  22.2 0.3 %collective-permute-start.6 = (f32[24,128]{1,0:T(8,128)S(1)}, f32[24,128]{1,0:T(8,128)S(1)}, u32[]{:S(2)}, u32[]{:S(2)}) collective-permute-start(f32[24,128]{1,0:T(8,128)S(1)} %get-tuple-element.86), channel_id=1, source_target_pairs={{0,5},{1,4},{2,7},{3,6},{4,1},{5,0},{6,3},{7,2},{8,13},{9,12},{10,... | collective-permute-start | bytes 36872 | tf_op jit(solution)/shard_map/ppermute | solution.py:876
  22.5 0.0 copy-start.1
  22.5 0.0 copy-start.2
  22.5 2.1 %advance.1 = f32[4,24,16,128]{3,2,1,0:T(8,128)} custom-call(f32[4,24,16,128]{3,2,1,0:T(8,128)S(1)} %get-tuple-element.88.refs_0_.tracer, f32[5,24,16,128]{3,2,1,0:T(8,128)S(1)} %get-tuple-element.89.refs_1_, f32[23,16,128]{2,1,0:T(8,128)S(1)} %get-tuple-element.53.refs_3_.refs_1_.refs_2_, f32[24,16,128]{2,1,0:T(8,128)S(1)} %get-tuple-element.56.refs_2_.refs_3_, ...), custom_call_target="tpu_custom_call" | custom-call | flops 6000000 | bytes 3543040 | tf_op jit(solution)/shard_map/advance/pallas_call | solution.py:22
  24.6 0.7 %collective-permute-done.6.refs_3_ = f32[24,128]{1,0:T(8,128)S(1)} collective-permute-done((f32[24,128]{1,0:T(8,128)S(1)}, f32[24,128]{1,0:T(8,128)S(1)}, u32[]{:S(2)}, u32[]{:S(2)}) %collective-permute-start.6) | collective-permute-done | bytes 12320 | tf_op jit(solution)/shard_map/ppermute | solution.py:876
  25.3 0.0 collective-permute-done.7.refs_4_
  25.3 0.0 copy-done.1
  25.3 0.0 copy-done.2
  25.3 0.7 %regrid.1 = f32[8,128]{1,0:T(8,128)S(1)} custom-call(s32[16,128]{1,0:T(8,128)S(1)} %bitcast.14, f32[16,128]{1,0:T(8,128)S(1)} %bitcast.15, f32[24,128]{1,0:T(8,128)S(1)} %get-tuple-element.91.refs_2_, f32[24,128]{1,0:T(8,128)S(1)} %collective-permute-done.6.refs_3_, f32[48,128]{1,0:T(8,128)S(1)} %collective-permute-done.7.refs_4_), custom_call_target="tpu_custom_call" | custom-call | flops 1000000 | bytes 69632 | tf_op jit(solution)/shard_map/regrid/pallas_call | solution.py:22
  26.1 0.1 collective-permute-start.8
  26.2 1.1 %collective-permute-done.8 = f32[4,128]{1,0:T(4,128)S(1)} collective-permute-done((f32[4,128]{1,0:T(4,128)S(1)}, f32[4,128]{1,0:T(4,128)S(1)}, u32[]{:S(2)}, u32[]{:S(2)}) %collective-permute-start.8) | collective-permute-done | bytes 2080 | tf_op jit(solution)/shard_map/ppermute | solution.py:876
  27.3 0.6 %slice_add_fusion = f32[4,128]{1,0:T(4,128)} fusion(f32[4,128]{1,0:T(4,128)S(1)} %collective-permute-done.8, f32[8,128]{1,0:T(8,128)S(1)} %regrid.1), kind=kLoop, calls=%fused_computation.2 | loop fusion | flops 512 | bytes 6144 | tf_op jit(solution)/shard_map/add | solution.py:1147
  (4 shorter events, 0.0 us)
Async XLA Ops:
  2.8 2.5 %copy-start = (f32[4,24,16,128]{3,2,1,0:T(8,128)S(1)}, f32[4,24,16,128]{3,2,1,0:T(8,128)}, u32[]{:S(2)}) copy-start(f32[4,24,16,128]{3,2,1,0:T(8,128)} %refs_4_.1) | copy-start | bytes 2359300
  2.8 4.7 %collective-permute-start = (f32[104,128]{1,0:T(8,128)S(1)}, f32[104,128]{1,0:T(8,128)S(1)}, u32[]{:S(2)}, u32[]{:S(2)}) collective-permute-start(f32[104,128]{1,0:T(8,128)S(1)} %get-tuple-element.49.y_sent.refs_12_.refs_9_), channel_id=1, source_target_pairs={{0,3},{1,2},{2,1},{3,0},{4,7},{5,6},{6,5},{7,4},{8,11},{9,10},{10,... | collective-permute-start | bytes 159752 | tf_op jit(solution)/shard_map/ppermute | solution.py:876
  7.5 10.2 %collective-permute-start.1 = (f32[168,128]{1,0:T(8,128)S(1)}, f32[168,128]{1,0:T(8,128)S(1)}, u32[]{:S(2)}, u32[]{:S(2)}) collective-permute-start(f32[168,128]{1,0:T(8,128)S(1)} %get-tuple-element.68.refs_8_.refs_5_), channel_id=1, source_target_pairs={{0,4},{1,5},{2,6},{3,7},{4,0},{5,1},{6,2},{7,3},{8,12},{9,13},{10,... | collective-permute-start | bytes 258056 | tf_op jit(solution)/shard_map/ppermute | solution.py:876
  10.0 7.7 %collective-permute-start.2 = (f32[168,128]{1,0:T(8,128)S(1)}, f32[168,128]{1,0:T(8,128)S(1)}, u32[]{:S(2)}, u32[]{:S(2)}) collective-permute-start(f32[168,128]{1,0:T(8,128)S(1)} %get-tuple-element.69.refs_9_.refs_6_), channel_id=1, source_target_pairs={{0,12},{1,13},{2,14},{3,15},{4,8},{5,9},{6,10},{7,11},{8,4},{9,5},... | collective-permute-start | bytes 258056 | tf_op jit(solution)/shard_map/ppermute | solution.py:876
  12.5 5.2 %collective-permute-start.3 = (f32[32,128]{1,0:T(8,128)S(1)}, f32[32,128]{1,0:T(8,128)S(1)}, u32[]{:S(2)}, u32[]{:S(2)}) collective-permute-start(f32[32,128]{1,0:T(8,128)S(1)} %get-tuple-element.70), channel_id=1, source_target_pairs={{0,9},{1,8},{2,11},{3,10},{4,13},{5,12},{6,15},{7,14},{8,1},{9,0},... | collective-permute-start | bytes 49160 | tf_op jit(solution)/shard_map/ppermute | solution.py:876
  13.0 3.1 %collective-permute-start.4 = (f32[16,128]{1,0:T(8,128)S(1)}, f32[16,128]{1,0:T(8,128)S(1)}, u32[]{:S(2)}, u32[]{:S(2)}) collective-permute-start(f32[16,128]{1,0:T(8,128)S(1)} %get-tuple-element.75), channel_id=1, source_target_pairs={{0,3},{1,2},{2,1},{3,0},{4,7},{5,6},{6,5},{7,4},{8,11},{9,10},{10,... | collective-permute-start | bytes 24584 | tf_op jit(solution)/shard_map/ppermute | solution.py:876
  18.4 1.3 %collective-permute-start.5 = (f32[104,128]{1,0:T(8,128)S(1)}, f32[104,128]{1,0:T(8,128)S(1)}, u32[]{:S(2)}, u32[]{:S(2)}) collective-permute-start(f32[104,128]{1,0:T(8,128)S(1)} %get-tuple-element.83.refs_0_), channel_id=1, source_target_pairs={{0,1},{1,0},{2,3},{3,2},{4,5},{5,4},{6,7},{7,6},{8,9},{9,8},{10,11... | collective-permute-start | bytes 159752 | tf_op jit(solution)/shard_map/ppermute | solution.py:876
  20.1 5.3 %collective-permute-start.7 = (f32[48,128]{1,0:T(8,128)S(1)}, f32[48,128]{1,0:T(8,128)S(1)}, u32[]{:S(2)}, u32[]{:S(2)}) collective-permute-start(f32[48,128]{1,0:T(8,128)S(1)} %get-tuple-element.87), channel_id=1, source_target_pairs={{0,13},{1,8},{2,15},{3,10},{4,9},{5,12},{6,11},{7,14},{8,5},{9,0},... | collective-permute-start | bytes 73736 | tf_op jit(solution)/shard_map/ppermute | solution.py:876
  22.2 3.1 %collective-permute-start.6 = (f32[24,128]{1,0:T(8,128)S(1)}, f32[24,128]{1,0:T(8,128)S(1)}, u32[]{:S(2)}, u32[]{:S(2)}) collective-permute-start(f32[24,128]{1,0:T(8,128)S(1)} %get-tuple-element.86), channel_id=1, source_target_pairs={{0,5},{1,4},{2,7},{3,6},{4,1},{5,0},{6,3},{7,2},{8,13},{9,12},{10,... | collective-permute-start | bytes 36872 | tf_op jit(solution)/shard_map/ppermute | solution.py:876
  22.5 2.8 %copy-start.1 = (s32[1,1,16,128]{3,2,1,0:T(8,128)S(1)}, s32[1,1,16,128]{3,2,1,0:T(8,128)}, u32[]{:S(2)}) copy-start(s32[1,1,16,128]{3,2,1,0:T(8,128)} %param.24) | copy-start | bytes 24580
  22.5 2.8 %copy-start.2 = (f32[1,1,16,128]{3,2,1,0:T(8,128)S(1)}, f32[1,1,16,128]{3,2,1,0:T(8,128)}, u32[]{:S(2)}) copy-start(f32[1,1,16,128]{3,2,1,0:T(8,128)} %param.25) | copy-start | bytes 24580
  26.1 1.2 %collective-permute-start.8 = (f32[4,128]{1,0:T(4,128)S(1)}, f32[4,128]{1,0:T(4,128)S(1)}, u32[]{:S(2)}, u32[]{:S(2)}) collective-permute-start(f32[4,128]{1,0:T(4,128)S(1)} %slice.19), channel_id=1, source_target_pairs={{0,1},{1,0},{2,3},{3,2},{4,5},{5,4},{6,7},{7,6},{8,9},{9,8},{10,11... | collective-permute-start | bytes 6152 | tf_op jit(solution)/shard_map/ppermute | solution.py:876

commit v4 on v3

--- a/solution.py
+++ b/solution.py
@@ -159,56 +159,79 @@
             lanes_out[0][at + number : at + number + 1, :] = cell[:, part].astype(F32)
             lanes_out[0][at + strips + number : at + strips + number + 1, :] = live[:, part]
 
-    even_y = is_even("facey")
-    edge = [
-        jnp.where(even_y if number == 0 else jnp.logical_not(even_y), cy - 1, 0)
-        for number in range(len(lanes_out))
-    ]
-    lane = iota((cx, cy), 1)
-    packed = [jnp.zeros((cx, cy), F32) for _ in lanes_out]
-    behind = jnp.zeros((cx, cy), F32)
-    inner_edge = jnp.where(edge[0] == 0, 1, cy - 2)
     for number in (1, 0, 8):
         copies[number].wait()
-    for level in range(levels):
-        spot = carried * levels + level
-        for number, at in enumerate(edge):
-            moved = pltpu.roll(south[level], lax.rem(spot + cy - at, cy), 1)
-            packed[number] = jnp.where(lane == spot, moved, packed[number])
-        if plan["relay"]:
-            for number, (values, at) in enumerate(
-                ((west[level], edge[0]), (south[level], inner_edge), (mixing[min(level, levels - 2)], edge[0]))
-            ):
-                spot = (number + 1) * levels + level
-                if number < 2 or level < levels - 1:
-                    moved = pltpu.roll(values, lax.rem(spot + cy - at, cy), 1)
-                    behind = jnp.where(lane == spot, moved, behind)
-    for t in range(carried):
-        copies[9 + t].wait()
+    lane = iota((cx, cy), 1)
+    if plan["relay"]:
+        edge = edge_of(0, cy)
+        inner = jnp.where(edge == 0, 1, cy - 2)
+        tiles = {name: LanePacker(lane, at) for name, at in zip("cdvwuk", (edge, inner, edge, inner, edge, edge))}
         for level in range(levels):
-            spot = t * levels + level
-            values = tracer[t, level]
-            for number, at in enumerate(edge):
-                moved = pltpu.roll(values, lax.rem(spot + cy - at, cy), 1)
-                packed[number] = jnp.where(lane == spot, moved, packed[number])
-    for values, out in zip(packed, lanes_out):
-        out[0:cx, :] = values
-    if plan["relay"]:
+            turned = pltpu.roll(south[level], level, 1) if level else south[level]
+            tiles["v"].put(level, turned)
+            tiles["w"].put(level, turned)
+            tiles["u"].put(level, pltpu.roll(west[level], level, 1) if level else west[level])
+            if level < levels - 1:
+                tiles["k"].put(level, pltpu.roll(mixing[level], level, 1) if level else mixing[level])
+        totals = None
+        for t in range(carried):
+            copies[9 + t].wait()
+            totals = [tracer[t, level] + (totals[level] if t else 0.0) for level in range(levels)]
         for level in range(levels):
-            total = tracer[0, level]
-            for t in range(1, carried):
-                total = total + tracer[t, level]
-            moved = pltpu.roll(total, lax.rem(level + cy - inner_edge, cy), 1)
-            behind = jnp.where(lane == level, moved, behind)
-        lanes_out[0][cx : 2 * cx, :] = behind
+            turned = pltpu.roll(totals[level], level, 1) if level else totals[level]
+            tiles["c"].put(level, turned)
+            tiles["d"].put(level, turned)
+        packed = jnp.zeros((cx, cy), F32)
+        for name in "cdvwu":
+            packed = packed + tiles[name].packed(plan["lane_" + name])
+        lanes_out[0][0:cx, :] = packed
+        lanes_out[0][cx : 2 * cx, :] = tiles["k"].packed(0)
+    else:
+        edges = [LanePacker(lane, edge_of(number, cy)) for number in range(len(lanes_out))]
+        for t in range(carried):
+            copies[9 + t].wait()
+        for f in range(carried + 1):
+            for level in range(levels):
+                spot = f * levels + level
+                values = tracer[f, level] if f < carried else south[level]
+                for tile in edges:
+                    tile.put(spot, pltpu.roll(values, spot, 1) if spot else values)
+        for tile, out in zip(edges, lanes_out):
+            out[0:cx, :] = tile.packed(0)
     copies[2].wait()
+
+
+class LanePacker:
+    def __init__(self, lane, edge):
+        self.lanes = lane.shape[1]
+        self.back = lax.rem(2 * self.lanes - edge, self.lanes)
+        self.place = lax.rem(lane + self.back, self.lanes)
+        self.tile = jnp.zeros(lane.shape, F32)
+
+    def put(self, spot, turned):
+        self.tile = jnp.where(self.place == spot, turned, self.tile)
+
+    def packed(self, start):
+        return pltpu.roll(self.tile, lax.rem(self.back + start, self.lanes), 1)
+
+
+def edge_of(number, lanes):
+    even_y = is_even("facey")
+    return jnp.where(even_y if number == 0 else jnp.logical_not(even_y), lanes - 1, 0)
 
 
 def rows_kernel(plan, tracer, west, scale, blocks, *outs):
     carried, levels, cx, cy = tracer.shape
     head = (carried + 1) * levels
     even_x = is_even("facex")
-    for number, out in enumerate(outs):
+    if plan["relay"]:
+        tile = LanePacker(iota((cx, cy), 1), edge_of(0, cy))
+        for t in range(carried):
+            for level in range(levels):
+                spot = t * levels + level
+                tile.put(spot, pltpu.roll(tracer[t, level], spot, 1) if spot else tracer[t, level])
+        outs[2][...] = tile.packed(0)
+    for number, out in enumerate(outs[:2]):
         row = jnp.where(even_x if number == 0 else jnp.logical_not(even_x), cx - 1, 0)
         for level in range(levels):
             for t in range(carried):
@@ -222,31 +245,27 @@
             out[head + 8 : head + 16, :] = blocks[at : at + 8, :]
 
 
-def relay_kernel(plan, head, cx, *refs):
-    rows, blocks, y_got = refs[:2], refs[2], refs[3]
-    outs = refs[4:6]
-    x_outs = refs[6:]
-    base = plan["y_tiles"] * cx
-
-    def fill(out, start, offset):
-        out[start : start + 16, :] = blocks[8 * offset : 8 * offset + 16, :]
-        out[start + 16 : start + 32, :] = y_got[base + 8 * offset : base + 8 * offset + 16, :]
-
+def relay_kernel(plan, head, cx, number, rows, blocks, y_got, out):
     even_x = is_even("facex")
-    for number, out in enumerate(outs):
-        out[0 : head + 8, :] = rows[number][0 : head + 8, :]
-        row = jnp.where(even_x if number == 0 else jnp.logical_not(even_x), cx - 1, 0)
-        for tile in range(2):
-            out[head + 8 + tile : head + 9 + tile, :] = y_got[pl.ds(tile * cx + row, 1), :]
-        out[head + 10 : head + 16, :] = jnp.zeros((6, out.shape[1]), F32)
-        if plan["x_blocks"][number]:
-            fill(out, head + 16, plan["x_blocks"][number])
-    for out, offset in zip(x_outs, plan["x_ops"]):
-        fill(out, 0, offset)
-
-
-def rim_kernel(plan, carried, levels, cx, y_sent, y_got, *refs):
-    inverse_out, ratio_out, mixing_out, pieces_out, columns_out, rows_out, picks_out, live_out, square = refs
+    out[0 : head + 8, :] = rows[0 : head + 8, :]
+    row = jnp.where(even_x if number == 0 else jnp.logical_not(even_x), cx - 1, 0)
+    out[head + 8 : head + 16, :] = jnp.broadcast_to(y_got[pl.ds(row, 1), :], (8, out.shape[1]))
+    offset = plan["x_blocks"][number]
+    if offset:
+        at = plan["y_tiles"] * cx + 8 * offset
+        out[head + 16 : head + 32, :] = blocks[8 * offset : 8 * offset + 16, :]
+        out[head + 32 : head + 48, :] = y_got[at : at + 16, :]
+
+
+def beyond_kernel(plan, cx, blocks, y_got, *outs):
+    for out, offset in zip(outs, plan["x_ops"]):
+        at = plan["y_tiles"] * cx + 8 * offset
+        out[0:16, :] = blocks[8 * offset : 8 * offset + 16, :]
+        out[16:32, :] = y_got[at : at + 16, :]
+
+
+def rim_kernel(plan, carried, levels, cx, y_sent, y_got, base, base_other, lanes, *refs):
+    inverse_out, ratio_out, mixing_out, pieces_out, columns_out, rows_out, picks_out, live_out, base_out, square = refs
     cy = y_got.shape[1]
     slots = live_out.shape[1]
 
@@ -255,27 +274,19 @@
         square[0:cx, :] = values
         return jnp.transpose(square[...])
 
-    def summed(values):
-        total = values[0:levels]
-        for t in range(1, carried):
-            total = total + values[t * levels : (t + 1) * levels]
-        return total
-
-    spot = carried * levels
+    def part(values, name):
+        return values[plan["lane_" + name] : plan["lane_" + name] + levels]
+
     beyond = turned(y_got[0:cx, :])
-    behind = turned(y_got[cx : 2 * cx, :])
     mine = turned(y_sent[0:cx, :])
+    mixing_out[...] = turned(y_got[cx : 2 * cx, :])[0:levels]
     north = is_even("facey")
-    second, inner_face = behind[0:levels], behind[2 * levels : 3 * levels]
-    edge_face, own_face = beyond[spot : spot + levels], mine[spot : spot + levels]
-    own_edge = summed(mine)
-    pieces_out[0] = summed(beyond)
-    pieces_out[1] = behind[levels : 2 * levels]
-    pieces_out[2] = edge_face
-    pieces_out[3] = jnp.where(north, inner_face, own_face)
-    pieces_out[4] = jnp.where(north, own_edge, second)
-    pieces_out[5] = jnp.where(north, second, own_edge)
-    mixing_out[...] = behind[3 * levels : 4 * levels]
+    pieces_out[0] = part(beyond, "c")
+    pieces_out[1] = part(beyond, "u")
+    pieces_out[2] = part(beyond, "v")
+    pieces_out[3] = jnp.where(north, part(beyond, "w"), part(mine, "v"))
+    pieces_out[4] = jnp.where(north, part(mine, "c"), part(beyond, "d"))
+    pieces_out[5] = jnp.where(north, part(beyond, "d"), part(mine, "c"))
 
     def level_of(ref, level):
         return jnp.broadcast_to(ref[level : level + 1, :], (8, LANES))
@@ -303,6 +314,13 @@
         weight[level] = first[level] + ratios[level] * weight[level + 1]
     for level in range(levels):
         square[level : level + 1, :] = weight[level][0:1]
+    weights = square[0:levels, :]
+    tile = LanePacker(iota((cx, cy), 1), edge_of(0, cy))
+    for t in range(2 * carried):
+        values = base[t] if t < carried else base_other[t - carried]
+        tile.put(t, pltpu.roll(values, t, 1) if t else values)
+    base_out[0:cx, :] = tile.packed(0)
+    base_out[cx : 2 * cx, :] = lanes[...]
     at = plan["y_tiles"] * cx + 8 * len(plan["y_blocks"])
     strips = slots // LANES
     cell = jnp.concatenate([y_got[at + n : at + n + 1, :] for n in range(strips)], axis=1).astype(jnp.int32)
@@ -313,7 +331,7 @@
     rows_out[...] = picks[0:cx]
     picks = picks.astype(BF16)
     picks_out[...] = picks
-    high, low = halves(square[0:levels, :])
+    high, low = halves(weights)
     columns_out[...] = jnp.dot(high, picks, preferred_element_type=F32) + jnp.dot(
         low, picks, preferred_element_type=F32
     )
@@ -321,7 +339,7 @@
 
 def factor_kernel(sizes, *refs):
     (tracer, west, south, mixing, adjoint, cells) = refs[:6]
-    inverse_out, ratio_out, base_out, inner_out, shares_out, columns_out, rows_out, picks_out, rim_out = refs[6:]
+    inverse_out, ratio_out, base_out, inner_out, shares_out, columns_out, rows_out, picks_out = refs[6:]
     carried, levels, cx, cy = tracer.shape
     slots = cells.shape[1]
     first = []
@@ -349,10 +367,6 @@
         for level in range(1, levels):
             total = total + weight[level] * adjoint[t, level]
         base_out[t] = total
-        edge = jnp.where(is_even("facey"), cy - 1, 0)
-        moved = pltpu.roll(total, lax.rem(t + cy - edge, cy), 1)
-        rim = jnp.where(iota((cx, cy), 1) == t, moved, jnp.zeros((cx, cy), F32) if t == 0 else rim)
-    rim_out[...] = rim
     for level in range(levels):
         total = tracer[0, level]
         for t in range(1, carried):
@@ -381,33 +395,35 @@
     return jnp.where(even_x, second, first), jnp.where(even_x, first, second)
 
 
-def seam_lanes(number, sent, got, carried, levels):
-    cy = sent.shape[1]
-    spot = carried * levels
-    lane = iota(sent.shape, 1)
-
-    def spread(values):
-        result = jnp.zeros_like(values)
-        for t in range(carried):
-            moved = pltpu.roll(values, (t * levels - spot) % cy, 1)
-            inside = jnp.logical_and(lane >= t * levels, lane < (t + 1) * levels)
-            result = jnp.where(inside, moved, result)
-        return result
-
+def seam(number, sent, got, sent_face, got_face):
     even_y = is_even("facey")
     north = even_y if number == 0 else jnp.logical_not(even_y)
-    beyond = spread(got)
-    inside = spread(sent)
-    to_north = -(jnp.maximum(beyond, 0.0) * sent + jnp.minimum(beyond, 0.0) * got)
-    to_south = jnp.maximum(inside, 0.0) * got
-    return jnp.where(north, to_north, to_south), jnp.where(north, cy - 1, 0)
+    to_north = -(jnp.maximum(got_face, 0.0) * sent + jnp.minimum(got_face, 0.0) * got)
+    to_south = jnp.maximum(sent_face, 0.0) * got
+    return jnp.where(north, to_north, to_south), jnp.where(north, sent.shape[1] - 1, 0)
+
+
+def spread_wind(values, start, carried, levels):
+    lane = iota(values.shape, 1)
+    result = jnp.zeros_like(values)
+    for t in range(carried):
+        moved = pltpu.roll(values, (t * levels - start) % values.shape[1], 1)
+        inside = jnp.logical_and(lane >= t * levels, lane < (t + 1) * levels)
+        result = jnp.where(inside, moved, result)
+    return result
+
+
+def seam_lanes(number, plan, sent, got, sent_wind, got_wind, carried, levels):
+    start = plan["lane_v"]
+    faces = [spread_wind(wind, start, carried, levels) for wind in (sent_wind, got_wind)]
+    return seam(number, sent, got, *faces)
 
 
 def observe_kernel(sizes, plan, carried, *refs):
     refs = list(refs)
-    inner, mixing, inverse, ratio, columns, in_row, in_lane, live = refs[:8]
-    sent = refs[8:10]
-    got = refs[10:12]
+    got = refs[1::-1]
+    inner, mixing, inverse, ratio, columns, in_row, in_lane, live = refs[2:10]
+    sent = refs[10:12]
     refs = refs[12:]
     y_sent = refs[: plan["y_ops"]]
     y_got = refs[plan["y_ops"] : 2 * plan["y_ops"]]
@@ -419,8 +435,8 @@
     if plan["relay"]:
         x_got = refs[1 : 1 + len(plan["x_ops"])]
         refs = refs[1 + len(plan["x_ops"]) :]
-        base, rim_base, *rim = refs[:10]
-        parcel, state_out, turn, rise = refs[10:]
+        rim = refs[:8]
+        parcel, state_out, turn, rise = refs[8:]
     else:
         modeled_out, state_out = refs[-2:]
     levels, cx, cy = inner.shape
@@ -444,11 +460,16 @@
     )
     lane_parts = []
     for number in range(plan["y_ops"]):
-        part, spot_y = seam_lanes(number, y_sent[number][0:cx, :], y_got[number][0:cx, :], carried, levels)
-        total = part
-        for t in range(1, carried):
-            total = total + pltpu.roll(part, (-t * levels) % cy, 1)
-        lane_parts.append((total, spot_y))
+        mine, beyond = y_sent[number][0:cx, :], y_got[number][0:cx, :]
+        if plan["relay"]:
+            faces = [pltpu.roll(values, cy - plan["lane_v"], 1) for values in (mine, beyond)]
+            total, spot_y = seam(number, mine, beyond, *faces)
+        else:
+            part, spot_y = seam_lanes(number, plan, mine, beyond, mine, beyond, carried, levels)
+            total = part
+            for t in range(1, carried):
+                total = total + pltpu.roll(part, (-t * levels) % cy, 1)
+        lane_parts.append((pltpu.roll(total, spot_y, 1), spot_y))
     lane = iota((cx, cy), 1)
     row = iota((cx, cy), 0)
     forward = []
@@ -457,7 +478,7 @@
         value = value + jnp.where(row == 0, from_west[level : level + 1], 0.0)
         value = value + jnp.where(row == cx - 1, from_east[level : level + 1], 0.0)
         for total, spot_y in lane_parts:
-            moved = pltpu.roll(total, lax.rem(spot_y - level + cy, cy), 1)
+            moved = pltpu.roll(total, cy - level, 1) if level else total
             value = value + jnp.where(lane == spot_y, moved, 0.0)
         if level > 0:
             value = value + mixing[level - 1] * forward[-1]
@@ -533,12 +554,9 @@
     turn[...] = jnp.zeros((LANES, LANES), F32)
     turn[0:1, :] = corners_west[0:1]
     turn[cx - 1 : cx, :] = corners_east[0:1]
-    turn[2 * cx - 1 : 2 * cx, :] = corners_east[1:2]
     turned = jnp.transpose(turn[...])
-    ends = turned[0:levels]
-    for t in range(1, carried):
-        ends = ends + turned[t * levels : (t + 1) * levels]
-    end_face = pltpu.roll(turned[levels : 2 * levels], LANES - cx, 1)
+    ends = turned[plan["lane_c"] : plan["lane_c"] + levels]
+    end_face = turned[plan["lane_u"] : plan["lane_u"] + levels]
     place = iota((levels, LANES), 1)
     cells, face_w, face_s, face_n, south_cells, north_cells = (pieces[n] for n in range(6))
     west_cells = jnp.where(place == 0, ends, pltpu.roll(cells, 1, 1))
@@ -580,12 +598,6 @@
         part = slice(number * LANES, (number + 1) * LANES)
         parcel[number : number + 1, :] = modeled[:, part]
         parcel[strips + number : strips + number + 1, :] = rim_modeled[:, part]
-    at = plan["parcel"]
-    for t in range(carried):
-        parcel[at + t * cx : at + (t + 1) * cx, :] = base[t]
-    at = at + carried * cx
-    parcel[at : at + cx, :] = rim_base[...]
-    parcel[at + cx : at + 2 * cx, :] = y_got[0][0:cx, :]
 
 
 def advance_cells(cells, west, east, south, north, face_w, face_e, face_s, face_n):
@@ -640,7 +652,7 @@
 
 
 def weigh_kernel(sizes, plan, carried, levels, *refs):
-    parcel, other, state, in_row, in_lane, base, rim_rows, rim_base = refs[:8]
+    parcel, other, state, in_row, in_lane, base, base_other, rim_rows, rim_base = refs[:9]
     cx, cy = base.shape[1:]
     strips = state.shape[1] // LANES
 
@@ -651,19 +663,17 @@
 
     scattered = scatter(misfit(0), in_row[...], in_lane[...])
     on_rim = jnp.sum(rim_rows[...] * misfit(1), axis=1, keepdims=True)
-    at = plan["parcel"]
     near = [scattered + base[t] for t in range(carried)]
-    near += [scattered + other[at + t * cx : at + (t + 1) * cx, :] for t in range(carried)]
-    at = at + carried * cx
-    mine, others = other[at : at + cx, :] + on_rim, rim_base[...] + on_rim
-    rims = [[mine if t < carried else others] for t in range(2 * carried)]
-    spread_surface(sizes, plan, carried, levels, near, rims, refs[8:11], refs[11:13], refs[13:14], refs[14:])
+    near += [scattered + base_other[t] for t in range(carried)]
+    rims = [[rim_base[0:cx, :] + on_rim] for _ in near]
+    spread_surface(sizes, plan, carried, levels, near, rims, refs[9:12], refs[12:14], refs[14:15], refs[15:])
 
 
 def spread_surface(sizes, plan, carried, levels, near, rim_values, fields, got, y_got, outs):
     west, south, scale = fields
     tracers = len(near)
     cx, cy = near[0].shape
+    spot_v = plan["lane_v"]
     band = cy // sizes[0]
     per_tile = min(tracers, LANES // band)
     spot = carried * levels
@@ -681,7 +691,7 @@
     norths = []
     for number in range(plan["y_ops"]):
         norths.append(even_y if number == 0 else jnp.logical_not(even_y))
-        moved = pltpu.roll(y_got[number][0:cx, :], cy - 1 - spot, 1)
+        moved = pltpu.roll(y_got[number][0:cx, :], cy - 1 - spot_v, 1)
         keep = jnp.logical_and(lane == cy - 1, norths[number])
         face_north = jnp.where(keep, moved, face_north)
     to_middle = 1.0 + jnp.minimum(face_west, 0.0) - jnp.maximum(face_east, 0.0)
@@ -700,11 +710,10 @@
         south_side = right(values)
         for number in range(plan["y_ops"]):
             rim = rim_values[t][number]
-            spot_t = t % carried if plan["relay"] else t
             at_north = jnp.logical_and(lane == cy - 1, norths[number])
             at_south = jnp.logical_and(lane == 0, jnp.logical_not(norths[number]))
-            north_side = jnp.where(at_north, pltpu.roll(rim, (cy - 1 - spot_t) % cy, 1), north_side)
-            south_side = jnp.where(at_south, pltpu.roll(rim, (-spot_t) % cy, 1), south_side)
+            north_side = jnp.where(at_north, pltpu.roll(rim, (cy - 1 - t) % cy, 1), north_side)
+            south_side = jnp.where(at_south, pltpu.roll(rim, (-t) % cy, 1), south_side)
         swept = to_middle * values + to_east * pltpu.roll(values, cx - 1, 0) - to_west * pltpu.roll(values, 1, 0)
         swept = swept + to_north * north_side - to_south * south_side
         grown.append(
@@ -793,8 +802,8 @@
     tracer, parts, mixing, inverse, ratio = refs[:5]
     sent = refs[5:7]
     got = refs[7:9]
-    y_sent = refs[9 : 9 + plan["y_ops"]]
-    y_got = refs[9 + plan["y_ops"] : 9 + 2 * plan["y_ops"]]
+    y_ops = plan["y_ops"]
+    y_sent, y_got, winds_sent, winds_got = (refs[9 + n * y_ops : 9 + (n + 1) * y_ops] for n in range(4))
     target, out, west_rows, east_rows, done = refs[-5:]
     carried, levels, cx, cy = tracer.shape
     head = (carried + 1) * levels
@@ -812,7 +821,17 @@
     lane = iota((cx, cy), 1)
     row = iota((cx, cy), 0)
     seams = [
-        seam_lanes(n, y_sent[n][0:cx, :], y_got[n][0:cx, :], carried, levels) for n in range(plan["y_ops"])
+        seam_lanes(
+            n,
+            plan,
+            y_sent[n][0:cx, :],
+            y_got[n][-cx:, :] if plan["relay"] else y_got[n][0:cx, :],
+            winds_sent[n][0:cx, :],
+            winds_got[n][0:cx, :],
+            carried,
+            levels,
+        )
+        for n in range(y_ops)
     ]
     stride = 4
 
@@ -909,6 +928,13 @@
     }
 
 
+def lane_plan(plan, carried, levels):
+    starts = {"c": 0, "d": levels, "v": 2 * levels, "w": 3 * levels, "u": 4 * levels}
+    if not plan["relay"]:
+        starts = {"v": carried * levels}
+    return {"lane_" + name: start for name, start in starts.items()}
+
+
 def local(
     sizes,
     tracer,
@@ -931,6 +957,7 @@
     owners, cap = send_cells.shape[2:]
     slots = owners * cap
     taps, ll = regrid_index.shape[2:]
+    plan.update(lane_plan(plan, carried, levels))
     head = (carried + 1) * levels
     y_ops = plan["y_ops"]
     band = cy // many_x
@@ -942,10 +969,10 @@
 
         return rule
 
-    def next_y(number):
+    def next_y(number, cross):
         def rule(x, y, c):
             to = y + (1 if (y % 2 == 0) == (number == 0) else -1)
-            return (x, to, c ^ plan["cross"]) if 0 <= to < many_y else None
+            return (x, to, c ^ cross) if 0 <= to < many_y else None
 
         return rule
 
@@ -1000,9 +1027,9 @@
     own_blocks = packed[y_ops]
     pair_sent = packed[1 + y_ops : -7]
     cell, live, tracer, west_courant, south_courant, emission_scale, mixing = packed[-7:]
-    lanes_got = [exchange(lanes_sent[n], sizes, next_y(n)) for n in range(y_ops)]
+    lanes_got = [exchange(lanes_sent[n], sizes, next_y(n, plan["cross"])) for n in range(y_ops)]
     held, *_ = lax.optimization_barrier((tracer, *lanes_sent))
-    inverse, ratio, base, inner, parts, columns, in_row, in_lane, base_rim = call(
+    inverse, ratio, base, inner, parts, columns, in_row, in_lane = call(
         functools.partial(factor_kernel, sizes),
         [
             shape(levels, cx, cy),
@@ -1013,18 +1040,19 @@
             shape(levels, slots),
             shape(cx, slots),
             shape(cy, slots, dtype=BF16),
-            shape(cx, cy),
         ],
         [held, west_courant, south_courant, mixing, adjoint_later, cell],
         "factor",
         3000000,
     )
-    rows_sent = call(
-        functools.partial(rows_kernel, plan),
-        row_shapes,
-        [tracer, west_courant, emission_scale, own_blocks],
-        "rows",
-        100000,
+    rows_sent = list(
+        call(
+            functools.partial(rows_kernel, plan),
+            row_shapes + ([shape(cx, cy)] if plan["relay"] else []),
+            [tracer, west_courant, emission_scale, own_blocks],
+            "rows",
+            100000,
+        )
     )
     per_tile = min(2 * carried, LANES // band)
 
@@ -1039,18 +1067,30 @@
     )
     if plan["relay"]:
         base, *lanes_got = lax.optimization_barrier((base, *lanes_got))
-        relayed = call(
-            functools.partial(relay_kernel, plan, head, cx),
-            row_shapes + [shape(32, LANES)] * len(plan["x_ops"]),
-            [*rows_sent, own_blocks, lanes_got[0]],
-            "relay",
+        lanes_each = rows_sent.pop()
+        base_other = other_core(base)
+
+        def relay(number, *after):
+            held, *_ = lax.optimization_barrier((rows_sent[number], *after))
+            return call(
+                functools.partial(relay_kernel, plan, head, cx, number),
+                [row_shapes[number]],
+                [held, own_blocks, lanes_got[0]],
+                "relay",
+                10000,
+            )[0]
+
+        rows_sent = [relay(0), relay(1)]
+        x_sent = call(
+            functools.partial(beyond_kernel, plan, cx),
+            [shape(32, LANES)] * len(plan["x_ops"]),
+            [own_blocks, lanes_got[0]],
+            "beyond",
             10000,
         )
-        rows_sent, x_sent = relayed[:2], relayed[2:]
-        second_got = exchange(rows_sent[1], sizes, next_x(1))
         x_got = [exchange(s, sizes, jump(d, d, 1)) for s, d in zip(x_sent, plan["x_ops"])]
-        rows_got = [exchange(rows_sent[0], sizes, next_x(0)), second_got]
-        held_y, *_ = lax.optimization_barrier((lanes_got[0], *rows_sent, *x_sent))
+        rows_got = [exchange(rows_sent[n], sizes, next_x(n)) for n in range(2)]
+        held_y, *_ = lax.optimization_barrier((lanes_got[0], *rows_sent))
         rim = call(
             functools.partial(rim_kernel, plan, carried, levels, cx),
             [
@@ -1062,30 +1102,32 @@
                 shape(cx, slots),
                 shape(LANES, slots, dtype=BF16),
                 shape(1, slots),
+                shape(2 * cx, cy),
             ],
-            [lanes_sent[0], held_y],
+            [lanes_sent[0], held_y, base, base_other, lanes_each],
             "rim",
             400000,
             scratch=[pltpu.VMEM((LANES, LANES), F32)],
         )
-        base_rim, _ = lax.optimization_barrier((base_rim, rim[0]))
-        rim_base = exchange(base_rim, sizes, next_y(0))
-        parcel_rows = plan["parcel"] + (carried + 2) * cx
+        *rim, rim_sent = rim
+        rim_got = exchange(rim_sent, sizes, next_y(0, 0))
         parcel, state = observe(
-            [shape(parcel_rows, cy), shape(4, slots)],
-            [inner, mixing, inverse, ratio, columns, in_row, in_lane, live, *rows_sent, *rows_got]
-            + [*lanes_sent, *lanes_got, own_blocks, *x_got, base, rim_base, *rim],
+            [shape(plan["parcel"], cy), shape(4, slots)],
+            [rows_got[1], rows_got[0], inner, mixing, inverse, ratio, columns, in_row, in_lane, live, *rows_sent]
+            + [*lanes_sent, *lanes_got, own_blocks, *x_got, *rim],
             scratch=[pltpu.VMEM((LANES, LANES), F32), pltpu.VMEM((levels, LANES), F32)],
         )
         parcel_other = other_core(parcel)
+        parcel_other, rim_got = lax.optimization_barrier((parcel_other, rim_got))
         band_sent = call(
             functools.partial(weigh_kernel, sizes, plan, carried, levels),
             band_shapes,
-            [parcel, parcel_other, state, in_row, in_lane, base, rim[5], rim_base, *fields, *rows_got, *lanes_got],
+            [parcel, parcel_other, state, in_row, in_lane, base, base_other, rim[5], rim_got, *fields]
+            + [*rows_got, *lanes_got],
             "weigh",
             500000,
         )
-        lanes_own = [parcel_other[parcel_rows - cx :]]
+        lanes_own = [lanes_each, rim_got]
         held, *_ = lax.optimization_barrier((tracer, *band_sent))
     else:
         rows_got = [exchange(rows_sent[n], sizes, next_x(n)) for n in range(2)]
@@ -1093,7 +1135,7 @@
         base_other = other_core(base)
         modeled, state = observe(
             [shape(1, slots), shape(2, slots)],
-            [inner, mixing, inverse, ratio, columns, in_row, in_lane, live, *rows_sent, *rows_got]
+            [rows_got[1], rows_got[0], inner, mixing, inverse, ratio, columns, in_row, in_lane, live, *rows_sent]
             + [*lanes_sent, *lanes_got, own_blocks, *pair_got]
             + [other_core(jnp.concatenate(pair_got, axis=0))],
         )
@@ -1104,7 +1146,7 @@
             "force",
             200000,
         )
-        rims_got = [exchange(rims_sent[n], sizes, next_y(n)) for n in range(y_ops)]
+        rims_got = [exchange(rims_sent[n], sizes, next_y(n, 0)) for n in range(y_ops)]
         band_sent = call(
             functools.partial(surface_kernel, sizes, plan, carried, levels),
             band_shapes,
@@ -1112,7 +1154,7 @@
             "surface",
             400000,
         )
-        lanes_own = lanes_got
+        lanes_own = [*lanes_sent, *lanes_got]
         held = tracer
     (advanced,) = call(
         functools.partial(advance_kernel, plan),
@@ -1120,8 +1162,9 @@
         [held, parts, mixing, inverse, ratio]
         + list(rows_sent)
         + rows_got
+        + lanes_own
         + list(lanes_sent)
-        + lanes_own,
+        + lanes_got,
         "advance",
         6000000,
         scratch=[pltpu.VMEM(tracer.shape, F32)]

time: 28 us -> 26.9 us (0.961)
  waiting for transfers between devices: 7.79 us -> 5.97 us
  starting transfers between devices: 11.6 us -> 12.4 us
    ppermute x9 -> x10, waiting for transfers between devices: 7.79 us -> 5.97 us  [exchange(): return lax.ppermute(values, GROUP, pairs)]
    ppermute x9 -> x10, starting transfers between devices: 11.6 us -> 12.4 us  [exchange(): return lax.ppermute(values, GROUP, pairs)]
    pallas_call x9 -> x11, Pallas kernels: 7.19 us -> 7.1 us  [call(): pl.pallas_call(body, out_shape=outs, in_specs=[pl.BlockSpec(memory_space=...]
  transfers between devices with their start and end apart: 9 -> 10, of which waited for: 6 -> 7; matrix products, arithmetic and copies ran while one was open for 0% -> 0% of each run, Pallas kernels for 12% -> 16%
where the time goes in v4:
time: 26.9 us; the launch traced here: 26.8 us
  starting transfers between devices  12.4 us (46%)
  Pallas kernels  7.1 us (26%)
  waiting for transfers between devices  5.97 us (22%)
  between operations  0.75 us (3%)
  other arithmetic  0.58 us (2%)
    ppermute x10, starting transfers between devices, exchange(): return lax.ppermute(values, GROUP, pairs)  12.4 us
    pallas_call x11, Pallas kernels, call(): pl.pallas_call(body, out_shape=outs, in_specs=[pl.BlockSpec(memory_space=...  7.1 us
    ppermute x10, waiting for transfers between devices, exchange(): return lax.ppermute(values, GROUP, pairs)  5.97 us
    add x1, other arithmetic, local(): latlon = sums[:carried] + sums_other  0.58 us
  transfers between devices with their start and end apart: 10, of which 7 were waited for; matrix products, arithmetic and copies ran while one was open for 0% of the time, Pallas kernels for 16%

profile of v4, /device:TPU:0, one launch (start us, length us, event | category | flops | bytes accessed | tf_op | source)
XLA Modules:
  0.0 26.8 jit_solution(2130831164740149249)
XLA Ops:
  0.6 1.8 %pack.1 = (f32[104,128]{1,0:T(8,128)S(1)}, f32[64,128]{1,0:T(8,128)S(1)}, s32[1,256]{1,0:T(1,128)S(1)}, f32[1,256]{1,0:T(1,128)S(1)}, f32[4,24,16,128]{3,2,1,0:T...) custom-call(f32[4,24,16,128]{3,2,1,0:T(8,128)} %refs_0_.1, ...), custom_call_target="tpu_custom_call" | custom-call | flops 100000 | bytes 2868256 | tf_op jit(solution)/shard_map/pack/pallas_call | solution.py:22
  2.4 0.0 copy-start
  2.5 2.4 %collective-permute-start = (f32[104,128]{1,0:T(8,128)S(1)}, f32[104,128]{1,0:T(8,128)S(1)}, u32[]{:S(2)}, u32[]{:S(2)}) collective-permute-start(f32[104,128]{1,0:T(8,128)S(1)} %get-tuple-element.52.y_sent.refs_12_.refs_11_), channel_id=1, source_target_pairs={{0,3},{1,2},{2,1},{3,0},{4,7},{5,6},{6,5},{7,4},{8,11},{9,10},{10,... | collective-permute-start | bytes 159752 | tf_op jit(solution)/shard_map/ppermute | solution.py:895
  4.9 0.4 %rows.1 = (f32[168,128]{1,0:T(8,128)S(1)}, f32[168,128]{1,0:T(8,128)S(1)}, f32[16,128]{1,0:T(8,128)S(1)}) custom-call(f32[4,24,16,128]{3,2,1,0:T(8,128)S(1)} %get-tuple-element.86.tracer.refs_0_, f32[24,16,128]{2,1,0:T(8,128)S(1)} %get-tuple-element.48.west.refs_1_, f32[16,128]{1,0:T(8,128)S(1)} %get-tuple-element.49.scale.refs_11_, ...), custom_call_target="tpu_custom_call" | custom-call | flops 100000 | bytes 1204224 | tf_op jit(solution)/shard_map/rows/pallas_call | solution.py:22
  5.3 0.0 copy-done
  5.3 0.7 %factor.1 = (f32[24,16,128]{2,1,0:T(8,128)S(1)}, f32[24,16,128]{2,1,0:T(8,128)S(1)}, f32[4,16,128]{2,1,0:T(8,128)S(1)}, f32[24,16,128]{2,1,0:T(8,128)S(1)}, f32[...) custom-call(f32[4,24,16,128]{3,2,1,0:T(8,128)S(1)} %get-tuple-element., ...), custom_call_target="tpu_custom_call" | custom-call | flops 3000000 | bytes 3933184 | tf_op jit(solution)/shard_map/factor/pallas_call | solution.py:22
  6.0 1.1 %collective-permute-done.y_got.refs_13_.refs_14_.refs_12_ = f32[104,128]{1,0:T(8,128)S(1)} collective-permute-done((f32[104,128]{1,0:T(8,128)S(1)}, f32[104,128]{1,0:T(8,128)S(1)}, u32[]{:S(2)}, u32[]{:S(2)}) %collective-permute-start) | collective-permute-done | bytes 53280 | tf_op jit(solution)/shard_map/ppermute | solution.py:895
  7.1 4.6 %collective-permute-start.1 = (f32[168,128]{1,0:T(8,128)S(1)}, f32[168,128]{1,0:T(8,128)S(1)}, u32[]{:S(2)}, u32[]{:S(2)}) collective-permute-start(f32[168,128]{1,0:T(8,128)S(1)} %relay.2.refs_11_.refs_6_), channel_id=1, source_target_pairs={{0,12},{1,13},{2,14},{3,15},{4,8},{5,9},{6,10},{7,11},{8,4},{9,5},... | collective-permute-start | bytes 258056 | tf_op jit(solution)/shard_map/ppermute | solution.py:895
  11.7 0.1 collective-permute-start.2
  11.8 0.1 collective-permute-start.4
  11.9 0.6 %collective-permute-start.3 = (f32[32,128]{1,0:T(8,128)S(1)}, f32[32,128]{1,0:T(8,128)S(1)}, u32[]{:S(2)}, u32[]{:S(2)}) collective-permute-start(f32[32,128]{1,0:T(8,128)S(1)} %beyond.1), channel_id=1, source_target_pairs={{0,9},{1,8},{2,11},{3,10},{4,13},{5,12},{6,15},{7,14},{8,1},{9,0},... | collective-permute-start | bytes 49160 | tf_op jit(solution)/shard_map/ppermute | solution.py:895
  12.5 0.6 %collective-permute-done.4.base_other.refs_6_ = f32[4,16,128]{2,1,0:T(8,128)S(1)} collective-permute-done((f32[4,16,128]{2,1,0:T(8,128)S(1)}, f32[4,16,128]{2,1,0:T(8,128)S(1)}, u32[]{:S(2)}, u32[]{:S(2)}) %collective-permute-start.4) | collective-permute-done | bytes 32800 | tf_op jit(solution)/shard_map/ppermute | solution.py:895
  13.1 0.4 %rim.1 = (f32[24,128]{1,0:T(8,128)S(1)}, f32[24,128]{1,0:T(8,128)S(1)}, f32[24,128]{1,0:T(8,128)S(1)}, f32[6,24,128]{2,1,0:T(8,128)S(1)}, f32[24,256]{1,0:T(8,12...) custom-call(f32[104,128]{1,0:T(8,128)S(1)} %get-tuple-element.52.y_s, ...), custom_call_target="tpu_custom_call" | custom-call | flops 400000 | bytes 480256 | tf_op jit(solution)/shard_map/rim/pallas_call | solution.py:22
  13.5 1.6 %collective-permute-start.6 = (f32[32,128]{1,0:T(8,128)S(1)}, f32[32,128]{1,0:T(8,128)S(1)}, u32[]{:S(2)}, u32[]{:S(2)}) collective-permute-start(f32[32,128]{1,0:T(8,128)S(1)} %get-tuple-element.79), channel_id=1, source_target_pairs={{0,2},{1,3},{2,0},{3,1},{4,6},{5,7},{6,4},{7,5},{8,10},{9,11},{10,... | collective-permute-start | bytes 49160 | tf_op jit(solution)/shard_map/ppermute | solution.py:895
  15.1 1.1 %collective-permute-done.3.refs_15_ = f32[32,128]{1,0:T(8,128)S(1)} collective-permute-done((f32[32,128]{1,0:T(8,128)S(1)}, f32[32,128]{1,0:T(8,128)S(1)}, u32[]{:S(2)}, u32[]{:S(2)}) %collective-permute-start.3) | collective-permute-done | bytes 16416 | tf_op jit(solution)/shard_map/ppermute | solution.py:895
  16.1 0.0 collective-permute-done.1.refs_0_.refs_13_.refs_8_
  16.1 0.7 %collective-permute-done.2.refs_1_.refs_12_.refs_7_ = f32[168,128]{1,0:T(8,128)S(1)} collective-permute-done((f32[168,128]{1,0:T(8,128)S(1)}, f32[168,128]{1,0:T(8,128)S(1)}, u32[]{:S(2)}, u32[]{:S(2)}) %collective-permute-start.2) | collective-permute-done | bytes 86048 | tf_op jit(solution)/shard_map/ppermute | solution.py:895
  16.9 0.6 %observe.1 = (f32[8,128]{1,0:T(8,128)S(1)}, f32[4,256]{1,0:T(4,128)S(1)}) custom-call(f32[168,128]{1,0:T(8,128)S(1)} %collective-permute-done.1.refs_0_.refs_13_.refs_8_, f32[168,128]{1,0:T(8,128)S(1)} %collective-permute-done.2.refs_1_.refs_12_.refs_7_, f32[24,16,128]{2,1,0:T(8,128)S(1)} %get-tuple-element.60.refs_2_, ...), custom_call_target="tpu_custom_call" | custom-call | flops 2000000 | bytes 1742848 | tf_op jit(solution)/shard_map/observe/pallas_call | solution.py:22
  17.5 0.1 collective-permute-start.5
  17.6 0.0 collective-permute-done.6.refs_8_.refs_10_
  17.6 1.1 %collective-permute-done.5.refs_1_ = f32[8,128]{1,0:T(8,128)S(1)} collective-permute-done((f32[8,128]{1,0:T(8,128)S(1)}, f32[8,128]{1,0:T(8,128)S(1)}, u32[]{:S(2)}, u32[]{:S(2)}) %collective-permute-start.5) | collective-permute-done | bytes 4128 | tf_op jit(solution)/shard_map/ppermute | solution.py:895
  18.7 0.3 %weigh.1 = (f32[24,128]{1,0:T(8,128)S(1)}, f32[24,128]{1,0:T(8,128)S(1)}, f32[48,128]{1,0:T(8,128)S(1)}) custom-call(f32[8,128]{1,0:T(8,128)S(1)} %get-tuple-element.78.refs_0_, f32[8,128]{1,0:T(8,128)S(1)} %collective-permute-done.5.refs_1_, f32[4,256]{1,0:T(4,128)S(1)} %get-tuple-element.81.refs_2_, f32[16,256]{1,0:T(8,128)S(1)} %get-tuple-element.64.refs_7_.refs_3_, ...), custom_call_target="tpu_custom_call" | custom-call | flops 500000 | bytes 557056 | tf_op jit(solution)/shard_map/weigh/pallas_call | solution.py:22
  19.1 1.9 %collective-permute-start.8 = (f32[48,128]{1,0:T(8,128)S(1)}, f32[48,128]{1,0:T(8,128)S(1)}, u32[]{:S(2)}, u32[]{:S(2)}) collective-permute-start(f32[48,128]{1,0:T(8,128)S(1)} %get-tuple-element.85), channel_id=1, source_target_pairs={{0,13},{1,8},{2,15},{3,10},{4,9},{5,12},{6,11},{7,14},{8,5},{9,0},... | collective-permute-start | bytes 73736 | tf_op jit(solution)/shard_map/ppermute | solution.py:895
  21.0 0.5 %collective-permute-start.7 = (f32[24,128]{1,0:T(8,128)S(1)}, f32[24,128]{1,0:T(8,128)S(1)}, u32[]{:S(2)}, u32[]{:S(2)}) collective-permute-start(f32[24,128]{1,0:T(8,128)S(1)} %get-tuple-element.84), channel_id=1, source_target_pairs={{0,5},{1,4},{2,7},{3,6},{4,1},{5,0},{6,3},{7,2},{8,13},{9,12},{10,... | collective-permute-start | bytes 36872 | tf_op jit(solution)/shard_map/ppermute | solution.py:895
  21.5 0.0 copy-start.1
  21.5 0.0 copy-start.2
  21.5 2.1 %advance.1 = f32[4,24,16,128]{3,2,1,0:T(8,128)} custom-call(f32[4,24,16,128]{3,2,1,0:T(8,128)S(1)} %get-tuple-element.86.tracer.refs_0_, f32[5,24,16,128]{3,2,1,0:T(8,128)S(1)} %get-tuple-element.87.refs_1_, f32[23,16,128]{2,1,0:T(8,128)S(1)} %get-tuple-element.55.refs_3_.refs_2_, f32[24,16,128]{2,1,0:T(8,128)S(1)} %get-tuple-element.61.refs_4_.refs_3_, ...), custom_call_target="tpu_custom_call" | custom-call | flops 6000000 | bytes 3612672 | tf_op jit(solution)/shard_map/advance/pallas_call | solution.py:22
  23.6 0.5 %collective-permute-done.7.refs_3_ = f32[24,128]{1,0:T(8,128)S(1)} collective-permute-done((f32[24,128]{1,0:T(8,128)S(1)}, f32[24,128]{1,0:T(8,128)S(1)}, u32[]{:S(2)}, u32[]{:S(2)}) %collective-permute-start.7) | collective-permute-done | bytes 12320 | tf_op jit(solution)/shard_map/ppermute | solution.py:895
  24.1 0.0 collective-permute-done.8.refs_4_
  24.1 0.0 copy-done.1
  24.1 0.0 copy-done.2
  24.1 0.7 %regrid.1 = f32[8,128]{1,0:T(8,128)S(1)} custom-call(s32[16,128]{1,0:T(8,128)S(1)} %bitcast.14, f32[16,128]{1,0:T(8,128)S(1)} %bitcast.15, f32[24,128]{1,0:T(8,128)S(1)} %get-tuple-element.89.refs_2_, f32[24,128]{1,0:T(8,128)S(1)} %collective-permute-done.7.refs_3_, f32[48,128]{1,0:T(8,128)S(1)} %collective-permute-done.8.refs_4_), custom_call_target="tpu_custom_call" | custom-call | flops 1000000 | bytes 69632 | tf_op jit(solution)/shard_map/regrid/pallas_call | solution.py:22
  24.8 0.5 %collective-permute-start.9 = (f32[4,128]{1,0:T(4,128)S(1)}, f32[4,128]{1,0:T(4,128)S(1)}, u32[]{:S(2)}, u32[]{:S(2)}) collective-permute-start(f32[4,128]{1,0:T(4,128)S(1)} %slice.15), channel_id=1, source_target_pairs={{0,1},{1,0},{2,3},{3,2},{4,5},{5,4},{6,7},{7,6},{8,9},{9,8},{10,11... | collective-permute-start | bytes 6152 | tf_op jit(solution)/shard_map/ppermute | solution.py:895
  25.4 0.8 %collective-permute-done.9 = f32[4,128]{1,0:T(4,128)S(1)} collective-permute-done((f32[4,128]{1,0:T(4,128)S(1)}, f32[4,128]{1,0:T(4,128)S(1)}, u32[]{:S(2)}, u32[]{:S(2)}) %collective-permute-start.9) | collective-permute-done | bytes 2080 | tf_op jit(solution)/shard_map/ppermute | solution.py:895
  26.2 0.6 %slice_add_fusion = f32[4,128]{1,0:T(4,128)} fusion(f32[4,128]{1,0:T(4,128)S(1)} %collective-permute-done.9, f32[8,128]{1,0:T(8,128)S(1)} %regrid.1), kind=kLoop, calls=%fused_computation.2 | loop fusion | flops 512 | bytes 6144 | tf_op jit(solution)/shard_map/add | solution.py:1190
  (5 shorter events, 0.0 us)
Async XLA Ops:
  2.4 2.8 %copy-start = (f32[4,24,16,128]{3,2,1,0:T(8,128)S(1)}, f32[4,24,16,128]{3,2,1,0:T(8,128)}, u32[]{:S(2)}) copy-start(f32[4,24,16,128]{3,2,1,0:T(8,128)} %refs_4_.1) | copy-start | bytes 2359300
  2.5 4.7 %collective-permute-start = (f32[104,128]{1,0:T(8,128)S(1)}, f32[104,128]{1,0:T(8,128)S(1)}, u32[]{:S(2)}, u32[]{:S(2)}) collective-permute-start(f32[104,128]{1,0:T(8,128)S(1)} %get-tuple-element.52.y_sent.refs_12_.refs_11_), channel_id=1, source_target_pairs={{0,3},{1,2},{2,1},{3,0},{4,7},{5,6},{6,5},{7,4},{8,11},{9,10},{10,... | collective-permute-start | bytes 159752 | tf_op jit(solution)/shard_map/ppermute | solution.py:895
  7.1 9.0 %collective-permute-start.1 = (f32[168,128]{1,0:T(8,128)S(1)}, f32[168,128]{1,0:T(8,128)S(1)}, u32[]{:S(2)}, u32[]{:S(2)}) collective-permute-start(f32[168,128]{1,0:T(8,128)S(1)} %relay.2.refs_11_.refs_6_), channel_id=1, source_target_pairs={{0,12},{1,13},{2,14},{3,15},{4,8},{5,9},{6,10},{7,11},{8,4},{9,5},... | collective-permute-start | bytes 258056 | tf_op jit(solution)/shard_map/ppermute | solution.py:895
  11.7 5.1 %collective-permute-start.2 = (f32[168,128]{1,0:T(8,128)S(1)}, f32[168,128]{1,0:T(8,128)S(1)}, u32[]{:S(2)}, u32[]{:S(2)}) collective-permute-start(f32[168,128]{1,0:T(8,128)S(1)} %relay.3.refs_10_.refs_5_), channel_id=1, source_target_pairs={{0,4},{1,5},{2,6},{3,7},{4,0},{5,1},{6,2},{7,3},{8,12},{9,13},{10,... | collective-permute-start | bytes 258056 | tf_op jit(solution)/shard_map/ppermute | solution.py:895
  11.8 1.3 %collective-permute-start.4 = (f32[4,16,128]{2,1,0:T(8,128)S(1)}, f32[4,16,128]{2,1,0:T(8,128)S(1)}, u32[]{:S(2)}, u32[]{:S(2)}) collective-permute-start(f32[4,16,128]{2,1,0:T(8,128)S(1)} %get-tuple-element.68.base.refs_5_), channel_id=1, source_target_pairs={{0,1},{1,0},{2,3},{3,2},{4,5},{5,4},{6,7},{7,6},{8,9},{9,8},{10,11... | collective-permute-start | bytes 98312 | tf_op jit(solution)/shard_map/ppermute | solution.py:895
  11.9 4.2 %collective-permute-start.3 = (f32[32,128]{1,0:T(8,128)S(1)}, f32[32,128]{1,0:T(8,128)S(1)}, u32[]{:S(2)}, u32[]{:S(2)}) collective-permute-start(f32[32,128]{1,0:T(8,128)S(1)} %beyond.1), channel_id=1, source_target_pairs={{0,9},{1,8},{2,11},{3,10},{4,13},{5,12},{6,15},{7,14},{8,1},{9,0},... | collective-permute-start | bytes 49160 | tf_op jit(solution)/shard_map/ppermute | solution.py:895
  13.5 4.1 %collective-permute-start.6 = (f32[32,128]{1,0:T(8,128)S(1)}, f32[32,128]{1,0:T(8,128)S(1)}, u32[]{:S(2)}, u32[]{:S(2)}) collective-permute-start(f32[32,128]{1,0:T(8,128)S(1)} %get-tuple-element.79), channel_id=1, source_target_pairs={{0,2},{1,3},{2,0},{3,1},{4,6},{5,7},{6,4},{7,5},{8,10},{9,11},{10,... | collective-permute-start | bytes 49160 | tf_op jit(solution)/shard_map/ppermute | solution.py:895
  17.5 1.2 %collective-permute-start.5 = (f32[8,128]{1,0:T(8,128)S(1)}, f32[8,128]{1,0:T(8,128)S(1)}, u32[]{:S(2)}, u32[]{:S(2)}) collective-permute-start(f32[8,128]{1,0:T(8,128)S(1)} %get-tuple-element.78.refs_0_), channel_id=1, source_target_pairs={{0,1},{1,0},{2,3},{3,2},{4,5},{5,4},{6,7},{7,6},{8,9},{9,8},{10,11... | collective-permute-start | bytes 12296 | tf_op jit(solution)/shard_map/ppermute | solution.py:895
  19.1 5.0 %collective-permute-start.8 = (f32[48,128]{1,0:T(8,128)S(1)}, f32[48,128]{1,0:T(8,128)S(1)}, u32[]{:S(2)}, u32[]{:S(2)}) collective-permute-start(f32[48,128]{1,0:T(8,128)S(1)} %get-tuple-element.85), channel_id=1, source_target_pairs={{0,13},{1,8},{2,15},{3,10},{4,9},{5,12},{6,11},{7,14},{8,5},{9,0},... | collective-permute-start | bytes 73736 | tf_op jit(solution)/shard_map/ppermute | solution.py:895
  21.0 3.1 %collective-permute-start.7 = (f32[24,128]{1,0:T(8,128)S(1)}, f32[24,128]{1,0:T(8,128)S(1)}, u32[]{:S(2)}, u32[]{:S(2)}) collective-permute-start(f32[24,128]{1,0:T(8,128)S(1)} %get-tuple-element.84), channel_id=1, source_target_pairs={{0,5},{1,4},{2,7},{3,6},{4,1},{5,0},{6,3},{7,2},{8,13},{9,12},{10,... | collective-permute-start | bytes 36872 | tf_op jit(solution)/shard_map/ppermute | solution.py:895
  21.5 2.6 %copy-start.1 = (s32[1,1,16,128]{3,2,1,0:T(8,128)S(1)}, s32[1,1,16,128]{3,2,1,0:T(8,128)}, u32[]{:S(2)}) copy-start(s32[1,1,16,128]{3,2,1,0:T(8,128)} %param.24) | copy-start | bytes 24580
  21.5 2.6 %copy-start.2 = (f32[1,1,16,128]{3,2,1,0:T(8,128)S(1)}, f32[1,1,16,128]{3,2,1,0:T(8,128)}, u32[]{:S(2)}) copy-start(f32[1,1,16,128]{3,2,1,0:T(8,128)} %param.25) | copy-start | bytes 24580
  24.8 1.4 %collective-permute-start.9 = (f32[4,128]{1,0:T(4,128)S(1)}, f32[4,128]{1,0:T(4,128)S(1)}, u32[]{:S(2)}, u32[]{:S(2)}) collective-permute-start(f32[4,128]{1,0:T(4,128)S(1)} %slice.15), channel_id=1, source_target_pairs={{0,1},{1,0},{2,3},{3,2},{4,5},{5,4},{6,7},{7,6},{8,9},{9,8},{10,11... | collective-permute-start | bytes 6152 | tf_op jit(solution)/shard_map/ppermute | solution.py:895

commit v5 on v4

--- a/solution.py
+++ b/solution.py
@@ -265,7 +265,7 @@
 
 
 def rim_kernel(plan, carried, levels, cx, y_sent, y_got, base, base_other, lanes, *refs):
-    inverse_out, ratio_out, mixing_out, pieces_out, columns_out, rows_out, picks_out, live_out, base_out, square = refs
+    inverse_out, ratio_out, lower_out, pieces_out, columns_out, rows_out, picks_out, live_out, base_out, square = refs
     cy = y_got.shape[1]
     slots = live_out.shape[1]
 
@@ -279,7 +279,7 @@
 
     beyond = turned(y_got[0:cx, :])
     mine = turned(y_sent[0:cx, :])
-    mixing_out[...] = turned(y_got[cx : 2 * cx, :])[0:levels]
+    coupling = turned(y_got[cx : 2 * cx, :])
     north = is_even("facey")
     pieces_out[0] = part(beyond, "c")
     pieces_out[1] = part(beyond, "u")
@@ -291,23 +291,26 @@
     def level_of(ref, level):
         return jnp.broadcast_to(ref[level : level + 1, :], (8, LANES))
 
+    square[...] = coupling
     first = []
     ratios = []
     before = None
     for level in range(levels):
         diagonal = jnp.ones((8, LANES), F32)
         if level > 0:
-            below = level_of(mixing_out, level - 1)
+            below = level_of(square, level - 1)
             diagonal = diagonal + below
         if level < levels - 1:
-            diagonal = diagonal + level_of(mixing_out, level)
+            diagonal = diagonal + level_of(square, level)
         if level > 0:
             diagonal = diagonal - below * below * before
         inverse = 1.0 / diagonal
-        ratios.append(level_of(mixing_out, level) * inverse if level < levels - 1 else jnp.zeros((8, LANES), F32))
+        ratios.append(level_of(square, level) * inverse if level < levels - 1 else jnp.zeros((8, LANES), F32))
+        lower = below * inverse if level > 0 else jnp.zeros((8, LANES), F32)
+        lower_out[level : level + 1, :] = lower[0:1]
         inverse_out[level : level + 1, :] = inverse[0:1]
         ratio_out[level : level + 1, :] = ratios[-1][0:1]
-        first.append(inverse if level == 0 else below * first[-1] * inverse)
+        first.append(inverse if level == 0 else lower * first[-1])
         before = inverse
     weight = first
     for level in range(levels - 2, -1, -1):
@@ -339,7 +342,7 @@
 
 def factor_kernel(sizes, *refs):
     (tracer, west, south, mixing, adjoint, cells) = refs[:6]
-    inverse_out, ratio_out, base_out, inner_out, shares_out, columns_out, rows_out, picks_out = refs[6:]
+    inverse_out, lower_out, ratio_out, base_out, inner_out, shares_out, columns_out, rows_out, picks_out = refs[6:]
     carried, levels, cx, cy = tracer.shape
     slots = cells.shape[1]
     first = []
@@ -356,7 +359,9 @@
         inverse_out[level] = inverse
         if level < levels - 1:
             ratio_out[level] = mixing[level] * inverse
-        first.append(inverse if level == 0 else mixing[level - 1] * first[-1] * inverse)
+        lower = mixing[level - 1] * inverse if level > 0 else jnp.zeros((cx, cy), F32)
+        lower_out[level] = lower
+        first.append(inverse if level == 0 else lower * first[-1])
         before = inverse
     ratio_out[levels - 1] = jnp.zeros((cx, cy), F32)
     weight = first
@@ -422,7 +427,7 @@
 def observe_kernel(sizes, plan, carried, *refs):
     refs = list(refs)
     got = refs[1::-1]
-    inner, mixing, inverse, ratio, columns, in_row, in_lane, live = refs[2:10]
+    inner, lower, inverse, ratio, columns, in_row, in_lane, live = refs[2:10]
     sent = refs[10:12]
     refs = refs[12:]
     y_sent = refs[: plan["y_ops"]]
@@ -480,9 +485,8 @@
         for total, spot_y in lane_parts:
             moved = pltpu.roll(total, cy - level, 1) if level else total
             value = value + jnp.where(lane == spot_y, moved, 0.0)
-        if level > 0:
-            value = value + mixing[level - 1] * forward[-1]
-        forward.append(value * inverse[level])
+        value = value * inverse[level]
+        forward.append(value + lower[level] * forward[-1] if level else value)
     result = forward
     for level in range(levels - 2, -1, -1):
         result[level] = forward[level] + ratio[level] * result[level + 1]
@@ -549,7 +553,7 @@
         state_out[...] = jnp.concatenate([gain, last[0:1]], axis=0)
         return
 
-    rim_inverse, rim_ratio, rim_mixing, pieces, rim_columns, rim_rows, rim_picks, rim_live = rim
+    rim_inverse, rim_ratio, rim_lower, pieces, rim_columns, rim_rows, rim_picks, rim_live = rim
     corners_west, corners_east = sides(got[0][head + 8 : head + 16, :], got[1][head + 8 : head + 16, :])
     turn[...] = jnp.zeros((LANES, LANES), F32)
     turn[0:1, :] = corners_west[0:1]
@@ -571,10 +575,8 @@
 
     climbed = []
     for level in range(levels):
-        value = level_of(rise, level)
-        if level > 0:
-            value = value + level_of(rim_mixing, level - 1) * climbed[-1]
-        climbed.append(value * level_of(rim_inverse, level))
+        value = level_of(rise, level) * level_of(rim_inverse, level)
+        climbed.append(value + level_of(rim_lower, level) * climbed[-1] if level else value)
     for level in range(levels - 2, -1, -1):
         climbed[level] = climbed[level] + level_of(rim_ratio, level) * climbed[level + 1]
     for level in range(levels):
@@ -738,7 +740,7 @@
             out[start // per_tile * rows : (start // per_tile + 1) * rows, :] = tile
 
 
-def regrid_kernel(sizes, plan, carried, cx, band, *refs):
+def regrid_kernel(sizes, plan, bands, carried, cx, band, *refs):
     index, weight = refs[:2]
     blocks = refs[2:-1]
     out = refs[-1]
@@ -753,7 +755,7 @@
     around = sizes[0] * cx
     parts = []
     row_places = []
-    for block, (for_first, for_second) in zip(blocks, plan["bands"]):
+    for block, (for_first, for_second) in zip(blocks, bands):
         from_first, from_second = (for_second, for_first) if plan["cross"] else (for_first, for_second)
         offset = for_first if for_first == for_second else jnp.where(first_core, from_first, from_second)
         start = jnp.bitwise_xor(place, offset) * cx
@@ -789,7 +791,7 @@
             for t in range(len(mine)):
                 totals[number][t] = totals[number][t] + chosen * picked[at : at + rows]
                 at += rows
-    sums = [jnp.zeros((1, cells), F32) for _ in range(tracers)]
+    sums = [jnp.zeros((1, cells), F32) for _ in range(out.shape[0])]
     for mine in totals:
         skip = carried if len(mine) == tracers and plan["cross"] else 0
         for t, total in enumerate(mine):
@@ -799,7 +801,7 @@
 
 
 def advance_kernel(plan, *refs):
-    tracer, parts, mixing, inverse, ratio = refs[:5]
+    tracer, parts, lower, inverse, ratio = refs[:5]
     sent = refs[5:7]
     got = refs[7:9]
     y_ops = plan["y_ops"]
@@ -851,11 +853,11 @@
                 mixed[k].append(value)
         for k in range(stride):
             level = step * stride + k
-            from_below = mixing[jnp.maximum(level - 1, 0)]
+            from_below = lower[level]
             scaled = inverse[level]
             after = []
             for t in range(carried):
-                value = (mixed[k][t] + from_below * before[t]) * scaled
+                value = mixed[k][t] * scaled + from_below * before[t]
                 out[t, level] = value
                 after.append(value)
             before = after
@@ -1029,9 +1031,10 @@
     cell, live, tracer, west_courant, south_courant, emission_scale, mixing = packed[-7:]
     lanes_got = [exchange(lanes_sent[n], sizes, next_y(n, plan["cross"])) for n in range(y_ops)]
     held, *_ = lax.optimization_barrier((tracer, *lanes_sent))
-    inverse, ratio, base, inner, parts, columns, in_row, in_lane = call(
+    inverse, lower, ratio, base, inner, parts, columns, in_row, in_lane = call(
         functools.partial(factor_kernel, sizes),
         [
+            shape(levels, cx, cy),
             shape(levels, cx, cy),
             shape(levels, cx, cy),
             shape(carried, cx, cy),
@@ -1113,7 +1116,7 @@
         rim_got = exchange(rim_sent, sizes, next_y(0, 0))
         parcel, state = observe(
             [shape(plan["parcel"], cy), shape(4, slots)],
-            [rows_got[1], rows_got[0], inner, mixing, inverse, ratio, columns, in_row, in_lane, live, *rows_sent]
+            [rows_got[1], rows_got[0], inner, lower, inverse, ratio, columns, in_row, in_lane, live, *rows_sent]
             + [*lanes_sent, *lanes_got, own_blocks, *x_got, *rim],
             scratch=[pltpu.VMEM((LANES, LANES), F32), pltpu.VMEM((levels, LANES), F32)],
         )
@@ -1135,7 +1138,7 @@
         base_other = other_core(base)
         modeled, state = observe(
             [shape(1, slots), shape(2, slots)],
-            [rows_got[1], rows_got[0], inner, mixing, inverse, ratio, columns, in_row, in_lane, live, *rows_sent]
+            [rows_got[1], rows_got[0], inner, lower, inverse, ratio, columns, in_row, in_lane, live, *rows_sent]
             + [*lanes_sent, *lanes_got, own_blocks, *pair_got]
             + [other_core(jnp.concatenate(pair_got, axis=0))],
         )
@@ -1159,7 +1162,7 @@
     (advanced,) = call(
         functools.partial(advance_kernel, plan),
         [shape(*tracer.shape)],
-        [held, parts, mixing, inverse, ratio]
+        [held, parts, lower, inverse, ratio]
         + list(rows_sent)
         + rows_got
         + lanes_own
@@ -1178,16 +1181,26 @@
         else exchange(s, sizes, jump(first * many_y, second * many_y, plan["cross"]))
         for s, (first, second) in zip(band_sent, plan["bands"])
     ]
-    advanced, *band_got = lax.optimization_barrier((advanced, *band_got))
-    (sums,) = call(
-        functools.partial(regrid_kernel, sizes, plan, carried, cx, band),
-        [shape(2 * carried, ll)],
-        [regrid_index.reshape(taps, ll), regrid_weight.reshape(taps, ll)] + band_got,
-        "regrid",
-        1000000,
-    )
-    sums_other = other_core(sums[carried:])
-    latlon = sums[:carried] + sums_other
+    tables = [regrid_index.reshape(taps, ll), regrid_weight.reshape(taps, ll)]
+    kinds = [first == second for first, second in plan["bands"]]
+
+    def regridded(near, blocks):
+        bands = [pair for pair, kind in zip(plan["bands"], kinds) if kind == near]
+        return call(
+            functools.partial(regrid_kernel, sizes, plan, bands, carried, cx, band),
+            [shape(carried if near else 2 * carried, ll)],
+            [*tables, *blocks],
+            "regrid",
+            1000000,
+        )[0]
+
+    near_got = [got for got, kind in zip(band_got, kinds) if kind]
+    far_got = [got for got, kind in zip(band_got, kinds) if not kind]
+    advanced, *far_got = lax.optimization_barrier((advanced, *far_got))
+    far = regridded(False, far_got)
+    far_other = other_core(far[carried:])
+    *near_got, _ = lax.optimization_barrier((*near_got, far))
+    latlon = far[:carried] + far_other + regridded(True, near_got)
     return (advanced, latlon[:, None, None, :])
 
 

time: 26.9 us -> 26.7 us (level)
  waiting for transfers between devices: 5.97 us -> 4.96 us
  starting transfers between devices: 12.4 us -> 12.9 us
    ppermute x10, waiting for transfers between devices: 5.97 us -> 4.96 us  [exchange(): return lax.ppermute(values, GROUP, pairs)]
    ppermute x10, starting transfers between devices: 12.4 us -> 12.9 us  [exchange(): return lax.ppermute(values, GROUP, pairs)]
    pallas_call x11 -> x12, Pallas kernels: 7.1 us -> 7.34 us  [call(): pl.pallas_call(body, out_shape=outs, in_specs=[pl.BlockSpec(memory_space=...]
  transfers between devices with their start and end apart: 10 -> 10, of which waited for: 7 -> 6; matrix products, arithmetic and copies ran while one was open for 0% -> 0% of each run, Pallas kernels for 16% -> 20%
where the time goes in v5:
time: 26.7 us; the launch traced here: 26.5 us
  starting transfers between devices  12.9 us (48%)
  Pallas kernels  7.34 us (27%)
  waiting for transfers between devices  4.96 us (19%)
  between operations  0.78 us (3%)
  other arithmetic  0.58 us (2%)
    ppermute x10, starting transfers between devices, exchange(): return lax.ppermute(values, GROUP, pairs)  12.9 us
    pallas_call x12, Pallas kernels, call(): pl.pallas_call(body, out_shape=outs, in_specs=[pl.BlockSpec(memory_space=...  7.34 us
    ppermute x10, waiting for transfers between devices, exchange(): return lax.ppermute(values, GROUP, pairs)  4.96 us
    add x1, other arithmetic, local(): latlon = far[:carried] + far_other + regridded(True, near_got)  0.58 us
  transfers between devices with their start and end apart: 10, of which 6 were waited for; matrix products, arithmetic and copies ran while one was open for 0% of the time, Pallas kernels for 20%

profile of v5, /device:TPU:0, one launch (start us, length us, event | category | flops | bytes accessed | tf_op | source)
XLA Modules:
  0.0 26.5 jit_solution(15341559285916766595)
XLA Ops:
  0.6 1.8 %pack.1 = (f32[104,128]{1,0:T(8,128)S(1)}, f32[64,128]{1,0:T(8,128)S(1)}, s32[1,256]{1,0:T(1,128)S(1)}, f32[1,256]{1,0:T(1,128)S(1)}, f32[4,24,16,128]{3,2,1,0:T...) custom-call(f32[4,24,16,128]{3,2,1,0:T(8,128)} %refs_0_.1, ...), custom_call_target="tpu_custom_call" | custom-call | flops 100000 | bytes 2868256 | tf_op jit(solution)/shard_map/pack/pallas_call | solution.py:22
  2.4 0.0 copy-start
  2.5 2.4 %collective-permute-start = (f32[104,128]{1,0:T(8,128)S(1)}, f32[104,128]{1,0:T(8,128)S(1)}, u32[]{:S(2)}, u32[]{:S(2)}) collective-permute-start(f32[104,128]{1,0:T(8,128)S(1)} %get-tuple-element.53.y_sent.refs_12_.refs_11_), channel_id=1, source_target_pairs={{0,3},{1,2},{2,1},{3,0},{4,7},{5,6},{6,5},{7,4},{8,11},{9,10},{10,... | collective-permute-start | bytes 159752 | tf_op jit(solution)/shard_map/ppermute | solution.py:897
  4.9 0.4 %rows.1 = (f32[168,128]{1,0:T(8,128)S(1)}, f32[168,128]{1,0:T(8,128)S(1)}, f32[16,128]{1,0:T(8,128)S(1)}) custom-call(f32[4,24,16,128]{3,2,1,0:T(8,128)S(1)} %get-tuple-element.88.tracer.refs_0_, f32[24,16,128]{2,1,0:T(8,128)S(1)} %get-tuple-element.49.west.refs_1_, f32[16,128]{1,0:T(8,128)S(1)} %get-tuple-element.50.scale.refs_11_, ...), custom_call_target="tpu_custom_call" | custom-call | flops 100000 | bytes 1204224 | tf_op jit(solution)/shard_map/rows/pallas_call | solution.py:22
  5.3 0.0 copy-done
  5.3 0.7 %factor.1 = (f32[24,16,128]{2,1,0:T(8,128)S(1)}, f32[24,16,128]{2,1,0:T(8,128)S(1)}, f32[24,16,128]{2,1,0:T(8,128)S(1)}, f32[4,16,128]{2,1,0:T(8,128)S(1)}, f32[...) custom-call(f32[4,24,16,128]{3,2,1,0:T(8,128)S(1)} %get-tuple-elemen, ...), custom_call_target="tpu_custom_call" | custom-call | flops 3000000 | bytes 4129792 | tf_op jit(solution)/shard_map/factor/pallas_call | solution.py:22
  6.0 1.2 %collective-permute-done.y_got.refs_13_.refs_14_.refs_12_ = f32[104,128]{1,0:T(8,128)S(1)} collective-permute-done((f32[104,128]{1,0:T(8,128)S(1)}, f32[104,128]{1,0:T(8,128)S(1)}, u32[]{:S(2)}, u32[]{:S(2)}) %collective-permute-start) | collective-permute-done | bytes 53280 | tf_op jit(solution)/shard_map/ppermute | solution.py:897
  7.1 4.6 %collective-permute-start.1 = (f32[168,128]{1,0:T(8,128)S(1)}, f32[168,128]{1,0:T(8,128)S(1)}, u32[]{:S(2)}, u32[]{:S(2)}) collective-permute-start(f32[168,128]{1,0:T(8,128)S(1)} %relay.2.refs_11_.refs_6_), channel_id=1, source_target_pairs={{0,12},{1,13},{2,14},{3,15},{4,8},{5,9},{6,10},{7,11},{8,4},{9,5},... | collective-permute-start | bytes 258056 | tf_op jit(solution)/shard_map/ppermute | solution.py:897
  11.7 0.1 collective-permute-start.2
  11.8 0.1 collective-permute-start.4
  11.9 0.6 %collective-permute-start.3 = (f32[32,128]{1,0:T(8,128)S(1)}, f32[32,128]{1,0:T(8,128)S(1)}, u32[]{:S(2)}, u32[]{:S(2)}) collective-permute-start(f32[32,128]{1,0:T(8,128)S(1)} %beyond.1), channel_id=1, source_target_pairs={{0,9},{1,8},{2,11},{3,10},{4,13},{5,12},{6,15},{7,14},{8,1},{9,0},... | collective-permute-start | bytes 49160 | tf_op jit(solution)/shard_map/ppermute | solution.py:897
  12.5 0.6 %collective-permute-done.4.base_other.refs_6_ = f32[4,16,128]{2,1,0:T(8,128)S(1)} collective-permute-done((f32[4,16,128]{2,1,0:T(8,128)S(1)}, f32[4,16,128]{2,1,0:T(8,128)S(1)}, u32[]{:S(2)}, u32[]{:S(2)}) %collective-permute-start.4) | collective-permute-done | bytes 32800 | tf_op jit(solution)/shard_map/ppermute | solution.py:897
  13.1 0.4 %rim.1 = (f32[24,128]{1,0:T(8,128)S(1)}, f32[24,128]{1,0:T(8,128)S(1)}, f32[24,128]{1,0:T(8,128)S(1)}, f32[6,24,128]{2,1,0:T(8,128)S(1)}, f32[24,256]{1,0:T(8,12...) custom-call(f32[104,128]{1,0:T(8,128)S(1)} %get-tuple-element.53.y_s, ...), custom_call_target="tpu_custom_call" | custom-call | flops 400000 | bytes 480256 | tf_op jit(solution)/shard_map/rim/pallas_call | solution.py:22
  13.5 1.6 %collective-permute-start.6 = (f32[32,128]{1,0:T(8,128)S(1)}, f32[32,128]{1,0:T(8,128)S(1)}, u32[]{:S(2)}, u32[]{:S(2)}) collective-permute-start(f32[32,128]{1,0:T(8,128)S(1)} %get-tuple-element.81), channel_id=1, source_target_pairs={{0,2},{1,3},{2,0},{3,1},{4,6},{5,7},{6,4},{7,5},{8,10},{9,11},{10,... | collective-permute-start | bytes 49160 | tf_op jit(solution)/shard_map/ppermute | solution.py:897
  15.1 1.1 %collective-permute-done.3.refs_15_ = f32[32,128]{1,0:T(8,128)S(1)} collective-permute-done((f32[32,128]{1,0:T(8,128)S(1)}, f32[32,128]{1,0:T(8,128)S(1)}, u32[]{:S(2)}, u32[]{:S(2)}) %collective-permute-start.3) | collective-permute-done | bytes 16416 | tf_op jit(solution)/shard_map/ppermute | solution.py:897
  16.1 0.0 collective-permute-done.1.refs_0_.refs_13_.refs_8_
  16.1 0.7 %collective-permute-done.2.refs_1_.refs_12_.refs_7_ = f32[168,128]{1,0:T(8,128)S(1)} collective-permute-done((f32[168,128]{1,0:T(8,128)S(1)}, f32[168,128]{1,0:T(8,128)S(1)}, u32[]{:S(2)}, u32[]{:S(2)}) %collective-permute-start.2) | collective-permute-done | bytes 86048 | tf_op jit(solution)/shard_map/ppermute | solution.py:897
  16.9 0.6 %observe.1 = (f32[8,128]{1,0:T(8,128)S(1)}, f32[4,256]{1,0:T(4,128)S(1)}) custom-call(f32[168,128]{1,0:T(8,128)S(1)} %collective-permute-done.1.refs_0_.refs_13_.refs_8_, f32[168,128]{1,0:T(8,128)S(1)} %collective-permute-done.2.refs_1_.refs_12_.refs_7_, f32[24,16,128]{2,1,0:T(8,128)S(1)} %get-tuple-element.61.refs_2_, ...), custom_call_target="tpu_custom_call" | custom-call | flops 2000000 | bytes 1751040 | tf_op jit(solution)/shard_map/observe/pallas_call | solution.py:22
  17.5 0.1 collective-permute-start.5
  17.6 0.0 collective-permute-done.6.refs_8_.refs_10_
  17.6 1.1 %collective-permute-done.5.refs_1_ = f32[8,128]{1,0:T(8,128)S(1)} collective-permute-done((f32[8,128]{1,0:T(8,128)S(1)}, f32[8,128]{1,0:T(8,128)S(1)}, u32[]{:S(2)}, u32[]{:S(2)}) %collective-permute-start.5) | collective-permute-done | bytes 4128 | tf_op jit(solution)/shard_map/ppermute | solution.py:897
  18.7 0.3 %weigh.1 = (f32[24,128]{1,0:T(8,128)S(1)}, f32[24,128]{1,0:T(8,128)S(1)}, f32[48,128]{1,0:T(8,128)S(1)}) custom-call(f32[8,128]{1,0:T(8,128)S(1)} %get-tuple-element.80.refs_0_, f32[8,128]{1,0:T(8,128)S(1)} %collective-permute-done.5.refs_1_, f32[4,256]{1,0:T(4,128)S(1)} %get-tuple-element.83.refs_2_, f32[16,256]{1,0:T(8,128)S(1)} %get-tuple-element.66.refs_7_.refs_3_, ...), custom_call_target="tpu_custom_call" | custom-call | flops 500000 | bytes 557056 | tf_op jit(solution)/shard_map/weigh/pallas_call | solution.py:22
  19.1 1.9 %collective-permute-start.7 = (f32[48,128]{1,0:T(8,128)S(1)}, f32[48,128]{1,0:T(8,128)S(1)}, u32[]{:S(2)}, u32[]{:S(2)}) collective-permute-start(f32[48,128]{1,0:T(8,128)S(1)} %get-tuple-element.87), channel_id=1, source_target_pairs={{0,13},{1,8},{2,15},{3,10},{4,9},{5,12},{6,11},{7,14},{8,5},{9,0},... | collective-permute-start | bytes 73736 | tf_op jit(solution)/shard_map/ppermute | solution.py:897
  20.9 0.5 %collective-permute-start.9 = (f32[24,128]{1,0:T(8,128)S(1)}, f32[24,128]{1,0:T(8,128)S(1)}, u32[]{:S(2)}, u32[]{:S(2)}) collective-permute-start(f32[24,128]{1,0:T(8,128)S(1)} %get-tuple-element.86), channel_id=1, source_target_pairs={{0,5},{1,4},{2,7},{3,6},{4,1},{5,0},{6,3},{7,2},{8,13},{9,12},{10,... | collective-permute-start | bytes 36872 | tf_op jit(solution)/shard_map/ppermute | solution.py:897
  21.4 0.0 copy-start.1
  21.4 0.0 copy-start.2
  21.4 2.1 %advance.1 = f32[4,24,16,128]{3,2,1,0:T(8,128)} custom-call(f32[4,24,16,128]{3,2,1,0:T(8,128)S(1)} %get-tuple-element.88.tracer.refs_0_, f32[5,24,16,128]{3,2,1,0:T(8,128)S(1)} %get-tuple-element.89.refs_1_, f32[24,16,128]{2,1,0:T(8,128)S(1)} %get-tuple-element.62.refs_3_.refs_2_, f32[24,16,128]{2,1,0:T(8,128)S(1)} %get-tuple-element.63.refs_4_.refs_3_, ...), custom_call_target="tpu_custom_call" | custom-call | flops 6000000 | bytes 3620864 | tf_op jit(solution)/shard_map/advance/pallas_call | solution.py:22
  23.5 0.0 collective-permute-done.7.refs_2_
  23.5 0.0 copy-done.1
  23.6 0.0 copy-done.2
  23.6 0.5 %regrid.2 = f32[8,128]{1,0:T(8,128)S(1)} custom-call(s32[16,128]{1,0:T(8,128)S(1)} %bitcast.14, f32[16,128]{1,0:T(8,128)S(1)} %bitcast.16, f32[48,128]{1,0:T(8,128)S(1)} %collective-permute-done.7.refs_2_), custom_call_target="tpu_custom_call" | custom-call | flops 1000000 | bytes 45056 | tf_op jit(solution)/shard_map/regrid/pallas_call | solution.py:22
  24.1 1.0 %collective-permute-start.8 = (f32[4,128]{1,0:T(4,128)S(1)}, f32[4,128]{1,0:T(4,128)S(1)}, u32[]{:S(2)}, u32[]{:S(2)}) collective-permute-start(f32[4,128]{1,0:T(4,128)S(1)} %slice.15), channel_id=1, source_target_pairs={{0,1},{1,0},{2,3},{3,2},{4,5},{5,4},{6,7},{7,6},{8,9},{9,8},{10,11... | collective-permute-start | bytes 6152 | tf_op jit(solution)/shard_map/ppermute | solution.py:897
  25.1 0.0 collective-permute-done.9.refs_3_
  25.1 0.5 %regrid.3 = f32[4,128]{1,0:T(4,128)S(1)} custom-call(s32[16,128]{1,0:T(8,128)S(1)} %bitcast.15, f32[16,128]{1,0:T(8,128)S(1)} %bitcast.17, f32[24,128]{1,0:T(8,128)S(1)} %get-tuple-element.92.refs_2_, f32[24,128]{1,0:T(8,128)S(1)} %collective-permute-done.9.refs_3_), custom_call_target="tpu_custom_call" | custom-call | flops 1000000 | bytes 43008 | tf_op jit(solution)/shard_map/regrid/pallas_call | solution.py:22
  25.6 0.3 %collective-permute-done.8 = f32[4,128]{1,0:T(4,128)S(1)} collective-permute-done((f32[4,128]{1,0:T(4,128)S(1)}, f32[4,128]{1,0:T(4,128)S(1)}, u32[]{:S(2)}, u32[]{:S(2)}) %collective-permute-start.8) | collective-permute-done | bytes 2080 | tf_op jit(solution)/shard_map/ppermute | solution.py:897
  25.9 0.6 %add_add_fusion = f32[4,128]{1,0:T(4,128)} fusion(f32[4,128]{1,0:T(4,128)S(1)} %regrid.3, f32[4,128]{1,0:T(4,128)S(1)} %collective-permute-done.8, f32[8,128]{1,0:T(8,128)S(1)} %regrid.2), kind=kLoop, calls=%fused_computation.2 | loop fusion | flops 1024 | bytes 8192 | tf_op jit(solution)/shard_map/add | solution.py:1203
  (5 shorter events, 0.0 us)
Async XLA Ops:
  2.4 2.8 %copy-start = (f32[4,24,16,128]{3,2,1,0:T(8,128)S(1)}, f32[4,24,16,128]{3,2,1,0:T(8,128)}, u32[]{:S(2)}) copy-start(f32[4,24,16,128]{3,2,1,0:T(8,128)} %refs_4_.1) | copy-start | bytes 2359300
  2.5 4.7 %collective-permute-start = (f32[104,128]{1,0:T(8,128)S(1)}, f32[104,128]{1,0:T(8,128)S(1)}, u32[]{:S(2)}, u32[]{:S(2)}) collective-permute-start(f32[104,128]{1,0:T(8,128)S(1)} %get-tuple-element.53.y_sent.refs_12_.refs_11_), channel_id=1, source_target_pairs={{0,3},{1,2},{2,1},{3,0},{4,7},{5,6},{6,5},{7,4},{8,11},{9,10},{10,... | collective-permute-start | bytes 159752 | tf_op jit(solution)/shard_map/ppermute | solution.py:897
  7.1 9.0 %collective-permute-start.1 = (f32[168,128]{1,0:T(8,128)S(1)}, f32[168,128]{1,0:T(8,128)S(1)}, u32[]{:S(2)}, u32[]{:S(2)}) collective-permute-start(f32[168,128]{1,0:T(8,128)S(1)} %relay.2.refs_11_.refs_6_), channel_id=1, source_target_pairs={{0,12},{1,13},{2,14},{3,15},{4,8},{5,9},{6,10},{7,11},{8,4},{9,5},... | collective-permute-start | bytes 258056 | tf_op jit(solution)/shard_map/ppermute | solution.py:897
  11.7 5.1 %collective-permute-start.2 = (f32[168,128]{1,0:T(8,128)S(1)}, f32[168,128]{1,0:T(8,128)S(1)}, u32[]{:S(2)}, u32[]{:S(2)}) collective-permute-start(f32[168,128]{1,0:T(8,128)S(1)} %relay.3.refs_10_.refs_5_), channel_id=1, source_target_pairs={{0,4},{1,5},{2,6},{3,7},{4,0},{5,1},{6,2},{7,3},{8,12},{9,13},{10,... | collective-permute-start | bytes 258056 | tf_op jit(solution)/shard_map/ppermute | solution.py:897
  11.8 1.3 %collective-permute-start.4 = (f32[4,16,128]{2,1,0:T(8,128)S(1)}, f32[4,16,128]{2,1,0:T(8,128)S(1)}, u32[]{:S(2)}, u32[]{:S(2)}) collective-permute-start(f32[4,16,128]{2,1,0:T(8,128)S(1)} %get-tuple-element.70.base.refs_5_), channel_id=1, source_target_pairs={{0,1},{1,0},{2,3},{3,2},{4,5},{5,4},{6,7},{7,6},{8,9},{9,8},{10,11... | collective-permute-start | bytes 98312 | tf_op jit(solution)/shard_map/ppermute | solution.py:897
  11.9 4.2 %collective-permute-start.3 = (f32[32,128]{1,0:T(8,128)S(1)}, f32[32,128]{1,0:T(8,128)S(1)}, u32[]{:S(2)}, u32[]{:S(2)}) collective-permute-start(f32[32,128]{1,0:T(8,128)S(1)} %beyond.1), channel_id=1, source_target_pairs={{0,9},{1,8},{2,11},{3,10},{4,13},{5,12},{6,15},{7,14},{8,1},{9,0},... | collective-permute-start | bytes 49160 | tf_op jit(solution)/shard_map/ppermute | solution.py:897
  13.5 4.1 %collective-permute-start.6 = (f32[32,128]{1,0:T(8,128)S(1)}, f32[32,128]{1,0:T(8,128)S(1)}, u32[]{:S(2)}, u32[]{:S(2)}) collective-permute-start(f32[32,128]{1,0:T(8,128)S(1)} %get-tuple-element.81), channel_id=1, source_target_pairs={{0,2},{1,3},{2,0},{3,1},{4,6},{5,7},{6,4},{7,5},{8,10},{9,11},{10,... | collective-permute-start | bytes 49160 | tf_op jit(solution)/shard_map/ppermute | solution.py:897
  17.5 1.2 %collective-permute-start.5 = (f32[8,128]{1,0:T(8,128)S(1)}, f32[8,128]{1,0:T(8,128)S(1)}, u32[]{:S(2)}, u32[]{:S(2)}) collective-permute-start(f32[8,128]{1,0:T(8,128)S(1)} %get-tuple-element.80.refs_0_), channel_id=1, source_target_pairs={{0,1},{1,0},{2,3},{3,2},{4,5},{5,4},{6,7},{7,6},{8,9},{9,8},{10,11... | collective-permute-start | bytes 12296 | tf_op jit(solution)/shard_map/ppermute | solution.py:897
  19.1 4.5 %collective-permute-start.7 = (f32[48,128]{1,0:T(8,128)S(1)}, f32[48,128]{1,0:T(8,128)S(1)}, u32[]{:S(2)}, u32[]{:S(2)}) collective-permute-start(f32[48,128]{1,0:T(8,128)S(1)} %get-tuple-element.87), channel_id=1, source_target_pairs={{0,13},{1,8},{2,15},{3,10},{4,9},{5,12},{6,11},{7,14},{8,5},{9,0},... | collective-permute-start | bytes 73736 | tf_op jit(solution)/shard_map/ppermute | solution.py:897
  20.9 4.2 %collective-permute-start.9 = (f32[24,128]{1,0:T(8,128)S(1)}, f32[24,128]{1,0:T(8,128)S(1)}, u32[]{:S(2)}, u32[]{:S(2)}) collective-permute-start(f32[24,128]{1,0:T(8,128)S(1)} %get-tuple-element.86), channel_id=1, source_target_pairs={{0,5},{1,4},{2,7},{3,6},{4,1},{5,0},{6,3},{7,2},{8,13},{9,12},{10,... | collective-permute-start | bytes 36872 | tf_op jit(solution)/shard_map/ppermute | solution.py:897
  21.4 2.1 %copy-start.1 = (s32[1,1,16,128]{3,2,1,0:T(8,128)S(1)}, s32[1,1,16,128]{3,2,1,0:T(8,128)}, u32[]{:S(2)}) copy-start(s32[1,1,16,128]{3,2,1,0:T(8,128)} %param.24) | copy-start | bytes 24580
  21.4 2.1 %copy-start.2 = (f32[1,1,16,128]{3,2,1,0:T(8,128)S(1)}, f32[1,1,16,128]{3,2,1,0:T(8,128)}, u32[]{:S(2)}) copy-start(f32[1,1,16,128]{3,2,1,0:T(8,128)} %param.25) | copy-start | bytes 24580
  24.1 1.9 %collective-permute-start.8 = (f32[4,128]{1,0:T(4,128)S(1)}, f32[4,128]{1,0:T(4,128)S(1)}, u32[]{:S(2)}, u32[]{:S(2)}) collective-permute-start(f32[4,128]{1,0:T(4,128)S(1)} %slice.15), channel_id=1, source_target_pairs={{0,1},{1,0},{2,3},{3,2},{4,5},{5,4},{6,7},{7,6},{8,9},{9,8},{10,11... | collective-permute-start | bytes 6152 | tf_op jit(solution)/shard_map/ppermute | solution.py:897

commit v6 on v5

--- a/solution.py
+++ b/solution.py
@@ -223,7 +223,6 @@
 def rows_kernel(plan, tracer, west, scale, blocks, *outs):
     carried, levels, cx, cy = tracer.shape
     head = (carried + 1) * levels
-    even_x = is_even("facex")
     if plan["relay"]:
         tile = LanePacker(iota((cx, cy), 1), edge_of(0, cy))
         for t in range(carried):
@@ -232,7 +231,7 @@
                 tile.put(spot, pltpu.roll(tracer[t, level], spot, 1) if spot else tracer[t, level])
         outs[2][...] = tile.packed(0)
     for number, out in enumerate(outs[:2]):
-        row = jnp.where(even_x if number == 0 else jnp.logical_not(even_x), cx - 1, 0)
+        row = sent_row(plan, number, cx)
         for level in range(levels):
             for t in range(carried):
                 spot = t * levels + level
@@ -246,15 +245,15 @@
 
 
 def relay_kernel(plan, head, cx, number, rows, blocks, y_got, out):
+    out[0 : head + 8, :] = rows[0 : head + 8, :]
+    row = sent_row(plan, number, cx)
+    out[head + 1 : head + 2, :] = y_got[pl.ds(row, 1), :]
+    near, far = plan["x_blocks"]
     even_x = is_even("facex")
-    out[0 : head + 8, :] = rows[0 : head + 8, :]
-    row = jnp.where(even_x if number == 0 else jnp.logical_not(even_x), cx - 1, 0)
-    out[head + 8 : head + 16, :] = jnp.broadcast_to(y_got[pl.ds(row, 1), :], (8, out.shape[1]))
-    offset = plan["x_blocks"][number]
-    if offset:
-        at = plan["y_tiles"] * cx + 8 * offset
-        out[head + 16 : head + 32, :] = blocks[8 * offset : 8 * offset + 16, :]
-        out[head + 32 : head + 48, :] = y_got[at : at + 16, :]
+    offset = jnp.where(even_x if number == 0 else jnp.logical_not(even_x), near, far)
+    at = plan["y_tiles"] * cx + 8 * offset
+    out[head + 8 : head + 24, :] = blocks[pl.ds(pl.multiple_of(8 * offset, 8), 16), :]
+    out[head + 24 : head + 40, :] = y_got[pl.ds(pl.multiple_of(at, 8), 16), :]
 
 
 def beyond_kernel(plan, cx, blocks, y_got, *outs):
@@ -395,9 +394,22 @@
         columns_out[level : level + 1, :] = jnp.sum(part, axis=0, keepdims=True)
 
 
-def sides(first, second):
+def sides(plan, first, second):
+    if plan["relay"]:
+        return first, second
     even_x = is_even("facex")
     return jnp.where(even_x, second, first), jnp.where(even_x, first, second)
+
+
+def own_sides(plan, first, second):
+    return (second, first) if plan["relay"] else sides(plan, first, second)
+
+
+def sent_row(plan, number, rows):
+    if plan["relay"]:
+        return rows - 1 if number == 0 else 0
+    even_x = is_even("facex")
+    return jnp.where(even_x if number == 0 else jnp.logical_not(even_x), rows - 1, 0)
 
 
 def seam(number, sent, got, sent_face, got_face):
@@ -426,7 +438,7 @@
 
 def observe_kernel(sizes, plan, carried, *refs):
     refs = list(refs)
-    got = refs[1::-1]
+    got = refs[0:2]
     inner, lower, inverse, ratio, columns, in_row, in_lane, live = refs[2:10]
     sent = refs[10:12]
     refs = refs[12:]
@@ -454,8 +466,8 @@
             total = total + rows[t * levels : (t + 1) * levels]
         return total
 
-    beyond_west, beyond_east = sides(got[0][0:head], got[1][0:head])
-    at_west, at_east = sides(sent[0][0:head], sent[1][0:head])
+    beyond_west, beyond_east = sides(plan, got[0][0:head], got[1][0:head])
+    at_west, at_east = own_sides(plan, sent[0][0:head], sent[1][0:head])
     spot = carried * levels
     face_west = at_west[spot:head]
     face_east = beyond_east[spot:head]
@@ -503,7 +515,12 @@
 
         blocks = {0: block_at(own, 0), 1: block_at(y_got[0], start + 8)}
         rim_blocks = {0: block_at(y_got[0], start), 1: block_at(own, 8)}
-        carriers = [(offset, got[n], head + 16) for n, offset in enumerate(plan["x_blocks"]) if offset]
+        even_x = is_even("facex")
+        from_west, from_east = (got[n][head + 8 : head + 40, :] for n in range(2))
+        carriers = [
+            (plan["x_blocks"][0], jnp.where(even_x, from_east, from_west), 0),
+            (plan["x_blocks"][1], jnp.where(even_x, from_west, from_east), 0),
+        ]
         carriers += [(offset, ref, 0) for offset, ref in zip(plan["x_ops"], x_got)]
         for offset, ref, row in carriers:
             blocks[offset], rim_blocks[offset + 1] = block_at(ref, row), block_at(ref, row + 8)
@@ -554,10 +571,10 @@
         return
 
     rim_inverse, rim_ratio, rim_lower, pieces, rim_columns, rim_rows, rim_picks, rim_live = rim
-    corners_west, corners_east = sides(got[0][head + 8 : head + 16, :], got[1][head + 8 : head + 16, :])
+    corners_west, corners_east = sides(plan, got[0][head + 1 : head + 2, :], got[1][head + 1 : head + 2, :])
     turn[...] = jnp.zeros((LANES, LANES), F32)
-    turn[0:1, :] = corners_west[0:1]
-    turn[cx - 1 : cx, :] = corners_east[0:1]
+    turn[0:1, :] = corners_west
+    turn[cx - 1 : cx, :] = corners_east
     turned = jnp.transpose(turn[...])
     ends = turned[plan["lane_c"] : plan["lane_c"] + levels]
     end_face = turned[plan["lane_u"] : plan["lane_u"] + levels]
@@ -686,8 +703,8 @@
     face_west = west[...]
     face_south = south[...]
     scales = scale[...]
-    beyond_west, beyond_east = sides(got[0][head : head + 1], got[1][head : head + 1])
-    _, east_wind = sides(got[0][spot : spot + 1], got[1][spot : spot + 1])
+    beyond_west, beyond_east = sides(plan, got[0][head : head + 1], got[1][head : head + 1])
+    _, east_wind = sides(plan, got[0][spot : spot + 1], got[1][spot : spot + 1])
     face_east = jnp.where(row == cx - 1, east_wind, pltpu.roll(face_west, cx - 1, 0))
     face_north = left(face_south)
     norths = []
@@ -742,12 +759,10 @@
 
 def regrid_kernel(sizes, plan, bands, carried, cx, band, *refs):
     index, weight = refs[:2]
-    blocks = refs[2:-1]
-    out = refs[-1]
+    blocks, more, out = refs[2 : 2 + len(bands)], refs[2 + len(bands) : -1], refs[-1]
     taps, cells = index.shape
-    tracers = 2 * carried
     rows = cx + 8
-    per_tile = min(tracers, LANES // band)
+    per_tile = min(2 * carried, LANES // band)
     lane = iota((rows, LANES), 1)
     row = iota((rows, cells), 0)
     first_core = lax.axis_index("lev") == 0
@@ -755,30 +770,28 @@
     around = sizes[0] * cx
     parts = []
     row_places = []
-    for block, (for_first, for_second) in zip(blocks, bands):
-        from_first, from_second = (for_second, for_first) if plan["cross"] else (for_first, for_second)
-        offset = for_first if for_first == for_second else jnp.where(first_core, from_first, from_second)
+    for block, ((for_first, for_second), fetched, first) in zip(blocks, bands):
+        if plan["cross"] != fetched:
+            for_first, for_second = for_second, for_first
+        offset = for_first if for_first == for_second else jnp.where(first_core, for_first, for_second)
         start = jnp.bitwise_xor(place, offset) * cx
         places = start + row
         places = jnp.where(row == cx, lax.rem(start + around - 1, around), places)
         places = jnp.where(row == cx + 1, lax.rem(start + cx, around), places)
         row_places.append(places)
-        count = carried if for_first == for_second else tracers
-        mine = []
-        for t in range(count):
+        for t in range(first, first + carried):
             tile = block[t // per_tile * rows : (t // per_tile + 1) * rows, :]
             a = t % per_tile
             values = tile if a == 0 else pltpu.roll(tile, (-band * a) % LANES, 1)
             high = values.astype(BF16).astype(F32)
             low = pltpu.roll(values - high, band, 1)
             both = jnp.where(lane < band, high, jnp.where(lane < 2 * band, low, 0.0))
-            mine.append(both.astype(BF16))
-        parts.append(mine)
-    left_side = jnp.concatenate([jnp.concatenate(mine, axis=0) for mine in parts], axis=0)
+            parts.append(both.astype(BF16))
+    left_side = jnp.concatenate(parts, axis=0)
     spread = iota((LANES, cells), 0)
     in_band = lax.rem(spread, band)
     used = spread < 2 * band
-    totals = [[jnp.zeros((rows, cells), F32) for _ in mine] for mine in parts]
+    totals = [jnp.zeros((rows, cells), F32) for _ in range(carried)]
     for tap in range(taps):
         place_of = index[tap : tap + 1, :]
         column = lax.div(place_of, band)
@@ -786,18 +799,15 @@
         picks = jnp.where(jnp.logical_and(in_band == in_lane, used), 1.0, 0.0).astype(BF16)
         picked = jnp.dot(left_side, picks, preferred_element_type=F32)
         at = 0
-        for number, mine in enumerate(parts):
-            chosen = jnp.where(row_places[number] == column, weight[tap : tap + 1, :], 0.0)
-            for t in range(len(mine)):
-                totals[number][t] = totals[number][t] + chosen * picked[at : at + rows]
+        for places in row_places:
+            chosen = jnp.where(places == column, weight[tap : tap + 1, :], 0.0)
+            for t in range(carried):
+                totals[t] = totals[t] + chosen * picked[at : at + rows]
                 at += rows
-    sums = [jnp.zeros((1, cells), F32) for _ in range(out.shape[0])]
-    for mine in totals:
-        skip = carried if len(mine) == tracers and plan["cross"] else 0
-        for t, total in enumerate(mine):
-            to = (t + skip) % tracers
-            sums[to] = sums[to] + jnp.sum(total, axis=0, keepdims=True)
-    out[...] = jnp.concatenate(sums, axis=0)
+    sums = jnp.concatenate([jnp.sum(total, axis=0, keepdims=True) for total in totals], axis=0)
+    for ref in more:
+        sums = sums + ref[...]
+    out[...] = sums
 
 
 def advance_kernel(plan, *refs):
@@ -810,8 +820,8 @@
     carried, levels, cx, cy = tracer.shape
     head = (carried + 1) * levels
     spot = carried * levels
-    beyond_west, beyond_east = sides(got[0][0:head], got[1][0:head])
-    at_west, at_east = sides(sent[0][0:head], sent[1][0:head])
+    beyond_west, beyond_east = sides(plan, got[0][0:head], got[1][0:head])
+    at_west, at_east = own_sides(plan, sent[0][0:head], sent[1][0:head])
     face_west = at_west[spot:head]
     face_east = beyond_east[spot:head]
     for t in range(carried):
@@ -901,7 +911,7 @@
     many_x, many_y, _ = sizes
     tiles = many_x * many_y
     x_blocks = [many_y, (many_x - 1) * many_y if many_x == 4 else 0]
-    relay = many_y == 2
+    relay = many_y == 2 and many_x == 4
     if relay:
         own_blocks = list(range(tiles))
         y_blocks = own_blocks
@@ -966,7 +976,7 @@
 
     def next_x(number):
         def rule(x, y, c):
-            step = 1 if (x % 2 == 0) == (number == 0) else -1
+            step = 1 if (plan["relay"] or x % 2 == 0) == (number == 0) else -1
             return ((x + step) % many_x, y, c)
 
         return rule
@@ -990,7 +1000,7 @@
 
     strips = slots // LANES
     plan["parcel"] = -(-2 * strips // 8) * 8
-    extra = 48 if plan["relay"] else 16
+    extra = 40 if plan["relay"] else 16
     row_shapes = [shape(head + extra, cy)] * 2
     y_rows = plan["y_tiles"] * cx + 8 * len(plan["y_blocks"]) + (plan["parcel"] if plan["relay"] else 0)
     lane_shapes = [shape(y_rows if n == 0 else cx, cy) for n in range(y_ops)]
@@ -1116,7 +1126,7 @@
         rim_got = exchange(rim_sent, sizes, next_y(0, 0))
         parcel, state = observe(
             [shape(plan["parcel"], cy), shape(4, slots)],
-            [rows_got[1], rows_got[0], inner, lower, inverse, ratio, columns, in_row, in_lane, live, *rows_sent]
+            [*rows_got, inner, lower, inverse, ratio, columns, in_row, in_lane, live, *rows_sent]
             + [*lanes_sent, *lanes_got, own_blocks, *x_got, *rim],
             scratch=[pltpu.VMEM((LANES, LANES), F32), pltpu.VMEM((levels, LANES), F32)],
         )
@@ -1138,7 +1148,7 @@
         base_other = other_core(base)
         modeled, state = observe(
             [shape(1, slots), shape(2, slots)],
-            [rows_got[1], rows_got[0], inner, lower, inverse, ratio, columns, in_row, in_lane, live, *rows_sent]
+            [*rows_got, inner, lower, inverse, ratio, columns, in_row, in_lane, live, *rows_sent]
             + [*lanes_sent, *lanes_got, own_blocks, *pair_got]
             + [other_core(jnp.concatenate(pair_got, axis=0))],
         )
@@ -1184,23 +1194,24 @@
     tables = [regrid_index.reshape(taps, ll), regrid_weight.reshape(taps, ll)]
     kinds = [first == second for first, second in plan["bands"]]
 
-    def regridded(near, blocks):
-        bands = [pair for pair, kind in zip(plan["bands"], kinds) if kind == near]
+    def regridded(bands, blocks, *more):
         return call(
             functools.partial(regrid_kernel, sizes, plan, bands, carried, cx, band),
-            [shape(carried if near else 2 * carried, ll)],
-            [*tables, *blocks],
+            [shape(carried, ll)],
+            [*tables, *blocks, *more],
             "regrid",
             1000000,
         )[0]
 
+    near = [(pair, 0, 0) for pair, kind in zip(plan["bands"], kinds) if kind]
+    far = [pair for pair, kind in zip(plan["bands"], kinds) if not kind]
     near_got = [got for got, kind in zip(band_got, kinds) if kind]
     far_got = [got for got, kind in zip(band_got, kinds) if not kind]
-    advanced, *far_got = lax.optimization_barrier((advanced, *far_got))
-    far = regridded(False, far_got)
-    far_other = other_core(far[carried:])
-    *near_got, _ = lax.optimization_barrier((*near_got, far))
-    latlon = far[:carried] + far_other + regridded(True, near_got)
+    advanced, near_got, far_got = lax.optimization_barrier((advanced, near_got, far_got))
+    far_fetched = [other_core(got) for got in far_got]
+    mine = carried if plan["cross"] else 0
+    partial = regridded(near + [(pair, 0, mine) for pair in far], near_got + far_got)
+    latlon = regridded([(pair, 1, carried - mine) for pair in far], far_fetched, partial)
     return (advanced, latlon[:, None, None, :])
 
 

time: 26.7 us -> 26.2 us (0.981)
  other arithmetic: 0.58 us -> 0 us
  Pallas kernels: 7.34 us -> 7.89 us
    add x1 -> x0, other arithmetic: 0.58 us -> none  [local(): latlon = far[:carried] + far_other + regridded(True, near_got)]
    pallas_call x12, Pallas kernels: 7.34 us -> 7.89 us  [call(): pl.pallas_call(body, out_shape=outs, in_specs=[pl.BlockSpec(memory_space=...]
  transfers between devices with their start and end apart: 10 -> 10, of which waited for: 6 -> 6; matrix products, arithmetic and copies ran while one was open for 0% -> 0% of each run, Pallas kernels for 20% -> 18%
where the time goes in v6:
time: 26.2 us; the launch traced here: 26.1 us
  starting transfers between devices  12.8 us (49%)
  Pallas kernels  7.89 us (30%)
  waiting for transfers between devices  4.71 us (18%)
  between operations  0.7 us (3%)
    ppermute x10, starting transfers between devices, exchange(): return lax.ppermute(values, GROUP, pairs)  12.8 us
    pallas_call x12, Pallas kernels, call(): pl.pallas_call(body, out_shape=outs, in_specs=[pl.BlockSpec(memory_space=...  7.89 us
    ppermute x10, waiting for transfers between devices, exchange(): return lax.ppermute(values, GROUP, pairs)  4.71 us
  transfers between devices with their start and end apart: 10, of which 6 were waited for; matrix products, arithmetic and copies ran while one was open for 0% of the time, Pallas kernels for 18%

profile of v6, /device:TPU:0, one launch (start us, length us, event | category | flops | bytes accessed | tf_op | source)
XLA Modules:
  0.0 26.1 jit_solution(15025676164265427538)
XLA Ops:
  0.6 1.8 %pack.1 = (f32[104,128]{1,0:T(8,128)S(1)}, f32[64,128]{1,0:T(8,128)S(1)}, s32[1,256]{1,0:T(1,128)S(1)}, f32[1,256]{1,0:T(1,128)S(1)}, f32[4,24,16,128]{3,2,1,0:T...) custom-call(f32[4,24,16,128]{3,2,1,0:T(8,128)} %refs_0_.1, ...), custom_call_target="tpu_custom_call" | custom-call | flops 100000 | bytes 2868256 | tf_op jit(solution)/shard_map/pack/pallas_call | solution.py:22
  2.4 0.0 copy-start
  2.5 2.4 %collective-permute-start = (f32[104,128]{1,0:T(8,128)S(1)}, f32[104,128]{1,0:T(8,128)S(1)}, u32[]{:S(2)}, u32[]{:S(2)}) collective-permute-start(f32[104,128]{1,0:T(8,128)S(1)} %get-tuple-element.53.y_sent.refs_12_.refs_11_), channel_id=1, source_target_pairs={{0,3},{1,2},{2,1},{3,0},{4,7},{5,6},{6,5},{7,4},{8,11},{9,10},{10,... | collective-permute-start | bytes 159752 | tf_op jit(solution)/shard_map/ppermute | solution.py:907
  4.9 0.3 %rows.1 = (f32[160,128]{1,0:T(8,128)S(1)}, f32[160,128]{1,0:T(8,128)S(1)}, f32[16,128]{1,0:T(8,128)S(1)}) custom-call(f32[4,24,16,128]{3,2,1,0:T(8,128)S(1)} %get-tuple-element.88.tracer.refs_0_, f32[24,16,128]{2,1,0:T(8,128)S(1)} %get-tuple-element.49.west.refs_1_, f32[16,128]{1,0:T(8,128)S(1)} %get-tuple-element.50.scale.refs_11_, ...), custom_call_target="tpu_custom_call" | custom-call | flops 100000 | bytes 1196032 | tf_op jit(solution)/shard_map/rows/pallas_call | solution.py:22
  5.2 0.0 copy-done
  5.2 0.7 %factor.1 = (f32[24,16,128]{2,1,0:T(8,128)S(1)}, f32[24,16,128]{2,1,0:T(8,128)S(1)}, f32[24,16,128]{2,1,0:T(8,128)S(1)}, f32[4,16,128]{2,1,0:T(8,128)S(1)}, f32[...) custom-call(f32[4,24,16,128]{3,2,1,0:T(8,128)S(1)} %get-tuple-elemen, ...), custom_call_target="tpu_custom_call" | custom-call | flops 3000000 | bytes 4129792 | tf_op jit(solution)/shard_map/factor/pallas_call | solution.py:22
  5.9 1.2 %collective-permute-done.y_got.refs_13_.refs_14_.refs_12_ = f32[104,128]{1,0:T(8,128)S(1)} collective-permute-done((f32[104,128]{1,0:T(8,128)S(1)}, f32[104,128]{1,0:T(8,128)S(1)}, u32[]{:S(2)}, u32[]{:S(2)}) %collective-permute-start) | collective-permute-done | bytes 53280 | tf_op jit(solution)/shard_map/ppermute | solution.py:907
  7.1 2.6 %collective-permute-start.1 = (f32[160,128]{1,0:T(8,128)S(1)}, f32[160,128]{1,0:T(8,128)S(1)}, u32[]{:S(2)}, u32[]{:S(2)}) collective-permute-start(f32[160,128]{1,0:T(8,128)S(1)} %relay.2.refs_10_.refs_5_), channel_id=1, source_target_pairs={{0,4},{1,5},{2,6},{3,7},{4,8},{5,9},{6,10},{7,11},{8,12},{9,13},{1... | collective-permute-start | bytes 245768 | tf_op jit(solution)/shard_map/ppermute | solution.py:907
  9.7 2.1 %collective-permute-start.2 = (f32[160,128]{1,0:T(8,128)S(1)}, f32[160,128]{1,0:T(8,128)S(1)}, u32[]{:S(2)}, u32[]{:S(2)}) collective-permute-start(f32[160,128]{1,0:T(8,128)S(1)} %relay.3.refs_11_.refs_6_), channel_id=1, source_target_pairs={{0,12},{1,13},{2,14},{3,15},{4,0},{5,1},{6,2},{7,3},{8,4},{9,5},{1... | collective-permute-start | bytes 245768 | tf_op jit(solution)/shard_map/ppermute | solution.py:907
  11.8 0.0 collective-permute-start.4
  11.8 1.1 %collective-permute-start.3 = (f32[32,128]{1,0:T(8,128)S(1)}, f32[32,128]{1,0:T(8,128)S(1)}, u32[]{:S(2)}, u32[]{:S(2)}) collective-permute-start(f32[32,128]{1,0:T(8,128)S(1)} %beyond.1), channel_id=1, source_target_pairs={{0,9},{1,8},{2,11},{3,10},{4,13},{5,12},{6,15},{7,14},{8,1},{9,0},... | collective-permute-start | bytes 49160 | tf_op jit(solution)/shard_map/ppermute | solution.py:907
  12.9 0.1 collective-permute-done.4.base_other.refs_6_
  13.0 0.4 %rim.1 = (f32[24,128]{1,0:T(8,128)S(1)}, f32[24,128]{1,0:T(8,128)S(1)}, f32[24,128]{1,0:T(8,128)S(1)}, f32[6,24,128]{2,1,0:T(8,128)S(1)}, f32[24,256]{1,0:T(8,12...) custom-call(f32[104,128]{1,0:T(8,128)S(1)} %get-tuple-element.53.y_s, ...), custom_call_target="tpu_custom_call" | custom-call | flops 400000 | bytes 480256 | tf_op jit(solution)/shard_map/rim/pallas_call | solution.py:22
  13.4 1.7 %collective-permute-start.6 = (f32[32,128]{1,0:T(8,128)S(1)}, f32[32,128]{1,0:T(8,128)S(1)}, u32[]{:S(2)}, u32[]{:S(2)}) collective-permute-start(f32[32,128]{1,0:T(8,128)S(1)} %get-tuple-element.81), channel_id=1, source_target_pairs={{0,2},{1,3},{2,0},{3,1},{4,6},{5,7},{6,4},{7,5},{8,10},{9,11},{10,... | collective-permute-start | bytes 49160 | tf_op jit(solution)/shard_map/ppermute | solution.py:907
  15.2 1.6 %collective-permute-done.3.refs_15_ = f32[32,128]{1,0:T(8,128)S(1)} collective-permute-done((f32[32,128]{1,0:T(8,128)S(1)}, f32[32,128]{1,0:T(8,128)S(1)}, u32[]{:S(2)}, u32[]{:S(2)}) %collective-permute-start.3) | collective-permute-done | bytes 16416 | tf_op jit(solution)/shard_map/ppermute | solution.py:907
  16.8 0.0 collective-permute-done.1.refs_0_.refs_12_.refs_7_
  16.8 0.0 collective-permute-done.2.refs_1_.refs_13_.refs_8_
  16.8 0.6 %observe.1 = (f32[8,128]{1,0:T(8,128)S(1)}, f32[4,256]{1,0:T(4,128)S(1)}) custom-call(f32[160,128]{1,0:T(8,128)S(1)} %collective-permute-done.1.refs_0_.refs_12_.refs_7_, f32[160,128]{1,0:T(8,128)S(1)} %collective-permute-done.2.refs_1_.refs_13_.refs_8_, f32[24,16,128]{2,1,0:T(8,128)S(1)} %get-tuple-element.61.refs_2_, ...), custom_call_target="tpu_custom_call" | custom-call | flops 2000000 | bytes 1734656 | tf_op jit(solution)/shard_map/observe/pallas_call | solution.py:22
  17.4 0.2 collective-permute-start.5
  17.6 0.0 collective-permute-done.6.refs_8_.refs_10_
  17.6 1.0 %collective-permute-done.5.refs_1_ = f32[8,128]{1,0:T(8,128)S(1)} collective-permute-done((f32[8,128]{1,0:T(8,128)S(1)}, f32[8,128]{1,0:T(8,128)S(1)}, u32[]{:S(2)}, u32[]{:S(2)}) %collective-permute-start.5) | collective-permute-done | bytes 4128 | tf_op jit(solution)/shard_map/ppermute | solution.py:907
  18.7 0.3 %weigh.1 = (f32[24,128]{1,0:T(8,128)S(1)}, f32[24,128]{1,0:T(8,128)S(1)}, f32[48,128]{1,0:T(8,128)S(1)}) custom-call(f32[8,128]{1,0:T(8,128)S(1)} %get-tuple-element.80.refs_0_, f32[8,128]{1,0:T(8,128)S(1)} %collective-permute-done.5.refs_1_, f32[4,256]{1,0:T(4,128)S(1)} %get-tuple-element.83.refs_2_, f32[16,256]{1,0:T(8,128)S(1)} %get-tuple-element.66.refs_7_.refs_3_, ...), custom_call_target="tpu_custom_call" | custom-call | flops 500000 | bytes 548864 | tf_op jit(solution)/shard_map/weigh/pallas_call | solution.py:22
  19.0 1.7 %collective-permute-start.8 = (f32[48,128]{1,0:T(8,128)S(1)}, f32[48,128]{1,0:T(8,128)S(1)}, u32[]{:S(2)}, u32[]{:S(2)}) collective-permute-start(f32[48,128]{1,0:T(8,128)S(1)} %get-tuple-element.87), channel_id=1, source_target_pairs={{0,13},{1,8},{2,15},{3,10},{4,9},{5,12},{6,11},{7,14},{8,5},{9,0},... | collective-permute-start | bytes 73736 | tf_op jit(solution)/shard_map/ppermute | solution.py:907
  20.7 0.5 %collective-permute-start.7 = (f32[24,128]{1,0:T(8,128)S(1)}, f32[24,128]{1,0:T(8,128)S(1)}, u32[]{:S(2)}, u32[]{:S(2)}) collective-permute-start(f32[24,128]{1,0:T(8,128)S(1)} %get-tuple-element.86), channel_id=1, source_target_pairs={{0,5},{1,4},{2,7},{3,6},{4,1},{5,0},{6,3},{7,2},{8,13},{9,12},{10,... | collective-permute-start | bytes 36872 | tf_op jit(solution)/shard_map/ppermute | solution.py:907
  21.2 0.0 copy-start.1
  21.3 0.0 copy-start.2
  21.3 2.1 %advance.1 = f32[4,24,16,128]{3,2,1,0:T(8,128)} custom-call(f32[4,24,16,128]{3,2,1,0:T(8,128)S(1)} %get-tuple-element.88.tracer.refs_0_, f32[5,24,16,128]{3,2,1,0:T(8,128)S(1)} %get-tuple-element.89.refs_1_, f32[24,16,128]{2,1,0:T(8,128)S(1)} %get-tuple-element.62.refs_3_.refs_2_, f32[24,16,128]{2,1,0:T(8,128)S(1)} %get-tuple-element.63.refs_4_.refs_3_, ...), custom_call_target="tpu_custom_call" | custom-call | flops 6000000 | bytes 3604480 | tf_op jit(solution)/shard_map/advance/pallas_call | solution.py:22
  23.3 0.5 %collective-permute-done.7.refs_3_ = f32[24,128]{1,0:T(8,128)S(1)} collective-permute-done((f32[24,128]{1,0:T(8,128)S(1)}, f32[24,128]{1,0:T(8,128)S(1)}, u32[]{:S(2)}, u32[]{:S(2)}) %collective-permute-start.7) | collective-permute-done | bytes 12320 | tf_op jit(solution)/shard_map/ppermute | solution.py:907
  23.9 0.0 collective-permute-done.8.refs_4_
  23.9 0.4 %collective-permute-start.9 = (f32[48,128]{1,0:T(8,128)S(1)}, f32[48,128]{1,0:T(8,128)S(1)}, u32[]{:S(2)}, u32[]{:S(2)}) collective-permute-start(f32[48,128]{1,0:T(8,128)S(1)} %collective-permute-done.8.refs_4_), channel_id=1, source_target_pairs={{0,1},{1,0},{2,3},{3,2},{4,5},{5,4},{6,7},{7,6},{8,9},{9,8},{10,11... | collective-permute-start | bytes 73736 | tf_op jit(solution)/shard_map/ppermute | solution.py:907
  24.3 0.0 copy-done.1
  24.3 0.0 copy-done.2
  24.3 0.6 %regrid.2.refs_3_ = f32[4,128]{1,0:T(4,128)S(1)} custom-call(s32[16,128]{1,0:T(8,128)S(1)} %bitcast.14, f32[16,128]{1,0:T(8,128)S(1)} %bitcast.16, f32[24,128]{1,0:T(8,128)S(1)} %get-tuple-element.92.refs_2_, f32[24,128]{1,0:T(8,128)S(1)} %collective-permute-done.7.refs_3_, f32[48,128]{1,0:T(8,128)S(1)} %collective-permute-done.8.refs_4_), custom_call_target="tpu_custom_call" | custom-call | flops 1000000 | bytes 67584 | tf_op jit(solution)/shard_map/regrid/pallas_call | solution.py:22
  24.9 0.2 collective-permute-done.9.refs_2_
  25.1 1.0 %regrid.3 = f32[4,128]{1,0:T(4,128)} custom-call(s32[16,128]{1,0:T(8,128)S(1)} %bitcast.15, f32[16,128]{1,0:T(8,128)S(1)} %bitcast.17, f32[48,128]{1,0:T(8,128)S(1)} %collective-permute-done.9.refs_2_, f32[4,128]{1,0:T(4,128)S(1)} %regrid.2.refs_3_), custom_call_target="tpu_custom_call" | custom-call | flops 1000000 | bytes 45056 | tf_op jit(solution)/shard_map/regrid/pallas_call | solution.py:22
  (4 shorter events, 0.0 us)
Async XLA Ops:
  2.4 2.8 %copy-start = (f32[4,24,16,128]{3,2,1,0:T(8,128)S(1)}, f32[4,24,16,128]{3,2,1,0:T(8,128)}, u32[]{:S(2)}) copy-start(f32[4,24,16,128]{3,2,1,0:T(8,128)} %refs_4_.1) | copy-start | bytes 2359300
  2.5 4.7 %collective-permute-start = (f32[104,128]{1,0:T(8,128)S(1)}, f32[104,128]{1,0:T(8,128)S(1)}, u32[]{:S(2)}, u32[]{:S(2)}) collective-permute-start(f32[104,128]{1,0:T(8,128)S(1)} %get-tuple-element.53.y_sent.refs_12_.refs_11_), channel_id=1, source_target_pairs={{0,3},{1,2},{2,1},{3,0},{4,7},{5,6},{6,5},{7,4},{8,11},{9,10},{10,... | collective-permute-start | bytes 159752 | tf_op jit(solution)/shard_map/ppermute | solution.py:907
  7.1 9.7 %collective-permute-start.1 = (f32[160,128]{1,0:T(8,128)S(1)}, f32[160,128]{1,0:T(8,128)S(1)}, u32[]{:S(2)}, u32[]{:S(2)}) collective-permute-start(f32[160,128]{1,0:T(8,128)S(1)} %relay.2.refs_10_.refs_5_), channel_id=1, source_target_pairs={{0,4},{1,5},{2,6},{3,7},{4,8},{5,9},{6,10},{7,11},{8,12},{9,13},{1... | collective-permute-start | bytes 245768 | tf_op jit(solution)/shard_map/ppermute | solution.py:907
  9.7 7.1 %collective-permute-start.2 = (f32[160,128]{1,0:T(8,128)S(1)}, f32[160,128]{1,0:T(8,128)S(1)}, u32[]{:S(2)}, u32[]{:S(2)}) collective-permute-start(f32[160,128]{1,0:T(8,128)S(1)} %relay.3.refs_11_.refs_6_), channel_id=1, source_target_pairs={{0,12},{1,13},{2,14},{3,15},{4,0},{5,1},{6,2},{7,3},{8,4},{9,5},{1... | collective-permute-start | bytes 245768 | tf_op jit(solution)/shard_map/ppermute | solution.py:907
  11.8 1.2 %collective-permute-start.4 = (f32[4,16,128]{2,1,0:T(8,128)S(1)}, f32[4,16,128]{2,1,0:T(8,128)S(1)}, u32[]{:S(2)}, u32[]{:S(2)}) collective-permute-start(f32[4,16,128]{2,1,0:T(8,128)S(1)} %get-tuple-element.70.base.refs_5_), channel_id=1, source_target_pairs={{0,1},{1,0},{2,3},{3,2},{4,5},{5,4},{6,7},{7,6},{8,9},{9,8},{10,11... | collective-permute-start | bytes 98312 | tf_op jit(solution)/shard_map/ppermute | solution.py:907
  11.8 5.0 %collective-permute-start.3 = (f32[32,128]{1,0:T(8,128)S(1)}, f32[32,128]{1,0:T(8,128)S(1)}, u32[]{:S(2)}, u32[]{:S(2)}) collective-permute-start(f32[32,128]{1,0:T(8,128)S(1)} %beyond.1), channel_id=1, source_target_pairs={{0,9},{1,8},{2,11},{3,10},{4,13},{5,12},{6,15},{7,14},{8,1},{9,0},... | collective-permute-start | bytes 49160 | tf_op jit(solution)/shard_map/ppermute | solution.py:907
  13.4 4.2 %collective-permute-start.6 = (f32[32,128]{1,0:T(8,128)S(1)}, f32[32,128]{1,0:T(8,128)S(1)}, u32[]{:S(2)}, u32[]{:S(2)}) collective-permute-start(f32[32,128]{1,0:T(8,128)S(1)} %get-tuple-element.81), channel_id=1, source_target_pairs={{0,2},{1,3},{2,0},{3,1},{4,6},{5,7},{6,4},{7,5},{8,10},{9,11},{10,... | collective-permute-start | bytes 49160 | tf_op jit(solution)/shard_map/ppermute | solution.py:907
  17.4 1.2 %collective-permute-start.5 = (f32[8,128]{1,0:T(8,128)S(1)}, f32[8,128]{1,0:T(8,128)S(1)}, u32[]{:S(2)}, u32[]{:S(2)}) collective-permute-start(f32[8,128]{1,0:T(8,128)S(1)} %get-tuple-element.80.refs_0_), channel_id=1, source_target_pairs={{0,1},{1,0},{2,3},{3,2},{4,5},{5,4},{6,7},{7,6},{8,9},{9,8},{10,11... | collective-permute-start | bytes 12296 | tf_op jit(solution)/shard_map/ppermute | solution.py:907
  19.0 4.9 %collective-permute-start.8 = (f32[48,128]{1,0:T(8,128)S(1)}, f32[48,128]{1,0:T(8,128)S(1)}, u32[]{:S(2)}, u32[]{:S(2)}) collective-permute-start(f32[48,128]{1,0:T(8,128)S(1)} %get-tuple-element.87), channel_id=1, source_target_pairs={{0,13},{1,8},{2,15},{3,10},{4,9},{5,12},{6,11},{7,14},{8,5},{9,0},... | collective-permute-start | bytes 73736 | tf_op jit(solution)/shard_map/ppermute | solution.py:907
  20.7 3.1 %collective-permute-start.7 = (f32[24,128]{1,0:T(8,128)S(1)}, f32[24,128]{1,0:T(8,128)S(1)}, u32[]{:S(2)}, u32[]{:S(2)}) collective-permute-start(f32[24,128]{1,0:T(8,128)S(1)} %get-tuple-element.86), channel_id=1, source_target_pairs={{0,5},{1,4},{2,7},{3,6},{4,1},{5,0},{6,3},{7,2},{8,13},{9,12},{10,... | collective-permute-start | bytes 36872 | tf_op jit(solution)/shard_map/ppermute | solution.py:907
  21.2 3.0 %copy-start.1 = (s32[1,1,16,128]{3,2,1,0:T(8,128)S(1)}, s32[1,1,16,128]{3,2,1,0:T(8,128)}, u32[]{:S(2)}) copy-start(s32[1,1,16,128]{3,2,1,0:T(8,128)} %param.24) | copy-start | bytes 24580
  21.3 3.0 %copy-start.2 = (f32[1,1,16,128]{3,2,1,0:T(8,128)S(1)}, f32[1,1,16,128]{3,2,1,0:T(8,128)}, u32[]{:S(2)}) copy-start(f32[1,1,16,128]{3,2,1,0:T(8,128)} %param.25) | copy-start | bytes 24580
  23.9 1.3 %collective-permute-start.9 = (f32[48,128]{1,0:T(8,128)S(1)}, f32[48,128]{1,0:T(8,128)S(1)}, u32[]{:S(2)}, u32[]{:S(2)}) collective-permute-start(f32[48,128]{1,0:T(8,128)S(1)} %collective-permute-done.8.refs_4_), channel_id=1, source_target_pairs={{0,1},{1,0},{2,3},{3,2},{4,5},{5,4},{6,7},{7,6},{8,9},{9,8},{10,11... | collective-permute-start | bytes 73736 | tf_op jit(solution)/shard_map/ppermute | solution.py:907

commit v7 on v6

--- a/solution.py
+++ b/solution.py
@@ -436,25 +436,59 @@
     return seam(number, sent, got, *faces)
 
 
+def block_groups(blocks, cap):
+    per_tile = LANES // cap
+    group_of_lane = lax.div(iota((8, LANES), 1), cap)
+    groups = []
+    for group in range(per_tile):
+        tiles = []
+        for start in range(0, len(blocks), per_tile):
+            tile = jnp.zeros((8, LANES), F32)
+            for a in range(per_tile):
+                moved = pltpu.roll(blocks[start + a], (cap * (a - group)) % LANES, 1)
+                tile = jnp.where(group_of_lane == a, moved, tile)
+            tiles.append(tile)
+        groups.append(jnp.concatenate(tiles, axis=1))
+    return groups
+
+
+def relayed_blocks(plan, head, cx, own, y_got, got, x_got):
+    start = plan["y_tiles"] * cx
+
+    def block_at(ref, row):
+        return ref[row : row + 8, :]
+
+    blocks = {0: block_at(own, 0), 1: block_at(y_got, start + 8)}
+    rim_blocks = {0: block_at(y_got, start), 1: block_at(own, 8)}
+    even_x = is_even("facex")
+    from_west, from_east = (got[n][head + 8 : head + 40, :] for n in range(2))
+    carriers = [
+        (plan["x_blocks"][0], jnp.where(even_x, from_east, from_west)),
+        (plan["x_blocks"][1], jnp.where(even_x, from_west, from_east)),
+    ]
+    carriers += [(offset, ref[...]) for offset, ref in zip(plan["x_ops"], x_got)]
+    for offset, values in carriers:
+        blocks[offset], rim_blocks[offset + 1] = block_at(values, 0), block_at(values, 8)
+        rim_blocks[offset], blocks[offset + 1] = block_at(values, 16), block_at(values, 24)
+    return blocks, rim_blocks
+
+
 def observe_kernel(sizes, plan, carried, *refs):
     refs = list(refs)
     got = refs[0:2]
-    inner, lower, inverse, ratio, columns, in_row, in_lane, live = refs[2:10]
-    sent = refs[10:12]
-    refs = refs[12:]
+    inner, lower, inverse, ratio, in_row, in_lane = refs[2:8]
+    sent = refs[8:10]
+    refs = refs[10:]
     y_sent = refs[: plan["y_ops"]]
     y_got = refs[plan["y_ops"] : 2 * plan["y_ops"]]
     refs = refs[2 * plan["y_ops"] :]
-    own = refs[0]
-    n_pairs = len(plan["pairs"])
-    pair_got = refs[1 : 1 + n_pairs]
-    swapped = refs[1 + n_pairs] if n_pairs else None
     if plan["relay"]:
-        x_got = refs[1 : 1 + len(plan["x_ops"])]
-        refs = refs[1 + len(plan["x_ops"]) :]
-        rim = refs[:8]
-        parcel, state_out, turn, rise = refs[8:]
+        rim_inverse, rim_ratio, rim_lower, pieces, rim_picks, parcel, turn, rise = refs
     else:
+        columns, live, own, *refs = refs
+        n_pairs = len(plan["pairs"])
+        pair_got = refs[:n_pairs]
+        swapped = refs[n_pairs] if n_pairs else None
         modeled_out, state_out = refs[-2:]
     levels, cx, cy = inner.shape
     slots = in_row.shape[1]
@@ -507,70 +541,40 @@
     picked = jnp.dot(high, picks, preferred_element_type=F32)
     picked = picked + jnp.dot(low, picks, preferred_element_type=F32)
 
-    start = plan["y_tiles"] * cx
-    if plan["relay"]:
-
-        def block_at(ref, row):
-            return ref[row : row + 8, :]
-
-        blocks = {0: block_at(own, 0), 1: block_at(y_got[0], start + 8)}
-        rim_blocks = {0: block_at(y_got[0], start), 1: block_at(own, 8)}
-        even_x = is_even("facex")
-        from_west, from_east = (got[n][head + 8 : head + 40, :] for n in range(2))
-        carriers = [
-            (plan["x_blocks"][0], jnp.where(even_x, from_east, from_west), 0),
-            (plan["x_blocks"][1], jnp.where(even_x, from_west, from_east), 0),
-        ]
-        carriers += [(offset, ref, 0) for offset, ref in zip(plan["x_ops"], x_got)]
-        for offset, ref, row in carriers:
-            blocks[offset], rim_blocks[offset + 1] = block_at(ref, row), block_at(ref, row + 8)
-            rim_blocks[offset], blocks[offset + 1] = block_at(ref, row + 16), block_at(ref, row + 24)
-    else:
+    if not plan["relay"]:
+        start = plan["y_tiles"] * cx
         blocks = {0: own[0:8, :], plan["y_blocks"][0]: y_got[0][start : start + 8, :]}
         for number in range(2):
             offset = plan["x_blocks"][number]
             if offset:
                 blocks[offset] = got[number][head + 8 : head + 16, :]
-    first_core = lax.axis_index("lev") == 0
-    for number, (for_first, for_second) in enumerate(plan["pairs"]):
-        mine = pair_got[number][...]
-        other = swapped[8 * number : 8 * number + 8, :]
-        if for_first == for_second:
-            blocks[for_first] = mine
-        else:
-            blocks[for_first] = jnp.where(first_core, mine, other)
-            blocks[for_second] = jnp.where(first_core, other, mine)
-    cap = slots // len(blocks)
-    per_tile = LANES // cap
-    group_of_lane = lax.div(iota((8, LANES), 1), cap)
-
-    def gathered(group, blocks):
-        tiles = []
-        for start in range(0, len(blocks), per_tile):
-            tile = jnp.zeros((8, LANES), F32)
-            for a in range(per_tile):
-                moved = pltpu.roll(blocks[start + a], (cap * (a - group)) % LANES, 1)
-                tile = jnp.where(group_of_lane == a, moved, tile)
-            tiles.append(tile)
-        return jnp.concatenate(tiles, axis=1)
-
-    groups = [gathered(g, blocks) for g in range(levels // 8)]
-    last = gathered(levels // 8, blocks)
-    total = jnp.zeros((cx, slots), F32)
-    sensitivity = jnp.zeros((8, slots), F32)
-    for g, kernel in enumerate(groups):
-        sensitivity = sensitivity + kernel * columns[8 * g : 8 * g + 8, :]
-        for l in range(8):
-            level = 8 * g + l
-            total = total + kernel[l : l + 1] * picked[level * cx : (level + 1) * cx]
-    modeled = jnp.sum(total * in_row[...], axis=0, keepdims=True)
-    gain = jnp.sum(sensitivity, axis=0, keepdims=True) * last[1:2] * live[...]
-    if not plan["relay"]:
-        modeled_out[...] = modeled
+        first_core = lax.axis_index("lev") == 0
+        for number, (for_first, for_second) in enumerate(plan["pairs"]):
+            mine = pair_got[number][...]
+            other = swapped[8 * number : 8 * number + 8, :]
+            if for_first == for_second:
+                blocks[for_first] = mine
+            else:
+                blocks[for_first] = jnp.where(first_core, mine, other)
+                blocks[for_second] = jnp.where(first_core, other, mine)
+        *groups, last = block_groups(blocks, slots // len(blocks))
+        total = jnp.zeros((cx, slots), F32)
+        sensitivity = jnp.zeros((8, slots), F32)
+        for g, kernel in enumerate(groups):
+            sensitivity = sensitivity + kernel * columns[8 * g : 8 * g + 8, :]
+            for l in range(8):
+                level = 8 * g + l
+                total = total + kernel[l : l + 1] * picked[level * cx : (level + 1) * cx]
+        modeled_out[...] = jnp.sum(total * in_row[...], axis=0, keepdims=True)
+        gain = jnp.sum(sensitivity, axis=0, keepdims=True) * last[1:2] * live[...]
         state_out[...] = jnp.concatenate([gain, last[0:1]], axis=0)
         return
 
-    rim_inverse, rim_ratio, rim_lower, pieces, rim_columns, rim_rows, rim_picks, rim_live = rim
+    chosen = in_row[...]
+    for level in range(levels):
+        part = picked[level * cx : (level + 1) * cx] * chosen
+        parcel[level : level + 1, :] = jnp.sum(part, axis=0, keepdims=True)
+
     corners_west, corners_east = sides(plan, got[0][head + 1 : head + 2, :], got[1][head + 1 : head + 2, :])
     turn[...] = jnp.zeros((LANES, LANES), F32)
     turn[0:1, :] = corners_west
@@ -602,21 +606,7 @@
     picks = rim_picks[...]
     picked = jnp.dot(high, picks, preferred_element_type=F32)
     picked = picked + jnp.dot(low, picks, preferred_element_type=F32)
-    rim_total = jnp.zeros((8, slots), F32)
-    sensitivity = jnp.zeros((8, slots), F32)
-    for g in range(levels // 8):
-        kernel = gathered(g, rim_blocks)
-        rim_total = rim_total + kernel * picked[8 * g : 8 * g + 8]
-        sensitivity = sensitivity + kernel * rim_columns[8 * g : 8 * g + 8, :]
-    rim_modeled = jnp.sum(rim_total, axis=0, keepdims=True)
-    rim_last = gathered(levels // 8, rim_blocks)
-    rim_gain = jnp.sum(sensitivity, axis=0, keepdims=True) * rim_last[1:2] * rim_live[...]
-    state_out[...] = jnp.concatenate([gain, last[0:1], rim_gain, rim_last[0:1]], axis=0)
-    strips = slots // LANES
-    for number in range(strips):
-        part = slice(number * LANES, (number + 1) * LANES)
-        parcel[number : number + 1, :] = modeled[:, part]
-        parcel[strips + number : strips + number + 1, :] = rim_modeled[:, part]
+    parcel[levels : 2 * levels, :] = picked
 
 
 def advance_cells(cells, west, east, south, north, face_w, face_e, face_s, face_n):
@@ -671,21 +661,31 @@
 
 
 def weigh_kernel(sizes, plan, carried, levels, *refs):
-    parcel, other, state, in_row, in_lane, base, base_other, rim_rows, rim_base = refs[:9]
+    parcel, other, columns, live, rim_columns, rim_live, own, *refs = refs
+    x_got, refs = refs[: len(plan["x_ops"])], refs[len(plan["x_ops"]) :]
+    in_row, in_lane, base, base_other, rim_rows, rim_base = refs[:6]
     cx, cy = base.shape[1:]
-    strips = state.shape[1] // LANES
-
-    def misfit(kind):
-        both = parcel[kind * strips : (kind + 1) * strips, :] + other[kind * strips : (kind + 1) * strips, :]
-        flat = jnp.concatenate([both[n : n + 1] for n in range(strips)], axis=1)
-        return state[2 * kind : 2 * kind + 1, :] * (flat - state[2 * kind + 1 : 2 * kind + 2, :])
-
-    scattered = scatter(misfit(0), in_row[...], in_lane[...])
-    on_rim = jnp.sum(rim_rows[...] * misfit(1), axis=1, keepdims=True)
+    slots = live.shape[1]
+
+    def force(blocks, start, weights, used):
+        *groups, last = block_groups(blocks, slots // len(blocks))
+        seen = jnp.zeros((8, slots), F32)
+        sensitivity = jnp.zeros((8, slots), F32)
+        for g, kernel in enumerate(groups):
+            part = slice(start + 8 * g, start + 8 * g + 8)
+            seen = seen + kernel * (parcel[part, :] + other[part, :])
+            sensitivity = sensitivity + kernel * weights[8 * g : 8 * g + 8, :]
+        modeled = jnp.sum(seen, axis=0, keepdims=True)
+        gain = jnp.sum(sensitivity, axis=0, keepdims=True) * last[1:2] * used[...]
+        return gain * (modeled - last[0:1])
+
+    blocks, rim_blocks = relayed_blocks(plan, (carried + 1) * levels, cx, own, refs[11], refs[9:11], x_got)
+    scattered = scatter(force(blocks, 0, columns, live), in_row[...], in_lane[...])
+    on_rim = jnp.sum(rim_rows[...] * force(rim_blocks, levels, rim_columns, rim_live), axis=1, keepdims=True)
     near = [scattered + base[t] for t in range(carried)]
     near += [scattered + base_other[t] for t in range(carried)]
     rims = [[rim_base[0:cx, :] + on_rim] for _ in near]
-    spread_surface(sizes, plan, carried, levels, near, rims, refs[9:12], refs[12:14], refs[14:15], refs[15:])
+    spread_surface(sizes, plan, carried, levels, near, rims, refs[6:9], refs[9:11], refs[11:12], refs[12:])
 
 
 def spread_surface(sizes, plan, carried, levels, near, rim_values, fields, got, y_got, outs):
@@ -1124,19 +1124,19 @@
         )
         *rim, rim_sent = rim
         rim_got = exchange(rim_sent, sizes, next_y(0, 0))
-        parcel, state = observe(
-            [shape(plan["parcel"], cy), shape(4, slots)],
-            [*rows_got, inner, lower, inverse, ratio, columns, in_row, in_lane, live, *rows_sent]
-            + [*lanes_sent, *lanes_got, own_blocks, *x_got, *rim],
+        (parcel,) = observe(
+            [shape(2 * levels, slots)],
+            [*rows_got, inner, lower, inverse, ratio, in_row, in_lane, *rows_sent, *lanes_sent, *lanes_got]
+            + [*rim[:4], rim[6]],
             scratch=[pltpu.VMEM((LANES, LANES), F32), pltpu.VMEM((levels, LANES), F32)],
         )
         parcel_other = other_core(parcel)
-        parcel_other, rim_got = lax.optimization_barrier((parcel_other, rim_got))
+        parcel_other, rim_got, *x_got = lax.optimization_barrier((parcel_other, rim_got, *x_got))
         band_sent = call(
             functools.partial(weigh_kernel, sizes, plan, carried, levels),
             band_shapes,
-            [parcel, parcel_other, state, in_row, in_lane, base, base_other, rim[5], rim_got, *fields]
-            + [*rows_got, *lanes_got],
+            [parcel, parcel_other, columns, live, rim[4], rim[7], own_blocks, *x_got, in_row, in_lane]
+            + [base, base_other, rim[5], rim_got, *fields, *rows_got, *lanes_got],
             "weigh",
             500000,
         )
@@ -1148,8 +1148,8 @@
         base_other = other_core(base)
         modeled, state = observe(
             [shape(1, slots), shape(2, slots)],
-            [*rows_got, inner, lower, inverse, ratio, columns, in_row, in_lane, live, *rows_sent]
-            + [*lanes_sent, *lanes_got, own_blocks, *pair_got]
+            [*rows_got, inner, lower, inverse, ratio, in_row, in_lane, *rows_sent, *lanes_sent, *lanes_got]
+            + [columns, live, own_blocks, *pair_got]
             + [other_core(jnp.concatenate(pair_got, axis=0))],
         )
         near, *rims_sent = call(

time: 26.2 us -> 25.9 us (0.989)
  waiting for transfers between devices: 4.71 us -> 4.1 us
    ppermute x10, waiting for transfers between devices: 4.71 us -> 4.1 us  [exchange(): return lax.ppermute(values, GROUP, pairs)]
  transfers between devices with their start and end apart: 10 -> 10, of which waited for: 6 -> 8; matrix products, arithmetic and copies ran while one was open for 0% -> 0% of each run, Pallas kernels for 18% -> 18%
where the time goes in v7:
time: 25.9 us; the launch traced here: 25.8 us
  starting transfers between devices  13 us (50%)
  Pallas kernels  7.94 us (31%)
  waiting for transfers between devices  4.1 us (16%)
  between operations  0.72 us (3%)
    ppermute x10, starting transfers between devices, exchange(): return lax.ppermute(values, GROUP, pairs)  13 us
    pallas_call x12, Pallas kernels, call(): pl.pallas_call(body, out_shape=outs, in_specs=[pl.BlockSpec(memory_space=...  7.94 us
    ppermute x10, waiting for transfers between devices, exchange(): return lax.ppermute(values, GROUP, pairs)  4.1 us
  transfers between devices with their start and end apart: 10, of which 8 were waited for; matrix products, arithmetic and copies ran while one was open for 0% of the time, Pallas kernels for 18%

profile of v7, /device:TPU:0, one launch (start us, length us, event | category | flops | bytes accessed | tf_op | source)
XLA Modules:
  0.0 25.8 jit_solution(4324499302122649351)
XLA Ops:
  0.6 1.8 %pack.1 = (f32[104,128]{1,0:T(8,128)S(1)}, f32[64,128]{1,0:T(8,128)S(1)}, s32[1,256]{1,0:T(1,128)S(1)}, f32[1,256]{1,0:T(1,128)S(1)}, f32[4,24,16,128]{3,2,1,0:T...) custom-call(f32[4,24,16,128]{3,2,1,0:T(8,128)} %refs_0_.1, ...), custom_call_target="tpu_custom_call" | custom-call | flops 100000 | bytes 2868256 | tf_op jit(solution)/shard_map/pack/pallas_call | solution.py:22
  2.4 0.0 copy-start
  2.5 2.4 %collective-permute-start = (f32[104,128]{1,0:T(8,128)S(1)}, f32[104,128]{1,0:T(8,128)S(1)}, u32[]{:S(2)}, u32[]{:S(2)}) collective-permute-start(f32[104,128]{1,0:T(8,128)S(1)} %get-tuple-element.52.y_sent.refs_10_.refs_11_), channel_id=1, source_target_pairs={{0,3},{1,2},{2,1},{3,0},{4,7},{5,6},{6,5},{7,4},{8,11},{9,10},{10,... | collective-permute-start | bytes 159752 | tf_op jit(solution)/shard_map/ppermute | solution.py:907
  4.9 0.3 %rows.1 = (f32[160,128]{1,0:T(8,128)S(1)}, f32[160,128]{1,0:T(8,128)S(1)}, f32[16,128]{1,0:T(8,128)S(1)}) custom-call(f32[4,24,16,128]{3,2,1,0:T(8,128)S(1)} %get-tuple-element.86.tracer.refs_0_, f32[24,16,128]{2,1,0:T(8,128)S(1)} %get-tuple-element.48.west.refs_1_, f32[16,128]{1,0:T(8,128)S(1)} %get-tuple-element.49.scale.refs_16_, ...), custom_call_target="tpu_custom_call" | custom-call | flops 100000 | bytes 1196032 | tf_op jit(solution)/shard_map/rows/pallas_call | solution.py:22
  5.2 0.0 copy-done
  5.2 0.7 %factor.1 = (f32[24,16,128]{2,1,0:T(8,128)S(1)}, f32[24,16,128]{2,1,0:T(8,128)S(1)}, f32[24,16,128]{2,1,0:T(8,128)S(1)}, f32[4,16,128]{2,1,0:T(8,128)S(1)}, f32[...) custom-call(f32[4,24,16,128]{3,2,1,0:T(8,128)S(1)} %get-tuple-elemen, ...), custom_call_target="tpu_custom_call" | custom-call | flops 3000000 | bytes 4129792 | tf_op jit(solution)/shard_map/factor/pallas_call | solution.py:22
  5.9 1.2 %collective-permute-done.y_got.refs_11_.refs_19_.refs_12_ = f32[104,128]{1,0:T(8,128)S(1)} collective-permute-done((f32[104,128]{1,0:T(8,128)S(1)}, f32[104,128]{1,0:T(8,128)S(1)}, u32[]{:S(2)}, u32[]{:S(2)}) %collective-permute-start) | collective-permute-done | bytes 53280 | tf_op jit(solution)/shard_map/ppermute | solution.py:907
  7.1 2.6 %collective-permute-start.1 = (f32[160,128]{1,0:T(8,128)S(1)}, f32[160,128]{1,0:T(8,128)S(1)}, u32[]{:S(2)}, u32[]{:S(2)}) collective-permute-start(f32[160,128]{1,0:T(8,128)S(1)} %relay.2.refs_8_.refs_5_), channel_id=1, source_target_pairs={{0,4},{1,5},{2,6},{3,7},{4,8},{5,9},{6,10},{7,11},{8,12},{9,13},{1... | collective-permute-start | bytes 245768 | tf_op jit(solution)/shard_map/ppermute | solution.py:907
  9.7 2.1 %collective-permute-start.2 = (f32[160,128]{1,0:T(8,128)S(1)}, f32[160,128]{1,0:T(8,128)S(1)}, u32[]{:S(2)}, u32[]{:S(2)}) collective-permute-start(f32[160,128]{1,0:T(8,128)S(1)} %relay.3.refs_9_.refs_6_), channel_id=1, source_target_pairs={{0,12},{1,13},{2,14},{3,15},{4,0},{5,1},{6,2},{7,3},{8,4},{9,5},{1... | collective-permute-start | bytes 245768 | tf_op jit(solution)/shard_map/ppermute | solution.py:907
  11.8 0.0 collective-permute-start.3
  11.8 1.1 %collective-permute-start.6 = (f32[32,128]{1,0:T(8,128)S(1)}, f32[32,128]{1,0:T(8,128)S(1)}, u32[]{:S(2)}, u32[]{:S(2)}) collective-permute-start(f32[32,128]{1,0:T(8,128)S(1)} %beyond.1), channel_id=1, source_target_pairs={{0,9},{1,8},{2,11},{3,10},{4,13},{5,12},{6,15},{7,14},{8,1},{9,0},... | collective-permute-start | bytes 49160 | tf_op jit(solution)/shard_map/ppermute | solution.py:907
  12.9 0.1 collective-permute-done.3.base_other.refs_11_
  13.0 0.4 %rim.1 = (f32[24,128]{1,0:T(8,128)S(1)}, f32[24,128]{1,0:T(8,128)S(1)}, f32[24,128]{1,0:T(8,128)S(1)}, f32[6,24,128]{2,1,0:T(8,128)S(1)}, f32[24,256]{1,0:T(8,12...) custom-call(f32[104,128]{1,0:T(8,128)S(1)} %get-tuple-element.52.y_s, ...), custom_call_target="tpu_custom_call" | custom-call | flops 400000 | bytes 480256 | tf_op jit(solution)/shard_map/rim/pallas_call | solution.py:22
  13.4 1.7 %collective-permute-start.5 = (f32[32,128]{1,0:T(8,128)S(1)}, f32[32,128]{1,0:T(8,128)S(1)}, u32[]{:S(2)}, u32[]{:S(2)}) collective-permute-start(f32[32,128]{1,0:T(8,128)S(1)} %get-tuple-element.74), channel_id=1, source_target_pairs={{0,2},{1,3},{2,0},{3,1},{4,6},{5,7},{6,4},{7,5},{8,10},{9,11},{10,... | collective-permute-start | bytes 49160 | tf_op jit(solution)/shard_map/ppermute | solution.py:907
  15.2 0.0 collective-permute-done.1.refs_0_.refs_17_.refs_7_
  15.2 0.5 %collective-permute-done.2.refs_1_.refs_18_.refs_8_ = f32[160,128]{1,0:T(8,128)S(1)} collective-permute-done((f32[160,128]{1,0:T(8,128)S(1)}, f32[160,128]{1,0:T(8,128)S(1)}, u32[]{:S(2)}, u32[]{:S(2)}) %collective-permute-start.2) | collective-permute-done | bytes 81952 | tf_op jit(solution)/shard_map/ppermute | solution.py:907
  15.7 0.6 %observe.1.refs_0_ = f32[48,256]{1,0:T(8,128)S(1)} custom-call(f32[160,128]{1,0:T(8,128)S(1)} %collective-permute-done.1.refs_0_.refs_17_.refs_7_, f32[160,128]{1,0:T(8,128)S(1)} %collective-permute-done.2.refs_1_.refs_18_.refs_8_, f32[24,16,128]{2,1,0:T(8,128)S(1)} %get-tuple-element.60.refs_2_, f32[24,16,128]{2,1,0:T(8,128)S(1)} %get-tuple-element.61.refs_3_.refs_2_, ...), custom_call_target="tpu_custom_call" | custom-call | flops 2000000 | bytes 1658880 | tf_op jit(solution)/shard_map/observe/pallas_call | solution.py:22
  16.3 0.1 collective-permute-start.4
  16.4 0.4 %collective-permute-done.6.refs_7_ = f32[32,128]{1,0:T(8,128)S(1)} collective-permute-done((f32[32,128]{1,0:T(8,128)S(1)}, f32[32,128]{1,0:T(8,128)S(1)}, u32[]{:S(2)}, u32[]{:S(2)}) %collective-permute-start.6) | collective-permute-done | bytes 16416 | tf_op jit(solution)/shard_map/ppermute | solution.py:907
  16.8 0.4 %collective-permute-done.5.refs_13_.refs_10_ = f32[32,128]{1,0:T(8,128)S(1)} collective-permute-done((f32[32,128]{1,0:T(8,128)S(1)}, f32[32,128]{1,0:T(8,128)S(1)}, u32[]{:S(2)}, u32[]{:S(2)}) %collective-permute-start.5) | collective-permute-done | bytes 16416 | tf_op jit(solution)/shard_map/ppermute | solution.py:907
  17.2 0.4 %collective-permute-done.4.refs_1_ = f32[48,256]{1,0:T(8,128)S(1)} collective-permute-done((f32[48,256]{1,0:T(8,128)S(1)}, f32[48,256]{1,0:T(8,128)S(1)}, u32[]{:S(2)}, u32[]{:S(2)}) %collective-permute-start.4) | collective-permute-done | bytes 49184 | tf_op jit(solution)/shard_map/ppermute | solution.py:907
  17.6 0.4 %weigh.1 = (f32[24,128]{1,0:T(8,128)S(1)}, f32[24,128]{1,0:T(8,128)S(1)}, f32[48,128]{1,0:T(8,128)S(1)}) custom-call(f32[48,256]{1,0:T(8,128)S(1)} %observe.1.refs_0_, f32[48,256]{1,0:T(8,128)S(1)} %collective-permute-done.4.refs_1_, f32[24,256]{1,0:T(8,128)S(1)} %get-tuple-element.76.refs_2_, f32[1,256]{1,0:T(1,128)S(1)} %get-tuple-element.77.refs_3_, ...), custom_call_target="tpu_custom_call" | custom-call | flops 500000 | bytes 735232 | tf_op jit(solution)/shard_map/weigh/pallas_call | solution.py:22
  18.0 2.4 %collective-permute-start.8 = (f32[48,128]{1,0:T(8,128)S(1)}, f32[48,128]{1,0:T(8,128)S(1)}, u32[]{:S(2)}, u32[]{:S(2)}) collective-permute-start(f32[48,128]{1,0:T(8,128)S(1)} %get-tuple-element.85), channel_id=1, source_target_pairs={{0,13},{1,8},{2,15},{3,10},{4,9},{5,12},{6,11},{7,14},{8,5},{9,0},... | collective-permute-start | bytes 73736 | tf_op jit(solution)/shard_map/ppermute | solution.py:907
  20.5 0.5 %collective-permute-start.7 = (f32[24,128]{1,0:T(8,128)S(1)}, f32[24,128]{1,0:T(8,128)S(1)}, u32[]{:S(2)}, u32[]{:S(2)}) collective-permute-start(f32[24,128]{1,0:T(8,128)S(1)} %get-tuple-element.84), channel_id=1, source_target_pairs={{0,5},{1,4},{2,7},{3,6},{4,1},{5,0},{6,3},{7,2},{8,13},{9,12},{10,... | collective-permute-start | bytes 36872 | tf_op jit(solution)/shard_map/ppermute | solution.py:907
  21.0 0.0 copy-start.1
  21.0 0.0 copy-start.2
  21.0 2.1 %advance.1 = f32[4,24,16,128]{3,2,1,0:T(8,128)} custom-call(f32[4,24,16,128]{3,2,1,0:T(8,128)S(1)} %get-tuple-element.86.tracer.refs_0_, f32[5,24,16,128]{3,2,1,0:T(8,128)S(1)} %get-tuple-element.87.refs_1_, f32[24,16,128]{2,1,0:T(8,128)S(1)} %get-tuple-element.61.refs_3_.refs_2_, f32[24,16,128]{2,1,0:T(8,128)S(1)} %get-tuple-element.62.refs_4_.refs_3_, ...), custom_call_target="tpu_custom_call" | custom-call | flops 6000000 | bytes 3604480 | tf_op jit(solution)/shard_map/advance/pallas_call | solution.py:22
  23.1 0.5 %collective-permute-done.7.refs_3_ = f32[24,128]{1,0:T(8,128)S(1)} collective-permute-done((f32[24,128]{1,0:T(8,128)S(1)}, f32[24,128]{1,0:T(8,128)S(1)}, u32[]{:S(2)}, u32[]{:S(2)}) %collective-permute-start.7) | collective-permute-done | bytes 12320 | tf_op jit(solution)/shard_map/ppermute | solution.py:907
  23.6 0.0 collective-permute-done.8.refs_4_
  23.6 0.0 collective-permute-start.9
  23.6 0.0 copy-done.1
  23.6 0.0 copy-done.2
  23.6 0.6 %regrid.2.refs_3_ = f32[4,128]{1,0:T(4,128)S(1)} custom-call(s32[16,128]{1,0:T(8,128)S(1)} %bitcast.14, f32[16,128]{1,0:T(8,128)S(1)} %bitcast.16, f32[24,128]{1,0:T(8,128)S(1)} %get-tuple-element.90.refs_2_, f32[24,128]{1,0:T(8,128)S(1)} %collective-permute-done.7.refs_3_, f32[48,128]{1,0:T(8,128)S(1)} %collective-permute-done.8.refs_4_), custom_call_target="tpu_custom_call" | custom-call | flops 1000000 | bytes 67584 | tf_op jit(solution)/shard_map/regrid/pallas_call | solution.py:22
  24.2 0.6 %collective-permute-done.9.refs_2_ = f32[48,128]{1,0:T(8,128)S(1)} collective-permute-done((f32[48,128]{1,0:T(8,128)S(1)}, f32[48,128]{1,0:T(8,128)S(1)}, u32[]{:S(2)}, u32[]{:S(2)}) %collective-permute-start.9) | collective-permute-done | bytes 24608 | tf_op jit(solution)/shard_map/ppermute | solution.py:907
  24.8 1.0 %regrid.3 = f32[4,128]{1,0:T(4,128)} custom-call(s32[16,128]{1,0:T(8,128)S(1)} %bitcast.15, f32[16,128]{1,0:T(8,128)S(1)} %bitcast.17, f32[48,128]{1,0:T(8,128)S(1)} %collective-permute-done.9.refs_2_, f32[4,128]{1,0:T(4,128)S(1)} %regrid.2.refs_3_), custom_call_target="tpu_custom_call" | custom-call | flops 1000000 | bytes 45056 | tf_op jit(solution)/shard_map/regrid/pallas_call | solution.py:22
  (4 shorter events, 0.0 us)
Async XLA Ops:
  2.4 2.8 %copy-start = (f32[4,24,16,128]{3,2,1,0:T(8,128)S(1)}, f32[4,24,16,128]{3,2,1,0:T(8,128)}, u32[]{:S(2)}) copy-start(f32[4,24,16,128]{3,2,1,0:T(8,128)} %refs_4_.1) | copy-start | bytes 2359300
  2.5 4.7 %collective-permute-start = (f32[104,128]{1,0:T(8,128)S(1)}, f32[104,128]{1,0:T(8,128)S(1)}, u32[]{:S(2)}, u32[]{:S(2)}) collective-permute-start(f32[104,128]{1,0:T(8,128)S(1)} %get-tuple-element.52.y_sent.refs_10_.refs_11_), channel_id=1, source_target_pairs={{0,3},{1,2},{2,1},{3,0},{4,7},{5,6},{6,5},{7,4},{8,11},{9,10},{10,... | collective-permute-start | bytes 159752 | tf_op jit(solution)/shard_map/ppermute | solution.py:907
  7.1 8.1 %collective-permute-start.1 = (f32[160,128]{1,0:T(8,128)S(1)}, f32[160,128]{1,0:T(8,128)S(1)}, u32[]{:S(2)}, u32[]{:S(2)}) collective-permute-start(f32[160,128]{1,0:T(8,128)S(1)} %relay.2.refs_8_.refs_5_), channel_id=1, source_target_pairs={{0,4},{1,5},{2,6},{3,7},{4,8},{5,9},{6,10},{7,11},{8,12},{9,13},{1... | collective-permute-start | bytes 245768 | tf_op jit(solution)/shard_map/ppermute | solution.py:907
  9.7 6.0 %collective-permute-start.2 = (f32[160,128]{1,0:T(8,128)S(1)}, f32[160,128]{1,0:T(8,128)S(1)}, u32[]{:S(2)}, u32[]{:S(2)}) collective-permute-start(f32[160,128]{1,0:T(8,128)S(1)} %relay.3.refs_9_.refs_6_), channel_id=1, source_target_pairs={{0,12},{1,13},{2,14},{3,15},{4,0},{5,1},{6,2},{7,3},{8,4},{9,5},{1... | collective-permute-start | bytes 245768 | tf_op jit(solution)/shard_map/ppermute | solution.py:907
  11.8 1.2 %collective-permute-start.3 = (f32[4,16,128]{2,1,0:T(8,128)S(1)}, f32[4,16,128]{2,1,0:T(8,128)S(1)}, u32[]{:S(2)}, u32[]{:S(2)}) collective-permute-start(f32[4,16,128]{2,1,0:T(8,128)S(1)} %get-tuple-element.67.base.refs_10_), channel_id=1, source_target_pairs={{0,1},{1,0},{2,3},{3,2},{4,5},{5,4},{6,7},{7,6},{8,9},{9,8},{10,11... | collective-permute-start | bytes 98312 | tf_op jit(solution)/shard_map/ppermute | solution.py:907
  11.8 5.0 %collective-permute-start.6 = (f32[32,128]{1,0:T(8,128)S(1)}, f32[32,128]{1,0:T(8,128)S(1)}, u32[]{:S(2)}, u32[]{:S(2)}) collective-permute-start(f32[32,128]{1,0:T(8,128)S(1)} %beyond.1), channel_id=1, source_target_pairs={{0,9},{1,8},{2,11},{3,10},{4,13},{5,12},{6,15},{7,14},{8,1},{9,0},... | collective-permute-start | bytes 49160 | tf_op jit(solution)/shard_map/ppermute | solution.py:907
  13.4 3.8 %collective-permute-start.5 = (f32[32,128]{1,0:T(8,128)S(1)}, f32[32,128]{1,0:T(8,128)S(1)}, u32[]{:S(2)}, u32[]{:S(2)}) collective-permute-start(f32[32,128]{1,0:T(8,128)S(1)} %get-tuple-element.74), channel_id=1, source_target_pairs={{0,2},{1,3},{2,0},{3,1},{4,6},{5,7},{6,4},{7,5},{8,10},{9,11},{10,... | collective-permute-start | bytes 49160 | tf_op jit(solution)/shard_map/ppermute | solution.py:907
  16.3 1.3 %collective-permute-start.4 = (f32[48,256]{1,0:T(8,128)S(1)}, f32[48,256]{1,0:T(8,128)S(1)}, u32[]{:S(2)}, u32[]{:S(2)}) collective-permute-start(f32[48,256]{1,0:T(8,128)S(1)} %observe.1.refs_0_), channel_id=1, source_target_pairs={{0,1},{1,0},{2,3},{3,2},{4,5},{5,4},{6,7},{7,6},{8,9},{9,8},{10,11... | collective-permute-start | bytes 147464 | tf_op jit(solution)/shard_map/ppermute | solution.py:907
  18.0 5.6 %collective-permute-start.8 = (f32[48,128]{1,0:T(8,128)S(1)}, f32[48,128]{1,0:T(8,128)S(1)}, u32[]{:S(2)}, u32[]{:S(2)}) collective-permute-start(f32[48,128]{1,0:T(8,128)S(1)} %get-tuple-element.85), channel_id=1, source_target_pairs={{0,13},{1,8},{2,15},{3,10},{4,9},{5,12},{6,11},{7,14},{8,5},{9,0},... | collective-permute-start | bytes 73736 | tf_op jit(solution)/shard_map/ppermute | solution.py:907
  20.5 3.1 %collective-permute-start.7 = (f32[24,128]{1,0:T(8,128)S(1)}, f32[24,128]{1,0:T(8,128)S(1)}, u32[]{:S(2)}, u32[]{:S(2)}) collective-permute-start(f32[24,128]{1,0:T(8,128)S(1)} %get-tuple-element.84), channel_id=1, source_target_pairs={{0,5},{1,4},{2,7},{3,6},{4,1},{5,0},{6,3},{7,2},{8,13},{9,12},{10,... | collective-permute-start | bytes 36872 | tf_op jit(solution)/shard_map/ppermute | solution.py:907
  21.0 2.6 %copy-start.1 = (s32[1,1,16,128]{3,2,1,0:T(8,128)S(1)}, s32[1,1,16,128]{3,2,1,0:T(8,128)}, u32[]{:S(2)}) copy-start(s32[1,1,16,128]{3,2,1,0:T(8,128)} %param.24) | copy-start | bytes 24580
  21.0 2.6 %copy-start.2 = (f32[1,1,16,128]{3,2,1,0:T(8,128)S(1)}, f32[1,1,16,128]{3,2,1,0:T(8,128)}, u32[]{:S(2)}) copy-start(f32[1,1,16,128]{3,2,1,0:T(8,128)} %param.25) | copy-start | bytes 24580
  23.6 1.2 %collective-permute-start.9 = (f32[48,128]{1,0:T(8,128)S(1)}, f32[48,128]{1,0:T(8,128)S(1)}, u32[]{:S(2)}, u32[]{:S(2)}) collective-permute-start(f32[48,128]{1,0:T(8,128)S(1)} %collective-permute-done.8.refs_4_), channel_id=1, source_target_pairs={{0,1},{1,0},{2,3},{3,2},{4,5},{5,4},{6,7},{7,6},{8,9},{9,8},{10,11... | collective-permute-start | bytes 73736 | tf_op jit(solution)/shard_map/ppermute | solution.py:907

commit v8 on v7

--- a/solution.py
+++ b/solution.py
@@ -251,19 +251,19 @@
     near, far = plan["x_blocks"]
     even_x = is_even("facex")
     offset = jnp.where(even_x if number == 0 else jnp.logical_not(even_x), near, far)
-    at = plan["y_tiles"] * cx + 8 * offset
+    at = plan["y_tiles"] * cx + 8 * (offset - plan["y_blocks"][0])
     out[head + 8 : head + 24, :] = blocks[pl.ds(pl.multiple_of(8 * offset, 8), 16), :]
     out[head + 24 : head + 40, :] = y_got[pl.ds(pl.multiple_of(at, 8), 16), :]
 
 
 def beyond_kernel(plan, cx, blocks, y_got, *outs):
     for out, offset in zip(outs, plan["x_ops"]):
-        at = plan["y_tiles"] * cx + 8 * offset
+        at = plan["y_tiles"] * cx + 8 * (offset - plan["y_blocks"][0])
         out[0:16, :] = blocks[8 * offset : 8 * offset + 16, :]
         out[16:32, :] = y_got[at : at + 16, :]
 
 
-def rim_kernel(plan, carried, levels, cx, y_sent, y_got, base, base_other, lanes, *refs):
+def rim_kernel(plan, carried, levels, cx, y_sent, y_got, base, base_other, lanes, own, *refs):
     inverse_out, ratio_out, lower_out, pieces_out, columns_out, rows_out, picks_out, live_out, base_out, square = refs
     cy = y_got.shape[1]
     slots = live_out.shape[1]
@@ -323,6 +323,7 @@
         tile.put(t, pltpu.roll(values, t, 1) if t else values)
     base_out[0:cx, :] = tile.packed(0)
     base_out[cx : 2 * cx, :] = lanes[...]
+    base_out[2 * cx :, :] = own[0:16, :]
     at = plan["y_tiles"] * cx + 8 * len(plan["y_blocks"])
     strips = slots // LANES
     cell = jnp.concatenate([y_got[at + n : at + n + 1, :] for n in range(strips)], axis=1).astype(jnp.int32)
@@ -452,14 +453,12 @@
     return groups
 
 
-def relayed_blocks(plan, head, cx, own, y_got, got, x_got):
-    start = plan["y_tiles"] * cx
-
+def relayed_blocks(plan, head, own, beyond, got, x_got):
     def block_at(ref, row):
         return ref[row : row + 8, :]
 
-    blocks = {0: block_at(own, 0), 1: block_at(y_got, start + 8)}
-    rim_blocks = {0: block_at(y_got, start), 1: block_at(own, 8)}
+    blocks = {0: block_at(own, 0), 1: block_at(beyond, 8)}
+    rim_blocks = {0: block_at(beyond, 0), 1: block_at(own, 8)}
     even_x = is_even("facex")
     from_west, from_east = (got[n][head + 8 : head + 40, :] for n in range(2))
     carriers = [
@@ -679,7 +678,9 @@
         gain = jnp.sum(sensitivity, axis=0, keepdims=True) * last[1:2] * used[...]
         return gain * (modeled - last[0:1])
 
-    blocks, rim_blocks = relayed_blocks(plan, (carried + 1) * levels, cx, own, refs[11], refs[9:11], x_got)
+    blocks, rim_blocks = relayed_blocks(
+        plan, (carried + 1) * levels, own, rim_base[2 * cx :, :], refs[9:11], x_got
+    )
     scattered = scatter(force(blocks, 0, columns, live), in_row[...], in_lane[...])
     on_rim = jnp.sum(rim_rows[...] * force(rim_blocks, levels, rim_columns, rim_live), axis=1, keepdims=True)
     near = [scattered + base[t] for t in range(carried)]
@@ -837,7 +838,7 @@
             n,
             plan,
             y_sent[n][0:cx, :],
-            y_got[n][-cx:, :] if plan["relay"] else y_got[n][0:cx, :],
+            y_got[n][cx : 2 * cx, :] if plan["relay"] else y_got[n][0:cx, :],
             winds_sent[n][0:cx, :],
             winds_got[n][0:cx, :],
             carried,
@@ -914,7 +915,7 @@
     relay = many_y == 2 and many_x == 4
     if relay:
         own_blocks = list(range(tiles))
-        y_blocks = own_blocks
+        y_blocks = own_blocks[2:]
         x_ops = [offset for offset in own_blocks[2::2] if offset not in x_blocks]
         pairs = []
     else:
@@ -1115,9 +1116,9 @@
                 shape(cx, slots),
                 shape(LANES, slots, dtype=BF16),
                 shape(1, slots),
-                shape(2 * cx, cy),
+                shape(2 * cx + 16, cy),
             ],
-            [lanes_sent[0], held_y, base, base_other, lanes_each],
+            [lanes_sent[0], held_y, base, base_other, lanes_each, own_blocks],
             "rim",
             400000,
             scratch=[pltpu.VMEM((LANES, LANES), F32)],

time: 25.9 us -> 25.7 us (level)
  transfers between devices with their start and end apart: 10 -> 10, of which waited for: 8 -> 8; matrix products, arithmetic and copies ran while one was open for 0% -> 0% of each run, Pallas kernels for 18% -> 19%
where the time goes in v8:
time: 25.7 us; the launch traced here: 25.6 us
  starting transfers between devices  13 us (51%)
  Pallas kernels  7.95 us (31%)
  waiting for transfers between devices  3.93 us (15%)
  between operations  0.72 us (3%)
    ppermute x10, starting transfers between devices, exchange(): return lax.ppermute(values, GROUP, pairs)  13 us
    pallas_call x12, Pallas kernels, call(): pl.pallas_call(body, out_shape=outs, in_specs=[pl.BlockSpec(memory_space=...  7.95 us
    ppermute x10, waiting for transfers between devices, exchange(): return lax.ppermute(values, GROUP, pairs)  3.93 us
  transfers between devices with their start and end apart: 10, of which 8 were waited for; matrix products, arithmetic and copies ran while one was open for 0% of the time, Pallas kernels for 19%

profile of v8, /device:TPU:0, one launch (start us, length us, event | category | flops | bytes accessed | tf_op | source)
XLA Modules:
  0.0 25.6 jit_solution(16910054303151201786)
XLA Ops:
  0.6 1.8 %pack.1 = (f32[88,128]{1,0:T(8,128)S(1)}, f32[64,128]{1,0:T(8,128)S(1)}, s32[1,256]{1,0:T(1,128)S(1)}, f32[1,256]{1,0:T(1,128)S(1)}, f32[4,24,16,128]{3,2,1,0:T(...) custom-call(f32[4,24,16,128]{3,2,1,0:T(8,128)} %refs_0_.1, ...), custom_call_target="tpu_custom_call" | custom-call | flops 100000 | bytes 2860064 | tf_op jit(solution)/shard_map/pack/pallas_call | solution.py:22
  2.4 0.0 copy-start
  2.5 2.4 %collective-permute-start = (f32[88,128]{1,0:T(8,128)S(1)}, f32[88,128]{1,0:T(8,128)S(1)}, u32[]{:S(2)}, u32[]{:S(2)}) collective-permute-start(f32[88,128]{1,0:T(8,128)S(1)} %get-tuple-element.52.y_sent.refs_10_.refs_11_), channel_id=1, source_target_pairs={{0,3},{1,2},{2,1},{3,0},{4,7},{5,6},{6,5},{7,4},{8,11},{9,10},{10,... | collective-permute-start | bytes 135176 | tf_op jit(solution)/shard_map/ppermute | solution.py:908
  4.9 0.3 %rows.1 = (f32[160,128]{1,0:T(8,128)S(1)}, f32[160,128]{1,0:T(8,128)S(1)}, f32[16,128]{1,0:T(8,128)S(1)}) custom-call(f32[4,24,16,128]{3,2,1,0:T(8,128)S(1)} %get-tuple-element.86.tracer.refs_0_, f32[24,16,128]{2,1,0:T(8,128)S(1)} %get-tuple-element.48.west.refs_1_, f32[16,128]{1,0:T(8,128)S(1)} %get-tuple-element.49.scale.refs_16_, ...), custom_call_target="tpu_custom_call" | custom-call | flops 100000 | bytes 1196032 | tf_op jit(solution)/shard_map/rows/pallas_call | solution.py:22
  5.2 0.0 copy-done
  5.2 0.7 %factor.1 = (f32[24,16,128]{2,1,0:T(8,128)S(1)}, f32[24,16,128]{2,1,0:T(8,128)S(1)}, f32[24,16,128]{2,1,0:T(8,128)S(1)}, f32[4,16,128]{2,1,0:T(8,128)S(1)}, f32[...) custom-call(f32[4,24,16,128]{3,2,1,0:T(8,128)S(1)} %get-tuple-elemen, ...), custom_call_target="tpu_custom_call" | custom-call | flops 3000000 | bytes 4129792 | tf_op jit(solution)/shard_map/factor/pallas_call | solution.py:22
  5.9 1.0 %collective-permute-done.y_got.refs_11_.refs_19_.refs_12_ = f32[88,128]{1,0:T(8,128)S(1)} collective-permute-done((f32[88,128]{1,0:T(8,128)S(1)}, f32[88,128]{1,0:T(8,128)S(1)}, u32[]{:S(2)}, u32[]{:S(2)}) %collective-permute-start) | collective-permute-done | bytes 45088 | tf_op jit(solution)/shard_map/ppermute | solution.py:908
  6.9 2.6 %collective-permute-start.1 = (f32[160,128]{1,0:T(8,128)S(1)}, f32[160,128]{1,0:T(8,128)S(1)}, u32[]{:S(2)}, u32[]{:S(2)}) collective-permute-start(f32[160,128]{1,0:T(8,128)S(1)} %relay.2.refs_8_.refs_5_), channel_id=1, source_target_pairs={{0,4},{1,5},{2,6},{3,7},{4,8},{5,9},{6,10},{7,11},{8,12},{9,13},{1... | collective-permute-start | bytes 245768 | tf_op jit(solution)/shard_map/ppermute | solution.py:908
  9.5 2.1 %collective-permute-start.2 = (f32[160,128]{1,0:T(8,128)S(1)}, f32[160,128]{1,0:T(8,128)S(1)}, u32[]{:S(2)}, u32[]{:S(2)}) collective-permute-start(f32[160,128]{1,0:T(8,128)S(1)} %relay.3.refs_9_.refs_6_), channel_id=1, source_target_pairs={{0,12},{1,13},{2,14},{3,15},{4,0},{5,1},{6,2},{7,3},{8,4},{9,5},{1... | collective-permute-start | bytes 245768 | tf_op jit(solution)/shard_map/ppermute | solution.py:908
  11.6 0.0 collective-permute-start.3
  11.6 1.1 %collective-permute-start.6 = (f32[32,128]{1,0:T(8,128)S(1)}, f32[32,128]{1,0:T(8,128)S(1)}, u32[]{:S(2)}, u32[]{:S(2)}) collective-permute-start(f32[32,128]{1,0:T(8,128)S(1)} %beyond.1), channel_id=1, source_target_pairs={{0,9},{1,8},{2,11},{3,10},{4,13},{5,12},{6,15},{7,14},{8,1},{9,0},... | collective-permute-start | bytes 49160 | tf_op jit(solution)/shard_map/ppermute | solution.py:908
  12.7 0.1 collective-permute-done.3.base_other.refs_11_
  12.8 0.4 %rim.1 = (f32[24,128]{1,0:T(8,128)S(1)}, f32[24,128]{1,0:T(8,128)S(1)}, f32[24,128]{1,0:T(8,128)S(1)}, f32[6,24,128]{2,1,0:T(8,128)S(1)}, f32[24,256]{1,0:T(8,12...) custom-call(f32[88,128]{1,0:T(8,128)S(1)} %get-tuple-element.52.y_se, ...), custom_call_target="tpu_custom_call" | custom-call | flops 400000 | bytes 504832 | tf_op jit(solution)/shard_map/rim/pallas_call | solution.py:22
  13.3 1.7 %collective-permute-start.5 = (f32[48,128]{1,0:T(8,128)S(1)}, f32[48,128]{1,0:T(8,128)S(1)}, u32[]{:S(2)}, u32[]{:S(2)}) collective-permute-start(f32[48,128]{1,0:T(8,128)S(1)} %get-tuple-element.74), channel_id=1, source_target_pairs={{0,2},{1,3},{2,0},{3,1},{4,6},{5,7},{6,4},{7,5},{8,10},{9,11},{10,... | collective-permute-start | bytes 73736 | tf_op jit(solution)/shard_map/ppermute | solution.py:908
  15.0 0.0 collective-permute-done.1.refs_0_.refs_17_.refs_7_
  15.0 0.5 %collective-permute-done.2.refs_1_.refs_18_.refs_8_ = f32[160,128]{1,0:T(8,128)S(1)} collective-permute-done((f32[160,128]{1,0:T(8,128)S(1)}, f32[160,128]{1,0:T(8,128)S(1)}, u32[]{:S(2)}, u32[]{:S(2)}) %collective-permute-start.2) | collective-permute-done | bytes 81952 | tf_op jit(solution)/shard_map/ppermute | solution.py:908
  15.5 0.6 %observe.1.refs_0_ = f32[48,256]{1,0:T(8,128)S(1)} custom-call(f32[160,128]{1,0:T(8,128)S(1)} %collective-permute-done.1.refs_0_.refs_17_.refs_7_, f32[160,128]{1,0:T(8,128)S(1)} %collective-permute-done.2.refs_1_.refs_18_.refs_8_, f32[24,16,128]{2,1,0:T(8,128)S(1)} %get-tuple-element.60.refs_2_, f32[24,16,128]{2,1,0:T(8,128)S(1)} %get-tuple-element.61.refs_3_.refs_2_, ...), custom_call_target="tpu_custom_call" | custom-call | flops 2000000 | bytes 1642496 | tf_op jit(solution)/shard_map/observe/pallas_call | solution.py:22
  16.1 0.1 collective-permute-start.4
  16.2 0.4 %collective-permute-done.6.refs_7_ = f32[32,128]{1,0:T(8,128)S(1)} collective-permute-done((f32[32,128]{1,0:T(8,128)S(1)}, f32[32,128]{1,0:T(8,128)S(1)}, u32[]{:S(2)}, u32[]{:S(2)}) %collective-permute-start.6) | collective-permute-done | bytes 16416 | tf_op jit(solution)/shard_map/ppermute | solution.py:908
  16.6 0.5 %collective-permute-done.5.refs_13_.refs_10_ = f32[48,128]{1,0:T(8,128)S(1)} collective-permute-done((f32[48,128]{1,0:T(8,128)S(1)}, f32[48,128]{1,0:T(8,128)S(1)}, u32[]{:S(2)}, u32[]{:S(2)}) %collective-permute-start.5) | collective-permute-done | bytes 24608 | tf_op jit(solution)/shard_map/ppermute | solution.py:908
  17.1 0.3 %collective-permute-done.4.refs_1_ = f32[48,256]{1,0:T(8,128)S(1)} collective-permute-done((f32[48,256]{1,0:T(8,128)S(1)}, f32[48,256]{1,0:T(8,128)S(1)}, u32[]{:S(2)}, u32[]{:S(2)}) %collective-permute-start.4) | collective-permute-done | bytes 49184 | tf_op jit(solution)/shard_map/ppermute | solution.py:908
  17.4 0.4 %weigh.1 = (f32[24,128]{1,0:T(8,128)S(1)}, f32[24,128]{1,0:T(8,128)S(1)}, f32[48,128]{1,0:T(8,128)S(1)}) custom-call(f32[48,256]{1,0:T(8,128)S(1)} %observe.1.refs_0_, f32[48,256]{1,0:T(8,128)S(1)} %collective-permute-done.4.refs_1_, f32[24,256]{1,0:T(8,128)S(1)} %get-tuple-element.76.refs_2_, f32[1,256]{1,0:T(1,128)S(1)} %get-tuple-element.77.refs_3_, ...), custom_call_target="tpu_custom_call" | custom-call | flops 500000 | bytes 735232 | tf_op jit(solution)/shard_map/weigh/pallas_call | solution.py:22
  17.8 2.4 %collective-permute-start.8 = (f32[48,128]{1,0:T(8,128)S(1)}, f32[48,128]{1,0:T(8,128)S(1)}, u32[]{:S(2)}, u32[]{:S(2)}) collective-permute-start(f32[48,128]{1,0:T(8,128)S(1)} %get-tuple-element.85), channel_id=1, source_target_pairs={{0,13},{1,8},{2,15},{3,10},{4,9},{5,12},{6,11},{7,14},{8,5},{9,0},... | collective-permute-start | bytes 73736 | tf_op jit(solution)/shard_map/ppermute | solution.py:908
  20.3 0.5 %collective-permute-start.7 = (f32[24,128]{1,0:T(8,128)S(1)}, f32[24,128]{1,0:T(8,128)S(1)}, u32[]{:S(2)}, u32[]{:S(2)}) collective-permute-start(f32[24,128]{1,0:T(8,128)S(1)} %get-tuple-element.84), channel_id=1, source_target_pairs={{0,5},{1,4},{2,7},{3,6},{4,1},{5,0},{6,3},{7,2},{8,13},{9,12},{10,... | collective-permute-start | bytes 36872 | tf_op jit(solution)/shard_map/ppermute | solution.py:908
  20.8 0.0 copy-start.1
  20.8 0.0 copy-start.2
  20.8 2.1 %advance.1 = f32[4,24,16,128]{3,2,1,0:T(8,128)} custom-call(f32[4,24,16,128]{3,2,1,0:T(8,128)S(1)} %get-tuple-element.86.tracer.refs_0_, f32[5,24,16,128]{3,2,1,0:T(8,128)S(1)} %get-tuple-element.87.refs_1_, f32[24,16,128]{2,1,0:T(8,128)S(1)} %get-tuple-element.61.refs_3_.refs_2_, f32[24,16,128]{2,1,0:T(8,128)S(1)} %get-tuple-element.62.refs_4_.refs_3_, ...), custom_call_target="tpu_custom_call" | custom-call | flops 6000000 | bytes 3596288 | tf_op jit(solution)/shard_map/advance/pallas_call | solution.py:22
  22.9 0.5 %collective-permute-done.7.refs_3_ = f32[24,128]{1,0:T(8,128)S(1)} collective-permute-done((f32[24,128]{1,0:T(8,128)S(1)}, f32[24,128]{1,0:T(8,128)S(1)}, u32[]{:S(2)}, u32[]{:S(2)}) %collective-permute-start.7) | collective-permute-done | bytes 12320 | tf_op jit(solution)/shard_map/ppermute | solution.py:908
  23.4 0.0 collective-permute-done.8.refs_4_
  23.4 0.0 collective-permute-start.9
  23.4 0.0 copy-done.1
  23.4 0.0 copy-done.2
  23.4 0.6 %regrid.2.refs_3_ = f32[4,128]{1,0:T(4,128)S(1)} custom-call(s32[16,128]{1,0:T(8,128)S(1)} %bitcast.14, f32[16,128]{1,0:T(8,128)S(1)} %bitcast.16, f32[24,128]{1,0:T(8,128)S(1)} %get-tuple-element.90.refs_2_, f32[24,128]{1,0:T(8,128)S(1)} %collective-permute-done.7.refs_3_, f32[48,128]{1,0:T(8,128)S(1)} %collective-permute-done.8.refs_4_), custom_call_target="tpu_custom_call" | custom-call | flops 1000000 | bytes 67584 | tf_op jit(solution)/shard_map/regrid/pallas_call | solution.py:22
  24.0 0.6 %collective-permute-done.9.refs_2_ = f32[48,128]{1,0:T(8,128)S(1)} collective-permute-done((f32[48,128]{1,0:T(8,128)S(1)}, f32[48,128]{1,0:T(8,128)S(1)}, u32[]{:S(2)}, u32[]{:S(2)}) %collective-permute-start.9) | collective-permute-done | bytes 24608 | tf_op jit(solution)/shard_map/ppermute | solution.py:908
  24.6 1.0 %regrid.3 = f32[4,128]{1,0:T(4,128)} custom-call(s32[16,128]{1,0:T(8,128)S(1)} %bitcast.15, f32[16,128]{1,0:T(8,128)S(1)} %bitcast.17, f32[48,128]{1,0:T(8,128)S(1)} %collective-permute-done.9.refs_2_, f32[4,128]{1,0:T(4,128)S(1)} %regrid.2.refs_3_), custom_call_target="tpu_custom_call" | custom-call | flops 1000000 | bytes 45056 | tf_op jit(solution)/shard_map/regrid/pallas_call | solution.py:22
  (4 shorter events, 0.0 us)
Async XLA Ops:
  2.4 2.8 %copy-start = (f32[4,24,16,128]{3,2,1,0:T(8,128)S(1)}, f32[4,24,16,128]{3,2,1,0:T(8,128)}, u32[]{:S(2)}) copy-start(f32[4,24,16,128]{3,2,1,0:T(8,128)} %refs_4_.1) | copy-start | bytes 2359300
  2.5 4.5 %collective-permute-start = (f32[88,128]{1,0:T(8,128)S(1)}, f32[88,128]{1,0:T(8,128)S(1)}, u32[]{:S(2)}, u32[]{:S(2)}) collective-permute-start(f32[88,128]{1,0:T(8,128)S(1)} %get-tuple-element.52.y_sent.refs_10_.refs_11_), channel_id=1, source_target_pairs={{0,3},{1,2},{2,1},{3,0},{4,7},{5,6},{6,5},{7,4},{8,11},{9,10},{10,... | collective-permute-start | bytes 135176 | tf_op jit(solution)/shard_map/ppermute | solution.py:908
  6.9 8.1 %collective-permute-start.1 = (f32[160,128]{1,0:T(8,128)S(1)}, f32[160,128]{1,0:T(8,128)S(1)}, u32[]{:S(2)}, u32[]{:S(2)}) collective-permute-start(f32[160,128]{1,0:T(8,128)S(1)} %relay.2.refs_8_.refs_5_), channel_id=1, source_target_pairs={{0,4},{1,5},{2,6},{3,7},{4,8},{5,9},{6,10},{7,11},{8,12},{9,13},{1... | collective-permute-start | bytes 245768 | tf_op jit(solution)/shard_map/ppermute | solution.py:908
  9.5 6.0 %collective-permute-start.2 = (f32[160,128]{1,0:T(8,128)S(1)}, f32[160,128]{1,0:T(8,128)S(1)}, u32[]{:S(2)}, u32[]{:S(2)}) collective-permute-start(f32[160,128]{1,0:T(8,128)S(1)} %relay.3.refs_9_.refs_6_), channel_id=1, source_target_pairs={{0,12},{1,13},{2,14},{3,15},{4,0},{5,1},{6,2},{7,3},{8,4},{9,5},{1... | collective-permute-start | bytes 245768 | tf_op jit(solution)/shard_map/ppermute | solution.py:908
  11.6 1.2 %collective-permute-start.3 = (f32[4,16,128]{2,1,0:T(8,128)S(1)}, f32[4,16,128]{2,1,0:T(8,128)S(1)}, u32[]{:S(2)}, u32[]{:S(2)}) collective-permute-start(f32[4,16,128]{2,1,0:T(8,128)S(1)} %get-tuple-element.67.base.refs_10_), channel_id=1, source_target_pairs={{0,1},{1,0},{2,3},{3,2},{4,5},{5,4},{6,7},{7,6},{8,9},{9,8},{10,11... | collective-permute-start | bytes 98312 | tf_op jit(solution)/shard_map/ppermute | solution.py:908
  11.6 5.0 %collective-permute-start.6 = (f32[32,128]{1,0:T(8,128)S(1)}, f32[32,128]{1,0:T(8,128)S(1)}, u32[]{:S(2)}, u32[]{:S(2)}) collective-permute-start(f32[32,128]{1,0:T(8,128)S(1)} %beyond.1), channel_id=1, source_target_pairs={{0,9},{1,8},{2,11},{3,10},{4,13},{5,12},{6,15},{7,14},{8,1},{9,0},... | collective-permute-start | bytes 49160 | tf_op jit(solution)/shard_map/ppermute | solution.py:908
  13.3 3.9 %collective-permute-start.5 = (f32[48,128]{1,0:T(8,128)S(1)}, f32[48,128]{1,0:T(8,128)S(1)}, u32[]{:S(2)}, u32[]{:S(2)}) collective-permute-start(f32[48,128]{1,0:T(8,128)S(1)} %get-tuple-element.74), channel_id=1, source_target_pairs={{0,2},{1,3},{2,0},{3,1},{4,6},{5,7},{6,4},{7,5},{8,10},{9,11},{10,... | collective-permute-start | bytes 73736 | tf_op jit(solution)/shard_map/ppermute | solution.py:908
  16.1 1.3 %collective-permute-start.4 = (f32[48,256]{1,0:T(8,128)S(1)}, f32[48,256]{1,0:T(8,128)S(1)}, u32[]{:S(2)}, u32[]{:S(2)}) collective-permute-start(f32[48,256]{1,0:T(8,128)S(1)} %observe.1.refs_0_), channel_id=1, source_target_pairs={{0,1},{1,0},{2,3},{3,2},{4,5},{5,4},{6,7},{7,6},{8,9},{9,8},{10,11... | collective-permute-start | bytes 147464 | tf_op jit(solution)/shard_map/ppermute | solution.py:908
  17.8 5.6 %collective-permute-start.8 = (f32[48,128]{1,0:T(8,128)S(1)}, f32[48,128]{1,0:T(8,128)S(1)}, u32[]{:S(2)}, u32[]{:S(2)}) collective-permute-start(f32[48,128]{1,0:T(8,128)S(1)} %get-tuple-element.85), channel_id=1, source_target_pairs={{0,13},{1,8},{2,15},{3,10},{4,9},{5,12},{6,11},{7,14},{8,5},{9,0},... | collective-permute-start | bytes 73736 | tf_op jit(solution)/shard_map/ppermute | solution.py:908
  20.3 3.1 %collective-permute-start.7 = (f32[24,128]{1,0:T(8,128)S(1)}, f32[24,128]{1,0:T(8,128)S(1)}, u32[]{:S(2)}, u32[]{:S(2)}) collective-permute-start(f32[24,128]{1,0:T(8,128)S(1)} %get-tuple-element.84), channel_id=1, source_target_pairs={{0,5},{1,4},{2,7},{3,6},{4,1},{5,0},{6,3},{7,2},{8,13},{9,12},{10,... | collective-permute-start | bytes 36872 | tf_op jit(solution)/shard_map/ppermute | solution.py:908
  20.8 2.6 %copy-start.1 = (s32[1,1,16,128]{3,2,1,0:T(8,128)S(1)}, s32[1,1,16,128]{3,2,1,0:T(8,128)}, u32[]{:S(2)}) copy-start(s32[1,1,16,128]{3,2,1,0:T(8,128)} %param.24) | copy-start | bytes 24580
  20.8 2.6 %copy-start.2 = (f32[1,1,16,128]{3,2,1,0:T(8,128)S(1)}, f32[1,1,16,128]{3,2,1,0:T(8,128)}, u32[]{:S(2)}) copy-start(f32[1,1,16,128]{3,2,1,0:T(8,128)} %param.25) | copy-start | bytes 24580
  23.4 1.2 %collective-permute-start.9 = (f32[48,128]{1,0:T(8,128)S(1)}, f32[48,128]{1,0:T(8,128)S(1)}, u32[]{:S(2)}, u32[]{:S(2)}) collective-permute-start(f32[48,128]{1,0:T(8,128)S(1)} %collective-permute-done.8.refs_4_), channel_id=1, source_target_pairs={{0,1},{1,0},{2,3},{3,2},{4,5},{5,4},{6,7},{7,6},{8,9},{9,8},{10,11... | collective-permute-start | bytes 73736 | tf_op jit(solution)/shard_map/ppermute | solution.py:908

commit v9 on v8

--- a/solution.py
+++ b/solution.py
@@ -482,7 +482,7 @@
     y_got = refs[plan["y_ops"] : 2 * plan["y_ops"]]
     refs = refs[2 * plan["y_ops"] :]
     if plan["relay"]:
-        rim_inverse, rim_ratio, rim_lower, pieces, rim_picks, parcel, turn, rise = refs
+        rim_inverse, rim_ratio, rim_lower, pieces, rim_picks, parcel, rows_out, turn, rise = refs
     else:
         columns, live, own, *refs = refs
         n_pairs = len(plan["pairs"])
@@ -606,6 +606,9 @@
     picked = jnp.dot(high, picks, preferred_element_type=F32)
     picked = picked + jnp.dot(low, picks, preferred_element_type=F32)
     parcel[levels : 2 * levels, :] = picked
+    rows = carried * levels
+    for number in range(2):
+        rows_out[number * rows : (number + 1) * rows, :] = got[number][0:rows, :]
 
 
 def advance_cells(cells, west, east, south, north, face_w, face_e, face_s, face_n):
@@ -815,16 +818,20 @@
     tracer, parts, lower, inverse, ratio = refs[:5]
     sent = refs[5:7]
     got = refs[7:9]
+    swapped, *refs = refs[9:]
     y_ops = plan["y_ops"]
-    y_sent, y_got, winds_sent, winds_got = (refs[9 + n * y_ops : 9 + (n + 1) * y_ops] for n in range(4))
+    y_sent, y_got, winds_sent, winds_got = (refs[n * y_ops : (n + 1) * y_ops] for n in range(4))
     target, out, west_rows, east_rows, done = refs[-5:]
     carried, levels, cx, cy = tracer.shape
     head = (carried + 1) * levels
     spot = carried * levels
-    beyond_west, beyond_east = sides(plan, got[0][0:head], got[1][0:head])
-    at_west, at_east = own_sides(plan, sent[0][0:head], sent[1][0:head])
-    face_west = at_west[spot:head]
-    face_east = beyond_east[spot:head]
+    face_west, _ = own_sides(plan, sent[0][spot:head, :], sent[1][spot:head, :])
+    _, face_east = sides(plan, got[0][spot:head, :], got[1][spot:head, :])
+    each = [got[number][0:spot, :] for number in range(2)]
+    if plan["cross"]:
+        each = [swapped[number * spot : (number + 1) * spot, :] for number in range(2)]
+    beyond_west, beyond_east = sides(plan, *each)
+    _, at_east = own_sides(plan, sent[0][0:spot, :], sent[1][0:spot, :])
     for t in range(carried):
         part = slice(t * levels, (t + 1) * levels)
         west_rows[part, :] = jnp.maximum(face_west, 0.0) * beyond_west[part]
@@ -926,7 +933,7 @@
         rest.sort(key=lambda d: (d // many_y != many_x // 2, d))
         pairs = [(rest[n], rest[min(n + 1, len(rest) - 1)]) for n in range(0, len(rest), 2)]
     others = list(range(many_x - 1, 1, -1))
-    bands = [(0, 0), (1, 1)] + [(others[n], others[n + 1]) for n in range(0, len(others), 2)]
+    bands = [(0, 0), (1, 1)] + [(others[n + 1], others[n]) for n in range(0, len(others), 2)]
     return {
         "relay": relay,
         "cross": 1 if relay else 0,
@@ -978,7 +985,7 @@
     def next_x(number):
         def rule(x, y, c):
             step = 1 if (plan["relay"] or x % 2 == 0) == (number == 0) else -1
-            return ((x + step) % many_x, y, c)
+            return ((x + step) % many_x, y, c ^ plan["cross"])
 
         return rule
 
@@ -1125,13 +1132,14 @@
         )
         *rim, rim_sent = rim
         rim_got = exchange(rim_sent, sizes, next_y(0, 0))
-        (parcel,) = observe(
-            [shape(2 * levels, slots)],
+        parcel, rows_crossed = observe(
+            [shape(2 * levels, slots), shape(2 * carried * levels, cy)],
             [*rows_got, inner, lower, inverse, ratio, in_row, in_lane, *rows_sent, *lanes_sent, *lanes_got]
             + [*rim[:4], rim[6]],
             scratch=[pltpu.VMEM((LANES, LANES), F32), pltpu.VMEM((levels, LANES), F32)],
         )
         parcel_other = other_core(parcel)
+        rows_swapped = other_core(rows_crossed)
         parcel_other, rim_got, *x_got = lax.optimization_barrier((parcel_other, rim_got, *x_got))
         band_sent = call(
             functools.partial(weigh_kernel, sizes, plan, carried, levels),
@@ -1169,6 +1177,7 @@
             400000,
         )
         lanes_own = [*lanes_sent, *lanes_got]
+        rows_swapped = rows_got[0]
         held = tracer
     (advanced,) = call(
         functools.partial(advance_kernel, plan),
@@ -1176,6 +1185,7 @@
         [held, parts, lower, inverse, ratio]
         + list(rows_sent)
         + rows_got
+        + [rows_swapped]
         + lanes_own
         + list(lanes_sent)
         + lanes_got,
@@ -1212,7 +1222,7 @@
     far_fetched = [other_core(got) for got in far_got]
     mine = carried if plan["cross"] else 0
     partial = regridded(near + [(pair, 0, mine) for pair in far], near_got + far_got)
-    latlon = regridded([(pair, 1, carried - mine) for pair in far], far_fetched, partial)
+    latlon = regridded([(pair, 1, carried - mine) for pair in far], far_fetched, partial) if far else partial
     return (advanced, latlon[:, None, None, :])
 
 

time: 25.7 us -> 25.5 us (level)
  starting transfers between devices: 13 us -> 12.4 us
  waiting for transfers between devices: 3.93 us -> 4.29 us
    ppermute x10 -> x11, starting transfers between devices: 13 us -> 12.4 us  [exchange(): return lax.ppermute(values, GROUP, pairs)]
    ppermute x10 -> x11, waiting for transfers between devices: 3.93 us -> 4.29 us  [exchange(): return lax.ppermute(values, GROUP, pairs)]
  transfers between devices with their start and end apart: 10 -> 11, of which waited for: 8 -> 8; matrix products, arithmetic and copies ran while one was open for 0% -> 0% of each run, Pallas kernels for 19% -> 20%
where the time goes in v9:
time: 25.5 us; the launch traced here: 25.4 us
  starting transfers between devices  12.4 us (49%)
  Pallas kernels  7.94 us (31%)
  waiting for transfers between devices  4.29 us (17%)
  between operations  0.69 us (3%)
    ppermute x11, starting transfers between devices, exchange(): return lax.ppermute(values, GROUP, pairs)  12.4 us
    pallas_call x12, Pallas kernels, call(): pl.pallas_call(body, out_shape=outs, in_specs=[pl.BlockSpec(memory_space=...  7.94 us
    ppermute x11, waiting for transfers between devices, exchange(): return lax.ppermute(values, GROUP, pairs)  4.29 us
  transfers between devices with their start and end apart: 11, of which 8 were waited for; matrix products, arithmetic and copies ran while one was open for 0% of the time, Pallas kernels for 20%

profile of v9, /device:TPU:0, one launch (start us, length us, event | category | flops | bytes accessed | tf_op | source)
XLA Modules:
  0.0 25.4 jit_solution(4327039455728600377)
XLA Ops:
  0.6 1.8 %pack.1 = (f32[88,128]{1,0:T(8,128)S(1)}, f32[64,128]{1,0:T(8,128)S(1)}, s32[1,256]{1,0:T(1,128)S(1)}, f32[1,256]{1,0:T(1,128)S(1)}, f32[4,24,16,128]{3,2,1,0:T(...) custom-call(f32[4,24,16,128]{3,2,1,0:T(8,128)} %refs_0_.1, ...), custom_call_target="tpu_custom_call" | custom-call | flops 100000 | bytes 2860064 | tf_op jit(solution)/shard_map/pack/pallas_call | solution.py:22
  2.4 0.0 copy-start
  2.5 2.4 %collective-permute-start = (f32[88,128]{1,0:T(8,128)S(1)}, f32[88,128]{1,0:T(8,128)S(1)}, u32[]{:S(2)}, u32[]{:S(2)}) collective-permute-start(f32[88,128]{1,0:T(8,128)S(1)} %get-tuple-element.54.y_sent.refs_10_.refs_12_), channel_id=1, source_target_pairs={{0,3},{1,2},{2,1},{3,0},{4,7},{5,6},{6,5},{7,4},{8,11},{9,10},{10,... | collective-permute-start | bytes 135176 | tf_op jit(solution)/shard_map/ppermute | solution.py:915
  4.9 0.3 %rows.1 = (f32[160,128]{1,0:T(8,128)S(1)}, f32[160,128]{1,0:T(8,128)S(1)}, f32[16,128]{1,0:T(8,128)S(1)}) custom-call(f32[4,24,16,128]{3,2,1,0:T(8,128)S(1)} %get-tuple-element.89.tracer.refs_0_, f32[24,16,128]{2,1,0:T(8,128)S(1)} %get-tuple-element.50.west.refs_1_, f32[16,128]{1,0:T(8,128)S(1)} %get-tuple-element.51.scale.refs_16_, ...), custom_call_target="tpu_custom_call" | custom-call | flops 100000 | bytes 1196032 | tf_op jit(solution)/shard_map/rows/pallas_call | solution.py:22
  5.2 0.0 copy-done
  5.2 0.7 %factor.1 = (f32[24,16,128]{2,1,0:T(8,128)S(1)}, f32[24,16,128]{2,1,0:T(8,128)S(1)}, f32[24,16,128]{2,1,0:T(8,128)S(1)}, f32[4,16,128]{2,1,0:T(8,128)S(1)}, f32[...) custom-call(f32[4,24,16,128]{3,2,1,0:T(8,128)S(1)} %get-tuple-elemen, ...), custom_call_target="tpu_custom_call" | custom-call | flops 3000000 | bytes 4129792 | tf_op jit(solution)/shard_map/factor/pallas_call | solution.py:22
  5.9 1.0 %collective-permute-done.y_got.refs_11_.refs_19_.refs_13_ = f32[88,128]{1,0:T(8,128)S(1)} collective-permute-done((f32[88,128]{1,0:T(8,128)S(1)}, f32[88,128]{1,0:T(8,128)S(1)}, u32[]{:S(2)}, u32[]{:S(2)}) %collective-permute-start) | collective-permute-done | bytes 45088 | tf_op jit(solution)/shard_map/ppermute | solution.py:915
  6.9 2.3 %collective-permute-start.1 = (f32[160,128]{1,0:T(8,128)S(1)}, f32[160,128]{1,0:T(8,128)S(1)}, u32[]{:S(2)}, u32[]{:S(2)}) collective-permute-start(f32[160,128]{1,0:T(8,128)S(1)} %relay.2.refs_8_.refs_5_), channel_id=1, source_target_pairs={{0,5},{1,4},{2,7},{3,6},{4,9},{5,8},{6,11},{7,10},{8,13},{9,12},{1... | collective-permute-start | bytes 245768 | tf_op jit(solution)/shard_map/ppermute | solution.py:915
  9.2 2.1 %collective-permute-start.2 = (f32[160,128]{1,0:T(8,128)S(1)}, f32[160,128]{1,0:T(8,128)S(1)}, u32[]{:S(2)}, u32[]{:S(2)}) collective-permute-start(f32[160,128]{1,0:T(8,128)S(1)} %relay.3.refs_9_.refs_6_), channel_id=1, source_target_pairs={{0,13},{1,12},{2,15},{3,14},{4,1},{5,0},{6,3},{7,2},{8,5},{9,4},{1... | collective-permute-start | bytes 245768 | tf_op jit(solution)/shard_map/ppermute | solution.py:915
  11.3 0.4 %collective-permute-start.3 = (f32[4,16,128]{2,1,0:T(8,128)S(1)}, f32[4,16,128]{2,1,0:T(8,128)S(1)}, u32[]{:S(2)}, u32[]{:S(2)}) collective-permute-start(f32[4,16,128]{2,1,0:T(8,128)S(1)} %get-tuple-element.69.base.refs_10_), channel_id=1, source_target_pairs={{0,1},{1,0},{2,3},{3,2},{4,5},{5,4},{6,7},{7,6},{8,9},{9,8},{10,11... | collective-permute-start | bytes 98312 | tf_op jit(solution)/shard_map/ppermute | solution.py:915
  11.7 0.7 %collective-permute-start.6 = (f32[32,128]{1,0:T(8,128)S(1)}, f32[32,128]{1,0:T(8,128)S(1)}, u32[]{:S(2)}, u32[]{:S(2)}) collective-permute-start(f32[32,128]{1,0:T(8,128)S(1)} %beyond.1), channel_id=1, source_target_pairs={{0,9},{1,8},{2,11},{3,10},{4,13},{5,12},{6,15},{7,14},{8,1},{9,0},... | collective-permute-start | bytes 49160 | tf_op jit(solution)/shard_map/ppermute | solution.py:915
  12.5 0.1 collective-permute-done.3.base_other.refs_11_
  12.6 0.4 %rim.1 = (f32[24,128]{1,0:T(8,128)S(1)}, f32[24,128]{1,0:T(8,128)S(1)}, f32[24,128]{1,0:T(8,128)S(1)}, f32[6,24,128]{2,1,0:T(8,128)S(1)}, f32[24,256]{1,0:T(8,12...) custom-call(f32[88,128]{1,0:T(8,128)S(1)} %get-tuple-element.54.y_se, ...), custom_call_target="tpu_custom_call" | custom-call | flops 400000 | bytes 504832 | tf_op jit(solution)/shard_map/rim/pallas_call | solution.py:22
  13.0 1.7 %collective-permute-start.5 = (f32[48,128]{1,0:T(8,128)S(1)}, f32[48,128]{1,0:T(8,128)S(1)}, u32[]{:S(2)}, u32[]{:S(2)}) collective-permute-start(f32[48,128]{1,0:T(8,128)S(1)} %get-tuple-element.77), channel_id=1, source_target_pairs={{0,2},{1,3},{2,0},{3,1},{4,6},{5,7},{6,4},{7,5},{8,10},{9,11},{10,... | collective-permute-start | bytes 73736 | tf_op jit(solution)/shard_map/ppermute | solution.py:915
  14.7 0.0 collective-permute-done.1.refs_0_.refs_17_.refs_7_
  14.7 0.7 %collective-permute-done.2.refs_1_.refs_18_.refs_8_ = f32[160,128]{1,0:T(8,128)S(1)} collective-permute-done((f32[160,128]{1,0:T(8,128)S(1)}, f32[160,128]{1,0:T(8,128)S(1)}, u32[]{:S(2)}, u32[]{:S(2)}) %collective-permute-start.2) | collective-permute-done | bytes 81952 | tf_op jit(solution)/shard_map/ppermute | solution.py:915
  15.5 0.6 %observe.1 = (f32[48,256]{1,0:T(8,128)S(1)}, f32[192,128]{1,0:T(8,128)S(1)}) custom-call(f32[160,128]{1,0:T(8,128)S(1)} %collective-permute-done.1.refs_0_.refs_17_.refs_7_, f32[160,128]{1,0:T(8,128)S(1)} %collective-permute-done.2.refs_1_.refs_18_.refs_8_, f32[24,16,128]{2,1,0:T(8,128)S(1)} %get-tuple-element.62.refs_2_, ...), custom_call_target="tpu_custom_call" | custom-call | flops 2000000 | bytes 1740800 | tf_op jit(solution)/shard_map/observe/pallas_call | solution.py:22
  16.1 0.2 collective-permute-start.4
  16.3 0.4 %collective-permute-start.7 = (f32[192,128]{1,0:T(8,128)S(1)}, f32[192,128]{1,0:T(8,128)S(1)}, u32[]{:S(2)}, u32[]{:S(2)}) collective-permute-start(f32[192,128]{1,0:T(8,128)S(1)} %get-tuple-element.91), channel_id=1, source_target_pairs={{0,1},{1,0},{2,3},{3,2},{4,5},{5,4},{6,7},{7,6},{8,9},{9,8},{10,11... | collective-permute-start | bytes 294920 | tf_op jit(solution)/shard_map/ppermute | solution.py:915
  16.6 0.0 collective-permute-done.6.refs_7_
  16.6 0.3 %collective-permute-done.5.refs_13_.refs_11_ = f32[48,128]{1,0:T(8,128)S(1)} collective-permute-done((f32[48,128]{1,0:T(8,128)S(1)}, f32[48,128]{1,0:T(8,128)S(1)}, u32[]{:S(2)}, u32[]{:S(2)}) %collective-permute-start.5) | collective-permute-done | bytes 24608 | tf_op jit(solution)/shard_map/ppermute | solution.py:915
  16.9 0.4 %collective-permute-done.4.refs_1_ = f32[48,256]{1,0:T(8,128)S(1)} collective-permute-done((f32[48,256]{1,0:T(8,128)S(1)}, f32[48,256]{1,0:T(8,128)S(1)}, u32[]{:S(2)}, u32[]{:S(2)}) %collective-permute-start.4) | collective-permute-done | bytes 49184 | tf_op jit(solution)/shard_map/ppermute | solution.py:915
  17.4 0.4 %weigh.1 = (f32[24,128]{1,0:T(8,128)S(1)}, f32[24,128]{1,0:T(8,128)S(1)}, f32[48,128]{1,0:T(8,128)S(1)}) custom-call(f32[48,256]{1,0:T(8,128)S(1)} %get-tuple-element.76.refs_0_, f32[48,256]{1,0:T(8,128)S(1)} %collective-permute-done.4.refs_1_, f32[24,256]{1,0:T(8,128)S(1)} %get-tuple-element.79.refs_2_, f32[1,256]{1,0:T(1,128)S(1)} %get-tuple-element.80.refs_3_, ...), custom_call_target="tpu_custom_call" | custom-call | flops 500000 | bytes 735232 | tf_op jit(solution)/shard_map/weigh/pallas_call | solution.py:22
  17.8 0.9 %collective-permute-start.9 = (f32[48,128]{1,0:T(8,128)S(1)}, f32[48,128]{1,0:T(8,128)S(1)}, u32[]{:S(2)}, u32[]{:S(2)}) collective-permute-start(f32[48,128]{1,0:T(8,128)S(1)} %get-tuple-element.88), channel_id=1, source_target_pairs={{0,9},{1,12},{2,11},{3,14},{4,13},{5,8},{6,15},{7,10},{8,1},{9,4},... | collective-permute-start | bytes 73736 | tf_op jit(solution)/shard_map/ppermute | solution.py:915
  18.7 0.7 %collective-permute-start.8 = (f32[24,128]{1,0:T(8,128)S(1)}, f32[24,128]{1,0:T(8,128)S(1)}, u32[]{:S(2)}, u32[]{:S(2)}) collective-permute-start(f32[24,128]{1,0:T(8,128)S(1)} %get-tuple-element.87), channel_id=1, source_target_pairs={{0,5},{1,4},{2,7},{3,6},{4,1},{5,0},{6,3},{7,2},{8,13},{9,12},{10,... | collective-permute-start | bytes 36872 | tf_op jit(solution)/shard_map/ppermute | solution.py:915
  19.5 0.0 collective-permute-done.7.refs_9_
  19.5 0.0 copy-start.1
  19.5 0.0 copy-start.2
  19.5 2.1 %advance.1 = f32[4,24,16,128]{3,2,1,0:T(8,128)} custom-call(f32[4,24,16,128]{3,2,1,0:T(8,128)S(1)} %get-tuple-element.89.tracer.refs_0_, f32[5,24,16,128]{3,2,1,0:T(8,128)S(1)} %get-tuple-element.90.refs_1_, f32[24,16,128]{2,1,0:T(8,128)S(1)} %get-tuple-element.63.refs_3_.refs_2_, f32[24,16,128]{2,1,0:T(8,128)S(1)} %get-tuple-element.64.refs_4_.refs_3_, ...), custom_call_target="tpu_custom_call" | custom-call | flops 6000000 | bytes 3694592 | tf_op jit(solution)/shard_map/advance/pallas_call | solution.py:22
  21.6 0.3 %collective-permute-done.8.refs_3_ = f32[24,128]{1,0:T(8,128)S(1)} collective-permute-done((f32[24,128]{1,0:T(8,128)S(1)}, f32[24,128]{1,0:T(8,128)S(1)}, u32[]{:S(2)}, u32[]{:S(2)}) %collective-permute-start.8) | collective-permute-done | bytes 12320 | tf_op jit(solution)/shard_map/ppermute | solution.py:915
  21.8 1.2 %collective-permute-done.9.refs_4_ = f32[48,128]{1,0:T(8,128)S(1)} collective-permute-done((f32[48,128]{1,0:T(8,128)S(1)}, f32[48,128]{1,0:T(8,128)S(1)}, u32[]{:S(2)}, u32[]{:S(2)}) %collective-permute-start.9) | collective-permute-done | bytes 24608 | tf_op jit(solution)/shard_map/ppermute | solution.py:915
  23.0 0.5 %collective-permute-start.10 = (f32[48,128]{1,0:T(8,128)S(1)}, f32[48,128]{1,0:T(8,128)S(1)}, u32[]{:S(2)}, u32[]{:S(2)}) collective-permute-start(f32[48,128]{1,0:T(8,128)S(1)} %collective-permute-done.9.refs_4_), channel_id=1, source_target_pairs={{0,1},{1,0},{2,3},{3,2},{4,5},{5,4},{6,7},{7,6},{8,9},{9,8},{10,11... | collective-permute-start | bytes 73736 | tf_op jit(solution)/shard_map/ppermute | solution.py:915
  23.5 0.0 copy-done.1
  23.5 0.0 copy-done.2
  23.5 0.6 %regrid.2.refs_3_ = f32[4,128]{1,0:T(4,128)S(1)} custom-call(s32[16,128]{1,0:T(8,128)S(1)} %bitcast.14, f32[16,128]{1,0:T(8,128)S(1)} %bitcast.16, f32[24,128]{1,0:T(8,128)S(1)} %get-tuple-element.94.refs_2_, f32[24,128]{1,0:T(8,128)S(1)} %collective-permute-done.8.refs_3_, f32[48,128]{1,0:T(8,128)S(1)} %collective-permute-done.9.refs_4_), custom_call_target="tpu_custom_call" | custom-call | flops 1000000 | bytes 67584 | tf_op jit(solution)/shard_map/regrid/pallas_call | solution.py:22
  24.1 0.2 collective-permute-done.10.refs_2_
  24.4 1.0 %regrid.3 = f32[4,128]{1,0:T(4,128)} custom-call(s32[16,128]{1,0:T(8,128)S(1)} %bitcast.15, f32[16,128]{1,0:T(8,128)S(1)} %bitcast.17, f32[48,128]{1,0:T(8,128)S(1)} %collective-permute-done.10.refs_2_, f32[4,128]{1,0:T(4,128)S(1)} %regrid.2.refs_3_), custom_call_target="tpu_custom_call" | custom-call | flops 1000000 | bytes 45056 | tf_op jit(solution)/shard_map/regrid/pallas_call | solution.py:22
  (4 shorter events, 0.0 us)
Async XLA Ops:
  2.4 2.8 %copy-start = (f32[4,24,16,128]{3,2,1,0:T(8,128)S(1)}, f32[4,24,16,128]{3,2,1,0:T(8,128)}, u32[]{:S(2)}) copy-start(f32[4,24,16,128]{3,2,1,0:T(8,128)} %refs_4_.1) | copy-start | bytes 2359300
  2.5 4.5 %collective-permute-start = (f32[88,128]{1,0:T(8,128)S(1)}, f32[88,128]{1,0:T(8,128)S(1)}, u32[]{:S(2)}, u32[]{:S(2)}) collective-permute-start(f32[88,128]{1,0:T(8,128)S(1)} %get-tuple-element.54.y_sent.refs_10_.refs_12_), channel_id=1, source_target_pairs={{0,3},{1,2},{2,1},{3,0},{4,7},{5,6},{6,5},{7,4},{8,11},{9,10},{10,... | collective-permute-start | bytes 135176 | tf_op jit(solution)/shard_map/ppermute | solution.py:915
  6.9 7.8 %collective-permute-start.1 = (f32[160,128]{1,0:T(8,128)S(1)}, f32[160,128]{1,0:T(8,128)S(1)}, u32[]{:S(2)}, u32[]{:S(2)}) collective-permute-start(f32[160,128]{1,0:T(8,128)S(1)} %relay.2.refs_8_.refs_5_), channel_id=1, source_target_pairs={{0,5},{1,4},{2,7},{3,6},{4,9},{5,8},{6,11},{7,10},{8,13},{9,12},{1... | collective-permute-start | bytes 245768 | tf_op jit(solution)/shard_map/ppermute | solution.py:915
  9.2 6.2 %collective-permute-start.2 = (f32[160,128]{1,0:T(8,128)S(1)}, f32[160,128]{1,0:T(8,128)S(1)}, u32[]{:S(2)}, u32[]{:S(2)}) collective-permute-start(f32[160,128]{1,0:T(8,128)S(1)} %relay.3.refs_9_.refs_6_), channel_id=1, source_target_pairs={{0,13},{1,12},{2,15},{3,14},{4,1},{5,0},{6,3},{7,2},{8,5},{9,4},{1... | collective-permute-start | bytes 245768 | tf_op jit(solution)/shard_map/ppermute | solution.py:915
  11.3 1.3 %collective-permute-start.3 = (f32[4,16,128]{2,1,0:T(8,128)S(1)}, f32[4,16,128]{2,1,0:T(8,128)S(1)}, u32[]{:S(2)}, u32[]{:S(2)}) collective-permute-start(f32[4,16,128]{2,1,0:T(8,128)S(1)} %get-tuple-element.69.base.refs_10_), channel_id=1, source_target_pairs={{0,1},{1,0},{2,3},{3,2},{4,5},{5,4},{6,7},{7,6},{8,9},{9,8},{10,11... | collective-permute-start | bytes 98312 | tf_op jit(solution)/shard_map/ppermute | solution.py:915
  11.7 4.9 %collective-permute-start.6 = (f32[32,128]{1,0:T(8,128)S(1)}, f32[32,128]{1,0:T(8,128)S(1)}, u32[]{:S(2)}, u32[]{:S(2)}) collective-permute-start(f32[32,128]{1,0:T(8,128)S(1)} %beyond.1), channel_id=1, source_target_pairs={{0,9},{1,8},{2,11},{3,10},{4,13},{5,12},{6,15},{7,14},{8,1},{9,0},... | collective-permute-start | bytes 49160 | tf_op jit(solution)/shard_map/ppermute | solution.py:915
  13.0 3.9 %collective-permute-start.5 = (f32[48,128]{1,0:T(8,128)S(1)}, f32[48,128]{1,0:T(8,128)S(1)}, u32[]{:S(2)}, u32[]{:S(2)}) collective-permute-start(f32[48,128]{1,0:T(8,128)S(1)} %get-tuple-element.77), channel_id=1, source_target_pairs={{0,2},{1,3},{2,0},{3,1},{4,6},{5,7},{6,4},{7,5},{8,10},{9,11},{10,... | collective-permute-start | bytes 73736 | tf_op jit(solution)/shard_map/ppermute | solution.py:915
  16.1 1.3 %collective-permute-start.4 = (f32[48,256]{1,0:T(8,128)S(1)}, f32[48,256]{1,0:T(8,128)S(1)}, u32[]{:S(2)}, u32[]{:S(2)}) collective-permute-start(f32[48,256]{1,0:T(8,128)S(1)} %get-tuple-element.76.refs_0_), channel_id=1, source_target_pairs={{0,1},{1,0},{2,3},{3,2},{4,5},{5,4},{6,7},{7,6},{8,9},{9,8},{10,11... | collective-permute-start | bytes 147464 | tf_op jit(solution)/shard_map/ppermute | solution.py:915
  16.3 3.2 %collective-permute-start.7 = (f32[192,128]{1,0:T(8,128)S(1)}, f32[192,128]{1,0:T(8,128)S(1)}, u32[]{:S(2)}, u32[]{:S(2)}) collective-permute-start(f32[192,128]{1,0:T(8,128)S(1)} %get-tuple-element.91), channel_id=1, source_target_pairs={{0,1},{1,0},{2,3},{3,2},{4,5},{5,4},{6,7},{7,6},{8,9},{9,8},{10,11... | collective-permute-start | bytes 294920 | tf_op jit(solution)/shard_map/ppermute | solution.py:915
  17.8 5.3 %collective-permute-start.9 = (f32[48,128]{1,0:T(8,128)S(1)}, f32[48,128]{1,0:T(8,128)S(1)}, u32[]{:S(2)}, u32[]{:S(2)}) collective-permute-start(f32[48,128]{1,0:T(8,128)S(1)} %get-tuple-element.88), channel_id=1, source_target_pairs={{0,9},{1,12},{2,11},{3,14},{4,13},{5,8},{6,15},{7,10},{8,1},{9,4},... | collective-permute-start | bytes 73736 | tf_op jit(solution)/shard_map/ppermute | solution.py:915
  18.7 3.1 %collective-permute-start.8 = (f32[24,128]{1,0:T(8,128)S(1)}, f32[24,128]{1,0:T(8,128)S(1)}, u32[]{:S(2)}, u32[]{:S(2)}) collective-permute-start(f32[24,128]{1,0:T(8,128)S(1)} %get-tuple-element.87), channel_id=1, source_target_pairs={{0,5},{1,4},{2,7},{3,6},{4,1},{5,0},{6,3},{7,2},{8,13},{9,12},{10,... | collective-permute-start | bytes 36872 | tf_op jit(solution)/shard_map/ppermute | solution.py:915
  19.5 4.1 %copy-start.1 = (s32[1,1,16,128]{3,2,1,0:T(8,128)S(1)}, s32[1,1,16,128]{3,2,1,0:T(8,128)}, u32[]{:S(2)}) copy-start(s32[1,1,16,128]{3,2,1,0:T(8,128)} %param.24) | copy-start | bytes 24580
  19.5 4.1 %copy-start.2 = (f32[1,1,16,128]{3,2,1,0:T(8,128)S(1)}, f32[1,1,16,128]{3,2,1,0:T(8,128)}, u32[]{:S(2)}) copy-start(f32[1,1,16,128]{3,2,1,0:T(8,128)} %param.25) | copy-start | bytes 24580
  23.0 1.3 %collective-permute-start.10 = (f32[48,128]{1,0:T(8,128)S(1)}, f32[48,128]{1,0:T(8,128)S(1)}, u32[]{:S(2)}, u32[]{:S(2)}) collective-permute-start(f32[48,128]{1,0:T(8,128)S(1)} %collective-permute-done.9.refs_4_), channel_id=1, source_target_pairs={{0,1},{1,0},{2,3},{3,2},{4,5},{5,4},{6,7},{7,6},{8,9},{9,8},{10,11... | collective-permute-start | bytes 73736 | tf_op jit(solution)/shard_map/ppermute | solution.py:915

commit v10 on v9

--- a/solution.py
+++ b/solution.py
@@ -759,6 +759,9 @@
                 moved = pltpu.roll(grown[skip + start + a], lax.rem(band * a + cy - band * target, cy), 1)
                 tile = jnp.where(group_of_lane == a, moved, tile)
             out[start // per_tile * rows : (start // per_tile + 1) * rows, :] = tile
+        full = -(-count // per_tile) * rows
+        if out.shape[0] > full:
+            out[full:, :] = jnp.zeros((out.shape[0] - full, cy), F32)
 
 
 def regrid_kernel(sizes, plan, bands, carried, cx, band, *refs):
@@ -1079,7 +1082,8 @@
 
     def band_shape(first, second):
         count = carried if first == second else 2 * carried
-        return shape(-(-count // per_tile) * (cx + 8), cy)
+        spare = 8 if plan["relay"] and first == second != 0 else 0
+        return shape(-(-count // per_tile) * (cx + 8) + spare, cy)
 
     band_shapes = [band_shape(*b) for b in plan["bands"]]
     fields = [west_courant[0], south_courant[0], emission_scale]
@@ -1218,10 +1222,12 @@
     far = [pair for pair, kind in zip(plan["bands"], kinds) if not kind]
     near_got = [got for got, kind in zip(band_got, kinds) if kind]
     far_got = [got for got, kind in zip(band_got, kinds) if not kind]
-    advanced, near_got, far_got = lax.optimization_barrier((advanced, near_got, far_got))
-    far_fetched = [other_core(got) for got in far_got]
+    advanced, far_got = lax.optimization_barrier((advanced, far_got))
+    far_fetched = [other_core(got[: cx + 8] if plan["relay"] else got) for got in far_got]
     mine = carried if plan["cross"] else 0
-    partial = regridded(near + [(pair, 0, mine) for pair in far], near_got + far_got)
+    partial = [regridded([(pair, 0, mine) for pair in far], far_got)] if far else []
+    near_got, partial = lax.optimization_barrier((near_got, partial))
+    partial = regridded(near, near_got, *partial)
     latlon = regridded([(pair, 1, carried - mine) for pair in far], far_fetched, partial) if far else partial
     return (advanced, latlon[:, None, None, :])
 

time: 25.5 us -> 25.4 us (level)
  starting transfers between devices: 12.4 us -> 12 us
  Pallas kernels: 7.94 us -> 8.25 us
    ppermute x11, starting transfers between devices: 12.4 us -> 12 us  [exchange(): return lax.ppermute(values, GROUP, pairs)]
    pallas_call x12 -> x13, Pallas kernels: 7.94 us -> 8.25 us  [call(): pl.pallas_call(body, out_shape=outs, in_specs=[pl.BlockSpec(memory_space=...]
  transfers between devices with their start and end apart: 11 -> 11, of which waited for: 8 -> 7; matrix products, arithmetic and copies ran while one was open for 0% -> 0% of each run, Pallas kernels for 20% -> 22%
where the time goes in v10:
time: 25.4 us; the launch traced here: 25.2 us
  starting transfers between devices  12 us (47%)
  Pallas kernels  8.25 us (32%)
  waiting for transfers between devices  4.21 us (17%)
  between operations  0.72 us (3%)
    ppermute x11, starting transfers between devices, exchange(): return lax.ppermute(values, GROUP, pairs)  12 us
    pallas_call x13, Pallas kernels, call(): pl.pallas_call(body, out_shape=outs, in_specs=[pl.BlockSpec(memory_space=...  8.25 us
    ppermute x11, waiting for transfers between devices, exchange(): return lax.ppermute(values, GROUP, pairs)  4.21 us
  transfers between devices with their start and end apart: 11, of which 7 were waited for; matrix products, arithmetic and copies ran while one was open for 0% of the time, Pallas kernels for 22%

profile of v10, /device:TPU:0, one launch (start us, length us, event | category | flops | bytes accessed | tf_op | source)
XLA Modules:
  0.0 25.2 jit_solution(2483985895354278782)
XLA Ops:
  0.6 1.8 %pack.1 = (f32[88,128]{1,0:T(8,128)S(1)}, f32[64,128]{1,0:T(8,128)S(1)}, s32[1,256]{1,0:T(1,128)S(1)}, f32[1,256]{1,0:T(1,128)S(1)}, f32[4,24,16,128]{3,2,1,0:T(...) custom-call(f32[4,24,16,128]{3,2,1,0:T(8,128)} %refs_0_.1, ...), custom_call_target="tpu_custom_call" | custom-call | flops 100000 | bytes 2860064 | tf_op jit(solution)/shard_map/pack/pallas_call | solution.py:22
  2.4 0.0 copy-start
  2.5 2.4 %collective-permute-start = (f32[88,128]{1,0:T(8,128)S(1)}, f32[88,128]{1,0:T(8,128)S(1)}, u32[]{:S(2)}, u32[]{:S(2)}) collective-permute-start(f32[88,128]{1,0:T(8,128)S(1)} %get-tuple-element.55.y_sent.refs_10_.refs_12_), channel_id=1, source_target_pairs={{0,3},{1,2},{2,1},{3,0},{4,7},{5,6},{6,5},{7,4},{8,11},{9,10},{10,... | collective-permute-start | bytes 135176 | tf_op jit(solution)/shard_map/ppermute | solution.py:918
  4.9 0.3 %rows.1 = (f32[160,128]{1,0:T(8,128)S(1)}, f32[160,128]{1,0:T(8,128)S(1)}, f32[16,128]{1,0:T(8,128)S(1)}) custom-call(f32[4,24,16,128]{3,2,1,0:T(8,128)S(1)} %get-tuple-element.90.tracer.refs_0_, f32[24,16,128]{2,1,0:T(8,128)S(1)} %get-tuple-element.51.west.refs_1_, f32[16,128]{1,0:T(8,128)S(1)} %get-tuple-element.52.scale.refs_16_, ...), custom_call_target="tpu_custom_call" | custom-call | flops 100000 | bytes 1196032 | tf_op jit(solution)/shard_map/rows/pallas_call | solution.py:22
  5.2 0.0 copy-done
  5.2 0.7 %factor.1 = (f32[24,16,128]{2,1,0:T(8,128)S(1)}, f32[24,16,128]{2,1,0:T(8,128)S(1)}, f32[24,16,128]{2,1,0:T(8,128)S(1)}, f32[4,16,128]{2,1,0:T(8,128)S(1)}, f32[...) custom-call(f32[4,24,16,128]{3,2,1,0:T(8,128)S(1)} %get-tuple-elemen, ...), custom_call_target="tpu_custom_call" | custom-call | flops 3000000 | bytes 4129792 | tf_op jit(solution)/shard_map/factor/pallas_call | solution.py:22
  5.9 1.0 %collective-permute-done.y_got.refs_11_.refs_19_.refs_13_ = f32[88,128]{1,0:T(8,128)S(1)} collective-permute-done((f32[88,128]{1,0:T(8,128)S(1)}, f32[88,128]{1,0:T(8,128)S(1)}, u32[]{:S(2)}, u32[]{:S(2)}) %collective-permute-start) | collective-permute-done | bytes 45088 | tf_op jit(solution)/shard_map/ppermute | solution.py:918
  6.9 2.3 %collective-permute-start.1 = (f32[160,128]{1,0:T(8,128)S(1)}, f32[160,128]{1,0:T(8,128)S(1)}, u32[]{:S(2)}, u32[]{:S(2)}) collective-permute-start(f32[160,128]{1,0:T(8,128)S(1)} %relay.2.refs_8_.refs_5_), channel_id=1, source_target_pairs={{0,5},{1,4},{2,7},{3,6},{4,9},{5,8},{6,11},{7,10},{8,13},{9,12},{1... | collective-permute-start | bytes 245768 | tf_op jit(solution)/shard_map/ppermute | solution.py:918
  9.2 2.1 %collective-permute-start.2 = (f32[160,128]{1,0:T(8,128)S(1)}, f32[160,128]{1,0:T(8,128)S(1)}, u32[]{:S(2)}, u32[]{:S(2)}) collective-permute-start(f32[160,128]{1,0:T(8,128)S(1)} %relay.3.refs_9_.refs_6_), channel_id=1, source_target_pairs={{0,13},{1,12},{2,15},{3,14},{4,1},{5,0},{6,3},{7,2},{8,5},{9,4},{1... | collective-permute-start | bytes 245768 | tf_op jit(solution)/shard_map/ppermute | solution.py:918
  11.3 0.4 %collective-permute-start.3 = (f32[4,16,128]{2,1,0:T(8,128)S(1)}, f32[4,16,128]{2,1,0:T(8,128)S(1)}, u32[]{:S(2)}, u32[]{:S(2)}) collective-permute-start(f32[4,16,128]{2,1,0:T(8,128)S(1)} %get-tuple-element.70.base.refs_10_), channel_id=1, source_target_pairs={{0,1},{1,0},{2,3},{3,2},{4,5},{5,4},{6,7},{7,6},{8,9},{9,8},{10,11... | collective-permute-start | bytes 98312 | tf_op jit(solution)/shard_map/ppermute | solution.py:918
  11.7 0.7 %collective-permute-start.6 = (f32[32,128]{1,0:T(8,128)S(1)}, f32[32,128]{1,0:T(8,128)S(1)}, u32[]{:S(2)}, u32[]{:S(2)}) collective-permute-start(f32[32,128]{1,0:T(8,128)S(1)} %beyond.1), channel_id=1, source_target_pairs={{0,9},{1,8},{2,11},{3,10},{4,13},{5,12},{6,15},{7,14},{8,1},{9,0},... | collective-permute-start | bytes 49160 | tf_op jit(solution)/shard_map/ppermute | solution.py:918
  12.5 0.1 collective-permute-done.3.base_other.refs_11_
  12.6 0.4 %rim.1 = (f32[24,128]{1,0:T(8,128)S(1)}, f32[24,128]{1,0:T(8,128)S(1)}, f32[24,128]{1,0:T(8,128)S(1)}, f32[6,24,128]{2,1,0:T(8,128)S(1)}, f32[24,256]{1,0:T(8,12...) custom-call(f32[88,128]{1,0:T(8,128)S(1)} %get-tuple-element.55.y_se, ...), custom_call_target="tpu_custom_call" | custom-call | flops 400000 | bytes 504832 | tf_op jit(solution)/shard_map/rim/pallas_call | solution.py:22
  13.0 1.7 %collective-permute-start.5 = (f32[48,128]{1,0:T(8,128)S(1)}, f32[48,128]{1,0:T(8,128)S(1)}, u32[]{:S(2)}, u32[]{:S(2)}) collective-permute-start(f32[48,128]{1,0:T(8,128)S(1)} %get-tuple-element.78), channel_id=1, source_target_pairs={{0,2},{1,3},{2,0},{3,1},{4,6},{5,7},{6,4},{7,5},{8,10},{9,11},{10,... | collective-permute-start | bytes 73736 | tf_op jit(solution)/shard_map/ppermute | solution.py:918
  14.7 0.0 collective-permute-done.1.refs_0_.refs_17_.refs_7_
  14.7 0.7 %collective-permute-done.2.refs_1_.refs_18_.refs_8_ = f32[160,128]{1,0:T(8,128)S(1)} collective-permute-done((f32[160,128]{1,0:T(8,128)S(1)}, f32[160,128]{1,0:T(8,128)S(1)}, u32[]{:S(2)}, u32[]{:S(2)}) %collective-permute-start.2) | collective-permute-done | bytes 81952 | tf_op jit(solution)/shard_map/ppermute | solution.py:918
  15.5 0.6 %observe.1 = (f32[48,256]{1,0:T(8,128)S(1)}, f32[192,128]{1,0:T(8,128)S(1)}) custom-call(f32[160,128]{1,0:T(8,128)S(1)} %collective-permute-done.1.refs_0_.refs_17_.refs_7_, f32[160,128]{1,0:T(8,128)S(1)} %collective-permute-done.2.refs_1_.refs_18_.refs_8_, f32[24,16,128]{2,1,0:T(8,128)S(1)} %get-tuple-element.63.refs_2_, ...), custom_call_target="tpu_custom_call" | custom-call | flops 2000000 | bytes 1740800 | tf_op jit(solution)/shard_map/observe/pallas_call | solution.py:22
  16.1 0.2 collective-permute-start.4
  16.3 0.4 %collective-permute-start.7 = (f32[192,128]{1,0:T(8,128)S(1)}, f32[192,128]{1,0:T(8,128)S(1)}, u32[]{:S(2)}, u32[]{:S(2)}) collective-permute-start(f32[192,128]{1,0:T(8,128)S(1)} %get-tuple-element.92), channel_id=1, source_target_pairs={{0,1},{1,0},{2,3},{3,2},{4,5},{5,4},{6,7},{7,6},{8,9},{9,8},{10,11... | collective-permute-start | bytes 294920 | tf_op jit(solution)/shard_map/ppermute | solution.py:918
  16.6 0.0 collective-permute-done.6.refs_7_
  16.6 0.3 %collective-permute-done.5.refs_13_.refs_11_ = f32[48,128]{1,0:T(8,128)S(1)} collective-permute-done((f32[48,128]{1,0:T(8,128)S(1)}, f32[48,128]{1,0:T(8,128)S(1)}, u32[]{:S(2)}, u32[]{:S(2)}) %collective-permute-start.5) | collective-permute-done | bytes 24608 | tf_op jit(solution)/shard_map/ppermute | solution.py:918
  16.9 0.4 %collective-permute-done.4.refs_1_ = f32[48,256]{1,0:T(8,128)S(1)} collective-permute-done((f32[48,256]{1,0:T(8,128)S(1)}, f32[48,256]{1,0:T(8,128)S(1)}, u32[]{:S(2)}, u32[]{:S(2)}) %collective-permute-start.4) | collective-permute-done | bytes 49184 | tf_op jit(solution)/shard_map/ppermute | solution.py:918
  17.4 0.4 %weigh.1 = (f32[24,128]{1,0:T(8,128)S(1)}, f32[32,128]{1,0:T(8,128)S(1)}, f32[48,128]{1,0:T(8,128)S(1)}) custom-call(f32[48,256]{1,0:T(8,128)S(1)} %get-tuple-element.77.refs_0_, f32[48,256]{1,0:T(8,128)S(1)} %collective-permute-done.4.refs_1_, f32[24,256]{1,0:T(8,128)S(1)} %get-tuple-element.80.refs_2_, f32[1,256]{1,0:T(1,128)S(1)} %get-tuple-element.81.refs_3_, ...), custom_call_target="tpu_custom_call" | custom-call | flops 500000 | bytes 739328 | tf_op jit(solution)/shard_map/weigh/pallas_call | solution.py:22
  17.8 0.9 %collective-permute-start.8 = (f32[48,128]{1,0:T(8,128)S(1)}, f32[48,128]{1,0:T(8,128)S(1)}, u32[]{:S(2)}, u32[]{:S(2)}) collective-permute-start(f32[48,128]{1,0:T(8,128)S(1)} %get-tuple-element.89), channel_id=1, source_target_pairs={{0,9},{1,12},{2,11},{3,14},{4,13},{5,8},{6,15},{7,10},{8,1},{9,4},... | collective-permute-start | bytes 73736 | tf_op jit(solution)/shard_map/ppermute | solution.py:918
  18.7 0.7 %collective-permute-start.10 = (f32[32,128]{1,0:T(8,128)S(1)}, f32[32,128]{1,0:T(8,128)S(1)}, u32[]{:S(2)}, u32[]{:S(2)}) collective-permute-start(f32[32,128]{1,0:T(8,128)S(1)} %get-tuple-element.88), channel_id=1, source_target_pairs={{0,5},{1,4},{2,7},{3,6},{4,1},{5,0},{6,3},{7,2},{8,13},{9,12},{10,... | collective-permute-start | bytes 49160 | tf_op jit(solution)/shard_map/ppermute | solution.py:918
  19.5 0.0 collective-permute-done.7.refs_9_
  19.5 2.1 %advance.1 = f32[4,24,16,128]{3,2,1,0:T(8,128)} custom-call(f32[4,24,16,128]{3,2,1,0:T(8,128)S(1)} %get-tuple-element.90.tracer.refs_0_, f32[5,24,16,128]{3,2,1,0:T(8,128)S(1)} %get-tuple-element.91.refs_1_, f32[24,16,128]{2,1,0:T(8,128)S(1)} %get-tuple-element.64.refs_3_.refs_2_, f32[24,16,128]{2,1,0:T(8,128)S(1)} %get-tuple-element.65.refs_4_.refs_3_, ...), custom_call_target="tpu_custom_call" | custom-call | flops 6000000 | bytes 3694592 | tf_op jit(solution)/shard_map/advance/pallas_call | solution.py:22
  21.6 0.0 copy-start.1
  21.6 0.0 copy-start.2
  21.6 1.5 %collective-permute-done.8.refs_2_ = f32[48,128]{1,0:T(8,128)S(1)} collective-permute-done((f32[48,128]{1,0:T(8,128)S(1)}, f32[48,128]{1,0:T(8,128)S(1)}, u32[]{:S(2)}, u32[]{:S(2)}) %collective-permute-start.8) | collective-permute-done | bytes 24608 | tf_op jit(solution)/shard_map/ppermute | solution.py:918
  23.0 0.1 collective-permute-start.9
  23.1 0.0 copy-done.1
  23.1 0.0 copy-done.2
  23.1 0.4 %regrid.3.refs_4_ = f32[4,128]{1,0:T(4,128)S(1)} custom-call(s32[16,128]{1,0:T(8,128)S(1)} %bitcast.14, f32[16,128]{1,0:T(8,128)S(1)} %bitcast.17, f32[48,128]{1,0:T(8,128)S(1)} %collective-permute-done.8.refs_2_), custom_call_target="tpu_custom_call" | custom-call | flops 1000000 | bytes 43008 | tf_op jit(solution)/shard_map/regrid/pallas_call | solution.py:22
  23.5 0.0 collective-permute-done.10.refs_3_
  23.5 0.5 %regrid.4.refs_3_ = f32[4,128]{1,0:T(4,128)S(1)} custom-call(s32[16,128]{1,0:T(8,128)S(1)} %bitcast.15, f32[16,128]{1,0:T(8,128)S(1)} %bitcast.18, f32[24,128]{1,0:T(8,128)S(1)} %get-tuple-element.95.refs_2_, f32[32,128]{1,0:T(8,128)S(1)} %collective-permute-done.10.refs_3_, f32[4,128]{1,0:T(4,128)S(1)} %regrid.3.refs_4_), custom_call_target="tpu_custom_call" | custom-call | flops 1000000 | bytes 49152 | tf_op jit(solution)/shard_map/regrid/pallas_call | solution.py:22
  24.0 0.2 collective-permute-done.9.refs_2_
  24.2 1.0 %regrid.5 = f32[4,128]{1,0:T(4,128)} custom-call(s32[16,128]{1,0:T(8,128)S(1)} %bitcast.16, f32[16,128]{1,0:T(8,128)S(1)} %bitcast.19, f32[24,128]{1,0:T(8,128)S(1)} %collective-permute-done.9.refs_2_, f32[4,128]{1,0:T(4,128)S(1)} %regrid.4.refs_3_), custom_call_target="tpu_custom_call" | custom-call | flops 1000000 | bytes 32768 | tf_op jit(solution)/shard_map/regrid/pallas_call | solution.py:22
  (5 shorter events, 0.0 us)
Async XLA Ops:
  2.4 2.8 %copy-start = (f32[4,24,16,128]{3,2,1,0:T(8,128)S(1)}, f32[4,24,16,128]{3,2,1,0:T(8,128)}, u32[]{:S(2)}) copy-start(f32[4,24,16,128]{3,2,1,0:T(8,128)} %refs_4_.1) | copy-start | bytes 2359300
  2.5 4.5 %collective-permute-start = (f32[88,128]{1,0:T(8,128)S(1)}, f32[88,128]{1,0:T(8,128)S(1)}, u32[]{:S(2)}, u32[]{:S(2)}) collective-permute-start(f32[88,128]{1,0:T(8,128)S(1)} %get-tuple-element.55.y_sent.refs_10_.refs_12_), channel_id=1, source_target_pairs={{0,3},{1,2},{2,1},{3,0},{4,7},{5,6},{6,5},{7,4},{8,11},{9,10},{10,... | collective-permute-start | bytes 135176 | tf_op jit(solution)/shard_map/ppermute | solution.py:918
  6.9 7.8 %collective-permute-start.1 = (f32[160,128]{1,0:T(8,128)S(1)}, f32[160,128]{1,0:T(8,128)S(1)}, u32[]{:S(2)}, u32[]{:S(2)}) collective-permute-start(f32[160,128]{1,0:T(8,128)S(1)} %relay.2.refs_8_.refs_5_), channel_id=1, source_target_pairs={{0,5},{1,4},{2,7},{3,6},{4,9},{5,8},{6,11},{7,10},{8,13},{9,12},{1... | collective-permute-start | bytes 245768 | tf_op jit(solution)/shard_map/ppermute | solution.py:918
  9.2 6.2 %collective-permute-start.2 = (f32[160,128]{1,0:T(8,128)S(1)}, f32[160,128]{1,0:T(8,128)S(1)}, u32[]{:S(2)}, u32[]{:S(2)}) collective-permute-start(f32[160,128]{1,0:T(8,128)S(1)} %relay.3.refs_9_.refs_6_), channel_id=1, source_target_pairs={{0,13},{1,12},{2,15},{3,14},{4,1},{5,0},{6,3},{7,2},{8,5},{9,4},{1... | collective-permute-start | bytes 245768 | tf_op jit(solution)/shard_map/ppermute | solution.py:918
  11.3 1.3 %collective-permute-start.3 = (f32[4,16,128]{2,1,0:T(8,128)S(1)}, f32[4,16,128]{2,1,0:T(8,128)S(1)}, u32[]{:S(2)}, u32[]{:S(2)}) collective-permute-start(f32[4,16,128]{2,1,0:T(8,128)S(1)} %get-tuple-element.70.base.refs_10_), channel_id=1, source_target_pairs={{0,1},{1,0},{2,3},{3,2},{4,5},{5,4},{6,7},{7,6},{8,9},{9,8},{10,11... | collective-permute-start | bytes 98312 | tf_op jit(solution)/shard_map/ppermute | solution.py:918
  11.7 4.9 %collective-permute-start.6 = (f32[32,128]{1,0:T(8,128)S(1)}, f32[32,128]{1,0:T(8,128)S(1)}, u32[]{:S(2)}, u32[]{:S(2)}) collective-permute-start(f32[32,128]{1,0:T(8,128)S(1)} %beyond.1), channel_id=1, source_target_pairs={{0,9},{1,8},{2,11},{3,10},{4,13},{5,12},{6,15},{7,14},{8,1},{9,0},... | collective-permute-start | bytes 49160 | tf_op jit(solution)/shard_map/ppermute | solution.py:918
  13.0 3.9 %collective-permute-start.5 = (f32[48,128]{1,0:T(8,128)S(1)}, f32[48,128]{1,0:T(8,128)S(1)}, u32[]{:S(2)}, u32[]{:S(2)}) collective-permute-start(f32[48,128]{1,0:T(8,128)S(1)} %get-tuple-element.78), channel_id=1, source_target_pairs={{0,2},{1,3},{2,0},{3,1},{4,6},{5,7},{6,4},{7,5},{8,10},{9,11},{10,... | collective-permute-start | bytes 73736 | tf_op jit(solution)/shard_map/ppermute | solution.py:918
  16.1 1.3 %collective-permute-start.4 = (f32[48,256]{1,0:T(8,128)S(1)}, f32[48,256]{1,0:T(8,128)S(1)}, u32[]{:S(2)}, u32[]{:S(2)}) collective-permute-start(f32[48,256]{1,0:T(8,128)S(1)} %get-tuple-element.77.refs_0_), channel_id=1, source_target_pairs={{0,1},{1,0},{2,3},{3,2},{4,5},{5,4},{6,7},{7,6},{8,9},{9,8},{10,11... | collective-permute-start | bytes 147464 | tf_op jit(solution)/shard_map/ppermute | solution.py:918
  16.3 3.2 %collective-permute-start.7 = (f32[192,128]{1,0:T(8,128)S(1)}, f32[192,128]{1,0:T(8,128)S(1)}, u32[]{:S(2)}, u32[]{:S(2)}) collective-permute-start(f32[192,128]{1,0:T(8,128)S(1)} %get-tuple-element.92), channel_id=1, source_target_pairs={{0,1},{1,0},{2,3},{3,2},{4,5},{5,4},{6,7},{7,6},{8,9},{9,8},{10,11... | collective-permute-start | bytes 294920 | tf_op jit(solution)/shard_map/ppermute | solution.py:918
  17.8 5.3 %collective-permute-start.8 = (f32[48,128]{1,0:T(8,128)S(1)}, f32[48,128]{1,0:T(8,128)S(1)}, u32[]{:S(2)}, u32[]{:S(2)}) collective-permute-start(f32[48,128]{1,0:T(8,128)S(1)} %get-tuple-element.89), channel_id=1, source_target_pairs={{0,9},{1,12},{2,11},{3,14},{4,13},{5,8},{6,15},{7,10},{8,1},{9,4},... | collective-permute-start | bytes 73736 | tf_op jit(solution)/shard_map/ppermute | solution.py:918
  18.7 4.8 %collective-permute-start.10 = (f32[32,128]{1,0:T(8,128)S(1)}, f32[32,128]{1,0:T(8,128)S(1)}, u32[]{:S(2)}, u32[]{:S(2)}) collective-permute-start(f32[32,128]{1,0:T(8,128)S(1)} %get-tuple-element.88), channel_id=1, source_target_pairs={{0,5},{1,4},{2,7},{3,6},{4,1},{5,0},{6,3},{7,2},{8,13},{9,12},{10,... | collective-permute-start | bytes 49160 | tf_op jit(solution)/shard_map/ppermute | solution.py:918
  21.6 1.6 %copy-start.1 = (s32[1,1,16,128]{3,2,1,0:T(8,128)S(1)}, s32[1,1,16,128]{3,2,1,0:T(8,128)}, u32[]{:S(2)}) copy-start(s32[1,1,16,128]{3,2,1,0:T(8,128)} %param.24) | copy-start | bytes 24580
  21.6 1.6 %copy-start.2 = (f32[1,1,16,128]{3,2,1,0:T(8,128)S(1)}, f32[1,1,16,128]{3,2,1,0:T(8,128)}, u32[]{:S(2)}) copy-start(f32[1,1,16,128]{3,2,1,0:T(8,128)} %param.25) | copy-start | bytes 24580
  23.0 1.2 %collective-permute-start.9 = (f32[24,128]{1,0:T(8,128)S(1)}, f32[24,128]{1,0:T(8,128)S(1)}, u32[]{:S(2)}, u32[]{:S(2)}) collective-permute-start(f32[24,128]{1,0:T(8,128)S(1)} %slice.11), channel_id=1, source_target_pairs={{0,1},{1,0},{2,3},{3,2},{4,5},{5,4},{6,7},{7,6},{8,9},{9,8},{10,11... | collective-permute-start | bytes 36872 | tf_op jit(solution)/shard_map/ppermute | solution.py:918

commit v11 on v10

--- a/solution.py
+++ b/solution.py
@@ -94,9 +94,9 @@
 
 def pack_kernel(sizes, plan, *refs):
     sources, refs = refs[:10], refs[10:]
-    lanes_out, refs = refs[: plan["y_ops"]], refs[plan["y_ops"] :]
+    lanes_out, refs = refs[: plan.y_ops], refs[plan.y_ops :]
     own_out, refs = refs[0], refs[1:]
-    block_outs, refs = refs[: len(plan["pairs"])], refs[len(plan["pairs"]) :]
+    block_outs, refs = refs[: len(plan.pairs)], refs[len(plan.pairs) :]
     cell_out, live_out, tracer, west, south, scale, mixing, *refs = refs
     kernels, observed, weights, cells, counts, done = refs
     carried, levels, cx, cy = tracer.shape
@@ -128,13 +128,13 @@
 
     for number in (3, 4, 5):
         copies[number].wait()
-    for number, offset in enumerate(plan["y_blocks"]):
-        at = plan["y_tiles"] * cx + 8 * number
+    for number, offset in enumerate(plan.y_blocks):
+        at = plan.y_tiles * cx + 8 * number
         lanes_out[0][at : at + 8, :] = block(offset)
-    for number, offset in enumerate(plan["own_blocks"]):
+    for number, offset in enumerate(plan.own_blocks):
         own_out[8 * number : 8 * number + 8, :] = block(offset)
     first_core = lax.axis_index("lev") == 0
-    for out, (for_first, for_second) in zip(block_outs, plan["pairs"]):
+    for out, (for_first, for_second) in zip(block_outs, plan.pairs):
         out[...] = block(jnp.where(first_core, for_first, for_second))
 
     owners, cap = cells.shape
@@ -151,8 +151,8 @@
     live = jnp.concatenate(live_parts, axis=1)
     cell_out[...] = cell
     live_out[...] = live
-    if plan["relay"]:
-        at = plan["y_tiles"] * cx + 8 * len(plan["y_blocks"])
+    if plan.relay:
+        at = plan.y_tiles * cx + 8 * len(plan.y_blocks)
         strips = owners * cap // LANES
         for number in range(strips):
             part = slice(number * LANES, (number + 1) * LANES)
@@ -162,7 +162,7 @@
     for number in (1, 0, 8):
         copies[number].wait()
     lane = iota((cx, cy), 1)
-    if plan["relay"]:
+    if plan.relay:
         edge = edge_of(0, cy)
         inner = jnp.where(edge == 0, 1, cy - 2)
         tiles = {name: LanePacker(lane, at) for name, at in zip("cdvwuk", (edge, inner, edge, inner, edge, edge))}
@@ -201,6 +201,10 @@
     copies[2].wait()
 
 
+class Plan(dict):
+    __getattr__ = dict.__getitem__
+
+
 class LanePacker:
     def __init__(self, lane, edge):
         self.lanes = lane.shape[1]
@@ -223,7 +227,7 @@
 def rows_kernel(plan, tracer, west, scale, blocks, *outs):
     carried, levels, cx, cy = tracer.shape
     head = (carried + 1) * levels
-    if plan["relay"]:
+    if plan.relay:
         tile = LanePacker(iota((cx, cy), 1), edge_of(0, cy))
         for t in range(carried):
             for level in range(levels):
@@ -239,8 +243,8 @@
             spot = carried * levels + level
             out[spot : spot + 1, :] = west[level, pl.ds(row, 1), :]
         out[head : head + 8, :] = jnp.broadcast_to(scale[pl.ds(row, 1), :], (8, cy))
-        if plan["x_blocks"][number] and not plan["relay"]:
-            at = 8 * plan["own_blocks"].index(plan["x_blocks"][number])
+        if plan.x_blocks[number] and not plan.relay:
+            at = 8 * plan.own_blocks.index(plan.x_blocks[number])
             out[head + 8 : head + 16, :] = blocks[at : at + 8, :]
 
 
@@ -248,17 +252,17 @@
     out[0 : head + 8, :] = rows[0 : head + 8, :]
     row = sent_row(plan, number, cx)
     out[head + 1 : head + 2, :] = y_got[pl.ds(row, 1), :]
-    near, far = plan["x_blocks"]
+    near, far = plan.x_blocks
     even_x = is_even("facex")
     offset = jnp.where(even_x if number == 0 else jnp.logical_not(even_x), near, far)
-    at = plan["y_tiles"] * cx + 8 * (offset - plan["y_blocks"][0])
+    at = plan.y_tiles * cx + 8 * (offset - plan.y_blocks[0])
     out[head + 8 : head + 24, :] = blocks[pl.ds(pl.multiple_of(8 * offset, 8), 16), :]
     out[head + 24 : head + 40, :] = y_got[pl.ds(pl.multiple_of(at, 8), 16), :]
 
 
 def beyond_kernel(plan, cx, blocks, y_got, *outs):
-    for out, offset in zip(outs, plan["x_ops"]):
-        at = plan["y_tiles"] * cx + 8 * (offset - plan["y_blocks"][0])
+    for out, offset in zip(outs, plan.x_ops):
+        at = plan.y_tiles * cx + 8 * (offset - plan.y_blocks[0])
         out[0:16, :] = blocks[8 * offset : 8 * offset + 16, :]
         out[16:32, :] = y_got[at : at + 16, :]
 
@@ -324,7 +328,7 @@
     base_out[0:cx, :] = tile.packed(0)
     base_out[cx : 2 * cx, :] = lanes[...]
     base_out[2 * cx :, :] = own[0:16, :]
-    at = plan["y_tiles"] * cx + 8 * len(plan["y_blocks"])
+    at = plan.y_tiles * cx + 8 * len(plan.y_blocks)
     strips = slots // LANES
     cell = jnp.concatenate([y_got[at + n : at + n + 1, :] for n in range(strips)], axis=1).astype(jnp.int32)
     live_out[...] = jnp.concatenate([y_got[at + strips + n : at + strips + n + 1, :] for n in range(strips)], axis=1)
@@ -396,18 +400,18 @@
 
 
 def sides(plan, first, second):
-    if plan["relay"]:
+    if plan.relay:
         return first, second
     even_x = is_even("facex")
     return jnp.where(even_x, second, first), jnp.where(even_x, first, second)
 
 
 def own_sides(plan, first, second):
-    return (second, first) if plan["relay"] else sides(plan, first, second)
+    return (second, first) if plan.relay else sides(plan, first, second)
 
 
 def sent_row(plan, number, rows):
-    if plan["relay"]:
+    if plan.relay:
         return rows - 1 if number == 0 else 0
     even_x = is_even("facex")
     return jnp.where(even_x if number == 0 else jnp.logical_not(even_x), rows - 1, 0)
@@ -432,7 +436,7 @@
 
 
 def seam_lanes(number, plan, sent, got, sent_wind, got_wind, carried, levels):
-    start = plan["lane_v"]
+    start = plan.lane_v
     faces = [spread_wind(wind, start, carried, levels) for wind in (sent_wind, got_wind)]
     return seam(number, sent, got, *faces)
 
@@ -462,10 +466,10 @@
     even_x = is_even("facex")
     from_west, from_east = (got[n][head + 8 : head + 40, :] for n in range(2))
     carriers = [
-        (plan["x_blocks"][0], jnp.where(even_x, from_east, from_west)),
-        (plan["x_blocks"][1], jnp.where(even_x, from_west, from_east)),
+        (plan.x_blocks[0], jnp.where(even_x, from_east, from_west)),
+        (plan.x_blocks[1], jnp.where(even_x, from_west, from_east)),
     ]
-    carriers += [(offset, ref[...]) for offset, ref in zip(plan["x_ops"], x_got)]
+    carriers += [(offset, ref[...]) for offset, ref in zip(plan.x_ops, x_got)]
     for offset, values in carriers:
         blocks[offset], rim_blocks[offset + 1] = block_at(values, 0), block_at(values, 8)
         rim_blocks[offset], blocks[offset + 1] = block_at(values, 16), block_at(values, 24)
@@ -478,14 +482,14 @@
     inner, lower, inverse, ratio, in_row, in_lane = refs[2:8]
     sent = refs[8:10]
     refs = refs[10:]
-    y_sent = refs[: plan["y_ops"]]
-    y_got = refs[plan["y_ops"] : 2 * plan["y_ops"]]
-    refs = refs[2 * plan["y_ops"] :]
-    if plan["relay"]:
+    y_sent = refs[: plan.y_ops]
+    y_got = refs[plan.y_ops : 2 * plan.y_ops]
+    refs = refs[2 * plan.y_ops :]
+    if plan.relay:
         rim_inverse, rim_ratio, rim_lower, pieces, rim_picks, parcel, rows_out, turn, rise = refs
     else:
         columns, live, own, *refs = refs
-        n_pairs = len(plan["pairs"])
+        n_pairs = len(plan.pairs)
         pair_got = refs[:n_pairs]
         swapped = refs[n_pairs] if n_pairs else None
         modeled_out, state_out = refs[-2:]
@@ -509,10 +513,10 @@
         jnp.maximum(face_east, 0.0) * summed(at_east) + jnp.minimum(face_east, 0.0) * summed(beyond_east)
     )
     lane_parts = []
-    for number in range(plan["y_ops"]):
+    for number in range(plan.y_ops):
         mine, beyond = y_sent[number][0:cx, :], y_got[number][0:cx, :]
-        if plan["relay"]:
-            faces = [pltpu.roll(values, cy - plan["lane_v"], 1) for values in (mine, beyond)]
+        if plan.relay:
+            faces = [pltpu.roll(values, cy - plan.lane_v, 1) for values in (mine, beyond)]
             total, spot_y = seam(number, mine, beyond, *faces)
         else:
             part, spot_y = seam_lanes(number, plan, mine, beyond, mine, beyond, carried, levels)
@@ -540,15 +544,15 @@
     picked = jnp.dot(high, picks, preferred_element_type=F32)
     picked = picked + jnp.dot(low, picks, preferred_element_type=F32)
 
-    if not plan["relay"]:
-        start = plan["y_tiles"] * cx
-        blocks = {0: own[0:8, :], plan["y_blocks"][0]: y_got[0][start : start + 8, :]}
+    if not plan.relay:
+        start = plan.y_tiles * cx
+        blocks = {0: own[0:8, :], plan.y_blocks[0]: y_got[0][start : start + 8, :]}
         for number in range(2):
-            offset = plan["x_blocks"][number]
+            offset = plan.x_blocks[number]
             if offset:
                 blocks[offset] = got[number][head + 8 : head + 16, :]
         first_core = lax.axis_index("lev") == 0
-        for number, (for_first, for_second) in enumerate(plan["pairs"]):
+        for number, (for_first, for_second) in enumerate(plan.pairs):
             mine = pair_got[number][...]
             other = swapped[8 * number : 8 * number + 8, :]
             if for_first == for_second:
@@ -579,8 +583,8 @@
     turn[0:1, :] = corners_west
     turn[cx - 1 : cx, :] = corners_east
     turned = jnp.transpose(turn[...])
-    ends = turned[plan["lane_c"] : plan["lane_c"] + levels]
-    end_face = turned[plan["lane_u"] : plan["lane_u"] + levels]
+    ends = turned[plan.lane_c : plan.lane_c + levels]
+    end_face = turned[plan.lane_u : plan.lane_u + levels]
     place = iota((levels, LANES), 1)
     cells, face_w, face_s, face_n, south_cells, north_cells = (pieces[n] for n in range(6))
     west_cells = jnp.where(place == 0, ends, pltpu.roll(cells, 1, 1))
@@ -652,7 +656,7 @@
 
 
 def surface_kernel(sizes, plan, carried, levels, *refs):
-    y_ops = plan["y_ops"]
+    y_ops = plan.y_ops
     near = refs[0]
     rims = refs[6 + y_ops : 6 + 2 * y_ops]
     rim_values = [[rim[...] for rim in rims] for _ in range(near.shape[0])]
@@ -664,7 +668,7 @@
 
 def weigh_kernel(sizes, plan, carried, levels, *refs):
     parcel, other, columns, live, rim_columns, rim_live, own, *refs = refs
-    x_got, refs = refs[: len(plan["x_ops"])], refs[len(plan["x_ops"]) :]
+    x_got, refs = refs[: len(plan.x_ops)], refs[len(plan.x_ops) :]
     in_row, in_lane, base, base_other, rim_rows, rim_base = refs[:6]
     cx, cy = base.shape[1:]
     slots = live.shape[1]
@@ -696,7 +700,7 @@
     west, south, scale = fields
     tracers = len(near)
     cx, cy = near[0].shape
-    spot_v = plan["lane_v"]
+    spot_v = plan.lane_v
     band = cy // sizes[0]
     per_tile = min(tracers, LANES // band)
     spot = carried * levels
@@ -712,7 +716,7 @@
     face_east = jnp.where(row == cx - 1, east_wind, pltpu.roll(face_west, cx - 1, 0))
     face_north = left(face_south)
     norths = []
-    for number in range(plan["y_ops"]):
+    for number in range(plan.y_ops):
         norths.append(even_y if number == 0 else jnp.logical_not(even_y))
         moved = pltpu.roll(y_got[number][0:cx, :], cy - 1 - spot_v, 1)
         keep = jnp.logical_and(lane == cy - 1, norths[number])
@@ -731,7 +735,7 @@
         values = near[t]
         north_side = left(values)
         south_side = right(values)
-        for number in range(plan["y_ops"]):
+        for number in range(plan.y_ops):
             rim = rim_values[t][number]
             at_north = jnp.logical_and(lane == cy - 1, norths[number])
             at_south = jnp.logical_and(lane == 0, jnp.logical_not(norths[number]))
@@ -748,11 +752,11 @@
     group_of_lane = lax.div(iota((rows, cy), 1), band)
     first_core = lax.axis_index("lev") == 0
     place = lax.axis_index("facex")
-    for out, (for_first, for_second) in zip(outs, plan["bands"]):
+    for out, (for_first, for_second) in zip(outs, plan.bands):
         offset = for_first if for_first == for_second else jnp.where(first_core, for_first, for_second)
         target = jnp.bitwise_xor(place, offset)
         count = carried if for_first == for_second else tracers
-        skip = carried if for_first == for_second != 0 and plan["cross"] else 0
+        skip = carried if for_first == for_second != 0 and plan.cross else 0
         for start in range(0, count, per_tile):
             tile = jnp.zeros((rows, cy), F32)
             for a in range(min(per_tile, count - start)):
@@ -778,7 +782,7 @@
     parts = []
     row_places = []
     for block, ((for_first, for_second), fetched, first) in zip(blocks, bands):
-        if plan["cross"] != fetched:
+        if plan.cross != fetched:
             for_first, for_second = for_second, for_first
         offset = for_first if for_first == for_second else jnp.where(first_core, for_first, for_second)
         start = jnp.bitwise_xor(place, offset) * cx
@@ -822,7 +826,7 @@
     sent = refs[5:7]
     got = refs[7:9]
     swapped, *refs = refs[9:]
-    y_ops = plan["y_ops"]
+    y_ops = plan.y_ops
     y_sent, y_got, winds_sent, winds_got = (refs[n * y_ops : (n + 1) * y_ops] for n in range(4))
     target, out, west_rows, east_rows, done = refs[-5:]
     carried, levels, cx, cy = tracer.shape
@@ -831,7 +835,7 @@
     face_west, _ = own_sides(plan, sent[0][spot:head, :], sent[1][spot:head, :])
     _, face_east = sides(plan, got[0][spot:head, :], got[1][spot:head, :])
     each = [got[number][0:spot, :] for number in range(2)]
-    if plan["cross"]:
+    if plan.cross:
         each = [swapped[number * spot : (number + 1) * spot, :] for number in range(2)]
     beyond_west, beyond_east = sides(plan, *each)
     _, at_east = own_sides(plan, sent[0][0:spot, :], sent[1][0:spot, :])
@@ -848,7 +852,7 @@
             n,
             plan,
             y_sent[n][0:cx, :],
-            y_got[n][cx : 2 * cx, :] if plan["relay"] else y_got[n][0:cx, :],
+            y_got[n][cx : 2 * cx, :] if plan.relay else y_got[n][0:cx, :],
             winds_sent[n][0:cx, :],
             winds_got[n][0:cx, :],
             carried,
@@ -937,7 +941,7 @@
         pairs = [(rest[n], rest[min(n + 1, len(rest) - 1)]) for n in range(0, len(rest), 2)]
     others = list(range(many_x - 1, 1, -1))
     bands = [(0, 0), (1, 1)] + [(others[n + 1], others[n]) for n in range(0, len(others), 2)]
-    return {
+    return Plan({
         "relay": relay,
         "cross": 1 if relay else 0,
         "x_blocks": x_blocks,
@@ -948,12 +952,12 @@
         "y_tiles": 2 if relay else 1,
         "pairs": pairs,
         "bands": bands,
-    }
+    })
 
 
 def lane_plan(plan, carried, levels):
     starts = {"c": 0, "d": levels, "v": 2 * levels, "w": 3 * levels, "u": 4 * levels}
-    if not plan["relay"]:
+    if not plan.relay:
         starts = {"v": carried * levels}
     return {"lane_" + name: start for name, start in starts.items()}
 
@@ -982,13 +986,13 @@
     taps, ll = regrid_index.shape[2:]
     plan.update(lane_plan(plan, carried, levels))
     head = (carried + 1) * levels
-    y_ops = plan["y_ops"]
+    y_ops = plan.y_ops
     band = cy // many_x
 
     def next_x(number):
         def rule(x, y, c):
-            step = 1 if (plan["relay"] or x % 2 == 0) == (number == 0) else -1
-            return ((x + step) % many_x, y, c ^ plan["cross"])
+            step = 1 if (plan.relay or x % 2 == 0) == (number == 0) else -1
+            return ((x + step) % many_x, y, c ^ plan.cross)
 
         return rule
 
@@ -1011,15 +1015,15 @@
 
     strips = slots // LANES
     plan["parcel"] = -(-2 * strips // 8) * 8
-    extra = 40 if plan["relay"] else 16
+    extra = 40 if plan.relay else 16
     row_shapes = [shape(head + extra, cy)] * 2
-    y_rows = plan["y_tiles"] * cx + 8 * len(plan["y_blocks"]) + (plan["parcel"] if plan["relay"] else 0)
+    y_rows = plan.y_tiles * cx + 8 * len(plan.y_blocks) + (plan.parcel if plan.relay else 0)
     lane_shapes = [shape(y_rows if n == 0 else cx, cy) for n in range(y_ops)]
     packed = call(
         functools.partial(pack_kernel, sizes, plan),
         lane_shapes
-        + [shape(8 * len(plan["own_blocks"]), LANES)]
-        + [shape(8, LANES)] * len(plan["pairs"])
+        + [shape(8 * len(plan.own_blocks), LANES)]
+        + [shape(8, LANES)] * len(plan.pairs)
         + [shape(1, slots, dtype=jnp.int32), shape(1, slots)]
         + [shape(*a.shape) for a in (tracer, west_courant, south_courant, emission_scale, mixing)],
         [
@@ -1050,7 +1054,7 @@
     own_blocks = packed[y_ops]
     pair_sent = packed[1 + y_ops : -7]
     cell, live, tracer, west_courant, south_courant, emission_scale, mixing = packed[-7:]
-    lanes_got = [exchange(lanes_sent[n], sizes, next_y(n, plan["cross"])) for n in range(y_ops)]
+    lanes_got = [exchange(lanes_sent[n], sizes, next_y(n, plan.cross)) for n in range(y_ops)]
     held, *_ = lax.optimization_barrier((tracer, *lanes_sent))
     inverse, lower, ratio, base, inner, parts, columns, in_row, in_lane = call(
         functools.partial(factor_kernel, sizes),
@@ -1072,7 +1076,7 @@
     rows_sent = list(
         call(
             functools.partial(rows_kernel, plan),
-            row_shapes + ([shape(cx, cy)] if plan["relay"] else []),
+            row_shapes + ([shape(cx, cy)] if plan.relay else []),
             [tracer, west_courant, emission_scale, own_blocks],
             "rows",
             100000,
@@ -1082,15 +1086,15 @@
 
     def band_shape(first, second):
         count = carried if first == second else 2 * carried
-        spare = 8 if plan["relay"] and first == second != 0 else 0
+        spare = 8 if plan.relay and first == second != 0 else 0
         return shape(-(-count // per_tile) * (cx + 8) + spare, cy)
 
-    band_shapes = [band_shape(*b) for b in plan["bands"]]
+    band_shapes = [band_shape(*b) for b in plan.bands]
     fields = [west_courant[0], south_courant[0], emission_scale]
     observe = functools.partial(
         call, functools.partial(observe_kernel, sizes, plan, carried), name="observe", flops=2000000
     )
-    if plan["relay"]:
+    if plan.relay:
         base, *lanes_got = lax.optimization_barrier((base, *lanes_got))
         lanes_each = rows_sent.pop()
         base_other = other_core(base)
@@ -1108,12 +1112,12 @@
         rows_sent = [relay(0), relay(1)]
         x_sent = call(
             functools.partial(beyond_kernel, plan, cx),
-            [shape(32, LANES)] * len(plan["x_ops"]),
+            [shape(32, LANES)] * len(plan.x_ops),
             [own_blocks, lanes_got[0]],
             "beyond",
             10000,
         )
-        x_got = [exchange(s, sizes, jump(d, d, 1)) for s, d in zip(x_sent, plan["x_ops"])]
+        x_got = [exchange(s, sizes, jump(d, d, 1)) for s, d in zip(x_sent, plan.x_ops)]
         rows_got = [exchange(rows_sent[n], sizes, next_x(n)) for n in range(2)]
         held_y, *_ = lax.optimization_barrier((lanes_got[0], *rows_sent))
         rim = call(
@@ -1157,7 +1161,7 @@
         held, *_ = lax.optimization_barrier((tracer, *band_sent))
     else:
         rows_got = [exchange(rows_sent[n], sizes, next_x(n)) for n in range(2)]
-        pair_got = [exchange(s, sizes, jump(*p)) for s, p in zip(pair_sent, plan["pairs"])]
+        pair_got = [exchange(s, sizes, jump(*p)) for s, p in zip(pair_sent, plan.pairs)]
         base_other = other_core(base)
         modeled, state = observe(
             [shape(1, slots), shape(2, slots)],
@@ -1203,11 +1207,11 @@
     band_got = [
         s
         if first == second == 0
-        else exchange(s, sizes, jump(first * many_y, second * many_y, plan["cross"]))
-        for s, (first, second) in zip(band_sent, plan["bands"])
+        else exchange(s, sizes, jump(first * many_y, second * many_y, plan.cross))
+        for s, (first, second) in zip(band_sent, plan.bands)
     ]
     tables = [regrid_index.reshape(taps, ll), regrid_weight.reshape(taps, ll)]
-    kinds = [first == second for first, second in plan["bands"]]
+    kinds = [first == second for first, second in plan.bands]
 
     def regridded(bands, blocks, *more):
         return call(
@@ -1218,13 +1222,13 @@
             1000000,
         )[0]
 
-    near = [(pair, 0, 0) for pair, kind in zip(plan["bands"], kinds) if kind]
-    far = [pair for pair, kind in zip(plan["bands"], kinds) if not kind]
+    near = [(pair, 0, 0) for pair, kind in zip(plan.bands, kinds) if kind]
+    far = [pair for pair, kind in zip(plan.bands, kinds) if not kind]
     near_got = [got for got, kind in zip(band_got, kinds) if kind]
     far_got = [got for got, kind in zip(band_got, kinds) if not kind]
     advanced, far_got = lax.optimization_barrier((advanced, far_got))
-    far_fetched = [other_core(got[: cx + 8] if plan["relay"] else got) for got in far_got]
-    mine = carried if plan["cross"] else 0
+    far_fetched = [other_core(got[: cx + 8] if plan.relay else got) for got in far_got]
+    mine = carried if plan.cross else 0
     partial = [regridded([(pair, 0, mine) for pair in far], far_got)] if far else []
     near_got, partial = lax.optimization_barrier((near_got, partial))
     partial = regridded(near, near_got, *partial)

time: 25.4 us -> 25.4 us (level)
  no operation moved by 1% of the time
where the time goes in v11:
time: 25.4 us; the launch traced here: 25.2 us
  starting transfers between devices  12 us (47%)
  Pallas kernels  8.25 us (32%)
  waiting for transfers between devices  4.21 us (17%)
  between operations  0.72 us (3%)
    ppermute x11, starting transfers between devices, exchange(): return lax.ppermute(values, GROUP, pairs)  12 us
    pallas_call x13, Pallas kernels, call(): pl.pallas_call(body, out_shape=outs, in_specs=[pl.BlockSpec(memory_space=...  8.25 us
    ppermute x11, waiting for transfers between devices, exchange(): return lax.ppermute(values, GROUP, pairs)  4.21 us
  transfers between devices with their start and end apart: 11, of which 7 were waited for; matrix products, arithmetic and copies ran while one was open for 0% of the time, Pallas kernels for 22%

profile of v11, /device:TPU:0, one launch (start us, length us, event | category | flops | bytes accessed | tf_op | source)
XLA Modules:
  0.0 25.2 jit_solution(2483985895354278782)
XLA Ops:
  0.6 1.8 %pack.1 = (f32[88,128]{1,0:T(8,128)S(1)}, f32[64,128]{1,0:T(8,128)S(1)}, s32[1,256]{1,0:T(1,128)S(1)}, f32[1,256]{1,0:T(1,128)S(1)}, f32[4,24,16,128]{3,2,1,0:T(...) custom-call(f32[4,24,16,128]{3,2,1,0:T(8,128)} %refs_0_.1, ...), custom_call_target="tpu_custom_call" | custom-call | flops 100000 | bytes 2860064 | tf_op jit(solution)/shard_map/pack/pallas_call | solution.py:22
  2.4 0.0 copy-start
  2.5 2.4 %collective-permute-start = (f32[88,128]{1,0:T(8,128)S(1)}, f32[88,128]{1,0:T(8,128)S(1)}, u32[]{:S(2)}, u32[]{:S(2)}) collective-permute-start(f32[88,128]{1,0:T(8,128)S(1)} %get-tuple-element.55.y_sent.refs_10_.refs_12_), channel_id=1, source_target_pairs={{0,3},{1,2},{2,1},{3,0},{4,7},{5,6},{6,5},{7,4},{8,11},{9,10},{10,... | collective-permute-start | bytes 135176 | tf_op jit(solution)/shard_map/ppermute | solution.py:922
  4.9 0.3 %rows.1 = (f32[160,128]{1,0:T(8,128)S(1)}, f32[160,128]{1,0:T(8,128)S(1)}, f32[16,128]{1,0:T(8,128)S(1)}) custom-call(f32[4,24,16,128]{3,2,1,0:T(8,128)S(1)} %get-tuple-element.90.tracer.refs_0_, f32[24,16,128]{2,1,0:T(8,128)S(1)} %get-tuple-element.51.west.refs_1_, f32[16,128]{1,0:T(8,128)S(1)} %get-tuple-element.52.scale.refs_16_, ...), custom_call_target="tpu_custom_call" | custom-call | flops 100000 | bytes 1196032 | tf_op jit(solution)/shard_map/rows/pallas_call | solution.py:22
  5.2 0.0 copy-done
  5.2 0.7 %factor.1 = (f32[24,16,128]{2,1,0:T(8,128)S(1)}, f32[24,16,128]{2,1,0:T(8,128)S(1)}, f32[24,16,128]{2,1,0:T(8,128)S(1)}, f32[4,16,128]{2,1,0:T(8,128)S(1)}, f32[...) custom-call(f32[4,24,16,128]{3,2,1,0:T(8,128)S(1)} %get-tuple-elemen, ...), custom_call_target="tpu_custom_call" | custom-call | flops 3000000 | bytes 4129792 | tf_op jit(solution)/shard_map/factor/pallas_call | solution.py:22
  5.9 1.0 %collective-permute-done.y_got.refs_11_.refs_19_.refs_13_ = f32[88,128]{1,0:T(8,128)S(1)} collective-permute-done((f32[88,128]{1,0:T(8,128)S(1)}, f32[88,128]{1,0:T(8,128)S(1)}, u32[]{:S(2)}, u32[]{:S(2)}) %collective-permute-start) | collective-permute-done | bytes 45088 | tf_op jit(solution)/shard_map/ppermute | solution.py:922
  6.9 2.3 %collective-permute-start.1 = (f32[160,128]{1,0:T(8,128)S(1)}, f32[160,128]{1,0:T(8,128)S(1)}, u32[]{:S(2)}, u32[]{:S(2)}) collective-permute-start(f32[160,128]{1,0:T(8,128)S(1)} %relay.2.refs_8_.refs_5_), channel_id=1, source_target_pairs={{0,5},{1,4},{2,7},{3,6},{4,9},{5,8},{6,11},{7,10},{8,13},{9,12},{1... | collective-permute-start | bytes 245768 | tf_op jit(solution)/shard_map/ppermute | solution.py:922
  9.2 2.1 %collective-permute-start.2 = (f32[160,128]{1,0:T(8,128)S(1)}, f32[160,128]{1,0:T(8,128)S(1)}, u32[]{:S(2)}, u32[]{:S(2)}) collective-permute-start(f32[160,128]{1,0:T(8,128)S(1)} %relay.3.refs_9_.refs_6_), channel_id=1, source_target_pairs={{0,13},{1,12},{2,15},{3,14},{4,1},{5,0},{6,3},{7,2},{8,5},{9,4},{1... | collective-permute-start | bytes 245768 | tf_op jit(solution)/shard_map/ppermute | solution.py:922
  11.3 0.4 %collective-permute-start.3 = (f32[4,16,128]{2,1,0:T(8,128)S(1)}, f32[4,16,128]{2,1,0:T(8,128)S(1)}, u32[]{:S(2)}, u32[]{:S(2)}) collective-permute-start(f32[4,16,128]{2,1,0:T(8,128)S(1)} %get-tuple-element.70.base.refs_10_), channel_id=1, source_target_pairs={{0,1},{1,0},{2,3},{3,2},{4,5},{5,4},{6,7},{7,6},{8,9},{9,8},{10,11... | collective-permute-start | bytes 98312 | tf_op jit(solution)/shard_map/ppermute | solution.py:922
  11.7 0.7 %collective-permute-start.6 = (f32[32,128]{1,0:T(8,128)S(1)}, f32[32,128]{1,0:T(8,128)S(1)}, u32[]{:S(2)}, u32[]{:S(2)}) collective-permute-start(f32[32,128]{1,0:T(8,128)S(1)} %beyond.1), channel_id=1, source_target_pairs={{0,9},{1,8},{2,11},{3,10},{4,13},{5,12},{6,15},{7,14},{8,1},{9,0},... | collective-permute-start | bytes 49160 | tf_op jit(solution)/shard_map/ppermute | solution.py:922
  12.5 0.1 collective-permute-done.3.base_other.refs_11_
  12.6 0.4 %rim.1 = (f32[24,128]{1,0:T(8,128)S(1)}, f32[24,128]{1,0:T(8,128)S(1)}, f32[24,128]{1,0:T(8,128)S(1)}, f32[6,24,128]{2,1,0:T(8,128)S(1)}, f32[24,256]{1,0:T(8,12...) custom-call(f32[88,128]{1,0:T(8,128)S(1)} %get-tuple-element.55.y_se, ...), custom_call_target="tpu_custom_call" | custom-call | flops 400000 | bytes 504832 | tf_op jit(solution)/shard_map/rim/pallas_call | solution.py:22
  13.0 1.7 %collective-permute-start.5 = (f32[48,128]{1,0:T(8,128)S(1)}, f32[48,128]{1,0:T(8,128)S(1)}, u32[]{:S(2)}, u32[]{:S(2)}) collective-permute-start(f32[48,128]{1,0:T(8,128)S(1)} %get-tuple-element.78), channel_id=1, source_target_pairs={{0,2},{1,3},{2,0},{3,1},{4,6},{5,7},{6,4},{7,5},{8,10},{9,11},{10,... | collective-permute-start | bytes 73736 | tf_op jit(solution)/shard_map/ppermute | solution.py:922
  14.7 0.0 collective-permute-done.1.refs_0_.refs_17_.refs_7_
  14.7 0.7 %collective-permute-done.2.refs_1_.refs_18_.refs_8_ = f32[160,128]{1,0:T(8,128)S(1)} collective-permute-done((f32[160,128]{1,0:T(8,128)S(1)}, f32[160,128]{1,0:T(8,128)S(1)}, u32[]{:S(2)}, u32[]{:S(2)}) %collective-permute-start.2) | collective-permute-done | bytes 81952 | tf_op jit(solution)/shard_map/ppermute | solution.py:922
  15.5 0.6 %observe.1 = (f32[48,256]{1,0:T(8,128)S(1)}, f32[192,128]{1,0:T(8,128)S(1)}) custom-call(f32[160,128]{1,0:T(8,128)S(1)} %collective-permute-done.1.refs_0_.refs_17_.refs_7_, f32[160,128]{1,0:T(8,128)S(1)} %collective-permute-done.2.refs_1_.refs_18_.refs_8_, f32[24,16,128]{2,1,0:T(8,128)S(1)} %get-tuple-element.63.refs_2_, ...), custom_call_target="tpu_custom_call" | custom-call | flops 2000000 | bytes 1740800 | tf_op jit(solution)/shard_map/observe/pallas_call | solution.py:22
  16.1 0.2 collective-permute-start.4
  16.3 0.4 %collective-permute-start.7 = (f32[192,128]{1,0:T(8,128)S(1)}, f32[192,128]{1,0:T(8,128)S(1)}, u32[]{:S(2)}, u32[]{:S(2)}) collective-permute-start(f32[192,128]{1,0:T(8,128)S(1)} %get-tuple-element.92), channel_id=1, source_target_pairs={{0,1},{1,0},{2,3},{3,2},{4,5},{5,4},{6,7},{7,6},{8,9},{9,8},{10,11... | collective-permute-start | bytes 294920 | tf_op jit(solution)/shard_map/ppermute | solution.py:922
  16.6 0.0 collective-permute-done.6.refs_7_
  16.6 0.3 %collective-permute-done.5.refs_13_.refs_11_ = f32[48,128]{1,0:T(8,128)S(1)} collective-permute-done((f32[48,128]{1,0:T(8,128)S(1)}, f32[48,128]{1,0:T(8,128)S(1)}, u32[]{:S(2)}, u32[]{:S(2)}) %collective-permute-start.5) | collective-permute-done | bytes 24608 | tf_op jit(solution)/shard_map/ppermute | solution.py:922
  16.9 0.4 %collective-permute-done.4.refs_1_ = f32[48,256]{1,0:T(8,128)S(1)} collective-permute-done((f32[48,256]{1,0:T(8,128)S(1)}, f32[48,256]{1,0:T(8,128)S(1)}, u32[]{:S(2)}, u32[]{:S(2)}) %collective-permute-start.4) | collective-permute-done | bytes 49184 | tf_op jit(solution)/shard_map/ppermute | solution.py:922
  17.4 0.4 %weigh.1 = (f32[24,128]{1,0:T(8,128)S(1)}, f32[32,128]{1,0:T(8,128)S(1)}, f32[48,128]{1,0:T(8,128)S(1)}) custom-call(f32[48,256]{1,0:T(8,128)S(1)} %get-tuple-element.77.refs_0_, f32[48,256]{1,0:T(8,128)S(1)} %collective-permute-done.4.refs_1_, f32[24,256]{1,0:T(8,128)S(1)} %get-tuple-element.80.refs_2_, f32[1,256]{1,0:T(1,128)S(1)} %get-tuple-element.81.refs_3_, ...), custom_call_target="tpu_custom_call" | custom-call | flops 500000 | bytes 739328 | tf_op jit(solution)/shard_map/weigh/pallas_call | solution.py:22
  17.8 0.9 %collective-permute-start.8 = (f32[48,128]{1,0:T(8,128)S(1)}, f32[48,128]{1,0:T(8,128)S(1)}, u32[]{:S(2)}, u32[]{:S(2)}) collective-permute-start(f32[48,128]{1,0:T(8,128)S(1)} %get-tuple-element.89), channel_id=1, source_target_pairs={{0,9},{1,12},{2,11},{3,14},{4,13},{5,8},{6,15},{7,10},{8,1},{9,4},... | collective-permute-start | bytes 73736 | tf_op jit(solution)/shard_map/ppermute | solution.py:922
  18.7 0.7 %collective-permute-start.10 = (f32[32,128]{1,0:T(8,128)S(1)}, f32[32,128]{1,0:T(8,128)S(1)}, u32[]{:S(2)}, u32[]{:S(2)}) collective-permute-start(f32[32,128]{1,0:T(8,128)S(1)} %get-tuple-element.88), channel_id=1, source_target_pairs={{0,5},{1,4},{2,7},{3,6},{4,1},{5,0},{6,3},{7,2},{8,13},{9,12},{10,... | collective-permute-start | bytes 49160 | tf_op jit(solution)/shard_map/ppermute | solution.py:922
  19.5 0.0 collective-permute-done.7.refs_9_
  19.5 2.1 %advance.1 = f32[4,24,16,128]{3,2,1,0:T(8,128)} custom-call(f32[4,24,16,128]{3,2,1,0:T(8,128)S(1)} %get-tuple-element.90.tracer.refs_0_, f32[5,24,16,128]{3,2,1,0:T(8,128)S(1)} %get-tuple-element.91.refs_1_, f32[24,16,128]{2,1,0:T(8,128)S(1)} %get-tuple-element.64.refs_3_.refs_2_, f32[24,16,128]{2,1,0:T(8,128)S(1)} %get-tuple-element.65.refs_4_.refs_3_, ...), custom_call_target="tpu_custom_call" | custom-call | flops 6000000 | bytes 3694592 | tf_op jit(solution)/shard_map/advance/pallas_call | solution.py:22
  21.6 0.0 copy-start.1
  21.6 0.0 copy-start.2
  21.6 1.5 %collective-permute-done.8.refs_2_ = f32[48,128]{1,0:T(8,128)S(1)} collective-permute-done((f32[48,128]{1,0:T(8,128)S(1)}, f32[48,128]{1,0:T(8,128)S(1)}, u32[]{:S(2)}, u32[]{:S(2)}) %collective-permute-start.8) | collective-permute-done | bytes 24608 | tf_op jit(solution)/shard_map/ppermute | solution.py:922
  23.0 0.1 collective-permute-start.9
  23.1 0.0 copy-done.1
  23.1 0.0 copy-done.2
  23.1 0.4 %regrid.3.refs_4_ = f32[4,128]{1,0:T(4,128)S(1)} custom-call(s32[16,128]{1,0:T(8,128)S(1)} %bitcast.14, f32[16,128]{1,0:T(8,128)S(1)} %bitcast.17, f32[48,128]{1,0:T(8,128)S(1)} %collective-permute-done.8.refs_2_), custom_call_target="tpu_custom_call" | custom-call | flops 1000000 | bytes 43008 | tf_op jit(solution)/shard_map/regrid/pallas_call | solution.py:22
  23.5 0.0 collective-permute-done.10.refs_3_
  23.5 0.5 %regrid.4.refs_3_ = f32[4,128]{1,0:T(4,128)S(1)} custom-call(s32[16,128]{1,0:T(8,128)S(1)} %bitcast.15, f32[16,128]{1,0:T(8,128)S(1)} %bitcast.18, f32[24,128]{1,0:T(8,128)S(1)} %get-tuple-element.95.refs_2_, f32[32,128]{1,0:T(8,128)S(1)} %collective-permute-done.10.refs_3_, f32[4,128]{1,0:T(4,128)S(1)} %regrid.3.refs_4_), custom_call_target="tpu_custom_call" | custom-call | flops 1000000 | bytes 49152 | tf_op jit(solution)/shard_map/regrid/pallas_call | solution.py:22
  24.0 0.2 collective-permute-done.9.refs_2_
  24.2 1.0 %regrid.5 = f32[4,128]{1,0:T(4,128)} custom-call(s32[16,128]{1,0:T(8,128)S(1)} %bitcast.16, f32[16,128]{1,0:T(8,128)S(1)} %bitcast.19, f32[24,128]{1,0:T(8,128)S(1)} %collective-permute-done.9.refs_2_, f32[4,128]{1,0:T(4,128)S(1)} %regrid.4.refs_3_), custom_call_target="tpu_custom_call" | custom-call | flops 1000000 | bytes 32768 | tf_op jit(solution)/shard_map/regrid/pallas_call | solution.py:22
  (5 shorter events, 0.0 us)
Async XLA Ops:
  2.4 2.8 %copy-start = (f32[4,24,16,128]{3,2,1,0:T(8,128)S(1)}, f32[4,24,16,128]{3,2,1,0:T(8,128)}, u32[]{:S(2)}) copy-start(f32[4,24,16,128]{3,2,1,0:T(8,128)} %refs_4_.1) | copy-start | bytes 2359300
  2.5 4.5 %collective-permute-start = (f32[88,128]{1,0:T(8,128)S(1)}, f32[88,128]{1,0:T(8,128)S(1)}, u32[]{:S(2)}, u32[]{:S(2)}) collective-permute-start(f32[88,128]{1,0:T(8,128)S(1)} %get-tuple-element.55.y_sent.refs_10_.refs_12_), channel_id=1, source_target_pairs={{0,3},{1,2},{2,1},{3,0},{4,7},{5,6},{6,5},{7,4},{8,11},{9,10},{10,... | collective-permute-start | bytes 135176 | tf_op jit(solution)/shard_map/ppermute | solution.py:922
  6.9 7.8 %collective-permute-start.1 = (f32[160,128]{1,0:T(8,128)S(1)}, f32[160,128]{1,0:T(8,128)S(1)}, u32[]{:S(2)}, u32[]{:S(2)}) collective-permute-start(f32[160,128]{1,0:T(8,128)S(1)} %relay.2.refs_8_.refs_5_), channel_id=1, source_target_pairs={{0,5},{1,4},{2,7},{3,6},{4,9},{5,8},{6,11},{7,10},{8,13},{9,12},{1... | collective-permute-start | bytes 245768 | tf_op jit(solution)/shard_map/ppermute | solution.py:922
  9.2 6.2 %collective-permute-start.2 = (f32[160,128]{1,0:T(8,128)S(1)}, f32[160,128]{1,0:T(8,128)S(1)}, u32[]{:S(2)}, u32[]{:S(2)}) collective-permute-start(f32[160,128]{1,0:T(8,128)S(1)} %relay.3.refs_9_.refs_6_), channel_id=1, source_target_pairs={{0,13},{1,12},{2,15},{3,14},{4,1},{5,0},{6,3},{7,2},{8,5},{9,4},{1... | collective-permute-start | bytes 245768 | tf_op jit(solution)/shard_map/ppermute | solution.py:922
  11.3 1.3 %collective-permute-start.3 = (f32[4,16,128]{2,1,0:T(8,128)S(1)}, f32[4,16,128]{2,1,0:T(8,128)S(1)}, u32[]{:S(2)}, u32[]{:S(2)}) collective-permute-start(f32[4,16,128]{2,1,0:T(8,128)S(1)} %get-tuple-element.70.base.refs_10_), channel_id=1, source_target_pairs={{0,1},{1,0},{2,3},{3,2},{4,5},{5,4},{6,7},{7,6},{8,9},{9,8},{10,11... | collective-permute-start | bytes 98312 | tf_op jit(solution)/shard_map/ppermute | solution.py:922
  11.7 4.9 %collective-permute-start.6 = (f32[32,128]{1,0:T(8,128)S(1)}, f32[32,128]{1,0:T(8,128)S(1)}, u32[]{:S(2)}, u32[]{:S(2)}) collective-permute-start(f32[32,128]{1,0:T(8,128)S(1)} %beyond.1), channel_id=1, source_target_pairs={{0,9},{1,8},{2,11},{3,10},{4,13},{5,12},{6,15},{7,14},{8,1},{9,0},... | collective-permute-start | bytes 49160 | tf_op jit(solution)/shard_map/ppermute | solution.py:922
  13.0 3.9 %collective-permute-start.5 = (f32[48,128]{1,0:T(8,128)S(1)}, f32[48,128]{1,0:T(8,128)S(1)}, u32[]{:S(2)}, u32[]{:S(2)}) collective-permute-start(f32[48,128]{1,0:T(8,128)S(1)} %get-tuple-element.78), channel_id=1, source_target_pairs={{0,2},{1,3},{2,0},{3,1},{4,6},{5,7},{6,4},{7,5},{8,10},{9,11},{10,... | collective-permute-start | bytes 73736 | tf_op jit(solution)/shard_map/ppermute | solution.py:922
  16.1 1.3 %collective-permute-start.4 = (f32[48,256]{1,0:T(8,128)S(1)}, f32[48,256]{1,0:T(8,128)S(1)}, u32[]{:S(2)}, u32[]{:S(2)}) collective-permute-start(f32[48,256]{1,0:T(8,128)S(1)} %get-tuple-element.77.refs_0_), channel_id=1, source_target_pairs={{0,1},{1,0},{2,3},{3,2},{4,5},{5,4},{6,7},{7,6},{8,9},{9,8},{10,11... | collective-permute-start | bytes 147464 | tf_op jit(solution)/shard_map/ppermute | solution.py:922
  16.3 3.2 %collective-permute-start.7 = (f32[192,128]{1,0:T(8,128)S(1)}, f32[192,128]{1,0:T(8,128)S(1)}, u32[]{:S(2)}, u32[]{:S(2)}) collective-permute-start(f32[192,128]{1,0:T(8,128)S(1)} %get-tuple-element.92), channel_id=1, source_target_pairs={{0,1},{1,0},{2,3},{3,2},{4,5},{5,4},{6,7},{7,6},{8,9},{9,8},{10,11... | collective-permute-start | bytes 294920 | tf_op jit(solution)/shard_map/ppermute | solution.py:922
  17.8 5.3 %collective-permute-start.8 = (f32[48,128]{1,0:T(8,128)S(1)}, f32[48,128]{1,0:T(8,128)S(1)}, u32[]{:S(2)}, u32[]{:S(2)}) collective-permute-start(f32[48,128]{1,0:T(8,128)S(1)} %get-tuple-element.89), channel_id=1, source_target_pairs={{0,9},{1,12},{2,11},{3,14},{4,13},{5,8},{6,15},{7,10},{8,1},{9,4},... | collective-permute-start | bytes 73736 | tf_op jit(solution)/shard_map/ppermute | solution.py:922
  18.7 4.8 %collective-permute-start.10 = (f32[32,128]{1,0:T(8,128)S(1)}, f32[32,128]{1,0:T(8,128)S(1)}, u32[]{:S(2)}, u32[]{:S(2)}) collective-permute-start(f32[32,128]{1,0:T(8,128)S(1)} %get-tuple-element.88), channel_id=1, source_target_pairs={{0,5},{1,4},{2,7},{3,6},{4,1},{5,0},{6,3},{7,2},{8,13},{9,12},{10,... | collective-permute-start | bytes 49160 | tf_op jit(solution)/shard_map/ppermute | solution.py:922
  21.6 1.6 %copy-start.1 = (s32[1,1,16,128]{3,2,1,0:T(8,128)S(1)}, s32[1,1,16,128]{3,2,1,0:T(8,128)}, u32[]{:S(2)}) copy-start(s32[1,1,16,128]{3,2,1,0:T(8,128)} %param.24) | copy-start | bytes 24580
  21.6 1.6 %copy-start.2 = (f32[1,1,16,128]{3,2,1,0:T(8,128)S(1)}, f32[1,1,16,128]{3,2,1,0:T(8,128)}, u32[]{:S(2)}) copy-start(f32[1,1,16,128]{3,2,1,0:T(8,128)} %param.25) | copy-start | bytes 24580
  23.0 1.2 %collective-permute-start.9 = (f32[24,128]{1,0:T(8,128)S(1)}, f32[24,128]{1,0:T(8,128)S(1)}, u32[]{:S(2)}, u32[]{:S(2)}) collective-permute-start(f32[24,128]{1,0:T(8,128)S(1)} %slice.11), channel_id=1, source_target_pairs={{0,1},{1,0},{2,3},{3,2},{4,5},{5,4},{6,7},{7,6},{8,9},{9,8},{10,11... | collective-permute-start | bytes 36872 | tf_op jit(solution)/shard_map/ppermute | solution.py:922
